TPU v7x, 32 devices: a whole 2x2x4 slice. The times are simulated.
32 devices in a mesh: dp: 4 (over y, x), mp: 8 (over z, core).
Axes of the slice: x: 2, y: 2, z: 4, core: 2. Of those that a mesh axis runs over, the one named last changes fastest.
Arguments:
- features: bfloat16 [2, 5120, 9216], P(None, 'dp', 'mp'), may hold values from -6 to 6
- counts: int32 [512], P('dp'), may hold values from 1 to 10, as said below
- weights: float32 [2, 9216, 4096], P(None, 'dp', 'mp'), may hold values from -0.09375 to 0.09375
- small_params: float32 [6, 4096], P(None, 'mp'), may hold values from 0.2 to 1
- out_grad: bfloat16 [2, 5120, 4096], P(None, 'dp', 'mp'), may hold values from -6 to 6
- moment_one: float32 [2, 9216, 4096], P(None, 'dp', 'mp'), may hold values from -128 to 128
- moment_two: float32 [2, 9216, 4096], P(None, 'dp', 'mp'), may hold values from 512 to 2048
- average: float32 [2, 9216, 4096], P(None, 'dp', 'mp'), may hold values from -0.0625 to 0.0625
- basis_left: float32 [2, 144, 64, 64, 64], P(None, 'dp', 'mp'), may hold values from -0.75 to 0.75
- basis_right: float32 [2, 144, 64, 64, 64], P(None, 'dp', 'mp'), may hold values from -0.75 to 0.75
- small_moment_one: float32 [6, 4096], P(None, 'mp'), may hold values from -128 to 128
- small_moment_two: float32 [6, 4096], P(None, 'mp'), may hold values from 512 to 2048
- small_average: float32 [6, 4096], P(None, 'mp'), may hold values from 0.2 to 1
Outputs:
- stitched: bfloat16 [2, 5120, 4096], P(None, 'dp')
- d_features: bfloat16 [2, 5120, 9216], P(None, 'dp', 'mp')
- new_moment_one: float32 [2, 9216, 4096], P(None, 'dp', 'mp')
- new_moment_two: float32 [2, 9216, 4096], P(None, 'dp', 'mp')
- new_weights: float32 [2, 9216, 4096], P(None, 'dp', 'mp')
- new_average: float32 [2, 9216, 4096], P(None, 'dp', 'mp')
- weights_copy: bfloat16 [2, 9216, 4096], P(None, 'dp', 'mp')
- small_new_one: float32 [6, 4096], P(None, 'mp')
- small_new_two: float32 [6, 4096], P(None, 'mp')
- small_new: float32 [6, 4096], P(None, 'mp')
- small_new_average: float32 [6, 4096], P(None, 'mp')
Inputs may be any that keep to these rules, and one draw needn't show every extreme that they name: `counts`: the images of one index of dp hold at most 1280 crops together, and some index holds exactly 1280; some image has 10 crops and some has 1.
All inputs are finite; a program needn't handle non-finite values.
Results may differ from a plain program's by a relative error of at most 0.0061.
Values may be sent and summed in bfloat16 or wider, within the bound.
A program may use at most 512 MiB of HBM per device.

v0:
```python
import jax
import jax.numpy as jnp
from jax import lax
from jax.sharding import PartitionSpec as P

BLOCK = 64
STEP = 5


beta_one = 0.5
beta_two = 0.5
ema_decay = 0.5
rate_main = 0.01
rate_small = 0.05
decay_weight = 0.01
eps = 1e-08


def stitch_local(product, small, live_rows):
    pre_act = product + small[0:2][:, None, :]
    activated = jax.nn.gelu(pre_act, approximate=True)
    first = small[2] * activated[0] + small[3] * activated[1]
    second = small[4] * activated[0] + small[5] * activated[1]
    return jnp.stack([first, second]) * live_rows[None, :, None]


def adam_part(moment_a, moment_b, grad):
    first = beta_one * moment_a + (1.0 - beta_one) * grad
    second = beta_two * moment_b + (1.0 - beta_two) * grad * grad
    direction = first / (1.0 - beta_one**STEP) / (jnp.sqrt(second / (1.0 - beta_two**STEP)) + eps)
    return (first, second, direction)


def body(
    features,
    counts,
    weights,
    small_params,
    out_grad,
    moment_one,
    moment_two,
    average,
    basis_left,
    basis_right,
    small_moment_one,
    small_moment_two,
    small_average,
):
    slot_count = features.shape[1]
    total = jnp.sum(counts)
    live_rows = (jnp.arange(slot_count, dtype=jnp.int32) < total).astype(jnp.float32)
    weights_low = lax.all_gather(weights.astype(jnp.bfloat16), "dp", axis=1, tiled=True)
    feats_full = lax.all_gather(features, "mp", axis=2, tiled=True)
    product = jnp.einsum(
        "tri,tio->tro", feats_full, weights_low, preferred_element_type=jnp.float32
    )
    result, back = jax.vjp(lambda a, b: stitch_local(a, b, live_rows), product, small_params)
    stitched = lax.all_gather(result.astype(jnp.bfloat16), "mp", axis=2, tiled=True)
    dz, small_part = back(out_grad.astype(jnp.float32))
    dz_low = dz.astype(jnp.bfloat16)
    grad_part = jnp.einsum("tri,tro->tio", feats_full, dz_low, preferred_element_type=jnp.float32)
    partial_sums = jnp.einsum(
        "tro,tio->tri", dz_low, weights_low, preferred_element_type=jnp.float32
    )
    d_feat = lax.psum_scatter(partial_sums, "mp", scatter_dimension=2, tiled=True)
    grad = lax.psum_scatter(grad_part, "dp", scatter_dimension=1, tiled=True)
    small_grad = lax.psum(small_part, "dp")
    towers, n_in, n_out = grad.shape
    blocks = grad.reshape(towers, n_in // BLOCK, BLOCK, n_out // BLOCK, BLOCK)
    rotated = jnp.einsum(
        "trcai,tracb,trcbj->tricj", basis_left, blocks, basis_right, precision=lax.Precision.HIGHEST
    ).reshape(towers, n_in, n_out)
    first, second, direction = adam_part(moment_one, moment_two, rotated)
    turned = direction.reshape(towers, n_in // BLOCK, BLOCK, n_out // BLOCK, BLOCK)
    step_back = jnp.einsum(
        "trcai,tricj,trcbj->tracb", basis_left, turned, basis_right, precision=lax.Precision.HIGHEST
    ).reshape(towers, n_in, n_out)
    new_weights = weights - rate_main * (step_back + decay_weight * weights)
    new_average = ema_decay * average + (1.0 - ema_decay) * new_weights
    small_first, small_second, small_dir = adam_part(small_moment_one, small_moment_two, small_grad)
    small_new = small_params - rate_small * small_dir
    small_avg_new = ema_decay * small_average + (1.0 - ema_decay) * small_new
    return (
        stitched,
        d_feat.astype(jnp.bfloat16),
        first,
        second,
        new_weights,
        new_average,
        new_weights.astype(jnp.bfloat16),
        small_first,
        small_second,
        small_new,
        small_avg_new,
    )


def solution(mesh):
    return jax.shard_map(
        body,
        mesh=mesh,
        in_specs=(
            P(None, "dp", "mp"),
            P("dp"),
            P(None, "dp", "mp"),
            P(None, "mp"),
            P(None, "dp", "mp"),
            P(None, "dp", "mp"),
            P(None, "dp", "mp"),
            P(None, "dp", "mp"),
            P(None, "dp", "mp", None, None),
            P(None, "dp", "mp", None, None),
            P(None, "mp"),
            P(None, "mp"),
            P(None, "mp"),
        ),
        out_specs=(
            P(None, "dp", None),
            P(None, "dp", "mp"),
            P(None, "dp", "mp"),
            P(None, "dp", "mp"),
            P(None, "dp", "mp"),
            P(None, "dp", "mp"),
            P(None, "dp", "mp"),
            P(None, "mp"),
            P(None, "mp"),
            P(None, "mp"),
            P(None, "mp"),
        ),
        check_vma=False,
    )
```

profile of v0, /device:TPU:17, one launch (start us, length us, event | category | flops | bytes accessed | tf_op | source)
XLA Modules:
  0.0 2076.0 jit_solution(13250856899496859555)
XLA Ops:
  18.6 171.3 %all-gather.6.cloned.1.call-done = bf16[2,9216,512]{2,1,0:T(8,128)(2,1)} async-done(((bf16[2,2304,512]{2,1,0:T(8,128)(2,1)}), bf16[2,9216,512]{2,1,0:T(8,128)(2,1)}) %all-gather.6.cloned.1.call-update) | async-done | bytes 18874384 | tf_op jit(solution)/shard_map/all_gather | solution.py:52
  189.9 402.0 %all-gather.4.cloned.1.call-done = bf16[2,1280,9216]{2,1,0:T(8,128)(2,1)} async-done(((bf16[2,1280,1152]{2,1,0:T(8,128)(2,1)}), bf16[2,1280,9216]{2,1,0:T(8,128)(2,1)}) %all-gather.4.cloned.1.call-update) | async-done | bytes 47185936 | tf_op jit(solution)/shard_map/all_gather | solution.py:53
  592.0 37.5 %multiply_multiply_fusion.3 = (f32[2,1280,512]{2,1,0:T(8,128)}, f32[2,1280,512]{2,1,0:T(8,128)}) fusion(f32[2,512]{1,0:T(2,128)S(1)} %slice-done, bf16[2,1280,9216]{2,1,0:T(8,128)(2,1)} %all-gather.4.cloned.1.call-done, bf16[2,9216,512]{2,1,0:T(8,128)(2,1)} %all-gather.6.cloned.1.call-done), kind=kOutput, calls=%fused_computation.24 | convolution fusion | flops 24170987520 | bytes 76550144 | tf_op jit(solution)/shard_map/tri,tio->tro/dot_general | solution.py:54
  638.8 7.9 fusion.18
  646.7 39.9 %convolution_bitcast_fusion = f32[2,9216,512]{1,2,0:T(8,128)} fusion(bf16[2,1280,9216]{2,1,0:T(8,128)(2,1)} %all-gather.4.cloned.1.call-done, bf16[2,1280,512]{2,1,0:T(8,128)(2,1)} %get-tuple-element.20), kind=kOutput, calls=%fused_computation | convolution fusion | flops 24159191040 | bytes 87556096 | tf_op jit(solution)/shard_map/tri,tro->tio/dot_general | solution.py:61
  688.4 41.9 %fusion.13 = f32[2,1280,9216]{2,1,0:T(8,128)} fusion(bf16[2,9216,512]{2,1,0:T(8,128)(2,1)} %all-gather.6.cloned.1.call-done, bf16[2,1280,512]{2,1,0:T(8,128)(2,1)S(1)} %copy-done), kind=kOutput, calls=%fused_computation.37 | convolution fusion | flops 24159191040 | bytes 115867648 | tf_op jit(solution)/shard_map/tro,tio->tri/dot_general | solution.py:62
  730.4 13.8 psum.7
  744.8 77.6 %all-gather.8.cloned.1.call-done = bf16[2,1280,4096]{2,1,0:T(8,128)(2,1)} async-done(((bf16[2,1280,512]{2,1,0:T(8,128)(2,1)}), bf16[2,1280,4096]{2,1,0:T(8,128)(2,1)}) %all-gather.8.cloned.1.call-update) | async-done | bytes 20971536 | tf_op jit(solution)/shard_map/all_gather | solution.py:58
  822.4 325.0 %reduce-scatter.5.cloned.1.call-done = f32[2,2304,512]{1,2,0:T(8,128)} async-done(((f32[2,9216,512]{1,2,0:T(8,128)}), f32[2,2304,512]{1,2,0:T(8,128)}) %reduce-scatter.5.cloned.1.call-update) | async-done | bytes 9437200 | tf_op jit(solution)/shard_map/reduce_scatter | solution.py:66
  1147.5 16.3 reshape.123
  1163.7 39.7 %fusion = f32[2,36,8,64,64]{3,4,2,1,0:T(8,128)} fusion(f32[2,36,8,64,64]{4,3,2,1,0:T(8,128)} %param.21, f32[2,36,64,8,64]{2,1,4,3,0:T(8,128)} %reshape.123), kind=kOutput, calls=%fused_computation.1 | convolution fusion | flops 1811939328 | bytes 28311552 | tf_op jit(solution)/shard_map/trcai,tracb,trcbj->tricj/dot_general | solution.py:70
  1203.4 27.4 %convolution_bitcast_fusion.2 = f32[2,36,64,8,64]{4,2,3,1,0:T(8,128)S(1)} fusion(f32[2,36,8,64,64]{3,4,2,1,0:T(8,128)} %fusion, f32[2,36,8,64,64]{4,3,2,1,0:T(8,128)} %param.22), kind=kOutput, calls=%fused_computation.14 | convolution fusion | flops 1811939328 | bytes 28311552 | tf_op jit(solution)/shard_map/trcai,tracb,trcbj->tricj/dot_general | solution.py:70
  1230.8 20.6 copy.27
  1251.4 16.4 reshape.116
  1267.8 22.3 %add_divide_fusion = (f32[2,2304,512]{2,1,0:T(8,128)}, f32[2,2304,512]{2,1,0:T(8,128)}, f32[2,2304,512]{2,1,0:T(8,128)}) fusion(f32[2,2304,512]{2,1,0:T(8,128)} %reshape.116, f32[2,2304,512]{2,1,0:T(8,128)} %param.19, f32[2,2304,512]{2,1,0:T(8,128)} %param.18), kind=kLoop, calls=%fused_computation.10 | loop fusion | flops 23592960 | bytes 56623104 | tf_op jit(solution)/shard_map/div | solution.py:30
  1290.1 14.5 reshape.117
  1304.6 30.9 %fusion.2 = f32[2,36,8,64,64]{3,4,2,1,0:T(8,128)S(1)} fusion(f32[2,36,8,64,64]{4,3,2,1,0:T(8,128)} %param.21, f32[2,36,64,8,64]{4,3,2,1,0:T(8,128)} %reshape.117), kind=kOutput, calls=%fused_computation.3 | convolution fusion | flops 1811939328 | bytes 28311552 | tf_op jit(solution)/shard_map/trcai,tricj,trcbj->tracb/dot_general | solution.py:75
  1335.5 35.8 %convolution_bitcast_fusion.1 = f32[2,36,64,8,64]{4,2,3,1,0:T(8,128)} fusion(f32[2,36,8,64,64]{3,4,2,1,0:T(8,128)S(1)} %fusion.2, f32[2,36,8,64,64]{4,3,2,1,0:T(8,128)} %param.22), kind=kOutput, calls=%fused_computation.13 | convolution fusion | flops 1811939328 | bytes 28311552 | tf_op jit(solution)/shard_map/trcai,tricj,trcbj->tracb/dot_general | solution.py:75
  1371.2 23.6 %copy.28 = f32[2,36,64,8,64]{4,3,2,1,0:T(8,128)} copy(f32[2,36,64,8,64]{4,2,3,1,0:T(8,128)} %convolution_bitcast_fusion.1) | data formatting | bytes 18874368 | tf_op jit(solution)/shard_map/trcai,tricj,trcbj->tracb/transpose | solution.py:75
  1394.8 16.2 reshape.118
  1411.1 13.1 fusion.20
  1424.2 12.7 add_multiply_fusion
  1436.9 607.3 %reduce-scatter.3.cloned.1.call-done = f32[2,1280,1152]{2,1,0:T(8,128)} async-done(((f32[2,1280,9216]{2,1,0:T(8,128)}), f32[2,1280,1152]{2,1,0:T(8,128)}) %reduce-scatter.3.cloned.1.call-update) | async-done | bytes 11796496 | tf_op jit(solution)/shard_map/reduce_scatter | solution.py:65
  2051.7 17.5 copy.39
  (38 shorter events, 30.6 us)
Async XLA Ops:
  7.2 182.8 %all-gather.6.cloned.1.call-start = ((), (), s32[]{:S(2)}) async-start(), calls=%async_computation.3 | async-start | bytes 23592960 | tf_op jit(solution)/shard_map/all_gather | solution.py:52
  13.7 0.8 copy-start.7
  13.7 2.1 copy-start.2
  13.7 2.2 copy-start.1
  13.7 578.2 %all-gather.4.cloned.1.call-start = ((), (), s32[]{:S(2)}) async-start(), calls=%async_computation.2 | async-start | bytes 53084160 | tf_op jit(solution)/shard_map/all_gather | solution.py:53
  14.5 577.5 %slice-start = ((f32[6,512]{1,0:T(8,128)}), f32[2,512]{1,0:T(2,128)S(1)}, s32[]{:S(2)}) async-start(f32[6,512]{1,0:T(8,128)} %param.16), calls=%async_computation.7 | async-start | bytes 8192 | tf_op jit(solution)/shard_map/jvp()/slice | solution.py:20
  14.5 807.9 %all-gather.8.cloned.1.call-start = ((), (), s32[]{:S(2)}) async-start(), calls=%async_computation.4 | async-start | bytes 23592960 | tf_op jit(solution)/shard_map/all_gather | solution.py:58
  638.6 508.8 %reduce-scatter.5.cloned.1.call-start = ((), (), s32[]{:S(2)}) async-start(), calls=%async_computation.6 | async-start | bytes 47185920 | tf_op jit(solution)/shard_map/reduce_scatter | solution.py:66
  686.6 1.8 copy-start
  686.7 1357.5 %reduce-scatter.3.cloned.1.call-start = ((), (), s32[]{:S(2)}) async-start(), calls=%async_computation.5 | async-start | bytes 106168320 | tf_op jit(solution)/shard_map/reduce_scatter | solution.py:65
  730.3 13.8 copy-start.3
  730.3 13.8 copy-start.4
  730.3 13.8 copy-start.5
  730.3 13.8 copy-start.6
Sparse Core Ops, SparseCore 0:
  13.9 176.0 all-gather.5
  191.6 400.3 all-gather.3
  638.7 183.6 all-gather.7
  825.4 322.0 reduce-scatter.4
  1149.8 894.3 reduce-scatter.2
where the time goes:
time: 2090 us; the launch traced here: 2080 us
  waiting for transfers between devices  1580 us (76%)
  matrix products  253 us (12%)
  local copies, waits for them, and re-layouts  127 us (6%)
  other arithmetic  83.8 us (4%)
    reduce_scatter x1, waiting for transfers between devices, body(): lax.psum_scatter(partial_sums, 'mp', scatter_dimension=2, tiled=True)  607 us
    all_gather x1, waiting for transfers between devices, body(): feats_full = lax.all_gather(features, 'mp', axis=2, tiled=True)  402 us
    reduce_scatter x1, waiting for transfers between devices, body(): grad = lax.psum_scatter(grad_part, 'dp', scatter_dimension=1, tiled=True)  325 us
    all_gather x1, waiting for transfers between devices, body(): lax.all_gather(weights.astype(jnp.bfloat16), 'dp', axis=1, tiled=True)  171 us
    all_gather x1, waiting for transfers between devices, body(): lax.all_gather(result.astype(jnp.bfloat16), 'mp', axis=2, tiled=True)  77.6 us
    dot_general x2, matrix products, body(): jnp.einsum('trcai,tracb,trcbj->tricj', basis_left, blocks, basis_right, p...  67.1 us
    dot_general x2, matrix products, body(): jnp.einsum('trcai,tricj,trcbj->tracb', basis_left, turned, basis_right, p...  66.6 us
    dot_general x1, matrix products, body(): jnp.einsum('tro,tio->tri', dz_low, weights_low, preferred_element_type=jn...  41.9 us
  transfers between devices with their start and end apart: 5, of which 5 were waited for; matrix products, arithmetic and copies ran while one was open for 18% of the time, Pallas kernels for 0%

commit v1 on v0

--- a/solution.py
+++ b/solution.py
@@ -62,8 +62,12 @@
     partial_sums = jnp.einsum(
         "tro,tio->tri", dz_low, weights_low, preferred_element_type=jnp.float32
     )
-    d_feat = lax.psum_scatter(partial_sums, "mp", scatter_dimension=2, tiled=True)
-    grad = lax.psum_scatter(grad_part, "dp", scatter_dimension=1, tiled=True)
+    d_feat = lax.psum_scatter(
+        partial_sums.astype(jnp.bfloat16), "mp", scatter_dimension=2, tiled=True
+    )
+    grad = lax.psum_scatter(
+        grad_part.astype(jnp.bfloat16), "dp", scatter_dimension=1, tiled=True
+    ).astype(jnp.float32)
     small_grad = lax.psum(small_part, "dp")
     towers, n_in, n_out = grad.shape
     blocks = grad.reshape(towers, n_in // BLOCK, BLOCK, n_out // BLOCK, BLOCK)

time: 2090 us -> 1520 us (0.73)
  waiting for transfers between devices: 1580 us -> 870 us
  local copies, waits for them, and re-layouts: 127 us -> 302 us
  matrix products: 253 us -> 227 us
    reduce_scatter x2 -> x1, waiting for transfers between devices: 932 us -> 113 us  [body(): lax.psum_scatter(grad_part.astype(jnp.bfloat16), 'dp', scatter_dimension=...]
    unnamed x5 -> x6, waiting for transfers between devices: 0.76 us -> 184 us
    unnamed x17 -> x31, local copies, waits for them, and re-layouts: 19.2 us -> 197 us
    all_gather x1, waiting for transfers between devices: 77.6 us -> 0.01 us  [body(): lax.all_gather(result.astype(jnp.bfloat16), 'mp', axis=2, tiled=True)]
  transfers between devices with their start and end apart: 5 -> 5, of which waited for: 5 -> 4; matrix products, arithmetic and copies ran while one was open for 18% -> 33% of each run, Pallas kernels for 0% -> 0%
where the time goes in v1:
time: 1520 us; the launch traced here: 1510 us
  waiting for transfers between devices  870 us (57%)
  local copies, waits for them, and re-layouts  302 us (20%)
  matrix products  227 us (15%)
  other arithmetic  77.4 us (5%)
    all_gather x1, waiting for transfers between devices, body(): feats_full = lax.all_gather(features, 'mp', axis=2, tiled=True)  402 us
    unnamed x31, local copies, waits for them, and re-layouts  197 us
    unnamed x6, waiting for transfers between devices  184 us
    all_gather x1, waiting for transfers between devices, body(): lax.all_gather(weights.astype(jnp.bfloat16), 'dp', axis=1, tiled=True)  171 us
    reduce_scatter x1, waiting for transfers between devices, body(): lax.psum_scatter(grad_part.astype(jnp.bfloat16), 'dp', scatter_dimension=...  113 us
    dot_general x2, matrix products, body(): jnp.einsum('trcai,tricj,trcbj->tracb', basis_left, turned, basis_right, p...  66.7 us
    dot_general x2, matrix products, body(): jnp.einsum('trcai,tracb,trcbj->tricj', basis_left, blocks, basis_right, p...  51.3 us
    dot_general x1, matrix products, body(): jnp.einsum('tri,tio->tro', feats_full, weights_low, preferred_element_typ...  37.4 us
  transfers between devices with their start and end apart: 5, of which 4 were waited for; matrix products, arithmetic and copies ran while one was open for 33% of the time, Pallas kernels for 0%

profile of v1, /device:TPU:17, one launch (start us, length us, event | category | flops | bytes accessed | tf_op | source)
XLA Modules:
  0.0 1505.2 jit_solution(2857583769454747388)
XLA Ops:
  18.6 171.3 %all-gather.6.cloned.1.call-done = bf16[2,9216,512]{2,1,0:T(8,128)(2,1)} async-done(((bf16[2,2304,512]{2,1,0:T(8,128)(2,1)}), bf16[2,9216,512]{2,1,0:T(8,128)(2,1)}) %all-gather.6.cloned.1.call-update) | async-done | bytes 18874384 | tf_op jit(solution)/shard_map/all_gather | solution.py:52
  189.9 402.0 %all-gather.4.cloned.1.call-done = bf16[2,1280,9216]{2,1,0:T(8,128)(2,1)} async-done(((bf16[2,1280,1152]{2,1,0:T(8,128)(2,1)}), bf16[2,1280,9216]{2,1,0:T(8,128)(2,1)}) %all-gather.4.cloned.1.call-update) | async-done | bytes 47185936 | tf_op jit(solution)/shard_map/all_gather | solution.py:53
  592.0 37.4 %multiply_multiply_fusion.3 = (f32[2,1280,512]{2,1,0:T(8,128)}, f32[2,1280,512]{2,1,0:T(8,128)}) fusion(f32[2,512]{1,0:T(2,128)S(1)} %slice-done, bf16[2,1280,9216]{2,1,0:T(8,128)(2,1)} %all-gather.4.cloned.1.call-done, bf16[2,9216,512]{2,1,0:T(8,128)(2,1)} %all-gather.6.cloned.1.call-done), kind=kOutput, calls=%fused_computation.25 | convolution fusion | flops 24170987520 | bytes 76550144 | tf_op jit(solution)/shard_map/tri,tio->tro/dot_general | solution.py:54
  648.2 35.3 %convert_bitcast_fusion = bf16[2,9216,512]{1,2,0:T(8,128)(2,1)} fusion(bf16[2,1280,9216]{2,1,0:T(8,128)(2,1)} %all-gather.4.cloned.1.call-done, bf16[2,1280,512]{2,1,0:T(8,128)(2,1)} %get-tuple-element.20), kind=kOutput, calls=%fused_computation.3 | convolution fusion | flops 24168628224 | bytes 68681728 | tf_op jit(solution)/shard_map/tri,tro->tio/dot_general | solution.py:61
  685.2 36.6 %convolution_convert_fusion = bf16[2,1280,9216]{2,1,0:T(8,128)(2,1)} fusion(bf16[2,9216,512]{2,1,0:T(8,128)(2,1)} %all-gather.6.cloned.1.call-done, bf16[2,1280,512]{2,1,0:T(8,128)(2,1)S(1)} %copy-done), kind=kOutput, calls=%fused_computation | convolution fusion | flops 24182784000 | bytes 68681728 | tf_op jit(solution)/shard_map/tro,tio->tri/dot_general | solution.py:62
  721.8 114.5 %copy.42 = bf16[2,1280,9216]{1,0,2:T(2,128)(2,1)} copy(bf16[2,1280,9216]{2,1,0:T(8,128)(2,1)} %convolution_convert_fusion) | data formatting | bytes 94371840
  836.4 33.1 %copy.44 = bf16[1152,8,2,1280]{3,1,2,0:T(8,128)(2,1)} copy(bf16[1152,8,2,1280]{3,2,1,0:T(2,128)(2,1)} %bitcast.37) | data formatting | bytes 94371840
  870.2 13.1 psum.7
  884.0 113.3 %reduce-scatter.5.cloned.1.call-done = bf16[2,2304,512]{1,2,0:T(8,128)(2,1)} async-done(((bf16[2,9216,512]{1,2,0:T(8,128)(2,1)}), bf16[2,2304,512]{1,2,0:T(8,128)(2,1)}) %reduce-scatter.5.cloned.1.call-update) | async-done | bytes 4718608 | tf_op jit(solution)/shard_map/reduce_scatter | solution.py:68
  997.3 14.2 reshape.123
  1011.5 24.0 %fusion.3 = f32[2,36,8,64,64]{3,4,2,1,0:T(8,128)} fusion(f32[2,36,8,64,64]{4,3,2,1,0:T(8,128)} %param.21, bf16[2,36,64,8,64]{2,1,4,3,0:T(8,128)(2,1)} %reshape.123), kind=kOutput, calls=%fused_computation.7 | convolution fusion | flops 1811939328 | bytes 23592960 | tf_op jit(solution)/shard_map/trcai,tracb,trcbj->tricj/dot_general | solution.py:74
  1035.5 27.2 %convolution_bitcast_fusion.1 = f32[2,36,64,8,64]{4,2,3,1,0:T(8,128)S(1)} fusion(f32[2,36,8,64,64]{3,4,2,1,0:T(8,128)} %fusion.3, f32[2,36,8,64,64]{4,3,2,1,0:T(8,128)} %param.22), kind=kOutput, calls=%fused_computation.15 | convolution fusion | flops 1811939328 | bytes 28311552 | tf_op jit(solution)/shard_map/trcai,tracb,trcbj->tricj/dot_general | solution.py:74
  1062.7 20.6 %copy.33 = f32[2,36,64,8,64]{4,3,2,1,0:T(8,128)} copy(f32[2,36,64,8,64]{4,2,3,1,0:T(8,128)S(1)} %convolution_bitcast_fusion.1) | data formatting | bytes 18874368 | tf_op jit(solution)/shard_map/trcai,tracb,trcbj->tricj/transpose | solution.py:74
  1083.3 16.2 %reshape.116 = f32[2,2304,512]{2,1,0:T(8,128)} reshape(f32[2,36,64,8,64]{4,3,2,1,0:T(8,128)} %copy.33) | data formatting | bytes 18874368 | tf_op jit(solution)/shard_map/reshape | solution.py:76
  1099.5 22.4 %add_divide_fusion = (f32[2,2304,512]{2,1,0:T(8,128)}, f32[2,2304,512]{2,1,0:T(8,128)}, f32[2,2304,512]{2,1,0:T(8,128)}) fusion(f32[2,2304,512]{2,1,0:T(8,128)} %reshape.116, f32[2,2304,512]{2,1,0:T(8,128)} %param.19, f32[2,2304,512]{2,1,0:T(8,128)} %param.18), kind=kLoop, calls=%fused_computation.11 | loop fusion | flops 23592960 | bytes 56623104 | tf_op jit(solution)/shard_map/div | solution.py:30
  1121.9 14.5 reshape.117
  1136.4 30.9 %fusion = f32[2,36,8,64,64]{3,4,2,1,0:T(8,128)S(1)} fusion(f32[2,36,8,64,64]{4,3,2,1,0:T(8,128)} %param.21, f32[2,36,64,8,64]{4,3,2,1,0:T(8,128)} %reshape.117), kind=kOutput, calls=%fused_computation.1 | convolution fusion | flops 1811939328 | bytes 28311552 | tf_op jit(solution)/shard_map/trcai,tricj,trcbj->tracb/dot_general | solution.py:79
  1167.3 35.8 %convolution_bitcast_fusion = f32[2,36,64,8,64]{4,2,3,1,0:T(8,128)} fusion(f32[2,36,8,64,64]{3,4,2,1,0:T(8,128)S(1)} %fusion, f32[2,36,8,64,64]{4,3,2,1,0:T(8,128)} %param.22), kind=kOutput, calls=%fused_computation.14 | convolution fusion | flops 1811939328 | bytes 28311552 | tf_op jit(solution)/shard_map/trcai,tricj,trcbj->tracb/dot_general | solution.py:79
  1203.1 23.4 %copy.36 = f32[2,36,64,8,64]{4,3,2,1,0:T(8,128)} copy(f32[2,36,64,8,64]{4,2,3,1,0:T(8,128)} %convolution_bitcast_fusion) | data formatting | bytes 18874368 | tf_op jit(solution)/shard_map/trcai,tricj,trcbj->tracb/transpose | solution.py:79
  1226.6 16.4 %reshape.118 = f32[2,2304,512]{2,1,0:T(8,128)} reshape(f32[2,36,64,8,64]{4,3,2,1,0:T(8,128)} %copy.36) | data formatting | bytes 18874368 | tf_op jit(solution)/shard_map/reshape | solution.py:81
  1242.9 13.1 fusion.19
  1268.7 183.0 %reduce-scatter.7.cloned.1.call-done = bf16[1152,2560]{1,0:T(8,128)(2,1)} async-done(((bf16[9216,2560]{1,0:T(8,128)(2,1)}), bf16[1152,2560]{1,0:T(8,128)(2,1)}) %reduce-scatter.7.cloned.1.call-update) | async-done | bytes 5898256
  1464.6 16.4 %copy.43 = bf16[2,1280,1152]{2,1,0:T(8,128)(2,1)} copy(bf16[2,1280,1152]{1,0,2:T(2,128)(2,1)} %bitcast.38) | data formatting | bytes 11796480
  1481.0 17.5 %copy.50 = bf16[2,1280,4096]{2,1,0:T(8,128)(2,1)} copy(bf16[2,1280,4096]{2,1,0:T(8,128)(2,1)} %all-gather.8.cloned.1.call-done) | data formatting | bytes 41943040
  (51 shorter events, 58.8 us)
Async XLA Ops:
  7.2 182.7 %all-gather.6.cloned.1.call-start = ((), (), s32[]{:S(2)}) async-start(), calls=%async_computation.3 | async-start | bytes 23592960 | tf_op jit(solution)/shard_map/all_gather | solution.py:52
  13.7 0.8 copy-start.12
  13.7 2.1 copy-start.2
  13.7 2.2 copy-start.1
  13.7 578.2 %all-gather.4.cloned.1.call-start = ((), (), s32[]{:S(2)}) async-start(), calls=%async_computation.2 | async-start | bytes 53084160 | tf_op jit(solution)/shard_map/all_gather | solution.py:53
  14.5 577.5 %slice-start = ((f32[6,512]{1,0:T(8,128)}), f32[2,512]{1,0:T(2,128)S(1)}, s32[]{:S(2)}) async-start(f32[6,512]{1,0:T(8,128)} %param.16), calls=%async_computation.7 | async-start | bytes 8192 | tf_op jit(solution)/shard_map/jvp()/slice | solution.py:20
  14.5 869.5 %all-gather.8.cloned.1.call-start = ((), (), s32[]{:S(2)}) async-start(), calls=%async_computation.4 | async-start | bytes 23592960 | tf_op jit(solution)/shard_map/all_gather | solution.py:58
  639.1 358.1 %reduce-scatter.5.cloned.1.call-start = ((), (), s32[]{:S(2)}) async-start(), calls=%async_computation.5 | async-start | bytes 23592960 | tf_op jit(solution)/shard_map/reduce_scatter | solution.py:68
  683.5 1.7 copy-start
  683.5 768.1 %reduce-scatter.7.cloned.1.call-start = ((), (), s32[]{:S(2)}) async-start(), calls=%async_computation.6 | async-start | bytes 53084160
  869.5 0.7 copy-start.4
  869.5 0.7 copy-start.8
  869.5 0.7 copy-start.9
  869.5 0.7 copy-start.10
  869.5 0.7 copy-start.11
  869.5 13.8 copy-start.3
  869.5 13.8 copy-start.5
  869.5 13.8 copy-start.6
  869.6 13.8 copy-start.7
Sparse Core Ops, SparseCore 0:
  13.8 176.0 all-gather.5
  191.5 400.3 all-gather.3
  639.3 183.6 all-gather.7
  826.5 170.7 reduce-scatter.4
  999.6 451.9 reduce-scatter.6

commit v2 on v0

--- a/solution.py
+++ b/solution.py
@@ -1,6 +1,10 @@
+import functools
+
 import jax
 import jax.numpy as jnp
 from jax import lax
+from jax.experimental import pallas as pl
+from jax.experimental.pallas import tpu as pltpu
 from jax.sharding import PartitionSpec as P
 
 BLOCK = 64
@@ -30,8 +34,462 @@
     direction = first / (1.0 - beta_one**STEP) / (jnp.sqrt(second / (1.0 - beta_two**STEP)) + eps)
     return (first, second, direction)
 
-
-def body(
+def split(v):
+    high = v.astype(jnp.bfloat16)
+    return high, (v - high.astype(jnp.float32)).astype(jnp.bfloat16)
+
+def soap_pair(grad, left, right, moment_a, moment_b):
+    row = lax.broadcasted_iota(jnp.int32, (2 * BLOCK, 2 * BLOCK), 0) // BLOCK
+    lane = lax.broadcasted_iota(jnp.int32, (2 * BLOCK, 2 * BLOCK), 1) // BLOCK
+    own = row == lane
+    def diagonal(v):
+        return jnp.where(own, jnp.concatenate([v, v], axis=0), 0.0)
+    def beside(v):
+        return jnp.concatenate([v[0], v[1]], axis=1)
+    def dot(a, b, ca, cb):
+        return lax.dot_general(a, b, (((ca,), (cb,)), ((), ())), preferred_element_type=jnp.float32)
+    right_high, right_low = split(diagonal(beside(right)))
+    left_high, left_low = split(beside(left))
+    up_high, up_low = split(left.reshape(2 * BLOCK, BLOCK))
+    def turn(v, cb):
+        high, low = split(v)
+        return (dot(jnp.concatenate([high, low], axis=1), jnp.concatenate([right_high, right_high], axis=cb), 1, cb)
+                + dot(high, right_low, 1, cb))
+    high, low = split(diagonal(turn(grad, 0)))
+    rotated = dot(jnp.concatenate([up_high, up_high, up_low], axis=0), jnp.concatenate([high, low, high], axis=0), 0, 0)
+    first, second, direction = adam_part(moment_a, moment_b, rotated)
+    high, low = split(diagonal(turn(direction, 1)))
+    step = dot(jnp.concatenate([left_high, left_high, left_low], axis=1), jnp.concatenate([high, low, high], axis=0), 1, 0)
+    return first, second, step
+
+def soap_body(parts, weights, moment_a, moment_b, average, left, right, first, second, new_weights, new_average, copy):
+    groups, pairs = left.shape[1], left.shape[2] // 2
+    def strip(g, _):
+        rows = pl.ds(pl.multiple_of(g * BLOCK, BLOCK), BLOCK)
+        for q in range(pairs):
+            cols = pl.ds(2 * BLOCK * q, 2 * BLOCK)
+            at = (0, rows, cols)
+            grad = parts[(0, 0) + at].astype(jnp.float32)
+            for k in range(1, parts.shape[0]):
+                grad = grad + parts[(k, 0) + at].astype(jnp.float32)
+            one, two, step = soap_pair(grad, left[0, g, 2 * q:2 * q + 2], right[0, g, 2 * q:2 * q + 2], moment_a[at], moment_b[at])
+            first[at] = one
+            second[at] = two
+            held = weights[at]
+            fresh = held - rate_main * (step + decay_weight * held)
+            new_weights[at] = fresh
+            new_average[at] = ema_decay * average[at] + (1.0 - ema_decay) * fresh
+            copy[at] = fresh.astype(jnp.bfloat16)
+        return 0
+    lax.fori_loop(0, groups, strip, 0)
+
+def soap(parts, weights, moment_a, moment_b, average, left, right, group=3):
+    towers, rows, cols = weights.shape
+    half = parts.shape[3]
+    steps = half // (BLOCK * group)
+    flat = lambda t, p, g: (t, p * steps + g, 0)
+    basis = lambda t, p, g: (t, p * steps + g, 0, 0, 0)
+    state = pl.BlockSpec((1, BLOCK * group, cols), flat)
+    base = pl.BlockSpec((1, group, cols // BLOCK, BLOCK, BLOCK), basis)
+    full = jax.ShapeDtypeStruct(weights.shape, jnp.float32)
+    return pl.pallas_call(
+        soap_body,
+        grid=(towers, 2, steps),
+        in_specs=[pl.BlockSpec((parts.shape[0], 1, 1, BLOCK * group, cols), lambda t, p, g: (0, p, t, g, 0)),
+                  state, state, state, state, base, base],
+        out_specs=[state] * 5,
+        out_shape=[full] * 4 + [jax.ShapeDtypeStruct(weights.shape, jnp.bfloat16)],
+        compiler_params=pltpu.CompilerParams(vmem_limit_bytes=48 * 2**20),
+        cost_estimate=pl.CostEstimate(flops=8 * 2 * towers * rows * cols * 64, bytes_accessed=130 * 2**20, transcendentals=0),
+        name="soap",
+    )(parts, weights, moment_a, moment_b, average, left, right)
+
+
+MESH = pl.DeviceIdType.MESH
+
+
+def place():
+    mp = lax.axis_index("mp")
+    return lax.axis_index("dp"), mp // 2, lax.rem(mp, 2)
+
+
+def meet(devices):
+    barrier = pltpu.get_barrier_semaphore()
+    expected = 0
+    for here, device in devices:
+        @pl.when(here)
+        def _():
+            pl.semaphore_signal(barrier, inc=1, device_id=device, device_id_type=MESH)
+        expected = expected + jnp.where(here, 1, 0)
+    pl.semaphore_wait(barrier, expected)
+
+
+def gather_kernel(chips, chunks, f_ref, w_ref, fg_ref, wg_ref, f_send, f_recv, w_send, w_recv, own_sem):
+    dp, chip, core = place()
+    towers, rows, depth = f_ref.shape
+    cols = w_ref.shape[2]
+    part = rows // chunks
+    across, along = dp ^ 1, dp ^ 2
+    at = lambda c, k: (c, 2 * chip + k)
+
+    meet([(chip > 0, (dp, 2 * (chip - 1) + core)), (chip < chips - 1, (dp, 2 * (chip + 1) + core)),
+          (chip >= 0, at(dp, 1 - core))] + [(chip >= 0, at(c, k)) for c in (across, along) for k in (0, 1)])
+
+    def feature(step, way, t, k):
+        shard = chip - step if way == 0 else chip + step
+        there = chip + 1 if way == 0 else chip - 1
+        lanes = pl.ds(pl.multiple_of(shard * depth, 128), depth)
+        rws = pl.ds(k * part, part)
+        src = f_ref.at[t, rws] if step == 0 else fg_ref.at[t, rws, lanes]
+        n = ((way * (chips - 1) + step) * towers + t) * chunks + k
+        return pltpu.make_async_remote_copy(
+            src_ref=src, dst_ref=fg_ref.at[t, rws, lanes], send_sem=f_send.at[n], recv_sem=f_recv.at[n],
+            device_id=(dp, 2 * there + core), device_id_type=MESH)
+
+    def sends(step, way):
+        return (chip < chips - 1) & (chip >= step) if way == 0 else (chip > 0) & (chip + step < chips)
+
+    def receives(step, way):
+        return chip > step if way == 0 else chip + step < chips - 1
+
+    def incoming(step, way, t, k):
+        shard = chip - 1 - step if way == 0 else chip + 1 + step
+        lanes = pl.ds(pl.multiple_of(shard * depth, 128), depth)
+        rws = pl.ds(k * part, part)
+        n = ((way * (chips - 1) + step) * towers + t) * chunks + k
+        return pltpu.make_async_remote_copy(
+            src_ref=f_ref.at[t, rws], dst_ref=fg_ref.at[t, rws, lanes], send_sem=f_send.at[n], recv_sem=f_recv.at[n],
+            device_id=(dp, 2 * chip + core), device_id_type=MESH)
+
+    def block(owner, slot, t):
+        return wg_ref.at[t, pl.ds(pl.multiple_of(owner * depth, 128), depth), pl.ds(pl.multiple_of(slot * cols, 128), cols)]
+
+    def weight(kind, k, t):
+        to = at((across, along, dp)[kind], k)
+        n = (kind * 2 + core) * 2 + t
+        return pltpu.make_async_remote_copy(
+            src_ref=w_ref.at[t, pl.ds(pl.multiple_of(k * depth, 128), depth)], dst_ref=block(dp, k ^ core, t),
+            send_sem=w_send.at[(kind * 2 + k) * 2 + t], recv_sem=w_recv.at[n], device_id=to, device_id_type=MESH)
+
+    def forward(kind, slot):
+        owner, to, t = ((across, along, 0), (along, across, 1))[kind]
+        n = 12 + kind * 2 + slot
+        return pltpu.make_async_remote_copy(
+            src_ref=block(owner, slot, t), dst_ref=block(owner, slot, t),
+            send_sem=w_send.at[n], recv_sem=w_recv.at[n], device_id=at(to, core), device_id_type=MESH)
+
+    def arrived(kind, slot, t):
+        owner = (across, along, dp)[kind]
+        n = (kind * 2 + (slot ^ core)) * 2 + t
+        pltpu.make_async_remote_copy(
+            src_ref=block(owner, slot, t), dst_ref=block(owner, slot, t), send_sem=w_send.at[n], recv_sem=w_recv.at[n],
+            device_id=at(dp, core), device_id_type=MESH).wait_recv()
+
+    own = [pltpu.make_async_copy(f_ref.at[t], fg_ref.at[t, :, pl.ds(pl.multiple_of(chip * depth, 128), depth)], own_sem.at[t])
+           for t in range(towers)]
+    own += [pltpu.make_async_copy(w_ref.at[t, pl.ds(pl.multiple_of(core * depth, 128), depth)], block(dp, 0, t), own_sem.at[2 + t])
+            for t in range(towers)]
+
+    pieces = [(t, k) for t in range(towers) for k in range(chunks)]
+    for t, k in pieces:
+        for way in (0, 1):
+            @pl.when(sends(0, way))
+            def _():
+                feature(0, way, t, k).start()
+    for t in (0, 1):
+        for k in (0, 1):
+            weight(0, k, t).start()
+            weight(1, k, 1 - t).start()
+    for t in (0, 1):
+        weight(2, 1 - core, t).start()
+    for copy in own:
+        copy.start()
+
+    for step in range(chips - 1):
+        for t, k in pieces:
+            for way in (0, 1):
+                @pl.when(receives(step, way))
+                def _():
+                    incoming(step, way, t, k).wait_recv()
+                if step + 1 < chips - 1:
+                    @pl.when(sends(step + 1, way))
+                    def _():
+                        feature(step + 1, way, t, k).start()
+            if step == 0 and (t, k) == pieces[len(pieces) // 2 - 1]:
+                for slot in (0, 1):
+                    arrived(0, slot, 0)
+                    forward(0, slot).start()
+                    arrived(1, slot, 1)
+                    forward(1, slot).start()
+
+    for slot in (0, 1):
+        arrived(0, slot, 1)
+        arrived(1, slot, 0)
+        forward(0, slot).wait_recv()
+        forward(1, slot).wait_recv()
+    for t in (0, 1):
+        arrived(2, 1, t)
+    for t in (0, 1):
+        for k in (0, 1):
+            weight(0, k, t).wait_send()
+            weight(1, k, t).wait_send()
+        weight(2, 1 - core, t).wait_send()
+    for slot in (0, 1):
+        forward(0, slot).wait_send()
+        forward(1, slot).wait_send()
+    for step in range(chips - 1):
+        for t, k in pieces:
+            for way in (0, 1):
+                @pl.when(sends(step, way))
+                def _():
+                    feature(step, way, t, k).wait_send()
+    for copy in own:
+        copy.wait()
+
+
+def gather(features, weights_low, chips, chunks, ident):
+    towers, rows, depth = features.shape
+    cols = weights_low.shape[2]
+    count = 2 * (chips - 1) * towers * chunks
+    dma = pltpu.SemaphoreType.DMA
+    return pl.pallas_call(
+        functools.partial(gather_kernel, chips, chunks),
+        out_shape=[jax.ShapeDtypeStruct((towers, rows, chips * depth), jnp.bfloat16),
+                   jax.ShapeDtypeStruct((towers, chips * depth, 2 * cols), jnp.bfloat16)],
+        in_specs=[pl.BlockSpec(memory_space=pl.ANY)] * 2,
+        out_specs=[pl.BlockSpec(memory_space=pl.ANY)] * 2,
+        scratch_shapes=[dma((count,)), dma((count,)), dma((16,)), dma((16,)), dma((4,))],
+        compiler_params=pltpu.CompilerParams(collective_id=ident, has_side_effects=True),
+        cost_estimate=pl.CostEstimate(flops=0, bytes_accessed=800 * 2**20, transcendentals=0),
+        name="gather",
+    )(features, weights_low)
+
+
+def reduce_kernel(chips, chunks, pd_ref, pg_ref, ps_ref, d_ref, gr_ref, sr_ref, held, term, total,
+                  d_send, d_recv, t_sem, o_sem, g_send, g_recv, s_send, s_recv, own_sem):
+    dp, chip, core = place()
+    towers, rows, depth = d_ref.shape
+    cols = pg_ref.shape[2] // 2
+    part = rows // chunks
+    across, along = dp ^ 1, dp ^ 2
+    others = (across, along, 3 - dp)
+    at = lambda c, k: (c, 2 * chip + k)
+
+    meet([(chip > 0, (dp, 2 * (chip - 1) + core)), (chip < chips - 1, (dp, 2 * (chip + 1) + core)),
+          (chip >= 0, at(dp, 1 - core))] + [(chip >= 0, at(c, k)) for c in others for k in (0, 1)])
+
+    def grad(kind, k, t):
+        owner = (others + (dp,))[kind]
+        return pltpu.make_async_remote_copy(
+            src_ref=pg_ref.at[t, pl.ds(pl.multiple_of(owner * depth, 128), depth), pl.ds(pl.multiple_of((k ^ core) * cols, 128), cols)],
+            dst_ref=gr_ref.at[dp, core, t], send_sem=g_send.at[(kind * 2 + k) * 2 + t],
+            recv_sem=g_recv.at[(kind * 2 + core) * 2 + t], device_id=at(owner, k), device_id_type=MESH)
+
+    def grad_arrived(kind, k, t):
+        owner = (others + (dp,))[kind]
+        pltpu.make_async_remote_copy(
+            src_ref=gr_ref.at[owner, k, t], dst_ref=gr_ref.at[owner, k, t], send_sem=g_send.at[0],
+            recv_sem=g_recv.at[(kind * 2 + k) * 2 + t], device_id=at(dp, core), device_id_type=MESH).wait_recv()
+
+    def small(kind):
+        return pltpu.make_async_remote_copy(
+            src_ref=ps_ref, dst_ref=sr_ref.at[dp], send_sem=s_send.at[kind], recv_sem=s_recv.at[kind],
+            device_id=at(others[kind], core), device_id_type=MESH)
+
+    def target(step, way):
+        return chip + chips - 1 - step if way == 0 else chip - (chips - 1 - step)
+
+    def sends(step, way):
+        return (chip < chips - 1) & (chip <= step) if way == 0 else (chip > 0) & (chips - 1 - chip <= step)
+
+    def receives(step, way):
+        return (chip > 0) & (chip <= step + 1) if way == 0 else (chip < chips - 1) & (chips - 1 - chip <= step + 1)
+
+    def own_term(goal, t, k):
+        return pd_ref.at[t, pl.ds(k * part, part), pl.ds(pl.multiple_of(goal * depth, 128), depth)]
+
+    def partial(step, way, t, k, first):
+        n = ((way * (chips - 1) + step) * towers + t) * chunks + k
+        src = own_term(target(step, way), t, k) if first else held.at[way, step - 1, t, pl.ds(k * part, part)]
+        there = chip + 1 if way == 0 else chip - 1
+        return pltpu.make_async_remote_copy(
+            src_ref=src, dst_ref=held.at[way, step, t, pl.ds(k * part, part)], send_sem=d_send.at[n], recv_sem=d_recv.at[n],
+            device_id=(dp, 2 * there + core), device_id_type=MESH)
+
+    def landed(step, way, t, k):
+        n = ((way * (chips - 1) + step) * towers + t) * chunks + k
+        ref = held.at[way, step, t, pl.ds(k * part, part)]
+        pltpu.make_async_remote_copy(src_ref=ref, dst_ref=ref, send_sem=d_send.at[n], recv_sem=d_recv.at[n],
+                                     device_id=(dp, 2 * chip + core), device_id_type=MESH).wait_recv()
+
+    pieces = [(t, k) for t in range(towers) for k in range(chunks)]
+    ends = (chip == 0, chip == chips - 1)
+    for t, k in pieces:
+        for way in (0, 1):
+            @pl.when(ends[way])
+            def _():
+                partial(0, way, t, k, True).start()
+    own = [pltpu.make_async_copy(
+        pg_ref.at[t, pl.ds(pl.multiple_of(dp * depth, 128), depth), pl.ds(0, cols)], gr_ref.at[dp, core, t], own_sem.at[t])
+        for t in range(towers)]
+    own.append(pltpu.make_async_copy(ps_ref, sr_ref.at[dp], own_sem.at[towers]))
+    for copy in own:
+        copy.start()
+    for kind in range(3):
+        small(kind).start()
+    for t in range(towers):
+        for kind in (2, 0, 1):
+            for k in (0, 1):
+                grad(kind, k, t).start()
+        grad(3, 1 - core, t).start()
+
+    strip = 32
+
+    for step in range(1, chips - 1):
+        for t, k in pieces:
+            for way in (0, 1):
+                @pl.when(sends(step, way) & ends[way])
+                def _():
+                    partial(step, way, t, k, True).start()
+
+                @pl.when(sends(step, way) & jnp.logical_not(ends[way]))
+                def _():
+                    load = pltpu.make_async_copy(own_term(target(step, way), t, k), term.at[way], t_sem.at[way])
+                    load.start()
+                    landed(step - 1, way, t, k)
+                    load.wait()
+
+                    def add(i, _):
+                        rws = pl.ds(pl.multiple_of(i * strip, strip), strip)
+                        all_rows = pl.ds(pl.multiple_of(k * part + i * strip, strip), strip)
+                        held[way, step - 1, t, all_rows] = (
+                            held[way, step - 1, t, all_rows].astype(jnp.float32) + term[way, rws].astype(jnp.float32)
+                        ).astype(jnp.bfloat16)
+                        return 0
+                    lax.fori_loop(0, part // strip, add, 0)
+                    partial(step, way, t, k, False).start()
+
+    for n, (t, k) in enumerate(pieces):
+        s = n % 2
+        load = pltpu.make_async_copy(own_term(chip, t, k), term.at[s], t_sem.at[s])
+        load.start()
+        for way in (0, 1):
+            @pl.when(receives(chips - 2, way))
+            def _():
+                landed(chips - 2, way, t, k)
+        load.wait()
+        store = pltpu.make_async_copy(total.at[s], d_ref.at[t, pl.ds(k * part, part)], o_sem.at[s])
+        if n >= 2:
+            store.wait()
+
+        def finish(i, _):
+            rws = pl.ds(pl.multiple_of(i * strip, strip), strip)
+            all_rows = pl.ds(pl.multiple_of(k * part + i * strip, strip), strip)
+            value = term[s, rws].astype(jnp.float32)
+            for way in (0, 1):
+                here = receives(chips - 2, way)
+                value = value + jnp.where(here, held[way, chips - 2, t, all_rows].astype(jnp.float32), 0.0)
+            total[s, rws] = value.astype(jnp.bfloat16)
+            return 0
+        lax.fori_loop(0, part // strip, finish, 0)
+        store.start()
+    for n in range(min(2, len(pieces))):
+        pltpu.make_async_copy(total.at[n], d_ref.at[0, pl.ds(0, part)], o_sem.at[n]).wait()
+
+    for t in range(towers):
+        for kind in range(3):
+            for k in (0, 1):
+                grad_arrived(kind, k, t)
+        grad_arrived(3, 1 - core, t)
+    for kind in range(3):
+        small(kind).wait()
+    for t in range(towers):
+        for kind in range(3):
+            for k in (0, 1):
+                grad(kind, k, t).wait_send()
+        grad(3, 1 - core, t).wait_send()
+    for step in range(chips - 1):
+        for t, k in pieces:
+            for way in (0, 1):
+                @pl.when(sends(step, way))
+                def _():
+                    partial(step, way, t, k, True).wait_send()
+    for copy in own:
+        copy.wait()
+
+
+def reduce(partial_d, partial_g, partial_s, chips, chunks, ident):
+    towers, rows, wide = partial_d.shape
+    depth, cols = wide // chips, partial_g.shape[2] // 2
+    count = 2 * (chips - 1) * towers * chunks
+    dma = pltpu.SemaphoreType.DMA
+    bf16 = jnp.bfloat16
+    return pl.pallas_call(
+        functools.partial(reduce_kernel, chips, chunks),
+        out_shape=[jax.ShapeDtypeStruct((towers, rows, depth), bf16),
+                   jax.ShapeDtypeStruct((4, 2, towers, depth, cols), bf16),
+                   jax.ShapeDtypeStruct((4,) + partial_s.shape, jnp.float32)],
+        in_specs=[pl.BlockSpec(memory_space=pl.ANY)] * 3,
+        out_specs=[pl.BlockSpec(memory_space=pl.ANY)] * 3,
+        scratch_shapes=[pltpu.VMEM((2, chips - 1, towers, rows, depth), bf16),
+                        pltpu.VMEM((2, rows // chunks, depth), bf16), pltpu.VMEM((2, rows // chunks, depth), bf16),
+                        dma((count,)), dma((count,)), dma((2,)), dma((2,)), dma((16,)), dma((16,)), dma((3,)), dma((3,)), dma((towers + 1,))],
+        compiler_params=pltpu.CompilerParams(collective_id=ident, has_side_effects=True, vmem_limit_bytes=56 * 2**20),
+        cost_estimate=pl.CostEstimate(flops=0, bytes_accessed=800 * 2**20, transcendentals=0),
+        name="reduce",
+    )(partial_d, partial_g, partial_s)
+
+
+def small_step(small_params, small_moment_one, small_moment_two, small_average, small_grad):
+    first, second, direction = adam_part(small_moment_one, small_moment_two, small_grad)
+    fresh = small_params - rate_small * direction
+    return first, second, fresh, ema_decay * small_average + (1.0 - ema_decay) * fresh
+
+
+def line_body(
+    features,
+    counts,
+    weights,
+    small_params,
+    out_grad,
+    moment_one,
+    moment_two,
+    average,
+    basis_left,
+    basis_right,
+    small_moment_one,
+    small_moment_two,
+    small_average,
+):
+    cores = lax.axis_size("mp")
+    chips = cores // 2
+    cols = weights.shape[2]
+    swap = [(i, i ^ 1) for i in range(cores)]
+    slot_count = features.shape[1]
+    total = jnp.sum(counts)
+    live_rows = (jnp.arange(slot_count, dtype=jnp.int32) < total).astype(jnp.float32)
+    wide_f, wide_w = gather(features, weights.astype(jnp.bfloat16), chips, 2, 1)
+    partial = jnp.einsum("tri,tio->tro", wide_f, wide_w, preferred_element_type=jnp.float32)
+    product = partial[:, :, :cols] + lax.ppermute(partial[:, :, cols:], "mp", swap)
+    result, back = jax.vjp(lambda a, b: stitch_local(a, b, live_rows), product, small_params)
+    stitched = lax.all_gather(result.astype(jnp.bfloat16), "mp", axis=2, tiled=True)
+    dz, small_part = back(out_grad.astype(jnp.float32))
+    dz_low = dz.astype(jnp.bfloat16)
+    wide_dz = jnp.concatenate([dz_low, lax.ppermute(dz_low, "mp", swap)], axis=2)
+    partial_d = jnp.einsum("tro,tio->tri", wide_dz, wide_w, preferred_element_type=jnp.float32)
+    partial_g = jnp.einsum("tri,tro->tio", wide_f, wide_dz, preferred_element_type=jnp.float32)
+    small_part = jnp.pad(small_part, ((0, 2), (0, 0)))
+    d_feat, parts, small_parts = reduce(
+        partial_d.astype(jnp.bfloat16), partial_g.astype(jnp.bfloat16), small_part, chips, 2, 2
+    )
+    states = soap(parts, weights, moment_one, moment_two, average, basis_left, basis_right)
+    small_states = small_step(
+        small_params, small_moment_one, small_moment_two, small_average, jnp.sum(small_parts, 0)[:6]
+    )
+    return (stitched, d_feat) + tuple(states) + small_states
+
+
+def plain_body(
     features,
     counts,
     weights,
@@ -62,7 +520,9 @@
     partial_sums = jnp.einsum(
         "tro,tio->tri", dz_low, weights_low, preferred_element_type=jnp.float32
     )
-    d_feat = lax.psum_scatter(partial_sums, "mp", scatter_dimension=2, tiled=True)
+    d_feat = lax.psum_scatter(
+        partial_sums.astype(jnp.float32), "mp", scatter_dimension=2, tiled=True
+    )
     grad = lax.psum_scatter(grad_part, "dp", scatter_dimension=1, tiled=True)
     small_grad = lax.psum(small_part, "dp")
     towers, n_in, n_out = grad.shape
@@ -77,9 +537,6 @@
     ).reshape(towers, n_in, n_out)
     new_weights = weights - rate_main * (step_back + decay_weight * weights)
     new_average = ema_decay * average + (1.0 - ema_decay) * new_weights
-    small_first, small_second, small_dir = adam_part(small_moment_one, small_moment_two, small_grad)
-    small_new = small_params - rate_small * small_dir
-    small_avg_new = ema_decay * small_average + (1.0 - ema_decay) * small_new
     return (
         stitched,
         d_feat.astype(jnp.bfloat16),
@@ -88,14 +545,16 @@
         new_weights,
         new_average,
         new_weights.astype(jnp.bfloat16),
-        small_first,
-        small_second,
-        small_new,
-        small_avg_new,
-    )
+    ) + small_step(small_params, small_moment_one, small_moment_two, small_average, small_grad)
 
 
 def solution(mesh):
+    def body(features, counts, weights, *rest):
+        dp, mp = mesh.shape["dp"], mesh.shape["mp"]
+        tiles = features.shape[2] % 128 == 0 and weights.shape[2] % 128 == 0
+        suits = dp == 4 and mp == 2 * dp and tiles and features.shape[1] % 64 == 0
+        return (line_body if suits else plain_body)(features, counts, weights, *rest)
+
     return jax.shard_map(
         body,
         mesh=mesh,

time: 2090 us -> 1200 us (0.57)
  waiting for transfers between devices: 1580 us -> 6.64 us
  Pallas kernels: 0 us -> 1030 us
  matrix products: 253 us -> 99.4 us
  local copies, waits for them, and re-layouts: 127 us -> 27.6 us
  other arithmetic: 83.8 us -> 26.2 us
    pallas_call x0 -> x3, Pallas kernels: none -> 1030 us  [the longest x1 494 us: reduce(): pl.pallas_call(functools.partial(reduce_kernel, chips, chunks), out_shape...]
    reduce_scatter x2 -> x0, waiting for transfers between devices: 932 us -> none  [the longest x1 607 us: body(): lax.psum_scatter(partial_sums, 'mp', scatter_dimension=2, tiled=True)]
    all_gather x3 -> x1, waiting for transfers between devices: 651 us -> 0.01 us  [line_body(): lax.all_gather(result.astype(jnp.bfloat16), 'mp', axis=2, tiled=True)]
    dot_general x7 -> x3, matrix products: 253 us -> 99.4 us  [the longest x1 34.2 us: line_body(): jnp.einsum('tri,tio->tro', wide_f, wide_w, preferred_element_type=jnp.flo...]
    reshape x4 -> x0, local copies, waits for them, and re-layouts: 63.4 us -> none  [the longest x1 16.4 us: body(): rotated = jnp.einsum('trcai,tracb,trcbj->tricj', basis_left, blocks, basi...]
    transpose x2 -> x0, local copies, waits for them, and re-layouts: 44.2 us -> none  [the longest x1 23.6 us: body(): jnp.einsum('trcai,tricj,trcbj->tracb', basis_left, turned, basis_right, p...]
    div x1 -> x0, other arithmetic: 22.3 us -> none  [adam_part(): first / (1.0 - beta_one ** STEP)]
  transfers between devices with their start and end apart: 5 -> 3, of which waited for: 5 -> 2; matrix products, arithmetic and copies ran while one was open for 18% -> 6% of each run, Pallas kernels for 0% -> 54%
where the time goes in v2:
time: 1200 us
  Pallas kernels  1030 us (86%)
  matrix products  99.4 us (8%)
  local copies, waits for them, and re-layouts  27.6 us (2%)
  other arithmetic  26.2 us (2%)
  between operations  14.2 us (1%)
    pallas_call x1, Pallas kernels, reduce(): pl.pallas_call(functools.partial(reduce_kernel, chips, chunks), out_shape...  494 us
    pallas_call x1, Pallas kernels, gather(): pl.pallas_call(functools.partial(gather_kernel, chips, chunks), out_shape...  382 us
    pallas_call x1, Pallas kernels, soap(): pl.pallas_call(soap_body, grid=(towers, 2, steps), in_specs=[pl.BlockSpec...  152 us
    dot_general x1, matrix products, line_body(): jnp.einsum('tri,tio->tro', wide_f, wide_w, preferred_element_type=jnp.flo...  34.2 us
    dot_general x1, matrix products, line_body(): jnp.einsum('tro,tio->tri', wide_dz, wide_w, preferred_element_type=jnp.fl...  33.8 us
    dot_general x1, matrix products, line_body(): jnp.einsum('tri,tro->tio', wide_f, wide_dz, preferred_element_type=jnp.fl...  31.4 us
  transfers between devices with their start and end apart: 3, of which 2 were waited for; matrix products, arithmetic and copies ran while one was open for 6% of the time, Pallas kernels for 54%

profile of v2, /device:TPU:17, one launch (start us, length us, event | category | flops | bytes accessed | tf_op | source)
XLA Modules:
  0.0 1203.9 jit_solution(1716403276050944978)
XLA Ops:
  7.2 6.5 convert_element_type.27.w_ref
  13.7 382.1 %gather.1 = (bf16[2,1280,4608]{2,1,0:T(8,128)(2,1)}, bf16[2,4608,1024]{2,1,0:T(8,128)(2,1)}) custom-call(bf16[2,1280,1152]{2,1,0:T(8,128)(2,1)} %f_ref.1, bf16[2,2304,512]{2,1,0:T(8,128)(2,1)} %convert_element_type.27.w_ref), custom_call_target="tpu_custom_call" | custom-call | bytes 838860800 | tf_op jit(solution)/shard_map/gather/pallas_call | solution.py:255
  395.8 34.2 %fusion.16 = f32[2,1280,1024]{2,1,0:T(8,128)} fusion(bf16[2,1280,4608]{2,1,0:T(8,128)(2,1)} %get-tuple-element.21, bf16[2,4608,1024]{2,1,0:T(8,128)(2,1)} %get-tuple-element.22), kind=kOutput, calls=%fused_computation.39 | convolution fusion | flops 24159191040 | bytes 52953088 | tf_op jit(solution)/shard_map/tri,tio->tro/dot_general | solution.py:472
  430.0 5.6 slice.43
  435.6 0.9 collective-permute-start
  436.5 0.6 reduce_sum.62
  437.2 0.6 fusion.9
  437.9 0.4 convert_multiply_fusion
  438.3 4.2 slice_multiply_fusion.3
  442.6 2.6 collective-permute-done
  445.2 9.0 fusion.13
  454.2 1.4 multiply_reduce_fusion.3
  455.7 1.9 fusion.7
  457.5 0.8 copy-done.2
  458.7 0.6 pad.40.ps_ref
  459.4 4.0 collective-permute-done.1
  463.4 31.4 %convolution_convert_fusion.1.pg_ref = bf16[2,4608,1024]{2,1,0:T(8,128)(2,1)} fusion(bf16[2,1280,4608]{2,1,0:T(8,128)(2,1)} %get-tuple-element.21, bf16[2,1280,512]{2,1,0:T(8,128)(2,1)} %collective-permute-done.1, bf16[2,1280,512]{2,1,0:T(8,128)(2,1)S(1)} %copy-done.2), kind=kOutput, calls=%fused_computation.1 | convolution fusion | flops 24179113984 | bytes 47710208 | tf_op jit(solution)/shard_map/tri,tro->tio/dot_general | solution.py:480
  494.8 33.8 %convolution_convert_fusion.pd_ref = bf16[2,1280,4608]{2,1,0:T(8,128)(2,1)} fusion(bf16[2,4608,1024]{2,1,0:T(8,128)(2,1)} %get-tuple-element.22, bf16[2,1280,512]{2,1,0:T(8,128)(2,1)} %collective-permute-done.1, bf16[2,1280,512]{2,1,0:T(8,128)(2,1)S(1)} %copy-done.2), kind=kOutput, calls=%fused_computation | convolution fusion | flops 24181473280 | bytes 47710208 | tf_op jit(solution)/shard_map/tro,tio->tri/dot_general | solution.py:479
  528.6 494.0 %reduce.5 = (bf16[2,1280,1152]{2,1,0:T(8,128)(2,1)}, bf16[4,2,2,1152,512]{4,3,2,1,0:T(8,128)(2,1)}, f32[4,8,512]{2,1,0:T(8,128)}) custom-call(bf16[2,1280,4608]{2,1,0:T(8,128)(2,1)} %convolution_convert_fusion.pd_ref, bf16[2,4608,1024]{2,1,0:T(8,128)(2,1)} %convolution_convert_fusion.1.pg_ref, f32[8,512]{1,0:T(8,128)} %pad.40.ps_ref), custom_call_target="tpu_custom_call" | custom-call | bytes 838860800 | tf_op jit(solution)/shard_map/reduce/pallas_call | solution.py:427
  1022.6 0.9 reduce_sum.71
  1023.5 152.4 %soap.1 = (f32[2,2304,512]{2,1,0:T(8,128)}, f32[2,2304,512]{2,1,0:T(8,128)}, f32[2,2304,512]{2,1,0:T(8,128)}, f32[2,2304,512]{2,1,0:T(8,128)}, bf16[2,2304,512]{2,1,0:T(8,128)(2,1)}) custom-call(bf16[4,2,2,1152,512]{4,3,2,1,0:T(8,128)(2,1)} %get-tuple-element.24.parts, f32[2,2304,512]{2,1,0:T(8,128)} %weights.1, f32[2,2304,512]{2,1,0:T(8,128)} %moment_a.1, ...), custom_call_target="tpu_custom_call" | custom-call | flops 2415919104 | bytes 136314880 | tf_op jit(solution)/shard_map/soap/pallas_call | solution.py:95
  1175.9 0.6 add_multiply_fusion
  1176.5 18.0 %copy.28 = bf16[2,1280,4096]{2,1,0:T(8,128)(2,1)} copy(bf16[2,1280,4096]{2,1,0:T(8,128)(2,1)} %all-gather.2.cloned.1.call-done) | data formatting | bytes 41943040
  1194.5 2.6 copy.29
  (32 shorter events, 0.5 us)
Async XLA Ops:
  7.2 1169.4 %all-gather.2.cloned.1.call-start = ((), (), s32[]{:S(2)}) async-start(), calls=%async_computation | async-start | bytes 23592960 | tf_op jit(solution)/shard_map/all_gather | solution.py:475
  430.0 6.5 copy-start.8
  430.0 7.8 copy-start.3
  430.0 7.8 copy-start.1
  435.6 9.6 collective-permute-start
  437.9 7.3 slice-start
  438.3 6.9 slice-start.1
  438.3 6.9 slice-start.2
  438.3 6.9 slice-start.3
  455.6 2.7 copy-start.2
  458.3 5.0 collective-permute-start.1
  1023.4 152.4 %copy-start.4 = (f32[6,512]{1,0:T(8,128)S(1)}, f32[6,512]{1,0:T(8,128)}, u32[]{:S(2)}) copy-start(f32[6,512]{1,0:T(8,128)} %param.16) | copy-start | bytes 36868
  1023.4 152.4 %copy-start.5 = (f32[6,512]{1,0:T(8,128)S(1)}, f32[6,512]{1,0:T(8,128)}, u32[]{:S(2)}) copy-start(f32[6,512]{1,0:T(8,128)} %param.25) | copy-start | bytes 36868
  1023.5 152.4 %copy-start.6 = (f32[6,512]{1,0:T(8,128)S(1)}, f32[6,512]{1,0:T(8,128)}, u32[]{:S(2)}) copy-start(f32[6,512]{1,0:T(8,128)} %param.24) | copy-start | bytes 36868
  1023.5 152.4 %copy-start.7 = (f32[6,512]{1,0:T(8,128)S(1)}, f32[6,512]{1,0:T(8,128)}, u32[]{:S(2)}) copy-start(f32[6,512]{1,0:T(8,128)} %param.23) | copy-start | bytes 36868
  1176.5 18.0 %copy-start = (bf16[2,1280,1152]{2,1,0:T(8,128)(2,1)S(1)}, bf16[2,1280,1152]{2,1,0:T(8,128)(2,1)}, u32[]{:S(2)}) copy-start(bf16[2,1280,1152]{2,1,0:T(8,128)(2,1)} %get-tuple-element.67) | copy-start | bytes 17694724
Sparse Core Ops, SparseCore 0:
  457.7 291.2 all-gather.1

commit v3 on v2

--- a/solution.py
+++ b/solution.py
@@ -124,42 +124,51 @@
     pl.semaphore_wait(barrier, expected)
 
 
-def gather_kernel(chips, chunks, f_ref, w_ref, fg_ref, wg_ref, f_send, f_recv, w_send, w_recv, own_sem):
+def gather_kernel(chips, ranges, share, *refs):
+    if share:
+        (f_ref, w_ref, o_ref, pick_ref, fg_ref, wg_ref, og_ref, offer_f, offer_o, taken_f, taken_o,
+         f_send, f_recv, w_send, w_recv, own_sem, x_send, x_recv, y_sem) = refs
+    else:
+        f_ref, w_ref, fg_ref, wg_ref, f_send, f_recv, w_send, w_recv, own_sem = refs
     dp, chip, core = place()
     towers, rows, depth = f_ref.shape
     cols = w_ref.shape[2]
-    part = rows // chunks
     across, along = dp ^ 1, dp ^ 2
+    others = (across, along, dp ^ 3)
     at = lambda c, k: (c, 2 * chip + k)
 
     meet([(chip > 0, (dp, 2 * (chip - 1) + core)), (chip < chips - 1, (dp, 2 * (chip + 1) + core)),
-          (chip >= 0, at(dp, 1 - core))] + [(chip >= 0, at(c, k)) for c in (across, along) for k in (0, 1)])
-
-    def feature(step, way, t, k):
-        shard = chip - step if way == 0 else chip + step
-        there = chip + 1 if way == 0 else chip - 1
+          (chip >= 0, at(dp, 1 - core))] + [(chip >= 0, at(c, k)) for c in (across, along) for k in (0, 1)]
+         + ([(chip >= 0, at(others[2], core))] if share else []))
+
+    def copies(step, way, t, k, shard, there):
         lanes = pl.ds(pl.multiple_of(shard * depth, 128), depth)
-        rws = pl.ds(k * part, part)
-        src = f_ref.at[t, rws] if step == 0 else fg_ref.at[t, rws, lanes]
-        n = ((way * (chips - 1) + step) * towers + t) * chunks + k
+        rws = pl.ds(*ranges[k])
+        src = fg_ref.at[t, rws, lanes]
+        if step == 0:
+            src = taken_f.at[t] if share and k == len(ranges) - 1 else f_ref.at[t, rws]
+        n = ((way * (chips - 1) + step) * towers + t) * len(ranges) + k
         return pltpu.make_async_remote_copy(
             src_ref=src, dst_ref=fg_ref.at[t, rws, lanes], send_sem=f_send.at[n], recv_sem=f_recv.at[n],
             device_id=(dp, 2 * there + core), device_id_type=MESH)
 
+    def feature(step, way, t, k):
+        return copies(step, way, t, k, chip - step if way == 0 else chip + step, chip + 1 if way == 0 else chip - 1)
+
+    def incoming(step, way, t, k):
+        return copies(step, way, t, k, chip - 1 - step if way == 0 else chip + 1 + step, chip)
+
     def sends(step, way):
         return (chip < chips - 1) & (chip >= step) if way == 0 else (chip > 0) & (chip + step < chips)
 
     def receives(step, way):
         return chip > step if way == 0 else chip + step < chips - 1
 
-    def incoming(step, way, t, k):
-        shard = chip - 1 - step if way == 0 else chip + 1 + step
-        lanes = pl.ds(pl.multiple_of(shard * depth, 128), depth)
-        rws = pl.ds(k * part, part)
-        n = ((way * (chips - 1) + step) * towers + t) * chunks + k
-        return pltpu.make_async_remote_copy(
-            src_ref=f_ref.at[t, rws], dst_ref=fg_ref.at[t, rws, lanes], send_sem=f_send.at[n], recv_sem=f_recv.at[n],
-            device_id=(dp, 2 * chip + core), device_id_type=MESH)
+    def launch(t, k):
+        for way in (0, 1):
+            @pl.when(sends(0, way))
+            def _():
+                feature(0, way, t, k).start()
 
     def block(owner, slot, t):
         return wg_ref.at[t, pl.ds(pl.multiple_of(owner * depth, 128), depth), pl.ds(pl.multiple_of(slot * cols, 128), cols)]
@@ -185,25 +194,63 @@
             src_ref=block(owner, slot, t), dst_ref=block(owner, slot, t), send_sem=w_send.at[n], recv_sem=w_recv.at[n],
             device_id=at(dp, core), device_id_type=MESH).wait_recv()
 
-    own = [pltpu.make_async_copy(f_ref.at[t], fg_ref.at[t, :, pl.ds(pl.multiple_of(chip * depth, 128), depth)], own_sem.at[t])
-           for t in range(towers)]
+    def offer(kind, what):
+        first, size = share[1 + kind]
+        src, dst = ((f_ref, offer_f), (o_ref, offer_o))[what]
+        n = kind * 2 + what
+        return pltpu.make_async_remote_copy(
+            src_ref=src.at[:, pl.ds(first, size)], dst_ref=dst.at[1 + kind], send_sem=x_send.at[n], recv_sem=x_recv.at[n],
+            device_id=at(others[kind], core), device_id_type=MESH)
+
+    def choose(offers, taken):
+        def strip(i, _):
+            rws = pl.ds(pl.multiple_of(i * 16, 16), 16)
+            for t in range(towers):
+                value = offers[0, t, rws].astype(jnp.float32) * pick_ref[0]
+                for kind in range(3):
+                    value = value + offers[1 + kind, t, rws].astype(jnp.float32) * pick_ref[1 + kind]
+                taken[t, rws] = value.astype(jnp.bfloat16)
+            return 0
+        lax.fori_loop(0, taken.shape[1] // 16, strip, 0)
+
+    fixed = len(ranges) - 1 if share else len(ranges)
+    kept = ranges[fixed][0] if share else rows
+    mine = pl.ds(pl.multiple_of(chip * depth, 128), depth)
+    own = [pltpu.make_async_copy(f_ref.at[t, pl.ds(0, kept)], fg_ref.at[t, pl.ds(0, kept), mine], own_sem.at[t]) for t in range(towers)]
     own += [pltpu.make_async_copy(w_ref.at[t, pl.ds(pl.multiple_of(core * depth, 128), depth)], block(dp, 0, t), own_sem.at[2 + t])
             for t in range(towers)]
 
-    pieces = [(t, k) for t in range(towers) for k in range(chunks)]
+    pieces = [(t, k) for k in range(len(ranges)) for t in range(towers)]
+    if share:
+        for kind in (2, 0, 1):
+            offer(kind, 0).start()
+        keep = [pltpu.make_async_copy(src.at[:, pl.ds(*share[0])], dst.at[0], y_sem.at[n])
+                for n, (src, dst) in enumerate(((f_ref, offer_f), (o_ref, offer_o)))]
+        for copy in keep:
+            copy.start()
     for t, k in pieces:
-        for way in (0, 1):
-            @pl.when(sends(0, way))
-            def _():
-                feature(0, way, t, k).start()
+        if k < fixed:
+            launch(t, k)
+    for copy in own:
+        copy.start()
+    if share:
+        for kind in range(3):
+            offer(kind, 0).wait_recv()
+        keep[0].wait()
+        choose(offer_f, taken_f)
+        own_share = [pltpu.make_async_copy(taken_f.at[t], fg_ref.at[t, pl.ds(*ranges[fixed]), mine], y_sem.at[2 + t]) for t in range(towers)]
+        for t in range(towers):
+            launch(t, fixed)
+            own_share[t].start()
     for t in (0, 1):
         for k in (0, 1):
             weight(0, k, t).start()
             weight(1, k, 1 - t).start()
     for t in (0, 1):
         weight(2, 1 - core, t).start()
-    for copy in own:
-        copy.start()
+    if share:
+        for kind in (2, 0, 1):
+            offer(kind, 1).start()
 
     for step in range(chips - 1):
         for t, k in pieces:
@@ -215,7 +262,7 @@
                     @pl.when(sends(step + 1, way))
                     def _():
                         feature(step + 1, way, t, k).start()
-            if step == 0 and (t, k) == pieces[len(pieces) // 2 - 1]:
+            if step == 0 and (t, k) == pieces[-1]:
                 for slot in (0, 1):
                     arrived(0, slot, 0)
                     forward(0, slot).start()
@@ -229,6 +276,19 @@
         forward(1, slot).wait_recv()
     for t in (0, 1):
         arrived(2, 1, t)
+    if share:
+        for kind in range(3):
+            offer(kind, 1).wait_recv()
+        keep[1].wait()
+        choose(offer_o, taken_o)
+        store = pltpu.make_async_copy(taken_o, og_ref, y_sem.at[1])
+        store.start()
+        store.wait()
+        for copy in own_share:
+            copy.wait()
+        for kind in range(3):
+            offer(kind, 0).wait_send()
+            offer(kind, 1).wait_send()
     for t in (0, 1):
         for k in (0, 1):
             weight(0, k, t).wait_send()
@@ -247,32 +307,48 @@
         copy.wait()
 
 
-def gather(features, weights_low, chips, chunks, ident):
-    towers, rows, depth = features.shape
+def gather(features, weights_low, chips, ranges, ident, share=None, out_grad=None, pick=None):
+    towers, _, depth = features.shape
     cols = weights_low.shape[2]
-    count = 2 * (chips - 1) * towers * chunks
+    rows = sum(ranges[-1])
+    count = 2 * (chips - 1) * towers * len(ranges)
     dma = pltpu.SemaphoreType.DMA
+    bf16 = jnp.bfloat16
+    anywhere = pl.BlockSpec(memory_space=pl.ANY)
+    out_shape = [jax.ShapeDtypeStruct((towers, rows, chips * depth), bf16),
+                 jax.ShapeDtypeStruct((towers, chips * depth, 2 * cols), bf16)]
+    scratch = [dma((count,)), dma((count,)), dma((16,)), dma((16,)), dma((4,))]
+    operands, in_specs = [features, weights_low], [anywhere] * 2
+    if share:
+        size = share[0][1]
+        out_shape.append(jax.ShapeDtypeStruct((towers, size, cols), bf16))
+        scratch = ([pltpu.VMEM((n + (towers, size, w)), bf16) for n in ((4,), ()) for w in (depth, cols)]
+                   + scratch + [dma((6,)), dma((6,)), dma((4,))])
+        operands += [out_grad, pick]
+        in_specs += [anywhere, pl.BlockSpec(memory_space=pltpu.SMEM)]
     return pl.pallas_call(
-        functools.partial(gather_kernel, chips, chunks),
-        out_shape=[jax.ShapeDtypeStruct((towers, rows, chips * depth), jnp.bfloat16),
-                   jax.ShapeDtypeStruct((towers, chips * depth, 2 * cols), jnp.bfloat16)],
-        in_specs=[pl.BlockSpec(memory_space=pl.ANY)] * 2,
-        out_specs=[pl.BlockSpec(memory_space=pl.ANY)] * 2,
-        scratch_shapes=[dma((count,)), dma((count,)), dma((16,)), dma((16,)), dma((4,))],
-        compiler_params=pltpu.CompilerParams(collective_id=ident, has_side_effects=True),
+        functools.partial(gather_kernel, chips, ranges, share),
+        out_shape=out_shape,
+        in_specs=in_specs,
+        out_specs=[anywhere] * len(out_shape),
+        scratch_shapes=scratch,
+        compiler_params=pltpu.CompilerParams(collective_id=ident, has_side_effects=True, vmem_limit_bytes=32 * 2**20),
         cost_estimate=pl.CostEstimate(flops=0, bytes_accessed=800 * 2**20, transcendentals=0),
         name="gather",
-    )(features, weights_low)
-
-
-def reduce_kernel(chips, chunks, pd_ref, pg_ref, ps_ref, d_ref, gr_ref, sr_ref, held, term, total,
-                  d_send, d_recv, t_sem, o_sem, g_send, g_recv, s_send, s_recv, own_sem):
+    )(*operands)
+
+
+def reduce_kernel(chips, ranges, share, pd_ref, pg_ref, ps_ref, d_ref, gr_ref, sr_ref, *refs):
+    if share:
+        back_ref, refs = refs[0], refs[1:]
+        held, term, total, d_send, d_recv, t_sem, o_sem, g_send, g_recv, s_send, s_recv, own_sem, b_send, b_recv = refs
+    else:
+        held, term, total, d_send, d_recv, t_sem, o_sem, g_send, g_recv, s_send, s_recv, own_sem = refs
     dp, chip, core = place()
     towers, rows, depth = d_ref.shape
     cols = pg_ref.shape[2] // 2
-    part = rows // chunks
     across, along = dp ^ 1, dp ^ 2
-    others = (across, along, 3 - dp)
+    others = (across, along, dp ^ 3)
     at = lambda c, k: (c, 2 * chip + k)
 
     meet([(chip > 0, (dp, 2 * (chip - 1) + core)), (chip < chips - 1, (dp, 2 * (chip + 1) + core)),
@@ -306,23 +382,26 @@
         return (chip > 0) & (chip <= step + 1) if way == 0 else (chip < chips - 1) & (chips - 1 - chip <= step + 1)
 
     def own_term(goal, t, k):
-        return pd_ref.at[t, pl.ds(k * part, part), pl.ds(pl.multiple_of(goal * depth, 128), depth)]
+        return pd_ref.at[t, pl.ds(*ranges[k]), pl.ds(pl.multiple_of(goal * depth, 128), depth)]
 
     def partial(step, way, t, k, first):
-        n = ((way * (chips - 1) + step) * towers + t) * chunks + k
-        src = own_term(target(step, way), t, k) if first else held.at[way, step - 1, t, pl.ds(k * part, part)]
+        n = ((way * (chips - 1) + step) * towers + t) * len(ranges) + k
+        src = own_term(target(step, way), t, k) if first else held.at[way, step - 1, t, pl.ds(*ranges[k])]
         there = chip + 1 if way == 0 else chip - 1
         return pltpu.make_async_remote_copy(
-            src_ref=src, dst_ref=held.at[way, step, t, pl.ds(k * part, part)], send_sem=d_send.at[n], recv_sem=d_recv.at[n],
+            src_ref=src, dst_ref=held.at[way, step, t, pl.ds(*ranges[k])], send_sem=d_send.at[n], recv_sem=d_recv.at[n],
             device_id=(dp, 2 * there + core), device_id_type=MESH)
 
     def landed(step, way, t, k):
-        n = ((way * (chips - 1) + step) * towers + t) * chunks + k
-        ref = held.at[way, step, t, pl.ds(k * part, part)]
+        n = ((way * (chips - 1) + step) * towers + t) * len(ranges) + k
+        ref = held.at[way, step, t, pl.ds(*ranges[k])]
         pltpu.make_async_remote_copy(src_ref=ref, dst_ref=ref, send_sem=d_send.at[n], recv_sem=d_recv.at[n],
                                      device_id=(dp, 2 * chip + core), device_id_type=MESH).wait_recv()
 
-    pieces = [(t, k) for t in range(towers) for k in range(chunks)]
+    order = range(len(ranges))
+    if share:
+        order = [len(ranges) - 1] + list(range(len(ranges) - 1))
+    pieces = [(t, k) for k in order for t in range(towers)]
     ends = (chip == 0, chip == chips - 1)
     for t, k in pieces:
         for way in (0, 1):
@@ -343,7 +422,7 @@
                 grad(kind, k, t).start()
         grad(3, 1 - core, t).start()
 
-    strip = 32
+    strip = 16
 
     for step in range(1, chips - 1):
         for t, k in pieces:
@@ -354,47 +433,66 @@
 
                 @pl.when(sends(step, way) & jnp.logical_not(ends[way]))
                 def _():
-                    load = pltpu.make_async_copy(own_term(target(step, way), t, k), term.at[way], t_sem.at[way])
+                    start, size = ranges[k]
+                    load = pltpu.make_async_copy(own_term(target(step, way), t, k), term.at[way, pl.ds(0, size)], t_sem.at[way])
                     load.start()
                     landed(step - 1, way, t, k)
                     load.wait()
 
                     def add(i, _):
                         rws = pl.ds(pl.multiple_of(i * strip, strip), strip)
-                        all_rows = pl.ds(pl.multiple_of(k * part + i * strip, strip), strip)
+                        all_rows = pl.ds(pl.multiple_of(start + i * strip, strip), strip)
                         held[way, step - 1, t, all_rows] = (
                             held[way, step - 1, t, all_rows].astype(jnp.float32) + term[way, rws].astype(jnp.float32)
                         ).astype(jnp.bfloat16)
                         return 0
-                    lax.fori_loop(0, part // strip, add, 0)
+                    lax.fori_loop(0, size // strip, add, 0)
                     partial(step, way, t, k, False).start()
+
+    stores = []
+    handed = towers if share else 0
+
+    def hand(kind, n):
+        t, k = pieces[n]
+        return pltpu.make_async_remote_copy(
+            src_ref=total.at[n % 2, pl.ds(0, ranges[k][1])], dst_ref=back_ref.at[kind, t], send_sem=b_send.at[kind * 2 + t],
+            recv_sem=b_recv.at[kind * 2 + t], device_id=at(others[kind], core), device_id_type=MESH)
 
     for n, (t, k) in enumerate(pieces):
         s = n % 2
-        load = pltpu.make_async_copy(own_term(chip, t, k), term.at[s], t_sem.at[s])
+        start, size = ranges[k]
+        load = pltpu.make_async_copy(own_term(chip, t, k), term.at[s, pl.ds(0, size)], t_sem.at[s])
         load.start()
         for way in (0, 1):
             @pl.when(receives(chips - 2, way))
             def _():
                 landed(chips - 2, way, t, k)
         load.wait()
-        store = pltpu.make_async_copy(total.at[s], d_ref.at[t, pl.ds(k * part, part)], o_sem.at[s])
         if n >= 2:
-            store.wait()
+            stores[n - 2].wait()
+            for kind in range(3 if n - 2 < handed else 0):
+                hand(kind, n - 2).wait_send()
 
         def finish(i, _):
             rws = pl.ds(pl.multiple_of(i * strip, strip), strip)
-            all_rows = pl.ds(pl.multiple_of(k * part + i * strip, strip), strip)
+            all_rows = pl.ds(pl.multiple_of(start + i * strip, strip), strip)
             value = term[s, rws].astype(jnp.float32)
             for way in (0, 1):
                 here = receives(chips - 2, way)
                 value = value + jnp.where(here, held[way, chips - 2, t, all_rows].astype(jnp.float32), 0.0)
             total[s, rws] = value.astype(jnp.bfloat16)
             return 0
-        lax.fori_loop(0, part // strip, finish, 0)
-        store.start()
-    for n in range(min(2, len(pieces))):
-        pltpu.make_async_copy(total.at[n], d_ref.at[0, pl.ds(0, part)], o_sem.at[n]).wait()
+        lax.fori_loop(0, size // strip, finish, 0)
+        stores.append(pltpu.make_async_copy(total.at[s, pl.ds(0, size)], d_ref.at[t, pl.ds(start, size)], o_sem.at[s]))
+        stores[n].start()
+        if n < handed:
+            for kind in (2, 0, 1):
+                hand(kind, n).start()
+    for store in stores[-2:]:
+        store.wait()
+    for n in range(handed):
+        for kind in range(3):
+            hand(kind, n).wait_recv()
 
     for t in range(towers):
         for kind in range(3):
@@ -418,22 +516,28 @@
         copy.wait()
 
 
-def reduce(partial_d, partial_g, partial_s, chips, chunks, ident):
+def reduce(partial_d, partial_g, partial_s, chips, ranges, ident, share=None):
     towers, rows, wide = partial_d.shape
     depth, cols = wide // chips, partial_g.shape[2] // 2
-    count = 2 * (chips - 1) * towers * chunks
+    count = 2 * (chips - 1) * towers * len(ranges)
+    part = max(size for _, size in ranges)
     dma = pltpu.SemaphoreType.DMA
     bf16 = jnp.bfloat16
+    out_shape = [jax.ShapeDtypeStruct((towers, rows, depth), bf16),
+                 jax.ShapeDtypeStruct((4, 2, towers, depth, cols), bf16),
+                 jax.ShapeDtypeStruct((4,) + partial_s.shape, jnp.float32)]
+    more = []
+    if share:
+        out_shape.append(jax.ShapeDtypeStruct((3, towers, ranges[-1][1], depth), bf16))
+        more = [dma((6,)), dma((6,))]
     return pl.pallas_call(
-        functools.partial(reduce_kernel, chips, chunks),
-        out_shape=[jax.ShapeDtypeStruct((towers, rows, depth), bf16),
-                   jax.ShapeDtypeStruct((4, 2, towers, depth, cols), bf16),
-                   jax.ShapeDtypeStruct((4,) + partial_s.shape, jnp.float32)],
+        functools.partial(reduce_kernel, chips, ranges, share),
+        out_shape=out_shape,
         in_specs=[pl.BlockSpec(memory_space=pl.ANY)] * 3,
-        out_specs=[pl.BlockSpec(memory_space=pl.ANY)] * 3,
+        out_specs=[pl.BlockSpec(memory_space=pl.ANY)] * len(out_shape),
         scratch_shapes=[pltpu.VMEM((2, chips - 1, towers, rows, depth), bf16),
-                        pltpu.VMEM((2, rows // chunks, depth), bf16), pltpu.VMEM((2, rows // chunks, depth), bf16),
-                        dma((count,)), dma((count,)), dma((2,)), dma((2,)), dma((16,)), dma((16,)), dma((3,)), dma((3,)), dma((towers + 1,))],
+                        pltpu.VMEM((2, part, depth), bf16), pltpu.VMEM((2, part, depth), bf16),
+                        dma((count,)), dma((count,)), dma((2,)), dma((2,)), dma((16,)), dma((16,)), dma((3,)), dma((3,)), dma((towers + 1,))] + more,
         compiler_params=pltpu.CompilerParams(collective_id=ident, has_side_effects=True, vmem_limit_bytes=56 * 2**20),
         cost_estimate=pl.CostEstimate(flops=0, bytes_accessed=800 * 2**20, transcendentals=0),
         name="reduce",
@@ -444,6 +548,78 @@
     first, second, direction = adam_part(small_moment_one, small_moment_two, small_grad)
     fresh = small_params - rate_small * direction
     return first, second, fresh, ema_decay * small_average + (1.0 - ema_decay) * fresh
+
+
+def towers_pass(wide_f, wide_w, small_params, out_grad, live_rows):
+    cols = out_grad.shape[2]
+    swap = [(i, i ^ 1) for i in range(lax.axis_size("mp"))]
+    partial = jnp.einsum("tri,tio->tro", wide_f, wide_w, preferred_element_type=jnp.float32)
+    product = partial[:, :, :cols] + lax.ppermute(partial[:, :, cols:], "mp", swap)
+    result, back = jax.vjp(lambda a, b: stitch_local(a, b, live_rows), product, small_params)
+    dz, small_part = back(out_grad.astype(jnp.float32))
+    dz_low = dz.astype(jnp.bfloat16)
+    wide_dz = jnp.concatenate([dz_low, lax.ppermute(dz_low, "mp", swap)], axis=2)
+    partial_d = jnp.einsum("tro,tio->tri", wide_dz, wide_w, preferred_element_type=jnp.float32)
+    partial_g = jnp.einsum("tri,tro->tio", wide_f, wide_dz, preferred_element_type=jnp.float32)
+    small_part = jnp.pad(small_part, ((0, 2), (0, 0)))
+    return result.astype(jnp.bfloat16), partial_d.astype(jnp.bfloat16), partial_g.astype(jnp.bfloat16), small_part
+
+
+def update(d_feat, stitched, parts, small_parts, states, small_states):
+    small_grad = jnp.sum(small_parts, 0)[: small_states[0].shape[0]]
+    return (stitched, d_feat) + tuple(soap(parts, *states)) + small_step(*small_states, small_grad)
+
+
+def own_rows(features, weights_low, small_params, out_grad, totals, states, small_states):
+    rows = features.shape[1]
+    chips = lax.axis_size("mp") // 2
+    ranges = ((0, rows // 2), (rows // 2, rows // 2))
+    live_rows = (jnp.arange(rows, dtype=jnp.int32) < totals[lax.axis_index("dp")]).astype(jnp.float32)
+    wide_f, wide_w = gather(features, weights_low, chips, ranges, 1)
+    result, partial_d, partial_g, small_part = towers_pass(wide_f, wide_w, small_params, out_grad, live_rows)
+    stitched = lax.all_gather(result, "mp", axis=2, tiled=True)
+    d_feat, parts, small_parts = reduce(partial_d, partial_g, small_part, chips, ranges, 2)
+    return update(d_feat, stitched, parts, small_parts, states, small_states)
+
+
+def shares(rows):
+    keep = rows * 15 // 32 // 16 * 16
+    size = -(-(rows - keep) // 64) * 16
+    return keep, ((keep, size), (keep + size, size), (keep + 2 * size, size), (rows - size, size))
+
+
+def shared_rows(features, weights_low, small_params, out_grad, totals, states, small_states):
+    rows = features.shape[1]
+    chips = lax.axis_size("mp") // 2
+    keep, share = shares(rows)
+    size = share[0][1]
+    again = share[2][0] + size - share[3][0]
+    half = keep // 32 * 16
+    ranges = ((0, half), (half, keep - half), share[0])
+    dp = lax.axis_index("dp")
+    giver = jnp.argmax(totals).astype(jnp.int32)
+    which = dp ^ giver
+    pick = (jnp.arange(4, dtype=jnp.int32) == which).astype(jnp.float32)
+    starts = jnp.array([first for first, _ in share], jnp.int32)
+    slot = starts[which] + jnp.arange(size, dtype=jnp.int32)
+    fresh = (jnp.arange(size, dtype=jnp.int32) >= again) | (which != 3)
+    live = jnp.concatenate([jnp.arange(keep, dtype=jnp.int32) < totals[dp], (slot < totals[giver]) & fresh])
+    wide_f, wide_w, taken = gather(features, weights_low, chips, ranges, 3, share, out_grad, pick)
+    out_grad = jnp.concatenate([out_grad[:, :keep], taken], axis=1)
+    result, partial_d, partial_g, small_part = towers_pass(
+        wide_f, wide_w, small_params, out_grad, live.astype(jnp.float32)
+    )
+
+    def whole(here, back):
+        rest = jnp.concatenate([here[:, keep:], back[0], back[1], back[2][:, again:]], axis=1)
+        return jnp.concatenate([here[:, :keep], jnp.where(which == 0, rest, 0)], axis=1)
+
+    perms = [[(i, i ^ k) for i in range(4)] for k in (1, 2, 3)]
+    stitched = lax.all_gather(
+        whole(result, [lax.ppermute(result[:, keep:], "dp", p) for p in perms]), "mp", axis=2, tiled=True
+    )
+    d_feat, parts, small_parts, back = reduce(partial_d, partial_g, small_part, chips, ranges, 4, share)
+    return update(whole(d_feat, back), stitched, parts, small_parts, states, small_states)
 
 
 def line_body(
@@ -461,32 +637,20 @@
     small_moment_two,
     small_average,
 ):
-    cores = lax.axis_size("mp")
-    chips = cores // 2
-    cols = weights.shape[2]
-    swap = [(i, i ^ 1) for i in range(cores)]
-    slot_count = features.shape[1]
-    total = jnp.sum(counts)
-    live_rows = (jnp.arange(slot_count, dtype=jnp.int32) < total).astype(jnp.float32)
-    wide_f, wide_w = gather(features, weights.astype(jnp.bfloat16), chips, 2, 1)
-    partial = jnp.einsum("tri,tio->tro", wide_f, wide_w, preferred_element_type=jnp.float32)
-    product = partial[:, :, :cols] + lax.ppermute(partial[:, :, cols:], "mp", swap)
-    result, back = jax.vjp(lambda a, b: stitch_local(a, b, live_rows), product, small_params)
-    stitched = lax.all_gather(result.astype(jnp.bfloat16), "mp", axis=2, tiled=True)
-    dz, small_part = back(out_grad.astype(jnp.float32))
-    dz_low = dz.astype(jnp.bfloat16)
-    wide_dz = jnp.concatenate([dz_low, lax.ppermute(dz_low, "mp", swap)], axis=2)
-    partial_d = jnp.einsum("tro,tio->tri", wide_dz, wide_w, preferred_element_type=jnp.float32)
-    partial_g = jnp.einsum("tri,tro->tio", wide_f, wide_dz, preferred_element_type=jnp.float32)
-    small_part = jnp.pad(small_part, ((0, 2), (0, 0)))
-    d_feat, parts, small_parts = reduce(
-        partial_d.astype(jnp.bfloat16), partial_g.astype(jnp.bfloat16), small_part, chips, 2, 2
+    totals = lax.all_gather(jnp.sum(counts), "dp")
+    keep, _ = shares(features.shape[1])
+    return lax.cond(
+        jnp.sum(totals > keep) == 1,
+        shared_rows,
+        own_rows,
+        features,
+        weights.astype(jnp.bfloat16),
+        small_params,
+        out_grad,
+        totals,
+        (weights, moment_one, moment_two, average, basis_left, basis_right),
+        (small_params, small_moment_one, small_moment_two, small_average),
     )
-    states = soap(parts, weights, moment_one, moment_two, average, basis_left, basis_right)
-    small_states = small_step(
-        small_params, small_moment_one, small_moment_two, small_average, jnp.sum(small_parts, 0)[:6]
-    )
-    return (stitched, d_feat) + tuple(states) + small_states
 
 
 def plain_body(

time: 1200 us -> 945 us (0.79); the launches traced: 1200 us -> 935 us
  Pallas kernels: 1030 us -> 749 us
  matrix products: 99.4 us -> 67.7 us
    pallas_call x2, Pallas kernels: 876 us -> 596 us  [the longest x1 363 us: reduce(): pl.pallas_call(functools.partial(reduce_kernel, chips, ranges, share), ou...]
    dot_general x3, matrix products: 99.4 us -> 67.7 us  [the longest x1 23.8 us: towers_pass(): jnp.einsum('tri,tro->tio', wide_f, wide_dz, preferred_element_type=jnp.fl...]
  transfers between devices with their start and end apart: 3 -> 6, of which waited for: 2 -> 3; matrix products, arithmetic and copies ran while one was open for 6% -> 7% of each run, Pallas kernels for 54% -> 55%
where the time goes in v3:
time: 945 us; the launch traced here: 935 us
  Pallas kernels  749 us (79%)
  matrix products  67.7 us (7%)
  local copies, waits for them, and re-layouts  36.7 us (4%)
  other arithmetic  27.9 us (3%)
  waiting for transfers between devices  17.8 us (2%)
  between operations  15 us (2%)
  loops' own time  11.7 us (1%)
    pallas_call x1, Pallas kernels, reduce(): pl.pallas_call(functools.partial(reduce_kernel, chips, ranges, share), ou...  363 us
    pallas_call x1, Pallas kernels, gather(): pl.pallas_call(functools.partial(gather_kernel, chips, ranges, share), ou...  233 us
    pallas_call x1, Pallas kernels, soap(): pl.pallas_call(soap_body, grid=(towers, 2, steps), in_specs=[pl.BlockSpec...  152 us
    dot_general x1, matrix products, towers_pass(): jnp.einsum('tri,tro->tio', wide_f, wide_dz, preferred_element_type=jnp.fl...  23.8 us
    unnamed x11, local copies, waits for them, and re-layouts  23.2 us
    dot_general x1, matrix products, towers_pass(): jnp.einsum('tro,tio->tri', wide_dz, wide_w, preferred_element_type=jnp.fl...  22.8 us
    dot_general x1, matrix products, towers_pass(): jnp.einsum('tri,tio->tro', wide_f, wide_w, preferred_element_type=jnp.flo...  21.2 us
  transfers between devices with their start and end apart: 6, of which 3 were waited for; matrix products, arithmetic and copies ran while one was open for 7% of the time, Pallas kernels for 55%

profile of v3, /device:TPU:17, one launch (start us, length us, event | category | flops | bytes accessed | tf_op | source)
XLA Modules:
  0.0 935.1 jit_solution(6360019109398644254)
XLA Ops:
  9.7 1.4 dynamic-update-slice
  11.1 5.4 all-reduce.20
  17.8 6.6 convert_element_type.65
  24.4 883.1 %conditional.1 = (bf16[2,1280,1152]{2,1,0:T(8,128)(2,1)}, f32[2,2304,512]{2,1,0:T(8,128)}, f32[2,2304,512]{2,1,0:T(8,128)}, f32[2,2304,512]{2,1,0:T(8,128)}, f32...) conditional(s32[]{:T(128)} %convert_element_type.64, ...), branch_computations={%region_2.9_spmd, %region_9.17_spmd} | conditional | flops 74989510656 | bytes 2269060096 | solution.py:642
  34.3 233.3 %gather.3 = (bf16[2,768,4608]{2,1,0:T(8,128)(2,1)S(1)}, bf16[2,4608,1024]{2,1,0:T(8,128)(2,1)}, bf16[2,176,512]{2,1,0:T(8,128)(2,1)S(1)}) custom-call(bf16[2,1280,1152]{2,1,0:T(8,128)(2,1)} %get-tuple-element.83.refs_0_, bf16[2,2304,512]{2,1,0:T(8,128)(2,1)} %get-tuple-element.84.refs_1_, bf16[2,1280,512]{2,1,0:T(8,128)(2,1)S(1)} %get-tuple-element.85.refs_2_, ...), custom_call_target="tpu_custom_call" | custom-call | bytes 838860800 | tf_op jit(solution)/shard_map/cond/branch_1_fun/gather/pallas_call | solution.py:329
  267.7 21.2 %fusion.34 = f32[2,768,1024]{2,1,0:T(8,128)S(1)} fusion(bf16[2,768,4608]{2,1,0:T(8,128)(2,1)S(1)} %get-tuple-element.88, bf16[2,4608,1024]{2,1,0:T(8,128)(2,1)} %get-tuple-element.89), kind=kOutput, calls=%fused_computation.92 | convolution fusion | flops 14495514624 | bytes 39321600 | tf_op jit(solution)/shard_map/cond/branch_1_fun/tri,tio->tro/dot_general | solution.py:556
  288.9 2.4 slice.103
  299.8 1.7 convert_multiply_fusion.1
  303.3 4.2 fusion.28
  311.4 8.4 collective-permute-done.5
  320.8 7.0 collective-permute-done.4
  327.8 1.4 maximum_select_fusion.1
  329.2 1.7 pad_maximum_fusion.5
  332.0 2.4 collective-permute-done.6
  334.4 23.8 %convolution_convert_fusion.2.pg_ref = bf16[2,4608,1024]{2,1,0:T(8,128)(2,1)} fusion(bf16[2,768,4608]{2,1,0:T(8,128)(2,1)} %copy-done.1, bf16[2,768,512]{2,1,0:T(8,128)(2,1)S(1)} %collective-permute-done.6, bf16[2,768,512]{2,1,0:T(8,128)(2,1)S(1)} %get-tuple-element.147), kind=kOutput, calls=%fused_computation.37 | convolution fusion | flops 14511243264 | bytes 36175872 | tf_op jit(solution)/shard_map/cond/branch_1_fun/tri,tro->tio/dot_general | solution.py:563
  358.2 22.8 %convolution_convert_fusion.3.pd_ref = bf16[2,768,4608]{2,1,0:T(8,128)(2,1)} fusion(bf16[2,4608,1024]{2,1,0:T(8,128)(2,1)} %get-tuple-element.89, bf16[2,768,512]{2,1,0:T(8,128)(2,1)S(1)} %collective-permute-done.6, bf16[2,768,512]{2,1,0:T(8,128)(2,1)S(1)} %get-tuple-element.147), kind=kOutput, calls=%fused_computation.38 | convolution fusion | flops 14508883968 | bytes 36175872 | tf_op jit(solution)/shard_map/cond/branch_1_fun/tro,tio->tri/dot_general | solution.py:562
  381.0 363.0 %reduce.29 = (bf16[2,768,1152]{2,1,0:T(8,128)(2,1)}, bf16[4,2,2,1152,512]{4,3,2,1,0:T(8,128)(2,1)}, f32[4,8,512]{2,1,0:T(8,128)}, bf16[3,2,176,1152]{3,2,1,0:T(8,128)(2,1)}) custom-call(bf16[2,768,4608]{2,1,0:T(8,128)(2,1)} %convolution_convert_fusion.3.pd_ref, bf16[2,4608,1024]{2,1,0:T(8,128)(2,1)} %convolution_convert_fusion.2.pg_ref, f32[8,512]{1,0:T(8,128)} %pad.60.ps_ref), custom_call_target="tpu_custom_call" | custom-call | bytes 838860800 | tf_op jit(solution)/shard_map/cond/branch_1_fun/reduce/pallas_call | solution.py:533
  745.2 2.0 slice.90
  747.2 1.5 reduce_sum.129
  748.7 1.8 slice_bitcast_fusion.2
  750.6 152.4 %soap.3 = (f32[2,2304,512]{2,1,0:T(8,128)}, f32[2,2304,512]{2,1,0:T(8,128)}, f32[2,2304,512]{2,1,0:T(8,128)}, f32[2,2304,512]{2,1,0:T(8,128)}, bf16[2,2304,512]{2,1,0:T(8,128)(2,1)}) custom-call(bf16[4,2,2,1152,512]{4,3,2,1,0:T(8,128)(2,1)} %get-tuple-element.94.parts, f32[2,2304,512]{2,1,0:T(8,128)} %get-tuple-element.95.weights, ...), custom_call_target="tpu_custom_call" | custom-call | flops 2415919104 | bytes 136314880 | tf_op jit(solution)/shard_map/cond/branch_1_fun/soap/pallas_call | solution.py:95
  904.3 3.0 pad_maximum_fusion.3
  907.5 18.0 %copy.65 = bf16[2,1280,4096]{2,1,0:T(8,128)(2,1)} copy(bf16[2,1280,4096]{2,1,0:T(8,128)(2,1)} %get-tuple-element.222) | data formatting | bytes 41943040
  925.5 2.6 copy.66
  (61 shorter events, 20.7 us)
Async XLA Ops:
  17.8 6.6 copy-start.2
  17.8 6.6 copy-start.6
  33.0 874.3 %all-gather.5.cloned.1.call-start = ((), (), s32[]{:S(2)}) async-start(), calls=%async_computation.1 | async-start | bytes 23592960 | tf_op jit(solution)/shard_map/cond/branch_1_fun/all_gather | solution.py:618
  267.7 21.2 %copy-start.1 = (bf16[2,768,4608]{2,1,0:T(8,128)(2,1)}, bf16[2,768,4608]{2,1,0:T(8,128)(2,1)S(1)}, u32[]{:S(2)}) copy-start(bf16[2,768,4608]{2,1,0:T(8,128)(2,1)S(1)} %get-tuple-element.88) | copy-start | bytes 42467332 | tf_op jit(solution)/shard_map/cond
  288.9 3.7 copy-start.3
  288.9 7.6 copy-start.14
  292.5 10.0 %collective-permute-start.2 = (f32[2,768,512]{2,1,0:T(8,128)}, f32[2,768,512]{2,1,0:T(8,128)}, u32[]{:S(2)}, u32[]{:S(2)}) collective-permute-start(f32[2,768,512]{2,1,0:T(8,128)} %slice.103), channel_id=1, source_target_pairs={{0,1},{1,0},{2,3},{3,2},{4,5},{5,4},{6,7},{7,6},{8,9},{9,8},{10,11... | collective-permute-start | bytes 9437192 | tf_op jit(solution)/shard_map/cond/branch_1_fun/ppermute | solution.py:557
  299.8 2.8 slice-start.3
  301.5 1.8 slice-start.4
  308.6 11.2 %collective-permute-start.5 = (bf16[2,176,512]{2,1,0:T(8,128)(2,1)S(1)}, bf16[2,176,512]{2,1,0:T(8,128)(2,1)}, u32[]{:S(2)}, u32[]{:S(2)}) collective-permute-start(bf16[2,176,512]{2,1,0:T(8,128)(2,1)S(1)} %slice.108), channel_id=1, source_target_pairs={{0,24},{8,16},{16,8},{24,0},{1,25},{9,17},{17,9},{25,1},{2,26},{10... | collective-permute-start | bytes 1081352 | tf_op jit(solution)/shard_map/cond/branch_1_fun/ppermute | solution.py:619
  309.9 17.9 %collective-permute-start.4 = (bf16[2,176,512]{2,1,0:T(8,128)(2,1)S(1)}, bf16[2,176,512]{2,1,0:T(8,128)(2,1)}, u32[]{:S(2)}, u32[]{:S(2)}) collective-permute-start(bf16[2,176,512]{2,1,0:T(8,128)(2,1)S(1)} %slice.108), channel_id=1, source_target_pairs={{0,16},{8,24},{16,0},{24,8},{1,17},{9,25},{17,1},{25,9},{2,18},{10... | collective-permute-start | bytes 1081352 | tf_op jit(solution)/shard_map/cond/branch_1_fun/ppermute | solution.py:619
  310.1 17.7 %collective-permute-start.3 = (bf16[2,176,512]{2,1,0:T(8,128)(2,1)S(1)}, bf16[2,176,512]{2,1,0:T(8,128)(2,1)}, u32[]{:S(2)}, u32[]{:S(2)}) collective-permute-start(bf16[2,176,512]{2,1,0:T(8,128)(2,1)S(1)} %slice.108), channel_id=1, source_target_pairs={{0,8},{8,0},{16,24},{24,16},{1,9},{9,1},{17,25},{25,17},{2,10},{10... | collective-permute-start | bytes 1081352 | tf_op jit(solution)/shard_map/cond/branch_1_fun/ppermute | solution.py:619
  330.8 3.6 collective-permute-start.6
  750.5 152.4 %copy-start.8 = (f32[6,512]{1,0:T(8,128)S(1)}, f32[6,512]{1,0:T(8,128)}, u32[]{:S(2)}) copy-start(f32[6,512]{1,0:T(8,128)} %get-tuple-element.106) | copy-start | bytes 36868 | tf_op jit(solution)/shard_map/cond
  750.6 152.4 %copy-start.10 = (f32[6,512]{1,0:T(8,128)S(1)}, f32[6,512]{1,0:T(8,128)}, u32[]{:S(2)}) copy-start(f32[6,512]{1,0:T(8,128)} %get-tuple-element.108) | copy-start | bytes 36868 | tf_op jit(solution)/shard_map/cond
  750.6 152.4 %copy-start.12 = (f32[6,512]{1,0:T(8,128)S(1)}, f32[6,512]{1,0:T(8,128)}, u32[]{:S(2)}) copy-start(f32[6,512]{1,0:T(8,128)} %get-tuple-element.109) | copy-start | bytes 36868 | tf_op jit(solution)/shard_map/cond
  750.6 152.4 %copy-start.13 = (f32[8,512]{1,0:T(8,128)S(1)}, f32[8,512]{1,0:T(8,128)}, u32[]{:S(2)}) copy-start(f32[8,512]{1,0:T(8,128)} %reduce_sum.129) | copy-start | bytes 49156 | tf_op jit(solution)/shard_map/cond
  907.5 18.0 %copy-start.4 = (bf16[2,1280,1152]{2,1,0:T(8,128)(2,1)S(1)}, bf16[2,1280,1152]{2,1,0:T(8,128)(2,1)}, u32[]{:S(2)}) copy-start(bf16[2,1280,1152]{2,1,0:T(8,128)(2,1)} %get-tuple-element.223) | copy-start | bytes 17694724
Sparse Core Ops, SparseCore 0:
  331.0 312.1 all-gather.4

commit v4 on v2

--- a/solution.py
+++ b/solution.py
@@ -1,4 +1,5 @@
 import functools
+import math
 
 import jax
 import jax.numpy as jnp
@@ -38,52 +39,69 @@
     high = v.astype(jnp.bfloat16)
     return high, (v - high.astype(jnp.float32)).astype(jnp.bfloat16)
 
-def soap_pair(grad, left, right, moment_a, moment_b):
+def soap_blocks(grads, lefts, rights, moments):
     row = lax.broadcasted_iota(jnp.int32, (2 * BLOCK, 2 * BLOCK), 0) // BLOCK
     lane = lax.broadcasted_iota(jnp.int32, (2 * BLOCK, 2 * BLOCK), 1) // BLOCK
     own = row == lane
+
     def diagonal(v):
         return jnp.where(own, jnp.concatenate([v, v], axis=0), 0.0)
+
     def beside(v):
         return jnp.concatenate([v[0], v[1]], axis=1)
-    def dot(a, b, ca, cb):
-        return lax.dot_general(a, b, (((ca,), (cb,)), ((), ())), preferred_element_type=jnp.float32)
-    right_high, right_low = split(diagonal(beside(right)))
-    left_high, left_low = split(beside(left))
-    up_high, up_low = split(left.reshape(2 * BLOCK, BLOCK))
-    def turn(v, cb):
+
+    def stationary(v, axis):
         high, low = split(v)
-        return (dot(jnp.concatenate([high, low], axis=1), jnp.concatenate([right_high, right_high], axis=cb), 1, cb)
-                + dot(high, right_low, 1, cb))
-    high, low = split(diagonal(turn(grad, 0)))
-    rotated = dot(jnp.concatenate([up_high, up_high, up_low], axis=0), jnp.concatenate([high, low, high], axis=0), 0, 0)
-    first, second, direction = adam_part(moment_a, moment_b, rotated)
-    high, low = split(diagonal(turn(direction, 1)))
-    step = dot(jnp.concatenate([left_high, left_high, left_low], axis=1), jnp.concatenate([high, low, high], axis=0), 1, 0)
-    return first, second, step
-
-def soap_body(parts, weights, moment_a, moment_b, average, left, right, first, second, new_weights, new_average, copy):
+        return jnp.concatenate([high, high, low], axis=axis)
+
+    def moving(v, axis):
+        high, low = split(v)
+        return jnp.concatenate([high, low, high], axis=axis)
+
+    def dots(a, b, ca, cb):
+        dims = (((ca,), (cb,)), ((), ()))
+        return [lax.dot_general(x, y, dims, preferred_element_type=jnp.float32) for x, y in zip(a, b)]
+
+    right = [diagonal(beside(v)) for v in rights]
+    values = dots([moving(v, 1) for v in grads], [stationary(v, 0) for v in right], 1, 0)
+    values = dots([stationary(v.reshape(2 * BLOCK, BLOCK), 0) for v in lefts], [moving(diagonal(v), 0) for v in values], 0, 0)
+    states = [adam_part(a, b, v) for (a, b), v in zip(moments, values)]
+    values = dots([moving(v[2], 1) for v in states], [stationary(v, 1) for v in right], 1, 1)
+    values = dots([stationary(beside(v), 1) for v in lefts], [moving(diagonal(v), 0) for v in values], 1, 0)
+    return [(first, second, step) for (first, second, _), step in zip(states, values)]
+
+
+def soap_body(together, parts, stitched, d_feat, weights, moment_a, moment_b, average, left, right,
+              first, second, new_weights, new_average, copy, stitched_out, d_feat_out):
     groups, pairs = left.shape[1], left.shape[2] // 2
-    def strip(g, _):
-        rows = pl.ds(pl.multiple_of(g * BLOCK, BLOCK), BLOCK)
-        for q in range(pairs):
-            cols = pl.ds(2 * BLOCK * q, 2 * BLOCK)
-            at = (0, rows, cols)
+    stitched_out[...] = stitched[...]
+    d_feat_out[...] = d_feat[...]
+
+    def strips(g, _):
+        places = [(g * together + s, q) for s in range(together) for q in range(pairs)]
+        ats = [(0, pl.ds(pl.multiple_of(r * BLOCK, BLOCK), BLOCK), pl.ds(2 * BLOCK * q, 2 * BLOCK)) for r, q in places]
+        grads = []
+        for at in ats:
             grad = parts[(0, 0) + at].astype(jnp.float32)
             for k in range(1, parts.shape[0]):
                 grad = grad + parts[(k, 0) + at].astype(jnp.float32)
-            one, two, step = soap_pair(grad, left[0, g, 2 * q:2 * q + 2], right[0, g, 2 * q:2 * q + 2], moment_a[at], moment_b[at])
+            grads.append(grad)
+        done = soap_blocks(grads, [left[0, r, 2 * q : 2 * q + 2] for r, q in places],
+                           [right[0, r, 2 * q : 2 * q + 2] for r, q in places], [(moment_a[at], moment_b[at]) for at in ats])
+        olds = [(weights[at], average[at]) for at in ats]
+        for at, (one, two, step), (held, mean) in zip(ats, done, olds):
             first[at] = one
             second[at] = two
-            held = weights[at]
             fresh = held - rate_main * (step + decay_weight * held)
             new_weights[at] = fresh
-            new_average[at] = ema_decay * average[at] + (1.0 - ema_decay) * fresh
+            new_average[at] = ema_decay * mean + (1.0 - ema_decay) * fresh
             copy[at] = fresh.astype(jnp.bfloat16)
         return 0
-    lax.fori_loop(0, groups, strip, 0)
-
-def soap(parts, weights, moment_a, moment_b, average, left, right, group=3):
+
+    lax.fori_loop(0, groups // together, strips, 0)
+
+
+def soap(parts, stitched, d_feat, weights, moment_a, moment_b, average, left, right, group=6):
     towers, rows, cols = weights.shape
     half = parts.shape[3]
     steps = half // (BLOCK * group)
@@ -92,17 +110,23 @@
     state = pl.BlockSpec((1, BLOCK * group, cols), flat)
     base = pl.BlockSpec((1, group, cols // BLOCK, BLOCK, BLOCK), basis)
     full = jax.ShapeDtypeStruct(weights.shape, jnp.float32)
+    strips = max(n for n in range(1, 2 * steps + 1) if stitched.shape[1] % (16 * n) == 0)
+
+    def through(v):
+        return pl.BlockSpec((1, v.shape[1] // strips, v.shape[2]), lambda t, p, g: (t, jnp.minimum(p * steps + g, strips - 1), 0))
+
     return pl.pallas_call(
-        soap_body,
+        functools.partial(soap_body, 2 - group % 2),
         grid=(towers, 2, steps),
         in_specs=[pl.BlockSpec((parts.shape[0], 1, 1, BLOCK * group, cols), lambda t, p, g: (0, p, t, g, 0)),
-                  state, state, state, state, base, base],
-        out_specs=[state] * 5,
-        out_shape=[full] * 4 + [jax.ShapeDtypeStruct(weights.shape, jnp.bfloat16)],
+                  through(stitched), through(d_feat), state, state, state, state, base, base],
+        out_specs=[state] * 5 + [through(stitched), through(d_feat)],
+        out_shape=[full] * 4 + [jax.ShapeDtypeStruct(weights.shape, jnp.bfloat16)]
+        + [jax.ShapeDtypeStruct(v.shape, v.dtype) for v in (stitched, d_feat)],
         compiler_params=pltpu.CompilerParams(vmem_limit_bytes=48 * 2**20),
         cost_estimate=pl.CostEstimate(flops=8 * 2 * towers * rows * cols * 64, bytes_accessed=130 * 2**20, transcendentals=0),
         name="soap",
-    )(parts, weights, moment_a, moment_b, average, left, right)
+    )(parts, stitched, d_feat, weights, moment_a, moment_b, average, left, right)
 
 
 MESH = pl.DeviceIdType.MESH
@@ -124,42 +148,44 @@
     pl.semaphore_wait(barrier, expected)
 
 
-def gather_kernel(chips, chunks, f_ref, w_ref, fg_ref, wg_ref, f_send, f_recv, w_send, w_recv, own_sem):
+def gather_kernel(chips, ranges, f_ref, w_ref, fg_ref, wg_ref, f_send, f_recv, w_send, w_recv, own_sem):
     dp, chip, core = place()
     towers, rows, depth = f_ref.shape
     cols = w_ref.shape[2]
-    part = rows // chunks
     across, along = dp ^ 1, dp ^ 2
     at = lambda c, k: (c, 2 * chip + k)
 
     meet([(chip > 0, (dp, 2 * (chip - 1) + core)), (chip < chips - 1, (dp, 2 * (chip + 1) + core)),
           (chip >= 0, at(dp, 1 - core))] + [(chip >= 0, at(c, k)) for c in (across, along) for k in (0, 1)])
 
-    def feature(step, way, t, k):
-        shard = chip - step if way == 0 else chip + step
-        there = chip + 1 if way == 0 else chip - 1
+    def copies(step, way, t, k, shard, there):
         lanes = pl.ds(pl.multiple_of(shard * depth, 128), depth)
-        rws = pl.ds(k * part, part)
-        src = f_ref.at[t, rws] if step == 0 else fg_ref.at[t, rws, lanes]
-        n = ((way * (chips - 1) + step) * towers + t) * chunks + k
+        rws = pl.ds(*ranges[k])
+        src = fg_ref.at[t, rws, lanes]
+        if step == 0:
+            src = f_ref.at[t, rws]
+        n = ((way * (chips - 1) + step) * towers + t) * len(ranges) + k
         return pltpu.make_async_remote_copy(
             src_ref=src, dst_ref=fg_ref.at[t, rws, lanes], send_sem=f_send.at[n], recv_sem=f_recv.at[n],
             device_id=(dp, 2 * there + core), device_id_type=MESH)
 
+    def feature(step, way, t, k):
+        return copies(step, way, t, k, chip - step if way == 0 else chip + step, chip + 1 if way == 0 else chip - 1)
+
+    def incoming(step, way, t, k):
+        return copies(step, way, t, k, chip - 1 - step if way == 0 else chip + 1 + step, chip)
+
     def sends(step, way):
         return (chip < chips - 1) & (chip >= step) if way == 0 else (chip > 0) & (chip + step < chips)
 
     def receives(step, way):
         return chip > step if way == 0 else chip + step < chips - 1
 
-    def incoming(step, way, t, k):
-        shard = chip - 1 - step if way == 0 else chip + 1 + step
-        lanes = pl.ds(pl.multiple_of(shard * depth, 128), depth)
-        rws = pl.ds(k * part, part)
-        n = ((way * (chips - 1) + step) * towers + t) * chunks + k
-        return pltpu.make_async_remote_copy(
-            src_ref=f_ref.at[t, rws], dst_ref=fg_ref.at[t, rws, lanes], send_sem=f_send.at[n], recv_sem=f_recv.at[n],
-            device_id=(dp, 2 * chip + core), device_id_type=MESH)
+    def launch(t, k):
+        for way in (0, 1):
+            @pl.when(sends(0, way))
+            def _():
+                feature(0, way, t, k).start()
 
     def block(owner, slot, t):
         return wg_ref.at[t, pl.ds(pl.multiple_of(owner * depth, 128), depth), pl.ds(pl.multiple_of(slot * cols, 128), cols)]
@@ -185,25 +211,22 @@
             src_ref=block(owner, slot, t), dst_ref=block(owner, slot, t), send_sem=w_send.at[n], recv_sem=w_recv.at[n],
             device_id=at(dp, core), device_id_type=MESH).wait_recv()
 
-    own = [pltpu.make_async_copy(f_ref.at[t], fg_ref.at[t, :, pl.ds(pl.multiple_of(chip * depth, 128), depth)], own_sem.at[t])
-           for t in range(towers)]
+    mine = pl.ds(pl.multiple_of(chip * depth, 128), depth)
+    own = [pltpu.make_async_copy(f_ref.at[t], fg_ref.at[t, :, mine], own_sem.at[t]) for t in range(towers)]
     own += [pltpu.make_async_copy(w_ref.at[t, pl.ds(pl.multiple_of(core * depth, 128), depth)], block(dp, 0, t), own_sem.at[2 + t])
             for t in range(towers)]
 
-    pieces = [(t, k) for t in range(towers) for k in range(chunks)]
+    pieces = [(t, k) for k in range(len(ranges)) for t in range(towers)]
     for t, k in pieces:
-        for way in (0, 1):
-            @pl.when(sends(0, way))
-            def _():
-                feature(0, way, t, k).start()
+        launch(t, k)
+    for copy in own:
+        copy.start()
     for t in (0, 1):
         for k in (0, 1):
             weight(0, k, t).start()
             weight(1, k, 1 - t).start()
     for t in (0, 1):
         weight(2, 1 - core, t).start()
-    for copy in own:
-        copy.start()
 
     for step in range(chips - 1):
         for t, k in pieces:
@@ -215,7 +238,7 @@
                     @pl.when(sends(step + 1, way))
                     def _():
                         feature(step + 1, way, t, k).start()
-            if step == 0 and (t, k) == pieces[len(pieces) // 2 - 1]:
+            if step == 0 and (t, k) == pieces[-1]:
                 for slot in (0, 1):
                     arrived(0, slot, 0)
                     forward(0, slot).start()
@@ -247,17 +270,18 @@
         copy.wait()
 
 
-def gather(features, weights_low, chips, chunks, ident):
+def gather(features, weights_low, chips, ranges, ident):
     towers, rows, depth = features.shape
     cols = weights_low.shape[2]
-    count = 2 * (chips - 1) * towers * chunks
+    count = 2 * (chips - 1) * towers * len(ranges)
     dma = pltpu.SemaphoreType.DMA
+    anywhere = pl.BlockSpec(memory_space=pl.ANY)
     return pl.pallas_call(
-        functools.partial(gather_kernel, chips, chunks),
+        functools.partial(gather_kernel, chips, ranges),
         out_shape=[jax.ShapeDtypeStruct((towers, rows, chips * depth), jnp.bfloat16),
                    jax.ShapeDtypeStruct((towers, chips * depth, 2 * cols), jnp.bfloat16)],
-        in_specs=[pl.BlockSpec(memory_space=pl.ANY)] * 2,
-        out_specs=[pl.BlockSpec(memory_space=pl.ANY)] * 2,
+        in_specs=[anywhere] * 2,
+        out_specs=[anywhere] * 2,
         scratch_shapes=[dma((count,)), dma((count,)), dma((16,)), dma((16,)), dma((4,))],
         compiler_params=pltpu.CompilerParams(collective_id=ident, has_side_effects=True),
         cost_estimate=pl.CostEstimate(flops=0, bytes_accessed=800 * 2**20, transcendentals=0),
@@ -265,14 +289,13 @@
     )(features, weights_low)
 
 
-def reduce_kernel(chips, chunks, pd_ref, pg_ref, ps_ref, d_ref, gr_ref, sr_ref, held, term, total,
+def reduce_kernel(chips, ranges, pd_ref, pg_ref, ps_ref, d_ref, gr_ref, sr_ref, held, term, total,
                   d_send, d_recv, t_sem, o_sem, g_send, g_recv, s_send, s_recv, own_sem):
     dp, chip, core = place()
     towers, rows, depth = d_ref.shape
     cols = pg_ref.shape[2] // 2
-    part = rows // chunks
     across, along = dp ^ 1, dp ^ 2
-    others = (across, along, 3 - dp)
+    others = (across, along, dp ^ 3)
     at = lambda c, k: (c, 2 * chip + k)
 
     meet([(chip > 0, (dp, 2 * (chip - 1) + core)), (chip < chips - 1, (dp, 2 * (chip + 1) + core)),
@@ -306,23 +329,23 @@
         return (chip > 0) & (chip <= step + 1) if way == 0 else (chip < chips - 1) & (chips - 1 - chip <= step + 1)
 
     def own_term(goal, t, k):
-        return pd_ref.at[t, pl.ds(k * part, part), pl.ds(pl.multiple_of(goal * depth, 128), depth)]
+        return pd_ref.at[t, pl.ds(*ranges[k]), pl.ds(pl.multiple_of(goal * depth, 128), depth)]
 
     def partial(step, way, t, k, first):
-        n = ((way * (chips - 1) + step) * towers + t) * chunks + k
-        src = own_term(target(step, way), t, k) if first else held.at[way, step - 1, t, pl.ds(k * part, part)]
+        n = ((way * (chips - 1) + step) * towers + t) * len(ranges) + k
+        src = own_term(target(step, way), t, k) if first else held.at[way, step - 1, t, pl.ds(*ranges[k])]
         there = chip + 1 if way == 0 else chip - 1
         return pltpu.make_async_remote_copy(
-            src_ref=src, dst_ref=held.at[way, step, t, pl.ds(k * part, part)], send_sem=d_send.at[n], recv_sem=d_recv.at[n],
+            src_ref=src, dst_ref=held.at[way, step, t, pl.ds(*ranges[k])], send_sem=d_send.at[n], recv_sem=d_recv.at[n],
             device_id=(dp, 2 * there + core), device_id_type=MESH)
 
     def landed(step, way, t, k):
-        n = ((way * (chips - 1) + step) * towers + t) * chunks + k
-        ref = held.at[way, step, t, pl.ds(k * part, part)]
+        n = ((way * (chips - 1) + step) * towers + t) * len(ranges) + k
+        ref = held.at[way, step, t, pl.ds(*ranges[k])]
         pltpu.make_async_remote_copy(src_ref=ref, dst_ref=ref, send_sem=d_send.at[n], recv_sem=d_recv.at[n],
                                      device_id=(dp, 2 * chip + core), device_id_type=MESH).wait_recv()
 
-    pieces = [(t, k) for t in range(towers) for k in range(chunks)]
+    pieces = [(t, k) for t in range(towers) for k in range(len(ranges))]
     ends = (chip == 0, chip == chips - 1)
     for t, k in pieces:
         for way in (0, 1):
@@ -343,7 +366,7 @@
                 grad(kind, k, t).start()
         grad(3, 1 - core, t).start()
 
-    strip = 32
+    strip = 16
 
     for step in range(1, chips - 1):
         for t, k in pieces:
@@ -354,47 +377,50 @@
 
                 @pl.when(sends(step, way) & jnp.logical_not(ends[way]))
                 def _():
-                    load = pltpu.make_async_copy(own_term(target(step, way), t, k), term.at[way], t_sem.at[way])
+                    start, size = ranges[k]
+                    load = pltpu.make_async_copy(own_term(target(step, way), t, k), term.at[way, pl.ds(0, size)], t_sem.at[way])
                     load.start()
                     landed(step - 1, way, t, k)
                     load.wait()
 
                     def add(i, _):
                         rws = pl.ds(pl.multiple_of(i * strip, strip), strip)
-                        all_rows = pl.ds(pl.multiple_of(k * part + i * strip, strip), strip)
+                        all_rows = pl.ds(pl.multiple_of(start + i * strip, strip), strip)
                         held[way, step - 1, t, all_rows] = (
                             held[way, step - 1, t, all_rows].astype(jnp.float32) + term[way, rws].astype(jnp.float32)
                         ).astype(jnp.bfloat16)
                         return 0
-                    lax.fori_loop(0, part // strip, add, 0)
+                    lax.fori_loop(0, size // strip, add, 0)
                     partial(step, way, t, k, False).start()
 
+    stores = []
     for n, (t, k) in enumerate(pieces):
         s = n % 2
-        load = pltpu.make_async_copy(own_term(chip, t, k), term.at[s], t_sem.at[s])
+        start, size = ranges[k]
+        load = pltpu.make_async_copy(own_term(chip, t, k), term.at[s, pl.ds(0, size)], t_sem.at[s])
         load.start()
         for way in (0, 1):
             @pl.when(receives(chips - 2, way))
             def _():
                 landed(chips - 2, way, t, k)
         load.wait()
-        store = pltpu.make_async_copy(total.at[s], d_ref.at[t, pl.ds(k * part, part)], o_sem.at[s])
         if n >= 2:
-            store.wait()
+            stores[n - 2].wait()
 
         def finish(i, _):
             rws = pl.ds(pl.multiple_of(i * strip, strip), strip)
-            all_rows = pl.ds(pl.multiple_of(k * part + i * strip, strip), strip)
+            all_rows = pl.ds(pl.multiple_of(start + i * strip, strip), strip)
             value = term[s, rws].astype(jnp.float32)
             for way in (0, 1):
                 here = receives(chips - 2, way)
                 value = value + jnp.where(here, held[way, chips - 2, t, all_rows].astype(jnp.float32), 0.0)
             total[s, rws] = value.astype(jnp.bfloat16)
             return 0
-        lax.fori_loop(0, part // strip, finish, 0)
-        store.start()
-    for n in range(min(2, len(pieces))):
-        pltpu.make_async_copy(total.at[n], d_ref.at[0, pl.ds(0, part)], o_sem.at[n]).wait()
+        lax.fori_loop(0, size // strip, finish, 0)
+        stores.append(pltpu.make_async_copy(total.at[s, pl.ds(0, size)], d_ref.at[t, pl.ds(start, size)], o_sem.at[s]))
+        stores[n].start()
+    for store in stores[-2:]:
+        store.wait()
 
     for t in range(towers):
         for kind in range(3):
@@ -418,21 +444,23 @@
         copy.wait()
 
 
-def reduce(partial_d, partial_g, partial_s, chips, chunks, ident):
+def reduce(partial_d, partial_g, partial_s, chips, ranges, ident):
     towers, rows, wide = partial_d.shape
     depth, cols = wide // chips, partial_g.shape[2] // 2
-    count = 2 * (chips - 1) * towers * chunks
+    count = 2 * (chips - 1) * towers * len(ranges)
+    part = max(size for _, size in ranges)
     dma = pltpu.SemaphoreType.DMA
     bf16 = jnp.bfloat16
+    out_shape = [jax.ShapeDtypeStruct((towers, rows, depth), bf16),
+                 jax.ShapeDtypeStruct((4, 2, towers, depth, cols), bf16),
+                 jax.ShapeDtypeStruct((4,) + partial_s.shape, jnp.float32)]
     return pl.pallas_call(
-        functools.partial(reduce_kernel, chips, chunks),
-        out_shape=[jax.ShapeDtypeStruct((towers, rows, depth), bf16),
-                   jax.ShapeDtypeStruct((4, 2, towers, depth, cols), bf16),
-                   jax.ShapeDtypeStruct((4,) + partial_s.shape, jnp.float32)],
+        functools.partial(reduce_kernel, chips, ranges),
+        out_shape=out_shape,
         in_specs=[pl.BlockSpec(memory_space=pl.ANY)] * 3,
-        out_specs=[pl.BlockSpec(memory_space=pl.ANY)] * 3,
+        out_specs=[pl.BlockSpec(memory_space=pl.ANY)] * len(out_shape),
         scratch_shapes=[pltpu.VMEM((2, chips - 1, towers, rows, depth), bf16),
-                        pltpu.VMEM((2, rows // chunks, depth), bf16), pltpu.VMEM((2, rows // chunks, depth), bf16),
+                        pltpu.VMEM((2, part, depth), bf16), pltpu.VMEM((2, part, depth), bf16),
                         dma((count,)), dma((count,)), dma((2,)), dma((2,)), dma((16,)), dma((16,)), dma((3,)), dma((3,)), dma((towers + 1,))],
         compiler_params=pltpu.CompilerParams(collective_id=ident, has_side_effects=True, vmem_limit_bytes=56 * 2**20),
         cost_estimate=pl.CostEstimate(flops=0, bytes_accessed=800 * 2**20, transcendentals=0),
@@ -440,10 +468,822 @@
     )(partial_d, partial_g, partial_s)
 
 
+def forward_kernel(chips, share, ranges, f_ref, w_ref, o_ref, n_ref, sp_ref, fg_ref, wg_ref, y_ref, dz_ref, sg_ref, tot_ref,
+                   offer_f, taken, offer_o, og, w_wide, w_low, f_tile, w_tile, acc, theirs, live, y_here, dz_here, sums_here,
+                   tot, f_send, f_recv, w_send, w_recv, own_sem, x_send, x_recv, k_sem, n_send, n_recv, l_sem, ft_sem, wt_sem,
+                   a_send, a_recv, z_send, z_recv, out_sem):
+    dp, chip, core = place()
+    towers, _, depth = f_ref.shape
+    cols = w_ref.shape[2]
+    steps = chips - 1
+    keep = share[0][0]
+    fixed = len(ranges) - 1
+    across, along = dp ^ 1, dp ^ 2
+    others = (across, along, dp ^ 3)
+    at = lambda c, k: (c, 2 * chip + k)
+    ends = (chip == 0) | (chip == steps)
+
+    meet([(chip > 0, (dp, 2 * (chip - 1) + core)), (chip < steps, (dp, 2 * (chip + 1) + core)),
+          (chip >= 0, at(dp, 1 - core))] + [(chip >= 0, at(c, k)) for c in (across, along) for k in (0, 1)]
+         + [(chip >= 0, at(others[2], core))])
+
+    def shard_lanes(shard):
+        return pl.ds(pl.multiple_of(shard * depth, 128), depth)
+
+    def copies(step, way, t, k, shard, there):
+        rws = pl.ds(*ranges[k])
+        dst = fg_ref.at[t, rws, shard_lanes(shard)]
+        src = dst
+        if step == 0:
+            src = taken.at[t] if k == fixed else f_ref.at[t, rws]
+        n = t * len(ranges) + k
+        return pltpu.make_async_remote_copy(
+            src_ref=src, dst_ref=dst, send_sem=f_send.at[way, step, n], recv_sem=f_recv.at[way, step, n],
+            device_id=(dp, 2 * there + core), device_id_type=MESH)
+
+    def feature(step, way, t, k):
+        return copies(step, way, t, k, chip - step if way == 0 else chip + step, chip + 1 if way == 0 else chip - 1)
+
+    def incoming(step, way, t, k):
+        return copies(step, way, t, k, chip - 1 - step if way == 0 else chip + 1 + step, chip)
+
+    def sends(step, way):
+        return (chip < steps) & (chip >= step) if way == 0 else (chip > 0) & (chip + step <= steps)
+
+    def receives(step, way):
+        return chip > step if way == 0 else chip + step < steps
+
+    def launch(t, k):
+        for way in (0, 1):
+            @pl.when(sends(0, way))
+            def _():
+                feature(0, way, t, k).start()
+
+    def block(owner, slot, t):
+        return wg_ref.at[t, pl.ds(pl.multiple_of(owner * depth, 128), depth), pl.ds(pl.multiple_of(slot * cols, 128), cols)]
+
+    def weight(kind, k, t):
+        return pltpu.make_async_remote_copy(
+            src_ref=w_low.at[t, k], dst_ref=block(dp, k ^ core, t),
+            send_sem=w_send.at[(kind * 2 + k) * 2 + t], recv_sem=w_recv.at[(kind * 2 + core) * 2 + t],
+            device_id=at((across, along, dp)[kind], k), device_id_type=MESH)
+
+    def pass_on(kind, slot):
+        owner, to, t = ((across, along, 0), (along, across, 1))[kind]
+        n = 12 + kind * 2 + slot
+        return pltpu.make_async_remote_copy(
+            src_ref=block(owner, slot, t), dst_ref=block(owner, slot, t),
+            send_sem=w_send.at[n], recv_sem=w_recv.at[n], device_id=at(to, core), device_id_type=MESH)
+
+    def arrived(kind, slot, t):
+        owner = (across, along, dp)[kind]
+        n = (kind * 2 + (slot ^ core)) * 2 + t
+        pltpu.make_async_remote_copy(
+            src_ref=block(owner, slot, t), dst_ref=block(owner, slot, t), send_sem=w_send.at[n], recv_sem=w_recv.at[n],
+            device_id=at(dp, core), device_id_type=MESH).wait_recv()
+
+    def offer(kind, what):
+        src, dst = ((f_ref, offer_f), (o_ref, offer_o))[what]
+        n = kind * 2 + what
+        return pltpu.make_async_remote_copy(
+            src_ref=src.at[:, pl.ds(*share[1 + kind])], dst_ref=dst.at[1 + kind], send_sem=x_send.at[n], recv_sem=x_recv.at[n],
+            device_id=at(others[kind], core), device_id_type=MESH)
+
+    def tell(kind):
+        return pltpu.make_async_remote_copy(
+            src_ref=n_ref, dst_ref=tot.at[1 + kind], send_sem=n_send.at[kind], recv_sem=n_recv.at[kind],
+            device_id=at(others[kind], core), device_id_type=MESH)
+
+    def choose(offers, into):
+        width = offers.shape[3]
+        weigh = [jnp.broadcast_to(jnp.where(tot[kind, :1, :width] > keep, 1.0, 0.0), (16, width)) for kind in range(4)]
+
+        def strip(i, _):
+            rws = pl.ds(pl.multiple_of(i * 16, 16), 16)
+            for t in range(towers):
+                value = offers[0, t, rws].astype(jnp.float32) * weigh[0]
+                for kind in range(1, 4):
+                    value = value + offers[kind, t, rws].astype(jnp.float32) * weigh[kind]
+                into(t, i, value.astype(jnp.bfloat16))
+            return 0
+        lax.fori_loop(0, share[0][1] // 16, strip, 0)
+
+    for kind in range(3):
+        tell(kind).start()
+    for kind in (2, 0, 1):
+        offer(kind, 0).start()
+    pieces = [(t, k) for k in range(len(ranges)) for t in range(towers)]
+    for t, k in pieces:
+        if k < fixed:
+            launch(t, k)
+    local = [(n_ref, tot.at[0]), (f_ref.at[:, pl.ds(*share[0])], offer_f.at[0]), (o_ref.at[:, pl.ds(*share[0])], offer_o.at[0]),
+             (o_ref.at[:, pl.ds(0, keep)], og.at[:, pl.ds(0, keep)])]
+    local = [pltpu.make_async_copy(src, dst, l_sem.at[n]) for n, (src, dst) in enumerate(local)]
+    for copy in local:
+        copy.start()
+    own = [pltpu.make_async_copy(f_ref.at[t, pl.ds(0, keep)], fg_ref.at[t, pl.ds(0, keep), shard_lanes(chip)], own_sem.at[t])
+           for t in range(towers)]
+    for copy in own:
+        copy.start()
+
+    halves = [(t, k) for t in range(towers) for k in (0, 1)]
+    wide = [pltpu.make_async_copy(w_ref.at[t, pl.ds(k * depth, depth)], w_wide.at[n % 2], k_sem.at[n % 2]) for n, (t, k) in enumerate(halves)]
+    wide[0].start()
+    for n, (t, k) in enumerate(halves):
+        wide[n].wait()
+        if n + 1 < len(halves):
+            wide[n + 1].start()
+
+        def round_strip(i, _):
+            rws = pl.ds(pl.multiple_of(i * 64, 64), 64)
+            w_low[t, k, rws] = w_wide[n % 2, rws].astype(jnp.bfloat16)
+            return 0
+        lax.fori_loop(0, depth // 64, round_strip, 0)
+    own_w = [pltpu.make_async_copy(w_low.at[t, core], block(dp, 0, t), own_sem.at[towers + t]) for t in range(towers)]
+    for copy in own_w:
+        copy.start()
+
+    local[0].wait()
+    local[1].wait()
+    for kind in range(3):
+        tell(kind).wait_recv()
+    totals = pltpu.make_async_copy(tot, tot_ref, l_sem.at[4])
+    totals.start()
+    for kind in range(3):
+        offer(kind, 0).wait_recv()
+
+    def take(t, i, value):
+        taken[t, pl.ds(pl.multiple_of(i * 16, 16), 16)] = value
+    choose(offer_f, take)
+    own_share = [pltpu.make_async_copy(taken.at[t], fg_ref.at[t, pl.ds(*ranges[fixed]), shard_lanes(chip)], own_sem.at[2 * towers + t])
+                 for t in range(towers)]
+    for t in range(towers):
+        launch(t, fixed)
+        own_share[t].start()
+    for t in (0, 1):
+        for k in (0, 1):
+            weight(0, k, t).start()
+            weight(1, k, 1 - t).start()
+    for t in (0, 1):
+        weight(2, 1 - core, t).start()
+    for kind in (2, 0, 1):
+        offer(kind, 1).start()
+
+    def alive(i, _):
+        rws = pl.ds(pl.multiple_of(i * 16, 16), 16)
+        row = lax.broadcasted_iota(jnp.int32, (16, cols), 0).astype(jnp.float32) + (i * 16).astype(jnp.float32)
+        here = jnp.where(row < tot[0, :1, :cols], 1.0, 0.0)
+        there = jnp.zeros_like(here)
+        for kind in range(4):
+            count = tot[kind, :1, :cols]
+            slot = row + float(share[kind][0] - keep)
+            valid = (slot < count) & (count > keep)
+            if kind == 3:
+                valid = valid & (slot >= share[2][0] + share[2][1])
+            there = there + jnp.where(valid, 1.0, 0.0)
+        live[rws] = jnp.where(row < keep, here, there)
+        return 0
+    lax.fori_loop(0, sum(ranges[fixed]) // 16, alive, 0)
+
+    for step in range(steps - 1):
+        for t, k in pieces:
+            for way in (0, 1):
+                @pl.when(receives(step, way))
+                def _():
+                    incoming(step, way, t, k).wait_recv()
+
+                @pl.when(sends(step + 1, way))
+                def _():
+                    feature(step + 1, way, t, k).start()
+        if step == 0:
+            for slot in (0, 1):
+                arrived(0, slot, 0)
+                pass_on(0, slot).start()
+                arrived(1, slot, 1)
+                pass_on(1, slot).start()
+
+    for copy in local[2:]:
+        copy.wait()
+    for kind in range(3):
+        offer(kind, 1).wait_recv()
+
+    def take_grad(t, i, value):
+        og[t, pl.ds(pl.multiple_of(keep + i * 16, 16), 16)] = value
+    choose(offer_o, take_grad)
+    for slot in (0, 1):
+        arrived(0, slot, 1)
+        arrived(1, slot, 0)
+        pass_on(0, slot).wait_recv()
+        pass_on(1, slot).wait_recv()
+    for t in (0, 1):
+        arrived(2, 1, t)
+    for copy in own + own_w + own_share:
+        copy.wait()
+
+    units = [(j, t) for j in range(chips) for t in range(towers)]
+    shard = lambda j: jnp.where(chip == steps, steps - j, j)
+
+    def load_w(n):
+        j, t = units[n]
+        return pltpu.make_async_copy(wg_ref.at[t, pl.ds(pl.multiple_of(shard(j) * depth, 128), depth)], w_tile.at[n % 2], wt_sem.at[n % 2])
+
+    def load_f(n):
+        j, t = units[n]
+        return pltpu.make_async_copy(fg_ref.at[t, :, shard_lanes(shard(j))], f_tile.at[n % 2], ft_sem.at[n % 2])
+
+    def add(t, slot, start, size, first):
+        for col in range(0, 2 * cols, cols):
+            value = jnp.dot(f_tile[slot, pl.ds(start, size)], w_tile[slot, :, pl.ds(col, cols)], preferred_element_type=jnp.float32)
+            where = (t, pl.ds(start, size), pl.ds(col, cols))
+            acc[where] = value if first else acc[where] + value
+
+    rows = sum(ranges[fixed])
+    part = rows // 4
+    load_w(0).start()
+    load_f(0).start()
+    for n, (j, t) in enumerate(units):
+        if n + 1 < len(units):
+            load_w(n + 1).start()
+            if units[n + 1][0] < steps:
+                load_f(n + 1).start()
+            else:
+                @pl.when(jnp.logical_not(ends))
+                def _():
+                    load_f(n + 1).start()
+        load_w(n).wait()
+
+        def multiply():
+            load_f(n).wait()
+
+            def one(i, _):
+                add(t, n % 2, pl.multiple_of(i * part, 16), part, j == 0)
+                return 0
+            lax.fori_loop(0, 4, one, 0)
+        if j < steps:
+            multiply()
+        else:
+            pl.when(jnp.logical_not(ends))(multiply)
+
+    def swap_sum(t, k):
+        rws = pl.ds(*ranges[k])
+        return pltpu.make_async_remote_copy(
+            src_ref=acc.at[t, rws, pl.ds(cols, cols)], dst_ref=theirs.at[t, rws], send_sem=a_send.at[t, k],
+            recv_sem=a_recv.at[t, k], device_id=at(dp, 1 - core), device_id_type=MESH)
+
+    for t, k in pieces:
+        slot = (len(units) - towers + t) % 2
+        for way in (0, 1):
+            @pl.when(receives(steps - 1, way))
+            def _():
+                incoming(steps - 1, way, t, k).wait_recv()
+                piece = pltpu.make_async_copy(
+                    fg_ref.at[t, pl.ds(*ranges[k]), shard_lanes(shard(steps))], f_tile.at[slot, pl.ds(*ranges[k])], ft_sem.at[slot])
+                piece.start()
+                piece.wait()
+                add(t, slot, *ranges[k], False)
+        swap_sum(t, k).start()
+
+    def swap_dz(t, k):
+        rws = pl.ds(*ranges[k])
+        return pltpu.make_async_remote_copy(
+            src_ref=dz_here.at[t, rws], dst_ref=dz_ref.at[t, rws, pl.ds(cols, cols)], send_sem=z_send.at[t, k],
+            recv_sem=z_recv.at[t, k], device_id=at(dp, 1 - core), device_id_type=MESH)
+
+    def keep_dz(t, k):
+        rws = pl.ds(*ranges[k])
+        return pltpu.make_async_copy(dz_here.at[t, rws], dz_ref.at[t, rws, pl.ds(0, cols)], out_sem.at[t, k])
+
+    sums_here[...] = jnp.zeros_like(sums_here)
+    factor, cubic = math.sqrt(2.0 / math.pi), 0.044715
+
+    def both(i, start):
+        rws = pl.ds(pl.multiple_of(start + i * 16, 16), 16)
+        activated, slope = [], []
+        for t in range(towers):
+            v = acc[t, rws, :cols] + theirs[t, rws] + sp_ref[t : t + 1]
+            square = v * v
+            th = jnp.tanh(factor * (v + cubic * (square * v)))
+            activated.append(0.5 * v * (1.0 + th))
+            slope.append(0.5 * (1.0 + th) + 0.5 * v * (1.0 - th * th) * (factor * (1.0 + 3.0 * cubic * square)))
+        mask = live[rws]
+        dy = [og[t, rws].astype(jnp.float32) * mask for t in range(towers)]
+        for t in range(towers):
+            y_here[t, rws] = ((sp_ref[2 + 2 * t : 3 + 2 * t] * activated[0] + sp_ref[3 + 2 * t : 4 + 2 * t] * activated[1]) * mask).astype(jnp.bfloat16)
+        dz = [slope[t] * (sp_ref[2 + t : 3 + t] * dy[0] + sp_ref[4 + t : 5 + t] * dy[1]) for t in range(towers)]
+        for t in range(towers):
+            dz_here[t, rws] = dz[t].astype(jnp.bfloat16)
+        terms = dz + [activated[0] * dy[0], activated[1] * dy[0], activated[0] * dy[1], activated[1] * dy[1]]
+        for n, term in enumerate(terms):
+            sums_here[n] += term[:8] + term[8:]
+        return start
+
+    for k in range(len(ranges)):
+        for t in range(towers):
+            swap_sum(t, k).wait_recv()
+        start, size = ranges[k]
+        lax.fori_loop(0, size // 16, lambda i, c: both(i, c), start)
+        for t in range(towers):
+            swap_dz(t, k).start()
+            keep_dz(t, k).start()
+    keep_y = pltpu.make_async_copy(y_here, y_ref, l_sem.at[5])
+    keep_y.start()
+    sg_ref[...] = jnp.zeros_like(sg_ref)
+    for n in range(6):
+        sg_ref[n : n + 1] = jnp.sum(sums_here[n], axis=0, keepdims=True)
+
+    for t, k in pieces:
+        swap_dz(t, k).wait_recv()
+    for t, k in pieces:
+        swap_dz(t, k).wait_send()
+        keep_dz(t, k).wait()
+        swap_sum(t, k).wait_send()
+    keep_y.wait()
+    totals.wait()
+    for kind in range(3):
+        tell(kind).wait_send()
+        offer(kind, 0).wait_send()
+        offer(kind, 1).wait_send()
+    for t in (0, 1):
+        for k in (0, 1):
+            weight(0, k, t).wait_send()
+            weight(1, k, t).wait_send()
+        weight(2, 1 - core, t).wait_send()
+    for slot in (0, 1):
+        pass_on(0, slot).wait_send()
+        pass_on(1, slot).wait_send()
+    for step in range(steps):
+        for t, k in pieces:
+            for way in (0, 1):
+                @pl.when(sends(step, way))
+                def _():
+                    feature(step, way, t, k).wait_send()
+
+
+def forward(features, weights, out_grad, count, small_params, chips, share, ident):
+    towers, _, depth = features.shape
+    cols = weights.shape[2]
+    keep, size = share[0]
+    rows = keep + size
+    half = keep // 32 * 16
+    ranges = ((0, half), (half, keep - half), share[0])
+    steps = chips - 1
+    dma, vmem = pltpu.SemaphoreType.DMA, pltpu.VMEM
+    bf16, f32 = jnp.bfloat16, jnp.float32
+    anywhere, here = pl.BlockSpec(memory_space=pl.ANY), pl.BlockSpec(memory_space=pltpu.VMEM)
+    many = (2, steps, towers * len(ranges))
+    told = jnp.broadcast_to(count.astype(f32), (8, depth))
+    return pl.pallas_call(
+        functools.partial(forward_kernel, chips, share, ranges),
+        out_shape=[jax.ShapeDtypeStruct((towers, rows, chips * depth), bf16),
+                   jax.ShapeDtypeStruct((towers, chips * depth, 2 * cols), bf16),
+                   jax.ShapeDtypeStruct((towers, rows, cols), bf16),
+                   jax.ShapeDtypeStruct((towers, rows, 2 * cols), bf16),
+                   jax.ShapeDtypeStruct((8, cols), f32),
+                   jax.ShapeDtypeStruct((4, 8, depth), f32)],
+        in_specs=[anywhere] * 3 + [anywhere, here],
+        out_specs=[anywhere] * 4 + [here, anywhere],
+        scratch_shapes=[vmem((4, towers, size, depth), bf16), vmem((towers, size, depth), bf16), vmem((4, towers, size, cols), bf16),
+                        vmem((towers, rows, cols), bf16), vmem((2, depth, cols), f32), vmem((towers, 2, depth, cols), bf16),
+                        vmem((2, rows, depth), bf16), vmem((2, depth, 2 * cols), bf16), vmem((towers, rows, 2 * cols), f32),
+                        vmem((towers, rows, cols), f32), vmem((rows, cols), f32), vmem((towers, rows, cols), bf16),
+                        vmem((towers, rows, cols), bf16), vmem((6, 8, cols), f32), vmem((4, 8, depth), f32),
+                        dma(many), dma(many), dma((16,)), dma((16,)), dma((3 * towers,)), dma((6,)), dma((6,)), dma((2,)),
+                        dma((3,)), dma((3,)), dma((6,)), dma((2,)), dma((2,))]
+        + [dma((towers, len(ranges)))] * 5,
+        compiler_params=pltpu.CompilerParams(collective_id=ident, has_side_effects=True, vmem_limit_bytes=58 * 2**20),
+        cost_estimate=pl.CostEstimate(flops=4 * towers * rows * cols * depth * chips, bytes_accessed=800 * 2**20, transcendentals=0),
+        name="forward",
+    )(features, weights, out_grad, told, small_params)
+
+
+def sum_kernel(chips, parts, share, y_ref, full_ref, dz_ref, w_ref, pg_ref, ps_ref, st_ref, d_ref, gr_ref, sr_ref,
+               given, rest, back, held, w_here, dz_here, total, d_send, d_recv, w_sem, o_sem, g_send, g_recv, s_send, s_recv, own_sem,
+               b_send, b_recv, v_send, v_recv, v_sem, y_send, y_recv, p_send, p_recv, l_sem):
+    dp, chip, core = place()
+    towers, rows, _ = dz_ref.shape
+    depth = d_ref.shape[2]
+    cols = pg_ref.shape[2] // 2
+    size = rows // parts
+    pieces = towers * parts
+    steps = chips - 1
+    across, along = dp ^ 1, dp ^ 2
+    others = (across, along, dp ^ 3)
+    at = lambda c, k: (c, 2 * chip + k)
+
+    meet([(chip > 0, (dp, 2 * (chip - 1) + core)), (chip < chips - 1, (dp, 2 * (chip + 1) + core)),
+          (chip >= 0, at(dp, 1 - core))] + [(chip >= 0, at(c, k)) for c in others for k in (0, 1)])
+
+    def grad(kind, k, t):
+        owner = (others + (dp,))[kind]
+        return pltpu.make_async_remote_copy(
+            src_ref=pg_ref.at[t, pl.ds(pl.multiple_of(owner * depth, 128), depth), pl.ds(pl.multiple_of((k ^ core) * cols, 128), cols)],
+            dst_ref=gr_ref.at[dp, core, t], send_sem=g_send.at[(kind * 2 + k) * 2 + t],
+            recv_sem=g_recv.at[(kind * 2 + core) * 2 + t], device_id=at(owner, k), device_id_type=MESH)
+
+    def grad_arrived(kind, k, t):
+        owner = (others + (dp,))[kind]
+        pltpu.make_async_remote_copy(
+            src_ref=gr_ref.at[owner, k, t], dst_ref=gr_ref.at[owner, k, t], send_sem=g_send.at[0],
+            recv_sem=g_recv.at[(kind * 2 + k) * 2 + t], device_id=at(dp, core), device_id_type=MESH).wait_recv()
+
+    def small(kind):
+        return pltpu.make_async_remote_copy(
+            src_ref=ps_ref, dst_ref=sr_ref.at[dp], send_sem=s_send.at[kind], recv_sem=s_recv.at[kind],
+            device_id=at(others[kind], core), device_id_type=MESH)
+
+    keep = share[0][0]
+    width = y_ref.shape[2]
+    slots = st_ref.shape[1]
+    again = share[2][0] + share[2][1] - share[3][0]
+    bands = ((0, keep), (keep, slots - keep))
+
+    def give(kind):
+        return pltpu.make_async_remote_copy(
+            src_ref=y_ref.at[:, pl.ds(*share[0])], dst_ref=given.at[1 + kind], send_sem=v_send.at[kind],
+            recv_sem=v_recv.at[kind], device_id=at(others[kind], core), device_id_type=MESH)
+
+    def channels(shard, k, t, b):
+        lanes = pl.ds(pl.multiple_of((2 * shard + k) * width, 128), width)
+        return st_ref.at[t, pl.ds(*bands[b]), lanes]
+
+    def own_channels(t, b):
+        return y_ref.at[t, pl.ds(*bands[b])] if b == 0 else rest.at[t]
+
+    def along_line(step, way, t, b, shard, there):
+        n = t * 2 + b
+        dst = channels(shard, core, t, b)
+        return pltpu.make_async_remote_copy(
+            src_ref=own_channels(t, b) if step == 0 else dst, dst_ref=dst, send_sem=y_send.at[way, step, n],
+            recv_sem=y_recv.at[way, step, n], device_id=(dp, 2 * there + core), device_id_type=MESH)
+
+    def leaves(step, way):
+        return (chip < steps) & (chip >= step) if way == 0 else (chip > 0) & (chip + step <= steps)
+
+    def comes(step, way):
+        return chip > step if way == 0 else chip + step < steps
+
+    def leaving(step, way, t, b):
+        return along_line(step, way, t, b, chip - step if way == 0 else chip + step, chip + 1 if way == 0 else chip - 1)
+
+    def coming(step, way, t, b):
+        return along_line(step, way, t, b, chip - 1 - step if way == 0 else chip + 1 + step, chip)
+
+    def to_core(shard, t, b, own=False):
+        dst = channels(shard, core, t, b)
+        return pltpu.make_async_remote_copy(
+            src_ref=own_channels(t, b) if own else dst, dst_ref=dst, send_sem=p_send.at[shard, t * 2 + b],
+            recv_sem=p_recv.at[shard, t * 2 + b], device_id=at(dp, 1 - core), device_id_type=MESH)
+
+    def from_core(shard, t, b):
+        dst = channels(shard, 1 - core, t, b)
+        return pltpu.make_async_remote_copy(
+            src_ref=dst, dst_ref=dst, send_sem=p_send.at[shard, t * 2 + b], recv_sem=p_recv.at[shard, t * 2 + b],
+            device_id=at(dp, core), device_id_type=MESH)
+
+    def pass_on(event):
+        step, t, b = event // 4, event % 4 // 2, event % 2
+        for way in (0, 1):
+            @pl.when(comes(step, way))
+            def _():
+                coming(step, way, t, b).wait_recv()
+                to_core(chip - 1 - step if way == 0 else chip + 1 + step, t, b).start()
+            if step + 1 < steps:
+                @pl.when(leaves(step + 1, way))
+                def _():
+                    leaving(step + 1, way, t, b).start()
+
+    def launch(b):
+        for t in range(towers):
+            for way in (0, 1):
+                @pl.when(leaves(0, way))
+                def _():
+                    leaving(0, way, t, b).start()
+            to_core(chip, t, b, True).start()
+            pltpu.make_async_copy(own_channels(t, b), channels(chip, core, t, b), v_sem.at[1 + t * 2 + b]).start()
+
+    ends = (chip == 0, chip == chips - 1)
+
+    def target(step, way):
+        return chip + steps - step if way == 0 else chip - (steps - step)
+
+    def sends(step, way):
+        return (chip < steps) & (chip <= step) if way == 0 else (chip > 0) & (steps - chip <= step)
+
+    def where(piece):
+        return lax.rem(piece, towers), pl.multiple_of(lax.rem(piece // towers + parts - 1, parts) * size, 16)
+
+    def passing(m, way, turn):
+        t, row = where(lax.rem(m, pieces))
+        there = chip + 1 if way == 0 else chip - 1
+        rws = pl.ds(row, size)
+        return pltpu.make_async_remote_copy(
+            src_ref=held.at[way, turn // pieces, t, rws], dst_ref=held.at[way, m // pieces, t, rws],
+            send_sem=d_send.at[way, m], recv_sem=d_recv.at[way, m], device_id=(dp, 2 * there + core), device_id_type=MESH)
+
+    def landed(m, way):
+        t, row = where(lax.rem(m, pieces))
+        ref = held.at[way, m // pieces, t, pl.ds(row, size)]
+        pltpu.make_async_remote_copy(src_ref=ref, dst_ref=ref, send_sem=d_send.at[way, m], recv_sem=d_recv.at[way, m],
+                                     device_id=(dp, 2 * chip + core), device_id_type=MESH).wait_recv()
+
+    third = depth // 3 if depth % 384 == 0 else depth
+
+    def product(goal, t, row, col):
+        return lax.dot_general(dz_here[t, pl.ds(row, size)], w_here[goal, t, pl.ds(col, third)], (((1,), (1,)), ((), ())),
+                               preferred_element_type=jnp.float32)
+
+    loads = []
+    for n in range(chips):
+        loads.append(pltpu.make_async_copy(w_ref.at[:, pl.ds(n * depth, depth)], w_here.at[n], w_sem.at[n]))
+    loads.append(pltpu.make_async_copy(dz_ref, dz_here, w_sem.at[chips]))
+    for load in loads:
+        load.start()
+    own = [pltpu.make_async_copy(
+        pg_ref.at[t, pl.ds(pl.multiple_of(dp * depth, 128), depth), pl.ds(0, cols)], gr_ref.at[dp, core, t], own_sem.at[t])
+        for t in range(towers)]
+    own.append(pltpu.make_async_copy(ps_ref, sr_ref.at[dp], own_sem.at[towers]))
+    for kind in (2, 0, 1):
+        give(kind).start()
+    mine = pltpu.make_async_copy(y_ref.at[:, pl.ds(*share[0])], given.at[0], v_sem.at[0])
+    mine.start()
+    launch(0)
+    for kind in range(3):
+        small(kind).start()
+    for t in range(towers):
+        for kind in (2, 0, 1):
+            for k in (0, 1):
+                grad(kind, k, t).start()
+        grad(3, 1 - core, t).start()
+    for copy in own:
+        copy.start()
+    for load in loads:
+        load.wait()
+
+    mine.wait()
+    for kind in range(3):
+        give(kind).wait_recv()
+
+    def fill(i, _):
+        for kind in range(4):
+            skip = again if kind == 3 else 0
+            place_of = (share[kind][0] if kind < 3 else share[2][0] + share[2][1]) - keep
+
+            @pl.when(i * 16 >= skip)
+            def _():
+                for t in range(towers):
+                    value = given[kind, t, pl.ds(pl.multiple_of(i * 16, 16), 16)].astype(jnp.float32) * full_ref[0]
+                    rest[t, pl.ds(pl.multiple_of(place_of - skip + i * 16, 16), 16)] = value.astype(jnp.bfloat16)
+        return 0
+
+    lax.fori_loop(0, share[0][1] // 16, fill, 0)
+    launch(1)
+
+    window = 3
+    lag = 2
+    turns = steps * pieces
+
+    def finish(piece):
+        t, row = where(piece)
+        s = lax.rem(piece, 2)
+        rws = pl.ds(row, size)
+
+        @pl.when(piece >= 2)
+        def _():
+            store(piece - 2, False)
+
+        @pl.when((piece >= 2) & (piece < 2 + towers))
+        def _():
+            for kind in range(3):
+                hand(kind, piece - 2).wait_send()
+        last = (steps - 1) * pieces + piece
+        for way in (0, 1):
+            @pl.when(jnp.logical_not(ends[way]))
+            def _():
+                landed(last, way)
+        for col in range(0, depth, third):
+            value = product(chip, t, row, col)
+            lanes = pl.ds(col, third)
+
+            @pl.when(ends[0])
+            def _():
+                total[s, :, lanes] = (value + held[1, steps - 1, t, rws, lanes].astype(jnp.float32)).astype(jnp.bfloat16)
+
+            @pl.when(ends[1])
+            def _():
+                total[s, :, lanes] = (value + held[0, steps - 1, t, rws, lanes].astype(jnp.float32)).astype(jnp.bfloat16)
+
+            @pl.when(jnp.logical_not(ends[0] | ends[1]))
+            def _():
+                total[s, :, lanes] = (value + held[0, steps - 1, t, rws, lanes].astype(jnp.float32)
+                                      + held[1, steps - 1, t, rws, lanes].astype(jnp.float32)).astype(jnp.bfloat16)
+        store(piece, True)
+
+        @pl.when(piece < towers)
+        def _():
+            for kind in (2, 0, 1):
+                hand(kind, piece).start()
+            back[0, t] = total[s, pl.ds(skip, size - skip)]
+
+    def store(piece, start):
+        t, row = where(piece)
+        s = lax.rem(piece, 2)
+        for here, length in ((piece < towers, skip), (piece >= towers, size)):
+            @pl.when(here)
+            def _():
+                copy = pltpu.make_async_copy(total.at[s, pl.ds(0, length)], d_ref.at[t, pl.ds(row, length)], o_sem.at[s])
+                (copy.start if start else copy.wait)()
+
+    skip = size - share[0][1]
+
+    def hand(kind, piece):
+        t, s = lax.rem(piece, towers), lax.rem(piece, 2)
+        return pltpu.make_async_remote_copy(
+            src_ref=total.at[s, pl.ds(skip, size - skip)], dst_ref=back.at[1 + kind, t], send_sem=b_send.at[kind, t],
+            recv_sem=b_recv.at[kind, t], device_id=at(others[kind], core), device_id_type=MESH)
+
+    def turn(m, _):
+        step, piece = m // pieces, lax.rem(m, pieces)
+        t, row = where(piece)
+        rws = pl.ds(row, size)
+        for way in (0, 1):
+            goes = (m < turns) & sends(step, way)
+
+            @pl.when(goes & ends[way])
+            def _():
+                for col in range(0, depth, third):
+                    held[way, step, t, rws, pl.ds(col, third)] = product(target(step, way), t, row, col).astype(jnp.bfloat16)
+
+                @pl.when(m >= window)
+                def _():
+                    passing(m - window, way, m - window).wait_send()
+                passing(m, way, m).start()
+
+            @pl.when(goes & jnp.logical_not(ends[way]))
+            def _():
+                landed(m - pieces, way)
+                for col in range(0, depth, third):
+                    lanes = pl.ds(col, third)
+                    held[way, step - 1, t, rws, lanes] = (
+                        product(target(step, way), t, row, col) + held[way, step - 1, t, rws, lanes].astype(jnp.float32)
+                    ).astype(jnp.bfloat16)
+                passing(m, way, m - pieces).start()
+
+        for event in range(4 * steps):
+            @pl.when(m == min(2 * event + 3, turns + lag - 1))
+            def _():
+                pass_on(event)
+
+        @pl.when(m >= turns - pieces + lag)
+        def _():
+            finish(m - (turns - pieces + lag))
+        return 0
+
+    lax.fori_loop(0, turns + lag, turn, 0)
+
+    def drain(m, _):
+        for way in (0, 1):
+            goes = sends(m // pieces, way)
+
+            @pl.when(goes & (jnp.logical_not(ends[way]) | (m >= turns - window)))
+            def _():
+                passing(m, way, m).wait_send()
+        return 0
+
+    lax.fori_loop(0, turns, drain, 0)
+    for t in range(towers):
+        for b in (0, 1):
+            pltpu.make_async_copy(own_channels(t, b), channels(chip, core, t, b), v_sem.at[1 + t * 2 + b]).wait()
+            for shard in range(chips):
+                from_core(shard, t, b).wait_recv()
+                to_core(shard, t, b).wait_send()
+            for step in range(steps):
+                for way in (0, 1):
+                    @pl.when(leaves(step, way))
+                    def _():
+                        leaving(step, way, t, b).wait_send()
+    for kind in range(3):
+        give(kind).wait_send()
+    for piece in (pieces - 2, pieces - 1):
+        store(piece, False)
+    for t in range(towers):
+        for kind in range(3):
+            hand(kind, t).wait_recv()
+
+    def mask(i, _):
+        rws = pl.ds(pl.multiple_of(i * 16, 16), 16)
+        for kind in range(4):
+            for t in range(towers):
+                back[kind, t, rws] = (back[kind, t, rws].astype(jnp.float32) * full_ref[0]).astype(jnp.bfloat16)
+        return 0
+
+    lax.fori_loop(0, share[0][1] // 16, mask, 0)
+    last = []
+    for kind in range(4):
+        skipped = again if kind == 3 else 0
+        first, length = share[kind][0] + skipped, share[kind][1] - skipped
+        last += [pltpu.make_async_copy(back.at[kind, t, pl.ds(skipped, length)], d_ref.at[t, pl.ds(first, length)], l_sem.at[kind, t])
+                 for t in range(towers)]
+    for copy in last:
+        copy.start()
+    for copy in last:
+        copy.wait()
+    for t in range(towers):
+        for kind in range(3):
+            for k in (0, 1):
+                grad_arrived(kind, k, t)
+        grad_arrived(3, 1 - core, t)
+    for kind in range(3):
+        small(kind).wait()
+    for t in range(towers):
+        for kind in range(3):
+            for k in (0, 1):
+                grad(kind, k, t).wait_send()
+        grad(3, 1 - core, t).wait_send()
+    for copy in own:
+        copy.wait()
+
+
+def sums(result, full, slots, wide_dz, wide_w, partial_g, partial_s, chips, parts, ident, share):
+    towers, rows, wide = wide_dz.shape
+    depth, cols = wide_w.shape[1] // chips, partial_g.shape[2] // 2
+    steps = chips - 1
+    dma = pltpu.SemaphoreType.DMA
+    bf16 = jnp.bfloat16
+    anywhere = pl.BlockSpec(memory_space=pl.ANY)
+    return pl.pallas_call(
+        functools.partial(sum_kernel, chips, parts, share),
+        out_shape=[jax.ShapeDtypeStruct((towers, slots, 2 * chips * cols), bf16),
+                   jax.ShapeDtypeStruct((towers, slots, depth), bf16),
+                   jax.ShapeDtypeStruct((4, 2, towers, depth, cols), bf16),
+                   jax.ShapeDtypeStruct((4,) + partial_s.shape, jnp.float32)],
+        in_specs=[anywhere, pl.BlockSpec(memory_space=pltpu.SMEM)] + [anywhere] * 4,
+        out_specs=[anywhere] * 4,
+        scratch_shapes=[pltpu.VMEM((4, towers, share[0][1], cols), bf16), pltpu.VMEM((towers, slots - share[0][0], cols), bf16),
+                        pltpu.VMEM((4, towers, share[0][1], depth), bf16),
+                        pltpu.VMEM((2, steps, towers, rows, depth), bf16), pltpu.VMEM((chips, towers, depth, wide), bf16),
+                        pltpu.VMEM((towers, rows, wide), bf16), pltpu.VMEM((2, rows // parts, depth), bf16),
+                        dma((2, steps * towers * parts)), dma((2, steps * towers * parts)), dma((chips + 1,)), dma((2,)),
+                        dma((16,)), dma((16,)), dma((3,)), dma((3,)), dma((towers + 1,)), dma((3, towers)), dma((3, towers)), dma((3,)), dma((3,)), dma((5,)),
+                        dma((2, steps, 4)), dma((2, steps, 4)), dma((chips, 4)), dma((chips, 4)), dma((4, towers))],
+        compiler_params=pltpu.CompilerParams(collective_id=ident, has_side_effects=True, vmem_limit_bytes=58 * 2**20),
+        cost_estimate=pl.CostEstimate(flops=2 * towers * rows * wide * depth * chips, bytes_accessed=800 * 2**20, transcendentals=0),
+        name="sums",
+    )(result, full, wide_dz, wide_w, partial_g, partial_s)
+
+
 def small_step(small_params, small_moment_one, small_moment_two, small_average, small_grad):
     first, second, direction = adam_part(small_moment_one, small_moment_two, small_grad)
     fresh = small_params - rate_small * direction
     return first, second, fresh, ema_decay * small_average + (1.0 - ema_decay) * fresh
+
+
+def update(d_feat, stitched, parts, small_parts, states, small_states):
+    small_grad = jnp.sum(small_parts, 0)[: small_states[0].shape[0]]
+    *fresh, stitched, d_feat = soap(parts, stitched, d_feat, *states)
+    return (stitched, d_feat) + tuple(fresh) + small_step(*small_states, small_grad)
+
+
+def own_rows(features, out_grad, totals, passed, states, small_states):
+    _, rows, _ = features.shape
+    weights, small_params = states[0], small_states[0]
+    cols = weights.shape[2]
+    cores = lax.axis_size("mp")
+    swap = [(i, i ^ 1) for i in range(cores)]
+    ranges = ((0, rows // 2), (rows // 2, rows // 2))
+    live_rows = (jnp.arange(rows, dtype=jnp.float32) < totals[0]).astype(jnp.float32)
+    wide_f, wide_w = gather(features, weights.astype(jnp.bfloat16), cores // 2, ranges, 1)
+    partial = jnp.einsum("tri,tio->tro", wide_f, wide_w, preferred_element_type=jnp.float32)
+    product = partial[:, :, :cols] + lax.ppermute(partial[:, :, cols:], "mp", swap)
+    result, back = jax.vjp(lambda a, b: stitch_local(a, b, live_rows), product, small_params)
+    stitched = lax.all_gather(result.astype(jnp.bfloat16), "mp", axis=2, tiled=True)
+    dz, small_part = back(out_grad.astype(jnp.float32))
+    dz_low = dz.astype(jnp.bfloat16)
+    wide_dz = jnp.concatenate([dz_low, lax.ppermute(dz_low, "mp", swap)], axis=2)
+    partial_d = jnp.einsum("tro,tio->tri", wide_dz, wide_w, preferred_element_type=jnp.float32)
+    partial_g = jnp.einsum("tri,tro->tio", wide_f, wide_dz, preferred_element_type=jnp.float32)
+    small_part = jnp.pad(small_part, ((0, 2), (0, 0)))
+    d_feat, parts, small_parts = reduce(
+        partial_d.astype(jnp.bfloat16), partial_g.astype(jnp.bfloat16), small_part, cores // 2, ranges, 2
+    )
+    return update(d_feat, stitched, parts, small_parts, states, small_states)
+
+
+def shares(rows):
+    keep = rows * 15 // 32 // 16 * 16
+    size = -(-(rows - keep) // 64) * 16
+    return keep, ((keep, size), (keep + size, size), (keep + 2 * size, size), (rows - size, size))
+
+
+def shared_rows(features, out_grad, totals, passed, states, small_states):
+    rows = features.shape[1]
+    keep, share = shares(rows)
+    wide_f, wide_w, result, wide_dz, small_part = passed
+    full = (totals[:1] > keep).astype(jnp.float32)
+    partial_g = jnp.einsum("tri,tro->tio", wide_f, wide_dz, preferred_element_type=jnp.float32)
+    stitched, d_feat, parts, small_parts = sums(
+        result, full, rows, wide_dz, wide_w, partial_g.astype(jnp.bfloat16), small_part, lax.axis_size("mp") // 2, 4, 4, share
+    )
+    return update(d_feat, stitched, parts, small_parts, states, small_states)
 
 
 def line_body(
@@ -461,32 +1301,22 @@
     small_moment_two,
     small_average,
 ):
-    cores = lax.axis_size("mp")
-    chips = cores // 2
-    cols = weights.shape[2]
-    swap = [(i, i ^ 1) for i in range(cores)]
-    slot_count = features.shape[1]
-    total = jnp.sum(counts)
-    live_rows = (jnp.arange(slot_count, dtype=jnp.int32) < total).astype(jnp.float32)
-    wide_f, wide_w = gather(features, weights.astype(jnp.bfloat16), chips, 2, 1)
-    partial = jnp.einsum("tri,tio->tro", wide_f, wide_w, preferred_element_type=jnp.float32)
-    product = partial[:, :, :cols] + lax.ppermute(partial[:, :, cols:], "mp", swap)
-    result, back = jax.vjp(lambda a, b: stitch_local(a, b, live_rows), product, small_params)
-    stitched = lax.all_gather(result.astype(jnp.bfloat16), "mp", axis=2, tiled=True)
-    dz, small_part = back(out_grad.astype(jnp.float32))
-    dz_low = dz.astype(jnp.bfloat16)
-    wide_dz = jnp.concatenate([dz_low, lax.ppermute(dz_low, "mp", swap)], axis=2)
-    partial_d = jnp.einsum("tro,tio->tri", wide_dz, wide_w, preferred_element_type=jnp.float32)
-    partial_g = jnp.einsum("tri,tro->tio", wide_f, wide_dz, preferred_element_type=jnp.float32)
-    small_part = jnp.pad(small_part, ((0, 2), (0, 0)))
-    d_feat, parts, small_parts = reduce(
-        partial_d.astype(jnp.bfloat16), partial_g.astype(jnp.bfloat16), small_part, chips, 2, 2
+    keep, share = shares(features.shape[1])
+    *passed, told = forward(
+        features, weights, out_grad, jnp.sum(counts), small_params, lax.axis_size("mp") // 2, share, 3
     )
-    states = soap(parts, weights, moment_one, moment_two, average, basis_left, basis_right)
-    small_states = small_step(
-        small_params, small_moment_one, small_moment_two, small_average, jnp.sum(small_parts, 0)[:6]
+    totals = told[:, 0, 0]
+    return lax.cond(
+        jnp.sum(totals > keep) == 1,
+        shared_rows,
+        own_rows,
+        features,
+        out_grad,
+        totals,
+        passed,
+        (weights, moment_one, moment_two, average, basis_left, basis_right),
+        (small_params, small_moment_one, small_moment_two, small_average),
     )
-    return (stitched, d_feat) + tuple(states) + small_states
 
 
 def plain_body(

time: 1200 us -> 674 us (0.56); the launches traced: 1200 us -> 665 us
  Pallas kernels: 1030 us -> 616 us
  matrix products: 99.4 us -> 21.5 us
  local copies, waits for them, and re-layouts: 27.6 us -> 4.15 us
  other arithmetic: 26.2 us -> 3.42 us
    pallas_call x3, Pallas kernels: 1030 us -> 616 us  [the longest x1 298 us: sums(): pl.pallas_call(functools.partial(sum_kernel, chips, parts, share), out_sh...]
    dot_general x3 -> x1, matrix products: 99.4 us -> 21.5 us  [shared_rows(): jnp.einsum('tri,tro->tio', wide_f, wide_dz, preferred_element_type=jnp.fl...]
    unnamed x26 -> x10, local copies, waits for them, and re-layouts: 21.4 us -> 0.02 us
  transfers between devices with their start and end apart: 3 -> 0, of which waited for: 2 -> 0; matrix products, arithmetic and copies ran while one was open for 6% -> 0% of each run, Pallas kernels for 54% -> 0%
where the time goes in v4:
time: 674 us; the launch traced here: 665 us
  Pallas kernels  616 us (91%)
  matrix products  21.5 us (3%)
  between operations  15.7 us (2%)
    pallas_call x1, Pallas kernels, sums(): pl.pallas_call(functools.partial(sum_kernel, chips, parts, share), out_sh...  298 us
    pallas_call x1, Pallas kernels, forward(): pl.pallas_call(functools.partial(forward_kernel, chips, share, ranges), o...  247 us
    pallas_call x1, Pallas kernels, soap(): pl.pallas_call(functools.partial(soap_body, 2 - group % 2), grid=(towers,...  70.3 us
    dot_general x1, matrix products, shared_rows(): jnp.einsum('tri,tro->tio', wide_f, wide_dz, preferred_element_type=jnp.fl...  21.5 us

profile of v4, /device:TPU:17, one launch (start us, length us, event | category | flops | bytes accessed | tf_op | source)
XLA Modules:
  0.0 665.2 jit_solution(11092824580875852652)
XLA Ops:
  7.2 1.3 reduce_sum.78
  9.1 0.6 broadcast_in_dim.2.n_ref
  9.7 0.0 copy-start.2
  9.7 0.0 copy-start.4
  9.8 0.0 copy-start.11
  9.8 247.2 %forward.1 = (bf16[2,768,4608]{2,1,0:T(8,128)(2,1)}, bf16[2,4608,1024]{2,1,0:T(8,128)(2,1)}, bf16[2,768,512]{2,1,0:T(8,128)(2,1)}, bf16[2,768,1024]{2,1,0:T(8,12...) custom-call(bf16[2,1280,1152]{2,1,0:T(8,128)(2,1)} %f_ref.1, f32[2,2304,512]{2,1,0:T(8,128)} %w_ref.1, ...), custom_call_target="tpu_custom_call" | custom-call | flops 14495514624 | bytes 838860800 | tf_op jit(solution)/shard_map/forward/pallas_call | solution.py:835
  257.0 0.8 slice_reduce_fusion
  257.8 0.6 fusion.13
  259.1 0.0 copy-done.2
  259.1 0.0 copy-done.4
  259.1 0.0 copy-done.5
  259.1 0.0 copy-done.8
  259.1 0.0 copy-done.11
  259.1 398.9 %conditional.1 = (bf16[2,1280,4096]{2,1,0:T(8,128)(2,1)}, bf16[2,1280,1152]{2,1,0:T(8,128)(2,1)}, f32[2,2304,512]{2,1,0:T(8,128)}, f32[2,2304,512]{2,1,0:T(8,128...) conditional(s32[]{:T(128)} %convert_element_type.44, ...), branch_computations={%region_2.9_spmd, %region_9.11_spmd} | conditional | flops 74991869952 | bytes 2231458816 | solution.py:1309
  263.6 0.0 copy-start.14
  263.6 0.0 copy-start.15
  263.6 21.5 %convolution_convert_fusion.2.pg_ref = bf16[2,4608,1024]{2,1,0:T(8,128)(2,1)} fusion(bf16[2,768,4608]{2,1,0:T(8,128)(2,1)} %get-tuple-element.154, bf16[2,768,1024]{2,1,0:T(8,128)(2,1)} %get-tuple-element.85.dz_ref), kind=kOutput, calls=%fused_computation.37 | convolution fusion | flops 14504951808 | bytes 36175872 | tf_op jit(solution)/shard_map/cond/branch_1_fun/tri,tro->tio/dot_general | solution.py:1282
  285.1 0.0 copy-done.14
  285.1 0.0 copy-done.15
  285.1 298.2 %sums.1 = (bf16[2,1280,4096]{2,1,0:T(8,128)(2,1)}, bf16[2,1280,1152]{2,1,0:T(8,128)(2,1)}, bf16[4,2,2,1152,512]{4,3,2,1,0:T(8,128)(2,1)}, f32[4,8,512]{2,1,0:T(8,128)}) custom-call(bf16[2,768,512]{2,1,0:T(8,128)(2,1)S(1)} %copy-done.15, f32[1]{0:T(128)S(6)} %convert_element_type.37.full_ref, bf16[2,768,1024]{2,1,0:T(8,128)(2,1)S(1)} %copy-done.14, ...), custom_call_target="tpu_custom_call" | custom-call | flops 14495514624 | bytes 838860800 | tf_op jit(solution)/shard_map/cond/branch_1_fun/sums/pallas_call | solution.py:1213
  583.3 0.9 reduce_sum.72
  584.2 0.6 add_multiply_fusion.1
  584.8 2.7 copy-done.1
  587.5 70.3 %soap.3 = (f32[2,2304,512]{2,1,0:T(8,128)}, f32[2,2304,512]{2,1,0:T(8,128)}, f32[2,2304,512]{2,1,0:T(8,128)}, f32[2,2304,512]{2,1,0:T(8,128)}, bf16[2,2304,512]{...) custom-call(bf16[4,2,2,1152,512]{4,3,2,1,0:T(8,128)(2,1)} %get-tuple-element.89.parts, ...), custom_call_target="tpu_custom_call" | custom-call | flops 2415919104 | bytes 136314880 | tf_op jit(solution)/shard_map/cond/branch_1_fun/soap/pallas_call | solution.py:118
  (3 shorter events, 0.0 us)
Async XLA Ops:
  9.7 249.3 %copy-start.2 = (bf16[2,1280,512]{2,1,0:T(8,128)(2,1)S(1)}, bf16[2,1280,512]{2,1,0:T(8,128)(2,1)}, u32[]{:S(2)}) copy-start(bf16[2,1280,512]{2,1,0:T(8,128)(2,1)} %o_ref.1) | copy-start | bytes 7864324
  9.7 249.3 %copy-start.4 = (f32[6,512]{1,0:T(8,128)S(1)}, f32[6,512]{1,0:T(8,128)}, u32[]{:S(2)}) copy-start(f32[6,512]{1,0:T(8,128)} %sp_ref.1) | copy-start | bytes 36868
  9.7 249.4 %copy-start.5 = (f32[6,512]{1,0:T(8,128)S(1)}, f32[6,512]{1,0:T(8,128)}, u32[]{:S(2)}) copy-start(f32[6,512]{1,0:T(8,128)} %param.25) | copy-start | bytes 36868
  9.7 249.4 %copy-start.8 = (f32[6,512]{1,0:T(8,128)S(1)}, f32[6,512]{1,0:T(8,128)}, u32[]{:S(2)}) copy-start(f32[6,512]{1,0:T(8,128)} %param.26) | copy-start | bytes 36868
  9.8 249.4 %copy-start.11 = (f32[6,512]{1,0:T(8,128)S(1)}, f32[6,512]{1,0:T(8,128)}, u32[]{:S(2)}) copy-start(f32[6,512]{1,0:T(8,128)} %param.27) | copy-start | bytes 36868
  263.6 21.5 %copy-start.14 = (bf16[2,768,1024]{2,1,0:T(8,128)(2,1)S(1)}, bf16[2,768,1024]{2,1,0:T(8,128)(2,1)}, u32[]{:S(2)}) copy-start(bf16[2,768,1024]{2,1,0:T(8,128)(2,1)} %get-tuple-element.85.dz_ref) | copy-start | bytes 9437188 | tf_op jit(solution)/shard_map/cond
  263.6 21.5 %copy-start.15 = (bf16[2,768,512]{2,1,0:T(8,128)(2,1)S(1)}, bf16[2,768,512]{2,1,0:T(8,128)(2,1)}, u32[]{:S(2)}) copy-start(bf16[2,768,512]{2,1,0:T(8,128)(2,1)} %get-tuple-element.83.y_ref) | copy-start | bytes 4718596 | tf_op jit(solution)/shard_map/cond
  584.8 2.7 copy-start.1

commit v5 on v4

--- a/solution.py
+++ b/solution.py
@@ -71,13 +71,27 @@
     return [(first, second, step) for (first, second, _), step in zip(states, values)]
 
 
-def soap_body(together, parts, stitched, d_feat, weights, moment_a, moment_b, average, left, right,
+def soap_body(together, strips, full, parts, stitched, d_feat, weights, moment_a, moment_b, average, left, right,
               first, second, new_weights, new_average, copy, stitched_out, d_feat_out):
     groups, pairs = left.shape[1], left.shape[2] // 2
-    stitched_out[...] = stitched[...]
-    d_feat_out[...] = d_feat[...]
-
-    def strips(g, _):
+    length = stitched.shape[1]
+    row = jnp.minimum(pl.program_id(1) * pl.num_programs(2) + pl.program_id(2), strips - 1) * length
+
+    @pl.when(row + length <= full[0])
+    def _():
+        stitched_out[...] = stitched[...]
+        d_feat_out[...] = d_feat[...]
+
+    @pl.when(row + length > full[0])
+    def _():
+        for source, target in ((stitched, stitched_out), (d_feat, d_feat_out)):
+            def clear(i, _):
+                rows = pl.ds(pl.multiple_of(i * 16, 16), 16)
+                target[0, rows] = jnp.where(row + i * 16 < full[0], source[0, rows], 0)
+                return 0
+            lax.fori_loop(0, length // 16, clear, 0)
+
+    def blocks(g, _):
         places = [(g * together + s, q) for s in range(together) for q in range(pairs)]
         ats = [(0, pl.ds(pl.multiple_of(r * BLOCK, BLOCK), BLOCK), pl.ds(2 * BLOCK * q, 2 * BLOCK)) for r, q in places]
         grads = []
@@ -98,10 +112,10 @@
             copy[at] = fresh.astype(jnp.bfloat16)
         return 0
 
-    lax.fori_loop(0, groups // together, strips, 0)
-
-
-def soap(parts, stitched, d_feat, weights, moment_a, moment_b, average, left, right, group=6):
+    lax.fori_loop(0, groups // together, blocks, 0)
+
+
+def soap(parts, wanted, stitched, d_feat, weights, moment_a, moment_b, average, left, right, group=6):
     towers, rows, cols = weights.shape
     half = parts.shape[3]
     steps = half // (BLOCK * group)
@@ -116,9 +130,10 @@
         return pl.BlockSpec((1, v.shape[1] // strips, v.shape[2]), lambda t, p, g: (t, jnp.minimum(p * steps + g, strips - 1), 0))
 
     return pl.pallas_call(
-        functools.partial(soap_body, 2 - group % 2),
+        functools.partial(soap_body, 2 - group % 2, strips),
         grid=(towers, 2, steps),
-        in_specs=[pl.BlockSpec((parts.shape[0], 1, 1, BLOCK * group, cols), lambda t, p, g: (0, p, t, g, 0)),
+        in_specs=[pl.BlockSpec(memory_space=pltpu.SMEM),
+                  pl.BlockSpec((parts.shape[0], 1, 1, BLOCK * group, cols), lambda t, p, g: (0, p, t, g, 0)),
                   through(stitched), through(d_feat), state, state, state, state, base, base],
         out_specs=[state] * 5 + [through(stitched), through(d_feat)],
         out_shape=[full] * 4 + [jax.ShapeDtypeStruct(weights.shape, jnp.bfloat16)]
@@ -126,7 +141,7 @@
         compiler_params=pltpu.CompilerParams(vmem_limit_bytes=48 * 2**20),
         cost_estimate=pl.CostEstimate(flops=8 * 2 * towers * rows * cols * 64, bytes_accessed=130 * 2**20, transcendentals=0),
         name="soap",
-    )(parts, stitched, d_feat, weights, moment_a, moment_b, average, left, right)
+    )(wanted, parts, stitched, d_feat, weights, moment_a, moment_b, average, left, right)
 
 
 MESH = pl.DeviceIdType.MESH
@@ -468,7 +483,7 @@
     )(partial_d, partial_g, partial_s)
 
 
-def forward_kernel(chips, share, ranges, f_ref, w_ref, o_ref, n_ref, sp_ref, fg_ref, wg_ref, y_ref, dz_ref, sg_ref, tot_ref,
+def forward_kernel(chips, parts, share, f_ref, w_ref, o_ref, n_ref, sp_ref, fg_ref, wg_ref, y_ref, dz_ref, sg_ref, tot_ref,
                    offer_f, taken, offer_o, og, w_wide, w_low, f_tile, w_tile, acc, theirs, live, y_here, dz_here, sums_here,
                    tot, f_send, f_recv, w_send, w_recv, own_sem, x_send, x_recv, k_sem, n_send, n_recv, l_sem, ft_sem, wt_sem,
                    a_send, a_recv, z_send, z_recv, out_sem):
@@ -476,8 +491,11 @@
     towers, _, depth = f_ref.shape
     cols = w_ref.shape[2]
     steps = chips - 1
-    keep = share[0][0]
-    fixed = len(ranges) - 1
+    keep, rows = share[0][0], sum(share[0])
+    size = rows // parts
+    pieces = towers * parts
+    fixed = rows - size
+    spare = keep - fixed
     across, along = dp ^ 1, dp ^ 2
     others = (across, along, dp ^ 3)
     at = lambda c, k: (c, 2 * chip + k)
@@ -490,22 +508,24 @@
     def shard_lanes(shard):
         return pl.ds(pl.multiple_of(shard * depth, 128), depth)
 
-    def copies(step, way, t, k, shard, there):
-        rws = pl.ds(*ranges[k])
+    def piece_of(p):
+        return lax.rem(p, towers), pl.ds(pl.multiple_of(p // towers * size, 16), size)
+
+    def copies(step, way, p, shard, there, last):
+        t, rws = piece_of(p)
         dst = fg_ref.at[t, rws, shard_lanes(shard)]
         src = dst
         if step == 0:
-            src = taken.at[t] if k == fixed else f_ref.at[t, rws]
-        n = t * len(ranges) + k
-        return pltpu.make_async_remote_copy(
-            src_ref=src, dst_ref=dst, send_sem=f_send.at[way, step, n], recv_sem=f_recv.at[way, step, n],
+            src = taken.at[t] if last else f_ref.at[t, rws]
+        return pltpu.make_async_remote_copy(
+            src_ref=src, dst_ref=dst, send_sem=f_send.at[way, step, p], recv_sem=f_recv.at[way, step, p],
             device_id=(dp, 2 * there + core), device_id_type=MESH)
 
-    def feature(step, way, t, k):
-        return copies(step, way, t, k, chip - step if way == 0 else chip + step, chip + 1 if way == 0 else chip - 1)
-
-    def incoming(step, way, t, k):
-        return copies(step, way, t, k, chip - 1 - step if way == 0 else chip + 1 + step, chip)
+    def feature(step, way, p, last=False):
+        return copies(step, way, p, chip - step if way == 0 else chip + step, chip + 1 if way == 0 else chip - 1, last)
+
+    def incoming(step, way, p):
+        return copies(step, way, p, chip - 1 - step if way == 0 else chip + 1 + step, chip, False)
 
     def sends(step, way):
         return (chip < steps) & (chip >= step) if way == 0 else (chip > 0) & (chip + step <= steps)
@@ -513,11 +533,11 @@
     def receives(step, way):
         return chip > step if way == 0 else chip + step < steps
 
-    def launch(t, k):
+    def launch(p, last):
         for way in (0, 1):
             @pl.when(sends(0, way))
             def _():
-                feature(0, way, t, k).start()
+                feature(0, way, p, last).start()
 
     def block(owner, slot, t):
         return wg_ref.at[t, pl.ds(pl.multiple_of(owner * depth, 128), depth), pl.ds(pl.multiple_of(slot * cols, 128), cols)]
@@ -554,7 +574,7 @@
             src_ref=n_ref, dst_ref=tot.at[1 + kind], send_sem=n_send.at[kind], recv_sem=n_recv.at[kind],
             device_id=at(others[kind], core), device_id_type=MESH)
 
-    def choose(offers, into):
+    def choose(offers, into, first):
         width = offers.shape[3]
         weigh = [jnp.broadcast_to(jnp.where(tot[kind, :1, :width] > keep, 1.0, 0.0), (16, width)) for kind in range(4)]
 
@@ -564,62 +584,66 @@
                 value = offers[0, t, rws].astype(jnp.float32) * weigh[0]
                 for kind in range(1, 4):
                     value = value + offers[kind, t, rws].astype(jnp.float32) * weigh[kind]
-                into(t, i, value.astype(jnp.bfloat16))
+                into[t, pl.ds(pl.multiple_of(first + i * 16, 16), 16)] = value.astype(jnp.bfloat16)
             return 0
         lax.fori_loop(0, share[0][1] // 16, strip, 0)
+
+    def loop(count, body):
+        def step(i, _):
+            body(i)
+            return 0
+        lax.fori_loop(0, count, step, 0)
 
     for kind in range(3):
         tell(kind).start()
     for kind in (2, 0, 1):
         offer(kind, 0).start()
-    pieces = [(t, k) for k in range(len(ranges)) for t in range(towers)]
-    for t, k in pieces:
-        if k < fixed:
-            launch(t, k)
-    local = [(n_ref, tot.at[0]), (f_ref.at[:, pl.ds(*share[0])], offer_f.at[0]), (o_ref.at[:, pl.ds(*share[0])], offer_o.at[0]),
-             (o_ref.at[:, pl.ds(0, keep)], og.at[:, pl.ds(0, keep)])]
+    loop(pieces - towers, lambda p: launch(p, False))
+    local = [(n_ref, tot.at[0]), (f_ref.at[:, pl.ds(*share[0])], offer_f.at[0]), (f_ref.at[:, pl.ds(fixed, spare)], taken.at[:, pl.ds(0, spare)]),
+             (o_ref.at[:, pl.ds(*share[0])], offer_o.at[0]), (o_ref.at[:, pl.ds(0, keep)], og.at[:, pl.ds(0, keep)])]
     local = [pltpu.make_async_copy(src, dst, l_sem.at[n]) for n, (src, dst) in enumerate(local)]
     for copy in local:
         copy.start()
-    own = [pltpu.make_async_copy(f_ref.at[t, pl.ds(0, keep)], fg_ref.at[t, pl.ds(0, keep), shard_lanes(chip)], own_sem.at[t])
+    own = [pltpu.make_async_copy(f_ref.at[t, pl.ds(0, fixed)], fg_ref.at[t, pl.ds(0, fixed), shard_lanes(chip)], own_sem.at[t])
            for t in range(towers)]
     for copy in own:
         copy.start()
 
-    halves = [(t, k) for t in range(towers) for k in (0, 1)]
-    wide = [pltpu.make_async_copy(w_ref.at[t, pl.ds(k * depth, depth)], w_wide.at[n % 2], k_sem.at[n % 2]) for n, (t, k) in enumerate(halves)]
-    wide[0].start()
-    for n, (t, k) in enumerate(halves):
-        wide[n].wait()
-        if n + 1 < len(halves):
-            wide[n + 1].start()
-
-        def round_strip(i, _):
+    def wide(n):
+        return pltpu.make_async_copy(w_ref.at[n // 2, pl.ds(pl.multiple_of(lax.rem(n, 2) * depth, 128), depth)], w_wide.at[lax.rem(n, 2)],
+                                     k_sem.at[lax.rem(n, 2)])
+
+    def round_half(n):
+        @pl.when(n + 1 < 2 * towers)
+        def _():
+            wide(n + 1).start()
+        wide(n).wait()
+
+        def strip(i):
             rws = pl.ds(pl.multiple_of(i * 64, 64), 64)
-            w_low[t, k, rws] = w_wide[n % 2, rws].astype(jnp.bfloat16)
-            return 0
-        lax.fori_loop(0, depth // 64, round_strip, 0)
+            w_low[n // 2, lax.rem(n, 2), rws] = w_wide[lax.rem(n, 2), rws].astype(jnp.bfloat16)
+        loop(depth // 64, strip)
+    wide(jnp.int32(0)).start()
+    loop(2 * towers, round_half)
     own_w = [pltpu.make_async_copy(w_low.at[t, core], block(dp, 0, t), own_sem.at[towers + t]) for t in range(towers)]
     for copy in own_w:
         copy.start()
 
-    local[0].wait()
-    local[1].wait()
+    for copy in local[:3]:
+        copy.wait()
     for kind in range(3):
         tell(kind).wait_recv()
-    totals = pltpu.make_async_copy(tot, tot_ref, l_sem.at[4])
+    totals = pltpu.make_async_copy(tot, tot_ref, l_sem.at[5])
     totals.start()
     for kind in range(3):
         offer(kind, 0).wait_recv()
-
-    def take(t, i, value):
-        taken[t, pl.ds(pl.multiple_of(i * 16, 16), 16)] = value
-    choose(offer_f, take)
-    own_share = [pltpu.make_async_copy(taken.at[t], fg_ref.at[t, pl.ds(*ranges[fixed]), shard_lanes(chip)], own_sem.at[2 * towers + t])
+    choose(offer_f, taken, spare)
+    own_share = [pltpu.make_async_copy(taken.at[t], fg_ref.at[t, pl.ds(fixed, size), shard_lanes(chip)], own_sem.at[2 * towers + t])
                  for t in range(towers)]
     for t in range(towers):
-        launch(t, fixed)
-        own_share[t].start()
+        launch(pieces - towers + t, True)
+    for copy in own_share:
+        copy.start()
     for t in (0, 1):
         for k in (0, 1):
             weight(0, k, t).start()
@@ -629,7 +653,7 @@
     for kind in (2, 0, 1):
         offer(kind, 1).start()
 
-    def alive(i, _):
+    def alive(i):
         rws = pl.ds(pl.multiple_of(i * 16, 16), 16)
         row = lax.broadcasted_iota(jnp.int32, (16, cols), 0).astype(jnp.float32) + (i * 16).astype(jnp.float32)
         here = jnp.where(row < tot[0, :1, :cols], 1.0, 0.0)
@@ -642,19 +666,21 @@
                 valid = valid & (slot >= share[2][0] + share[2][1])
             there = there + jnp.where(valid, 1.0, 0.0)
         live[rws] = jnp.where(row < keep, here, there)
-        return 0
-    lax.fori_loop(0, sum(ranges[fixed]) // 16, alive, 0)
+        for t in range(towers):
+            acc[t, rws] = jnp.zeros((16, 2 * cols), jnp.float32)
+    loop(rows // 16, alive)
 
     for step in range(steps - 1):
-        for t, k in pieces:
+        def serve(p):
             for way in (0, 1):
                 @pl.when(receives(step, way))
                 def _():
-                    incoming(step, way, t, k).wait_recv()
+                    incoming(step, way, p).wait_recv()
 
                 @pl.when(sends(step + 1, way))
                 def _():
-                    feature(step + 1, way, t, k).start()
+                    feature(step + 1, way, p).start()
+        loop(pieces, serve)
         if step == 0:
             for slot in (0, 1):
                 arrived(0, slot, 0)
@@ -662,14 +688,11 @@
                 arrived(1, slot, 1)
                 pass_on(1, slot).start()
 
-    for copy in local[2:]:
+    for copy in local[3:]:
         copy.wait()
     for kind in range(3):
         offer(kind, 1).wait_recv()
-
-    def take_grad(t, i, value):
-        og[t, pl.ds(pl.multiple_of(keep + i * 16, 16), 16)] = value
-    choose(offer_o, take_grad)
+    choose(offer_o, og, keep)
     for slot in (0, 1):
         arrived(0, slot, 1)
         arrived(1, slot, 0)
@@ -680,84 +703,78 @@
     for copy in own + own_w + own_share:
         copy.wait()
 
-    units = [(j, t) for j in range(chips) for t in range(towers)]
-    shard = lambda j: jnp.where(chip == steps, steps - j, j)
+    def shard(j):
+        return jnp.where(chip == steps, steps - j, j)
 
     def load_w(n):
-        j, t = units[n]
-        return pltpu.make_async_copy(wg_ref.at[t, pl.ds(pl.multiple_of(shard(j) * depth, 128), depth)], w_tile.at[n % 2], wt_sem.at[n % 2])
+        rws = pl.ds(pl.multiple_of(shard(n // towers) * depth, 128), depth)
+        return pltpu.make_async_copy(wg_ref.at[lax.rem(n, towers), rws], w_tile.at[lax.rem(n, 2)], wt_sem.at[lax.rem(n, 2)])
 
     def load_f(n):
-        j, t = units[n]
-        return pltpu.make_async_copy(fg_ref.at[t, :, shard_lanes(shard(j))], f_tile.at[n % 2], ft_sem.at[n % 2])
-
-    def add(t, slot, start, size, first):
+        return pltpu.make_async_copy(fg_ref.at[lax.rem(n, towers), :, shard_lanes(shard(n // towers))], f_tile.at[lax.rem(n, 2)],
+                                     ft_sem.at[lax.rem(n, 2)])
+
+    def add(t, slot, rws):
         for col in range(0, 2 * cols, cols):
-            value = jnp.dot(f_tile[slot, pl.ds(start, size)], w_tile[slot, :, pl.ds(col, cols)], preferred_element_type=jnp.float32)
-            where = (t, pl.ds(start, size), pl.ds(col, cols))
-            acc[where] = value if first else acc[where] + value
-
-    rows = sum(ranges[fixed])
-    part = rows // 4
-    load_w(0).start()
-    load_f(0).start()
-    for n, (j, t) in enumerate(units):
-        if n + 1 < len(units):
+            lanes = pl.ds(col, cols)
+            acc[t, rws, lanes] += jnp.dot(f_tile[slot, rws], w_tile[slot, :, lanes], preferred_element_type=jnp.float32)
+
+    def here(n):
+        return (n < steps * towers) | jnp.logical_not(ends)
+
+    def unit(n):
+        @pl.when(n + 1 < chips * towers)
+        def _():
             load_w(n + 1).start()
-            if units[n + 1][0] < steps:
-                load_f(n + 1).start()
-            else:
-                @pl.when(jnp.logical_not(ends))
-                def _():
-                    load_f(n + 1).start()
+
+        @pl.when((n + 1 < chips * towers) & here(n + 1))
+        def _():
+            load_f(n + 1).start()
         load_w(n).wait()
 
-        def multiply():
+        @pl.when(here(n))
+        def _():
             load_f(n).wait()
-
-            def one(i, _):
-                add(t, n % 2, pl.multiple_of(i * part, 16), part, j == 0)
-                return 0
-            lax.fori_loop(0, 4, one, 0)
-        if j < steps:
-            multiply()
-        else:
-            pl.when(jnp.logical_not(ends))(multiply)
-
-    def swap_sum(t, k):
-        rws = pl.ds(*ranges[k])
-        return pltpu.make_async_remote_copy(
-            src_ref=acc.at[t, rws, pl.ds(cols, cols)], dst_ref=theirs.at[t, rws], send_sem=a_send.at[t, k],
-            recv_sem=a_recv.at[t, k], device_id=at(dp, 1 - core), device_id_type=MESH)
-
-    for t, k in pieces:
-        slot = (len(units) - towers + t) % 2
+            loop(parts, lambda i: add(lax.rem(n, towers), lax.rem(n, 2), pl.ds(pl.multiple_of(i * size, 16), size)))
+    load_w(jnp.int32(0)).start()
+    load_f(jnp.int32(0)).start()
+    loop(chips * towers, unit)
+
+    def swap_sum(p):
+        t, rws = piece_of(p)
+        return pltpu.make_async_remote_copy(
+            src_ref=acc.at[t, rws, pl.ds(cols, cols)], dst_ref=theirs.at[t, rws], send_sem=a_send.at[p],
+            recv_sem=a_recv.at[p], device_id=at(dp, 1 - core), device_id_type=MESH)
+
+    def complete(p):
+        t, rws = piece_of(p)
         for way in (0, 1):
             @pl.when(receives(steps - 1, way))
             def _():
-                incoming(steps - 1, way, t, k).wait_recv()
-                piece = pltpu.make_async_copy(
-                    fg_ref.at[t, pl.ds(*ranges[k]), shard_lanes(shard(steps))], f_tile.at[slot, pl.ds(*ranges[k])], ft_sem.at[slot])
-                piece.start()
-                piece.wait()
-                add(t, slot, *ranges[k], False)
-        swap_sum(t, k).start()
-
-    def swap_dz(t, k):
-        rws = pl.ds(*ranges[k])
-        return pltpu.make_async_remote_copy(
-            src_ref=dz_here.at[t, rws], dst_ref=dz_ref.at[t, rws, pl.ds(cols, cols)], send_sem=z_send.at[t, k],
-            recv_sem=z_recv.at[t, k], device_id=at(dp, 1 - core), device_id_type=MESH)
-
-    def keep_dz(t, k):
-        rws = pl.ds(*ranges[k])
-        return pltpu.make_async_copy(dz_here.at[t, rws], dz_ref.at[t, rws, pl.ds(0, cols)], out_sem.at[t, k])
+                incoming(steps - 1, way, p).wait_recv()
+
+        @pl.when(ends)
+        def _():
+            copy = pltpu.make_async_copy(fg_ref.at[t, rws, shard_lanes(shard(steps))], f_tile.at[t, rws], ft_sem.at[t])
+            copy.start()
+            copy.wait()
+            add(t, t, rws)
+        swap_sum(p).start()
+
+    def swap_dz(p):
+        t, rws = piece_of(p)
+        return pltpu.make_async_remote_copy(
+            src_ref=dz_here.at[t, rws], dst_ref=dz_ref.at[t, rws, pl.ds(cols, cols)], send_sem=z_send.at[p],
+            recv_sem=z_recv.at[p], device_id=at(dp, 1 - core), device_id_type=MESH)
+
+    def keep_dz(p):
+        t, rws = piece_of(p)
+        return pltpu.make_async_copy(dz_here.at[t, rws], dz_ref.at[t, rws, pl.ds(0, cols)], out_sem.at[p])
 
     sums_here[...] = jnp.zeros_like(sums_here)
     factor, cubic = math.sqrt(2.0 / math.pi), 0.044715
 
-    def both(i, start):
-        rws = pl.ds(pl.multiple_of(start + i * 16, 16), 16)
+    def both(rws):
         activated, slope = [], []
         for t in range(towers):
             v = acc[t, rws, :cols] + theirs[t, rws] + sp_ref[t : t + 1]
@@ -775,28 +792,41 @@
         terms = dz + [activated[0] * dy[0], activated[1] * dy[0], activated[0] * dy[1], activated[1] * dy[1]]
         for n, term in enumerate(terms):
             sums_here[n] += term[:8] + term[8:]
-        return start
-
-    for k in range(len(ranges)):
+
+    def backward(k):
         for t in range(towers):
-            swap_sum(t, k).wait_recv()
-        start, size = ranges[k]
-        lax.fori_loop(0, size // 16, lambda i, c: both(i, c), start)
+            swap_sum(k * towers + t).wait_recv()
+        loop(size // 16, lambda i: both(pl.ds(pl.multiple_of(k * size + i * 16, 16), 16)))
         for t in range(towers):
-            swap_dz(t, k).start()
-            keep_dz(t, k).start()
-    keep_y = pltpu.make_async_copy(y_here, y_ref, l_sem.at[5])
+            swap_dz(k * towers + t).start()
+            keep_dz(k * towers + t).start()
+
+    def stage(k):
+        @pl.when(k < parts)
+        def _():
+            loop(towers, lambda t: complete(k * towers + t))
+
+        @pl.when(k > 0)
+        def _():
+            backward(k - 1)
+    loop(parts + 1, stage)
+    keep_y = pltpu.make_async_copy(y_here, y_ref, l_sem.at[6])
     keep_y.start()
     sg_ref[...] = jnp.zeros_like(sg_ref)
     for n in range(6):
         sg_ref[n : n + 1] = jnp.sum(sums_here[n], axis=0, keepdims=True)
 
-    for t, k in pieces:
-        swap_dz(t, k).wait_recv()
-    for t, k in pieces:
-        swap_dz(t, k).wait_send()
-        keep_dz(t, k).wait()
-        swap_sum(t, k).wait_send()
+    def settle(p):
+        swap_dz(p).wait_recv()
+        swap_dz(p).wait_send()
+        keep_dz(p).wait()
+        swap_sum(p).wait_send()
+        for step in range(steps):
+            for way in (0, 1):
+                @pl.when(sends(step, way))
+                def _():
+                    feature(step, way, p).wait_send()
+    loop(pieces, settle)
     keep_y.wait()
     totals.wait()
     for kind in range(3):
@@ -811,29 +841,21 @@
     for slot in (0, 1):
         pass_on(0, slot).wait_send()
         pass_on(1, slot).wait_send()
-    for step in range(steps):
-        for t, k in pieces:
-            for way in (0, 1):
-                @pl.when(sends(step, way))
-                def _():
-                    feature(step, way, t, k).wait_send()
-
-
-def forward(features, weights, out_grad, count, small_params, chips, share, ident):
+
+
+def forward(features, weights, out_grad, count, small_params, chips, parts, share, ident):
     towers, _, depth = features.shape
     cols = weights.shape[2]
     keep, size = share[0]
     rows = keep + size
-    half = keep // 32 * 16
-    ranges = ((0, half), (half, keep - half), share[0])
     steps = chips - 1
     dma, vmem = pltpu.SemaphoreType.DMA, pltpu.VMEM
     bf16, f32 = jnp.bfloat16, jnp.float32
     anywhere, here = pl.BlockSpec(memory_space=pl.ANY), pl.BlockSpec(memory_space=pltpu.VMEM)
-    many = (2, steps, towers * len(ranges))
+    pieces = towers * parts
     told = jnp.broadcast_to(count.astype(f32), (8, depth))
     return pl.pallas_call(
-        functools.partial(forward_kernel, chips, share, ranges),
+        functools.partial(forward_kernel, chips, parts, share),
         out_shape=[jax.ShapeDtypeStruct((towers, rows, chips * depth), bf16),
                    jax.ShapeDtypeStruct((towers, chips * depth, 2 * cols), bf16),
                    jax.ShapeDtypeStruct((towers, rows, cols), bf16),
@@ -842,30 +864,31 @@
                    jax.ShapeDtypeStruct((4, 8, depth), f32)],
         in_specs=[anywhere] * 3 + [anywhere, here],
         out_specs=[anywhere] * 4 + [here, anywhere],
-        scratch_shapes=[vmem((4, towers, size, depth), bf16), vmem((towers, size, depth), bf16), vmem((4, towers, size, cols), bf16),
+        scratch_shapes=[vmem((4, towers, size, depth), bf16), vmem((towers, rows // parts, depth), bf16), vmem((4, towers, size, cols), bf16),
                         vmem((towers, rows, cols), bf16), vmem((2, depth, cols), f32), vmem((towers, 2, depth, cols), bf16),
                         vmem((2, rows, depth), bf16), vmem((2, depth, 2 * cols), bf16), vmem((towers, rows, 2 * cols), f32),
                         vmem((towers, rows, cols), f32), vmem((rows, cols), f32), vmem((towers, rows, cols), bf16),
                         vmem((towers, rows, cols), bf16), vmem((6, 8, cols), f32), vmem((4, 8, depth), f32),
-                        dma(many), dma(many), dma((16,)), dma((16,)), dma((3 * towers,)), dma((6,)), dma((6,)), dma((2,)),
-                        dma((3,)), dma((3,)), dma((6,)), dma((2,)), dma((2,))]
-        + [dma((towers, len(ranges)))] * 5,
+                        dma((2, steps, pieces)), dma((2, steps, pieces)), dma((16,)), dma((16,)), dma((3 * towers,)), dma((6,)), dma((6,)),
+                        dma((2,)), dma((3,)), dma((3,)), dma((7,)), dma((2,)), dma((2,))] + [dma((pieces,))] * 5,
         compiler_params=pltpu.CompilerParams(collective_id=ident, has_side_effects=True, vmem_limit_bytes=58 * 2**20),
         cost_estimate=pl.CostEstimate(flops=4 * towers * rows * cols * depth * chips, bytes_accessed=800 * 2**20, transcendentals=0),
         name="forward",
     )(features, weights, out_grad, told, small_params)
 
 
-def sum_kernel(chips, parts, share, y_ref, full_ref, dz_ref, w_ref, pg_ref, ps_ref, st_ref, d_ref, gr_ref, sr_ref,
-               given, rest, back, held, w_here, dz_here, total, d_send, d_recv, w_sem, o_sem, g_send, g_recv, s_send, s_recv, own_sem,
-               b_send, b_recv, v_send, v_recv, v_sem, y_send, y_recv, p_send, p_recv, l_sem):
+def sum_kernel(chips, parts, share, y_ref, dz_ref, w_ref, f_ref, ps_ref, st_ref, d_ref, gr_ref, sr_ref, pg_ref, relay_ref,
+               held, w_here, dz_here, total, f_part, g_part, r_part, d_send, d_recv, w_sem, o_sem, g_send, g_recv, s_send, s_recv,
+               own_sem, b_send, b_recv, v_send, v_recv, y_send, y_recv, p_send, p_recv, y_sem, q_send, q_recv, f_sem, h_sem, r_sem,
+               rs_send, rs_recv):
     dp, chip, core = place()
     towers, rows, _ = dz_ref.shape
     depth = d_ref.shape[2]
-    cols = pg_ref.shape[2] // 2
+    cols = y_ref.shape[2]
     size = rows // parts
     pieces = towers * parts
     steps = chips - 1
+    turns = steps * pieces
     across, along = dp ^ 1, dp ^ 2
     others = (across, along, dp ^ 3)
     at = lambda c, k: (c, 2 * chip + k)
@@ -873,48 +896,139 @@
     meet([(chip > 0, (dp, 2 * (chip - 1) + core)), (chip < chips - 1, (dp, 2 * (chip + 1) + core)),
           (chip >= 0, at(dp, 1 - core))] + [(chip >= 0, at(c, k)) for c in others for k in (0, 1)])
 
-    def grad(kind, k, t):
-        owner = (others + (dp,))[kind]
-        return pltpu.make_async_remote_copy(
-            src_ref=pg_ref.at[t, pl.ds(pl.multiple_of(owner * depth, 128), depth), pl.ds(pl.multiple_of((k ^ core) * cols, 128), cols)],
-            dst_ref=gr_ref.at[dp, core, t], send_sem=g_send.at[(kind * 2 + k) * 2 + t],
-            recv_sem=g_recv.at[(kind * 2 + core) * 2 + t], device_id=at(owner, k), device_id_type=MESH)
-
-    def grad_arrived(kind, k, t):
-        owner = (others + (dp,))[kind]
+    def loop(count, body):
+        def step(i, _):
+            body(i)
+            return 0
+        lax.fori_loop(0, count, step, 0)
+
+    blocks = 4 * towers
+    thirds = 3
+
+    def owner_of(m):
+        return jnp.where(m < 2, 3, jnp.where((m == 4) | (m == 5), 0, jnp.where((m == 2) | (m == 7), 1, 2)))
+
+    def third(n):
+        return pl.ds(pl.multiple_of(lax.rem(n, thirds) * (depth // thirds), 128), depth // thirds)
+
+    def f_load(n):
+        m = n // thirds
+        first = (dp ^ owner_of(m)) * depth + lax.rem(n, thirds) * (depth // thirds)
+        lanes = pl.ds(pl.multiple_of(first, 128), depth // thirds)
+        return pltpu.make_async_copy(f_ref.at[lax.rem(m, 2), :, lanes], f_part.at[lax.rem(n, 2)], f_sem.at[lax.rem(n, 2)])
+
+    def g_store(n):
+        return pltpu.make_async_copy(g_part.at[lax.rem(n, 2)], pg_ref.at[n // thirds, third(n)], h_sem.at[lax.rem(n, 2)])
+
+    def relay(m):
+        return pltpu.make_async_remote_copy(
+            src_ref=pg_ref.at[m], dst_ref=relay_ref.at[m], send_sem=rs_send.at[m], recv_sem=rs_recv.at[m],
+            device_id=at(dp ^ (m + 1), core), device_id_type=MESH)
+
+    def r_load(n):
+        return pltpu.make_async_copy(relay_ref.at[jnp.maximum(n // thirds - (blocks - 2), 0), third(n)], r_part.at[lax.rem(n, 2)],
+                                     r_sem.at[lax.rem(n, 2)])
+
+    def grad_block(m):
+        joins = m >= blocks - 2
+
+        @pl.when(joins)
+        def _():
+            relay(jnp.maximum(m - (blocks - 2), 0)).wait_recv()
+            r_load(m * thirds).start()
+
+        def part(c):
+            n = m * thirds + c
+
+            @pl.when(joins & (c + 1 < thirds))
+            def _():
+                r_load(n + 1).start()
+
+            @pl.when(n + 1 < blocks * thirds)
+            def _():
+                f_load(n + 1).start()
+            f_load(n).wait()
+
+            @pl.when((n >= 2) & (n != (blocks - 2) * thirds) & (n != (blocks - 2) * thirds + 1))
+            def _():
+                g_store(n - 2).wait()
+
+            @pl.when(joins)
+            def _():
+                r_load(n).wait()
+
+            def half(h):
+                lanes = pl.ds(pl.multiple_of(h * cols, 128), cols)
+                value = lax.dot_general(
+                    f_part[lax.rem(n, 2)], dz_here[lax.rem(m, 2), :, lanes], (((0,), (0,)), ((), ())),
+                    preferred_element_type=jnp.float32)
+
+                @pl.when(joins)
+                def _():
+                    g_part[lax.rem(n, 2), :, lanes] = (value + r_part[lax.rem(n, 2), :, lanes].astype(jnp.float32)).astype(jnp.bfloat16)
+
+                @pl.when(jnp.logical_not(joins))
+                def _():
+                    g_part[lax.rem(n, 2), :, lanes] = value.astype(jnp.bfloat16)
+            loop(2, half)
+            g_store(n).start()
+        loop(thirds, part)
+
+    def grad(m, k):
+        away = owner_of(m)
+        return pltpu.make_async_remote_copy(
+            src_ref=pg_ref.at[m, :, pl.ds(pl.multiple_of((k ^ core) * cols, 128), cols)],
+            dst_ref=gr_ref.at[away, core, lax.rem(m, 2)], send_sem=g_send.at[m, k],
+            recv_sem=g_recv.at[away, core, lax.rem(m, 2)], device_id=at(dp ^ away, k), device_id_type=MESH)
+
+    def grad_own(t):
+        return pltpu.make_async_copy(pg_ref.at[4 + t, :, pl.ds(0, cols)], gr_ref.at[0, core, t], own_sem.at[t])
+
+    def grad_start(m):
+        @pl.when(m < 2)
+        def _():
+            relay(jnp.minimum(m, 1)).start()
+
+        @pl.when(m >= 2)
+        def _():
+            for k in (0, 1):
+                @pl.when((owner_of(m) != 0) | (core != k))
+                def _():
+                    grad(m, k).start()
+
+        @pl.when(owner_of(m) == 0)
+        def _():
+            grad_own(lax.rem(m, 2)).start()
+
+    def grad_arrived(away, k, t):
+        ref = gr_ref.at[away, k, t]
         pltpu.make_async_remote_copy(
-            src_ref=gr_ref.at[owner, k, t], dst_ref=gr_ref.at[owner, k, t], send_sem=g_send.at[0],
-            recv_sem=g_recv.at[(kind * 2 + k) * 2 + t], device_id=at(dp, core), device_id_type=MESH).wait_recv()
+            src_ref=ref, dst_ref=ref, send_sem=g_send.at[2, 0], recv_sem=g_recv.at[away, k, t], device_id=at(dp, core),
+            device_id_type=MESH).wait_recv()
+
+    early, late = blocks - 2, blocks + 3
+
+    def block_at(m):
+        return jnp.where(m < early, m, m - late + early)
 
     def small(kind):
         return pltpu.make_async_remote_copy(
             src_ref=ps_ref, dst_ref=sr_ref.at[dp], send_sem=s_send.at[kind], recv_sem=s_recv.at[kind],
             device_id=at(others[kind], core), device_id_type=MESH)
 
-    keep = share[0][0]
-    width = y_ref.shape[2]
-    slots = st_ref.shape[1]
-    again = share[2][0] + share[2][1] - share[3][0]
-    bands = ((0, keep), (keep, slots - keep))
-
-    def give(kind):
-        return pltpu.make_async_remote_copy(
-            src_ref=y_ref.at[:, pl.ds(*share[0])], dst_ref=given.at[1 + kind], send_sem=v_send.at[kind],
-            recv_sem=v_recv.at[kind], device_id=at(others[kind], core), device_id_type=MESH)
+    bands = (share[0], (0, share[0][0]))
+
+    def lanes_of(shard, k):
+        return pl.ds(pl.multiple_of((2 * shard + k) * cols, 128), cols)
 
     def channels(shard, k, t, b):
-        lanes = pl.ds(pl.multiple_of((2 * shard + k) * width, 128), width)
-        return st_ref.at[t, pl.ds(*bands[b]), lanes]
-
-    def own_channels(t, b):
-        return y_ref.at[t, pl.ds(*bands[b])] if b == 0 else rest.at[t]
-
-    def along_line(step, way, t, b, shard, there):
-        n = t * 2 + b
+        return st_ref.at[t, pl.ds(*bands[b]), lanes_of(shard, k)]
+
+    def along_line(step, way, t, b, shard, there, own):
         dst = channels(shard, core, t, b)
         return pltpu.make_async_remote_copy(
-            src_ref=own_channels(t, b) if step == 0 else dst, dst_ref=dst, send_sem=y_send.at[way, step, n],
-            recv_sem=y_recv.at[way, step, n], device_id=(dp, 2 * there + core), device_id_type=MESH)
+            src_ref=y_ref.at[t, pl.ds(*bands[b])] if own else dst, dst_ref=dst, send_sem=y_send.at[way, step, b, t],
+            recv_sem=y_recv.at[way, step, b, t], device_id=(dp, 2 * there + core), device_id_type=MESH)
 
     def leaves(step, way):
         return (chip < steps) & (chip >= step) if way == 0 else (chip > 0) & (chip + step <= steps)
@@ -922,313 +1036,320 @@
     def comes(step, way):
         return chip > step if way == 0 else chip + step < steps
 
-    def leaving(step, way, t, b):
-        return along_line(step, way, t, b, chip - step if way == 0 else chip + step, chip + 1 if way == 0 else chip - 1)
+    def leaving(step, way, t, b, own=False):
+        return along_line(step, way, t, b, chip - step if way == 0 else chip + step, chip + 1 if way == 0 else chip - 1, own)
 
     def coming(step, way, t, b):
-        return along_line(step, way, t, b, chip - 1 - step if way == 0 else chip + 1 + step, chip)
+        return along_line(step, way, t, b, chip - 1 - step if way == 0 else chip + 1 + step, chip, False)
 
     def to_core(shard, t, b, own=False):
         dst = channels(shard, core, t, b)
         return pltpu.make_async_remote_copy(
-            src_ref=own_channels(t, b) if own else dst, dst_ref=dst, send_sem=p_send.at[shard, t * 2 + b],
-            recv_sem=p_recv.at[shard, t * 2 + b], device_id=at(dp, 1 - core), device_id_type=MESH)
+            src_ref=y_ref.at[t, pl.ds(*bands[b])] if own else dst, dst_ref=dst, send_sem=p_send.at[shard, b, t],
+            recv_sem=p_recv.at[shard, b, t], device_id=at(dp, 1 - core), device_id_type=MESH)
 
     def from_core(shard, t, b):
         dst = channels(shard, 1 - core, t, b)
         return pltpu.make_async_remote_copy(
-            src_ref=dst, dst_ref=dst, send_sem=p_send.at[shard, t * 2 + b], recv_sem=p_recv.at[shard, t * 2 + b],
+            src_ref=dst, dst_ref=dst, send_sem=p_send.at[shard, b, t], recv_sem=p_recv.at[shard, b, t],
             device_id=at(dp, core), device_id_type=MESH)
 
+    def share_rows(kind):
+        skip = share[2][0] + share[2][1] - share[3][0] if kind == 2 else 0
+        first, length = share[1 + kind]
+        return pl.ds(first + skip, length - skip), pl.ds(skip, length - skip)
+
+    def give(kind, shard, t, own=False):
+        to, taken = share_rows(kind)
+        src = pl.ds(share[0][0] + taken.start, taken.size)
+        return pltpu.make_async_remote_copy(
+            src_ref=y_ref.at[t, src] if own else st_ref.at[t, src, lanes_of(shard, core)], dst_ref=st_ref.at[t, to, lanes_of(shard, core)],
+            send_sem=v_send.at[kind, shard, t], recv_sem=v_recv.at[kind, shard, t], device_id=at(others[kind], core), device_id_type=MESH)
+
+    def given_to_core(kind, shard, t, k):
+        ref = st_ref.at[t, share_rows(kind)[0], lanes_of(shard, k)]
+        return pltpu.make_async_remote_copy(
+            src_ref=ref, dst_ref=ref, send_sem=q_send.at[kind, shard, t], recv_sem=q_recv.at[kind, shard, t],
+            device_id=at(dp, 1 - core), device_id_type=MESH)
+
     def pass_on(event):
-        step, t, b = event // 4, event % 4 // 2, event % 2
+        step, t = event // (2 * towers), lax.rem(event, towers)
+        for b in (0, 1):
+            @pl.when(lax.rem(event, 2 * towers) // towers == b)
+            def _():
+                for way in (0, 1):
+                    @pl.when(comes(step, way))
+                    def _():
+                        shard = chip - 1 - step if way == 0 else chip + 1 + step
+                        coming(step, way, t, b).wait_recv()
+
+                        @pl.when((step + 1 < steps) & leaves(step + 1, way))
+                        def _():
+                            leaving(jnp.minimum(step + 1, steps - 1), way, t, b).start()
+                        to_core(shard, t, b).start()
+                        if b == 0:
+                            for kind in (2, 0, 1):
+                                give(kind, shard, t).start()
+
+    ends = (chip == 0) | (chip == steps)
+    skip = size - share[0][1]
+
+    def where(piece):
+        row = pl.multiple_of(lax.rem(piece // towers + parts - 1, parts) * size, 16)
+        return lax.rem(piece, towers), pl.ds(row, size)
+
+    def passed(way):
+        return jnp.where(way == 0, chip, steps - chip)
+
+    def sends(step, way):
+        return (passed(way) < steps) & (passed(way) <= step)
+
+    def onward(way, n):
+        return jnp.where(way == 0, chip + n, chip - n)
+
+    def passing(m, way, turn):
+        t, rws = where(lax.rem(m, pieces))
+        return pltpu.make_async_remote_copy(
+            src_ref=held.at[way, turn // pieces, t, rws], dst_ref=held.at[way, m // pieces, t, rws],
+            send_sem=d_send.at[way, m], recv_sem=d_recv.at[way, m], device_id=(dp, 2 * onward(way, 1) + core), device_id_type=MESH)
+
+    def landed(m, way):
+        t, rws = where(lax.rem(m, pieces))
+        ref = held.at[way, m // pieces, t, rws]
+        pltpu.make_async_remote_copy(src_ref=ref, dst_ref=ref, send_sem=d_send.at[way, m], recv_sem=d_recv.at[way, m],
+                                     device_id=(dp, 2 * chip + core), device_id_type=MESH).wait_recv()
+
+    def product(goal, t, rws, col):
+        return lax.dot_general(dz_here[t, rws], w_here[goal, t, third(col)], (((1,), (1,)), ((), ())),
+                               preferred_element_type=jnp.float32)
+
+    def store(piece):
+        t, rws = where(piece)
+        s = lax.rem(piece, 2)
+        return pltpu.make_async_copy(total.at[s], d_ref.at[t, rws], o_sem.at[s])
+
+    def hand(kind, piece):
+        t, s = lax.rem(piece, towers), lax.rem(piece, 2)
+        to, taken = share_rows(kind)
+        return pltpu.make_async_remote_copy(
+            src_ref=total.at[s, pl.ds(skip + taken.start, taken.size)], dst_ref=d_ref.at[t, to], send_sem=b_send.at[kind, t],
+            recv_sem=b_recv.at[kind, t], device_id=at(others[kind], core), device_id_type=MESH)
+
+    def finish(piece):
+        t, rws = where(piece)
+        s = lax.rem(piece, 2)
+
+        @pl.when(piece >= 2)
+        def _():
+            store(piece - 2).wait()
+
+        @pl.when((piece >= 2) & (piece < 2 + towers))
+        def _():
+            for kind in range(3):
+                hand(kind, piece - 2).wait_send()
         for way in (0, 1):
-            @pl.when(comes(step, way))
-            def _():
-                coming(step, way, t, b).wait_recv()
-                to_core(chip - 1 - step if way == 0 else chip + 1 + step, t, b).start()
-            if step + 1 < steps:
-                @pl.when(leaves(step + 1, way))
-                def _():
-                    leaving(step + 1, way, t, b).start()
-
-    def launch(b):
-        for t in range(towers):
+            @pl.when(passed(way) > 0)
+            def _():
+                landed(turns - pieces + piece, way)
+
+        def column(col):
+            value = product(chip, t, rws, col)
+            lanes = third(col)
+            last = steps - 1
+
+            @pl.when(ends)
+            def _():
+                way = jnp.where(chip == 0, 1, 0)
+                total[s, :, lanes] = (value + held[way, last, t, rws, lanes].astype(jnp.float32)).astype(jnp.bfloat16)
+
+            @pl.when(jnp.logical_not(ends))
+            def _():
+                total[s, :, lanes] = (value + held[0, last, t, rws, lanes].astype(jnp.float32)
+                                      + held[1, last, t, rws, lanes].astype(jnp.float32)).astype(jnp.bfloat16)
+        loop(thirds, column)
+        store(piece).start()
+
+        @pl.when(piece < towers)
+        def _():
+            for kind in (2, 0, 1):
+                hand(kind, piece).start()
+
+    window = 3
+    lag = 2
+
+    def send_sum(m, way):
+        step = m // pieces
+        t, rws = where(lax.rem(m, pieces))
+        first = passed(way) == 0
+
+        @pl.when(first & (m >= window))
+        def _():
+            passing(jnp.maximum(m - window, 0), way, 0).wait_send()
+
+        @pl.when(jnp.logical_not(first))
+        def _():
+            landed(m - pieces, way)
+
+        def column(col):
+            lanes = third(col)
+            value = product(onward(way, steps - step), t, rws, col)
+
+            @pl.when(first)
+            def _():
+                held[way, step, t, rws, lanes] = value.astype(jnp.bfloat16)
+
+            @pl.when(jnp.logical_not(first))
+            def _():
+                held[way, step - 1, t, rws, lanes] = (value + held[way, step - 1, t, rws, lanes].astype(jnp.float32)).astype(jnp.bfloat16)
+        loop(thirds, column)
+        passing(m, way, jnp.where(first, m, m - pieces)).start()
+
+    def turn(m):
+        def each_way(way):
+            @pl.when((m < turns) & sends(m // pieces, way))
+            def _():
+                send_sum(m, way)
+        loop(2, each_way)
+
+        @pl.when((m == early) | (m == late + 2))
+        def _():
+            for c in (1, 2):
+                g_store(block_at(m - 1) * thirds + c).wait()
+
+        @pl.when((m < early) | (m == late) | (m == late + 1))
+        def _():
+            grad_block(block_at(m))
+
+        @pl.when(((m > 0) & (m <= early)) | (m == late + 1) | (m == late + 2))
+        def _():
+            grad_start(block_at(m - 1))
+
+        @pl.when((lax.rem(m, 2) == 1) & (m < 4 * towers * steps))
+        def _():
+            pass_on(m // 2)
+
+        @pl.when(m >= turns - pieces + lag)
+        def _():
+            finish(m - (turns - pieces + lag))
+
+    loads = [pltpu.make_async_copy(w_ref.at[:, pl.ds(n * depth, depth)], w_here.at[n], w_sem.at[n]) for n in range(chips)]
+    loads.append(pltpu.make_async_copy(dz_ref, dz_here, w_sem.at[chips]))
+    for load in reversed(loads):
+        load.start()
+    own = pltpu.make_async_copy(ps_ref, sr_ref.at[dp], own_sem.at[towers])
+    own.start()
+    f_load(jnp.int32(0)).start()
+    own_y = [pltpu.make_async_copy(y_ref.at[t, pl.ds(*bands[b])], channels(chip, core, t, b), y_sem.at[t, b])
+             for t in range(towers) for b in (0, 1)]
+    for b in (0, 1):
+        def start_y(t):
             for way in (0, 1):
                 @pl.when(leaves(0, way))
                 def _():
-                    leaving(0, way, t, b).start()
+                    leaving(0, way, t, b, True).start()
             to_core(chip, t, b, True).start()
-            pltpu.make_async_copy(own_channels(t, b), channels(chip, core, t, b), v_sem.at[1 + t * 2 + b]).start()
-
-    ends = (chip == 0, chip == chips - 1)
-
-    def target(step, way):
-        return chip + steps - step if way == 0 else chip - (steps - step)
-
-    def sends(step, way):
-        return (chip < steps) & (chip <= step) if way == 0 else (chip > 0) & (steps - chip <= step)
-
-    def where(piece):
-        return lax.rem(piece, towers), pl.multiple_of(lax.rem(piece // towers + parts - 1, parts) * size, 16)
-
-    def passing(m, way, turn):
-        t, row = where(lax.rem(m, pieces))
-        there = chip + 1 if way == 0 else chip - 1
-        rws = pl.ds(row, size)
-        return pltpu.make_async_remote_copy(
-            src_ref=held.at[way, turn // pieces, t, rws], dst_ref=held.at[way, m // pieces, t, rws],
-            send_sem=d_send.at[way, m], recv_sem=d_recv.at[way, m], device_id=(dp, 2 * there + core), device_id_type=MESH)
-
-    def landed(m, way):
-        t, row = where(lax.rem(m, pieces))
-        ref = held.at[way, m // pieces, t, pl.ds(row, size)]
-        pltpu.make_async_remote_copy(src_ref=ref, dst_ref=ref, send_sem=d_send.at[way, m], recv_sem=d_recv.at[way, m],
-                                     device_id=(dp, 2 * chip + core), device_id_type=MESH).wait_recv()
-
-    third = depth // 3 if depth % 384 == 0 else depth
-
-    def product(goal, t, row, col):
-        return lax.dot_general(dz_here[t, pl.ds(row, size)], w_here[goal, t, pl.ds(col, third)], (((1,), (1,)), ((), ())),
-                               preferred_element_type=jnp.float32)
-
-    loads = []
-    for n in range(chips):
-        loads.append(pltpu.make_async_copy(w_ref.at[:, pl.ds(n * depth, depth)], w_here.at[n], w_sem.at[n]))
-    loads.append(pltpu.make_async_copy(dz_ref, dz_here, w_sem.at[chips]))
-    for load in loads:
-        load.start()
-    own = [pltpu.make_async_copy(
-        pg_ref.at[t, pl.ds(pl.multiple_of(dp * depth, 128), depth), pl.ds(0, cols)], gr_ref.at[dp, core, t], own_sem.at[t])
-        for t in range(towers)]
-    own.append(pltpu.make_async_copy(ps_ref, sr_ref.at[dp], own_sem.at[towers]))
-    for kind in (2, 0, 1):
-        give(kind).start()
-    mine = pltpu.make_async_copy(y_ref.at[:, pl.ds(*share[0])], given.at[0], v_sem.at[0])
-    mine.start()
-    launch(0)
+            if b == 0:
+                for kind in (2, 0, 1):
+                    give(kind, chip, t, True).start()
+        loop(towers, start_y)
+    for copy in own_y:
+        copy.start()
     for kind in range(3):
         small(kind).start()
-    for t in range(towers):
-        for kind in (2, 0, 1):
-            for k in (0, 1):
-                grad(kind, k, t).start()
-        grad(3, 1 - core, t).start()
-    for copy in own:
-        copy.start()
     for load in loads:
         load.wait()
 
-    mine.wait()
-    for kind in range(3):
-        give(kind).wait_recv()
-
-    def fill(i, _):
-        for kind in range(4):
-            skip = again if kind == 3 else 0
-            place_of = (share[kind][0] if kind < 3 else share[2][0] + share[2][1]) - keep
-
-            @pl.when(i * 16 >= skip)
-            def _():
-                for t in range(towers):
-                    value = given[kind, t, pl.ds(pl.multiple_of(i * 16, 16), 16)].astype(jnp.float32) * full_ref[0]
-                    rest[t, pl.ds(pl.multiple_of(place_of - skip + i * 16, 16), 16)] = value.astype(jnp.bfloat16)
-        return 0
-
-    lax.fori_loop(0, share[0][1] // 16, fill, 0)
-    launch(1)
-
-    window = 3
-    lag = 2
-    turns = steps * pieces
-
-    def finish(piece):
-        t, row = where(piece)
-        s = lax.rem(piece, 2)
-        rws = pl.ds(row, size)
-
-        @pl.when(piece >= 2)
-        def _():
-            store(piece - 2, False)
-
-        @pl.when((piece >= 2) & (piece < 2 + towers))
-        def _():
-            for kind in range(3):
-                hand(kind, piece - 2).wait_send()
-        last = (steps - 1) * pieces + piece
-        for way in (0, 1):
-            @pl.when(jnp.logical_not(ends[way]))
-            def _():
-                landed(last, way)
-        for col in range(0, depth, third):
-            value = product(chip, t, row, col)
-            lanes = pl.ds(col, third)
-
-            @pl.when(ends[0])
-            def _():
-                total[s, :, lanes] = (value + held[1, steps - 1, t, rws, lanes].astype(jnp.float32)).astype(jnp.bfloat16)
-
-            @pl.when(ends[1])
-            def _():
-                total[s, :, lanes] = (value + held[0, steps - 1, t, rws, lanes].astype(jnp.float32)).astype(jnp.bfloat16)
-
-            @pl.when(jnp.logical_not(ends[0] | ends[1]))
-            def _():
-                total[s, :, lanes] = (value + held[0, steps - 1, t, rws, lanes].astype(jnp.float32)
-                                      + held[1, steps - 1, t, rws, lanes].astype(jnp.float32)).astype(jnp.bfloat16)
-        store(piece, True)
-
-        @pl.when(piece < towers)
-        def _():
-            for kind in (2, 0, 1):
-                hand(kind, piece).start()
-            back[0, t] = total[s, pl.ds(skip, size - skip)]
-
-    def store(piece, start):
-        t, row = where(piece)
-        s = lax.rem(piece, 2)
-        for here, length in ((piece < towers, skip), (piece >= towers, size)):
-            @pl.when(here)
-            def _():
-                copy = pltpu.make_async_copy(total.at[s, pl.ds(0, length)], d_ref.at[t, pl.ds(row, length)], o_sem.at[s])
-                (copy.start if start else copy.wait)()
-
-    skip = size - share[0][1]
-
-    def hand(kind, piece):
-        t, s = lax.rem(piece, towers), lax.rem(piece, 2)
-        return pltpu.make_async_remote_copy(
-            src_ref=total.at[s, pl.ds(skip, size - skip)], dst_ref=back.at[1 + kind, t], send_sem=b_send.at[kind, t],
-            recv_sem=b_recv.at[kind, t], device_id=at(others[kind], core), device_id_type=MESH)
-
-    def turn(m, _):
-        step, piece = m // pieces, lax.rem(m, pieces)
-        t, row = where(piece)
-        rws = pl.ds(row, size)
-        for way in (0, 1):
-            goes = (m < turns) & sends(step, way)
-
-            @pl.when(goes & ends[way])
-            def _():
-                for col in range(0, depth, third):
-                    held[way, step, t, rws, pl.ds(col, third)] = product(target(step, way), t, row, col).astype(jnp.bfloat16)
-
-                @pl.when(m >= window)
-                def _():
-                    passing(m - window, way, m - window).wait_send()
-                passing(m, way, m).start()
-
-            @pl.when(goes & jnp.logical_not(ends[way]))
-            def _():
-                landed(m - pieces, way)
-                for col in range(0, depth, third):
-                    lanes = pl.ds(col, third)
-                    held[way, step - 1, t, rws, lanes] = (
-                        product(target(step, way), t, row, col) + held[way, step - 1, t, rws, lanes].astype(jnp.float32)
-                    ).astype(jnp.bfloat16)
-                passing(m, way, m - pieces).start()
-
-        for event in range(4 * steps):
-            @pl.when(m == min(2 * event + 3, turns + lag - 1))
-            def _():
-                pass_on(event)
-
-        @pl.when(m >= turns - pieces + lag)
-        def _():
-            finish(m - (turns - pieces + lag))
-        return 0
-
-    lax.fori_loop(0, turns + lag, turn, 0)
-
-    def drain(m, _):
-        for way in (0, 1):
-            goes = sends(m // pieces, way)
-
-            @pl.when(goes & (jnp.logical_not(ends[way]) | (m >= turns - window)))
-            def _():
-                passing(m, way, m).wait_send()
-        return 0
-
-    lax.fori_loop(0, turns, drain, 0)
-    for t in range(towers):
+    loop(turns + lag, turn)
+
+    def receive_given(n):
+        shard, t = n // towers, lax.rem(n, towers)
+        for kind in range(3):
+            give(kind, shard, t).wait_recv()
+            given_to_core(kind, shard, t, core).start()
+    loop(chips * towers, receive_given)
+
+    def drain(m):
+        def each_way(way):
+            first = passed(way) == 0
+
+            @pl.when(sends(m // pieces, way) & (jnp.logical_not(first) | (m >= turns - window)))
+            def _():
+                passing(m, way, 0).wait_send()
+        loop(2, each_way)
+    loop(turns, drain)
+    for copy in own_y:
+        copy.wait()
+
+    def settle(n):
+        shard, t = n // towers, lax.rem(n, towers)
         for b in (0, 1):
-            pltpu.make_async_copy(own_channels(t, b), channels(chip, core, t, b), v_sem.at[1 + t * 2 + b]).wait()
-            for shard in range(chips):
-                from_core(shard, t, b).wait_recv()
-                to_core(shard, t, b).wait_send()
-            for step in range(steps):
+            from_core(shard, t, b).wait_recv()
+            to_core(shard, t, b).wait_send()
+
+            @pl.when(shard < steps)
+            def _():
                 for way in (0, 1):
-                    @pl.when(leaves(step, way))
+                    @pl.when(leaves(shard, way))
                     def _():
-                        leaving(step, way, t, b).wait_send()
-    for kind in range(3):
-        give(kind).wait_send()
+                        leaving(jnp.minimum(shard, steps - 1), way, t, b).wait_send()
+        for kind in range(3):
+            give(kind, shard, t).wait_send()
+            given_to_core(kind, shard, t, core).wait_send()
+            given_to_core(kind, shard, t, 1 - core).wait_recv()
+    loop(chips * towers, settle)
     for piece in (pieces - 2, pieces - 1):
-        store(piece, False)
+        store(piece).wait()
     for t in range(towers):
         for kind in range(3):
             hand(kind, t).wait_recv()
-
-    def mask(i, _):
-        rws = pl.ds(pl.multiple_of(i * 16, 16), 16)
-        for kind in range(4):
-            for t in range(towers):
-                back[kind, t, rws] = (back[kind, t, rws].astype(jnp.float32) * full_ref[0]).astype(jnp.bfloat16)
-        return 0
-
-    lax.fori_loop(0, share[0][1] // 16, mask, 0)
-    last = []
-    for kind in range(4):
-        skipped = again if kind == 3 else 0
-        first, length = share[kind][0] + skipped, share[kind][1] - skipped
-        last += [pltpu.make_async_copy(back.at[kind, t, pl.ds(skipped, length)], d_ref.at[t, pl.ds(first, length)], l_sem.at[kind, t])
-                 for t in range(towers)]
-    for copy in last:
-        copy.start()
-    for copy in last:
-        copy.wait()
-    for t in range(towers):
-        for kind in range(3):
+        for away in range(3):
             for k in (0, 1):
-                grad_arrived(kind, k, t)
-        grad_arrived(3, 1 - core, t)
+                @pl.when((away != 0) | (core != k))
+                def _():
+                    grad_arrived(away, k, t)
+        grad_own(t).wait()
+        relay(t).wait_send()
     for kind in range(3):
         small(kind).wait()
-    for t in range(towers):
-        for kind in range(3):
-            for k in (0, 1):
-                grad(kind, k, t).wait_send()
-        grad(3, 1 - core, t).wait_send()
-    for copy in own:
-        copy.wait()
-
-
-def sums(result, full, slots, wide_dz, wide_w, partial_g, partial_s, chips, parts, ident, share):
+
+    def sent(m):
+        for k in (0, 1):
+            @pl.when((owner_of(m) != 0) | (core != k))
+            def _():
+                grad(m, k).wait_send()
+    loop(blocks - 2, lambda m: sent(m + 2))
+    own.wait()
+
+
+def sums(result, slots, wide_dz, wide_w, wide_f, partial_s, chips, parts, ident, share):
     towers, rows, wide = wide_dz.shape
-    depth, cols = wide_w.shape[1] // chips, partial_g.shape[2] // 2
+    depth, cols = wide_w.shape[1] // chips, wide // 2
     steps = chips - 1
-    dma = pltpu.SemaphoreType.DMA
+    dma, vmem = pltpu.SemaphoreType.DMA, pltpu.VMEM
     bf16 = jnp.bfloat16
     anywhere = pl.BlockSpec(memory_space=pl.ANY)
+    pair = (2, steps * towers * parts)
     return pl.pallas_call(
         functools.partial(sum_kernel, chips, parts, share),
         out_shape=[jax.ShapeDtypeStruct((towers, slots, 2 * chips * cols), bf16),
                    jax.ShapeDtypeStruct((towers, slots, depth), bf16),
-                   jax.ShapeDtypeStruct((4, 2, towers, depth, cols), bf16),
-                   jax.ShapeDtypeStruct((4,) + partial_s.shape, jnp.float32)],
-        in_specs=[anywhere, pl.BlockSpec(memory_space=pltpu.SMEM)] + [anywhere] * 4,
-        out_specs=[anywhere] * 4,
-        scratch_shapes=[pltpu.VMEM((4, towers, share[0][1], cols), bf16), pltpu.VMEM((towers, slots - share[0][0], cols), bf16),
-                        pltpu.VMEM((4, towers, share[0][1], depth), bf16),
-                        pltpu.VMEM((2, steps, towers, rows, depth), bf16), pltpu.VMEM((chips, towers, depth, wide), bf16),
-                        pltpu.VMEM((towers, rows, wide), bf16), pltpu.VMEM((2, rows // parts, depth), bf16),
-                        dma((2, steps * towers * parts)), dma((2, steps * towers * parts)), dma((chips + 1,)), dma((2,)),
-                        dma((16,)), dma((16,)), dma((3,)), dma((3,)), dma((towers + 1,)), dma((3, towers)), dma((3, towers)), dma((3,)), dma((3,)), dma((5,)),
-                        dma((2, steps, 4)), dma((2, steps, 4)), dma((chips, 4)), dma((chips, 4)), dma((4, towers))],
+                   jax.ShapeDtypeStruct((3, 2, towers, depth, cols), bf16),
+                   jax.ShapeDtypeStruct((4,) + partial_s.shape, jnp.float32),
+                   jax.ShapeDtypeStruct((4 * towers, depth, wide), bf16),
+                   jax.ShapeDtypeStruct((towers, depth, wide), bf16)],
+        in_specs=[anywhere] * 5,
+        out_specs=[anywhere] * 6,
+        scratch_shapes=[vmem((2, steps, towers, rows, depth), bf16), vmem((chips, towers, depth, wide), bf16),
+                        vmem((towers, rows, wide), bf16), vmem((2, rows // parts, depth), bf16), vmem((2, rows, depth // 3), bf16),
+                        vmem((2, depth // 3, wide), bf16), vmem((2, depth // 3, wide), bf16),
+                        dma(pair), dma(pair), dma((chips + 1,)), dma((2,)), dma((4 * towers, 2)), dma((3, 2, towers)), dma((3,)), dma((3,)),
+                        dma((towers + 1,)), dma((3, towers)), dma((3, towers)), dma((3, chips, towers)), dma((3, chips, towers)),
+                        dma((2, steps, 2, towers)), dma((2, steps, 2, towers)), dma((chips, 2, towers)), dma((chips, 2, towers)),
+                        dma((towers, 2)), dma((3, chips, towers)), dma((3, chips, towers)), dma((2,)), dma((2,)), dma((2,)), dma((2,)), dma((2,))],
         compiler_params=pltpu.CompilerParams(collective_id=ident, has_side_effects=True, vmem_limit_bytes=58 * 2**20),
-        cost_estimate=pl.CostEstimate(flops=2 * towers * rows * wide * depth * chips, bytes_accessed=800 * 2**20, transcendentals=0),
+        cost_estimate=pl.CostEstimate(flops=4 * towers * rows * wide * depth * chips, bytes_accessed=800 * 2**20, transcendentals=0),
         name="sums",
-    )(result, full, wide_dz, wide_w, partial_g, partial_s)
+    )(result, wide_dz, wide_w, wide_f, partial_s)
 
 
 def small_step(small_params, small_moment_one, small_moment_two, small_average, small_grad):
@@ -1237,9 +1358,9 @@
     return first, second, fresh, ema_decay * small_average + (1.0 - ema_decay) * fresh
 
 
-def update(d_feat, stitched, parts, small_parts, states, small_states):
+def update(d_feat, stitched, full, parts, small_parts, states, small_states):
     small_grad = jnp.sum(small_parts, 0)[: small_states[0].shape[0]]
-    *fresh, stitched, d_feat = soap(parts, stitched, d_feat, *states)
+    *fresh, stitched, d_feat = soap(parts, full, stitched, d_feat, *states)
     return (stitched, d_feat) + tuple(fresh) + small_step(*small_states, small_grad)
 
 
@@ -1265,7 +1386,8 @@
     d_feat, parts, small_parts = reduce(
         partial_d.astype(jnp.bfloat16), partial_g.astype(jnp.bfloat16), small_part, cores // 2, ranges, 2
     )
-    return update(d_feat, stitched, parts, small_parts, states, small_states)
+    full = jnp.full((1,), rows, jnp.int32)
+    return update(d_feat, stitched, full, parts, small_parts, states, small_states)
 
 
 def shares(rows):
@@ -1278,12 +1400,11 @@
     rows = features.shape[1]
     keep, share = shares(rows)
     wide_f, wide_w, result, wide_dz, small_part = passed
-    full = (totals[:1] > keep).astype(jnp.float32)
-    partial_g = jnp.einsum("tri,tro->tio", wide_f, wide_dz, preferred_element_type=jnp.float32)
-    stitched, d_feat, parts, small_parts = sums(
-        result, full, rows, wide_dz, wide_w, partial_g.astype(jnp.bfloat16), small_part, lax.axis_size("mp") // 2, 4, 4, share
+    full = jnp.where(totals[:1] > keep, rows, keep)
+    stitched, d_feat, parts, small_parts, *_ = sums(
+        result, rows, wide_dz, wide_w, wide_f, small_part, lax.axis_size("mp") // 2, 4, 4, share
     )
-    return update(d_feat, stitched, parts, small_parts, states, small_states)
+    return update(d_feat, stitched, full, parts, small_parts, states, small_states)
 
 
 def line_body(
@@ -1303,7 +1424,7 @@
 ):
     keep, share = shares(features.shape[1])
     *passed, told = forward(
-        features, weights, out_grad, jnp.sum(counts), small_params, lax.axis_size("mp") // 2, share, 3
+        features, weights, out_grad, jnp.sum(counts), small_params, lax.axis_size("mp") // 2, 4, share, 3
     )
     totals = told[:, 0, 0]
     return lax.cond(

time: 674 us -> 634 us (0.941); the launches traced: 665 us -> 633 us
  matrix products: 21.5 us -> 0 us
    dot_general x1 -> x0, matrix products: 21.5 us -> none  [shared_rows(): jnp.einsum('tri,tro->tio', wide_f, wide_dz, preferred_element_type=jnp.fl...]
where the time goes in v5:
time: 634 us; the launch traced here: 633 us
  Pallas kernels  610 us (96%)
  between operations  15.4 us (2%)
    pallas_call x1, Pallas kernels, sums(): pl.pallas_call(functools.partial(sum_kernel, chips, parts, share), out_sh...  293 us
    pallas_call x1, Pallas kernels, forward(): pl.pallas_call(functools.partial(forward_kernel, chips, parts, share), ou...  247 us
    pallas_call x1, Pallas kernels, soap(): pl.pallas_call(functools.partial(soap_body, 2 - group % 2, strips), grid=...  69.5 us

profile of v5, /device:TPU:17, one launch (start us, length us, event | category | flops | bytes accessed | tf_op | source)
XLA Modules:
  0.0 632.8 jit_solution(1888089587851863785)
XLA Ops:
  7.2 1.3 reduce_sum.78
  9.1 0.6 broadcast_in_dim.4.n_ref
  9.7 0.0 copy-start.2
  9.7 0.0 copy-start.4
  9.7 0.0 copy-start.5
  9.7 0.0 copy-start.8
  9.8 0.0 copy-start.11
  9.8 247.3 %forward.1 = (bf16[2,768,4608]{2,1,0:T(8,128)(2,1)}, bf16[2,4608,1024]{2,1,0:T(8,128)(2,1)}, bf16[2,768,512]{2,1,0:T(8,128)(2,1)}, bf16[2,768,1024]{2,1,0:T(8,12...) custom-call(bf16[2,1280,1152]{2,1,0:T(8,128)(2,1)} %f_ref.1, f32[2,2304,512]{2,1,0:T(8,128)} %w_ref.1, ...), custom_call_target="tpu_custom_call" | custom-call | flops 14495514624 | bytes 838860800 | tf_op jit(solution)/shard_map/forward/pallas_call | solution.py:857
  257.1 0.8 slice_reduce_fusion
  257.9 0.6 fusion.13
  259.2 0.0 copy-done.2
  259.2 0.0 copy-done.4
  259.2 0.0 copy-done.5
  259.2 0.0 copy-done.8
  259.2 0.0 copy-done.11
  259.2 366.7 %conditional.1 = (bf16[2,1280,4096]{2,1,0:T(8,128)(2,1)}, bf16[2,1280,1152]{2,1,0:T(8,128)(2,1)}, f32[2,2304,512]{2,1,0:T(8,128)}, f32[2,2304,512]{2,1,0:T(8,128...) conditional(s32[]{:T(128)} %convert_element_type.38, ...), branch_computations={%region_2.9_spmd, %region_9.11_spmd} | conditional | flops 74991869952 | bytes 2231458816 | solution.py:1430
  259.5 292.8 %sums.1 = (bf16[2,1280,4096]{2,1,0:T(8,128)(2,1)}, bf16[2,1280,1152]{2,1,0:T(8,128)(2,1)}, bf16[3,2,2,1152,512]{4,3,2,1,0:T(8,128)(2,1)}, f32[4,8,512]{2,1,0:T(8...) custom-call(bf16[2,768,512]{2,1,0:T(8,128)(2,1)} %get-tuple-element.84.y_ref, ...), custom_call_target="tpu_custom_call" | custom-call | flops 28991029248 | bytes 838860800 | tf_op jit(solution)/shard_map/cond/branch_1_fun/sums/pallas_call | solution.py:1332
  552.4 0.9 reduce_sum.72
  553.2 0.6 add_multiply_fusion.1
  553.8 0.0 copy-start.1
  553.8 2.7 copy-done.1
  556.5 69.5 %soap.3 = (f32[2,2304,512]{2,1,0:T(8,128)}, f32[2,2304,512]{2,1,0:T(8,128)}, f32[2,2304,512]{2,1,0:T(8,128)}, f32[2,2304,512]{2,1,0:T(8,128)}, bf16[2,2304,512]{...) custom-call(s32[1]{0:T(128)S(6)} %select_n.3.full, ...), custom_call_target="tpu_custom_call" | custom-call | flops 2415919104 | bytes 136314880 | tf_op jit(solution)/shard_map/cond/branch_1_fun/soap/pallas_call | solution.py:132
Async XLA Ops:
  9.7 249.5 %copy-start.2 = (bf16[2,1280,512]{2,1,0:T(8,128)(2,1)S(1)}, bf16[2,1280,512]{2,1,0:T(8,128)(2,1)}, u32[]{:S(2)}) copy-start(bf16[2,1280,512]{2,1,0:T(8,128)(2,1)} %o_ref.1) | copy-start | bytes 7864324
  9.7 249.5 %copy-start.4 = (f32[6,512]{1,0:T(8,128)S(1)}, f32[6,512]{1,0:T(8,128)}, u32[]{:S(2)}) copy-start(f32[6,512]{1,0:T(8,128)} %sp_ref.1) | copy-start | bytes 36868
  9.7 249.5 %copy-start.5 = (f32[6,512]{1,0:T(8,128)S(1)}, f32[6,512]{1,0:T(8,128)}, u32[]{:S(2)}) copy-start(f32[6,512]{1,0:T(8,128)} %param.25) | copy-start | bytes 36868
  9.7 249.5 %copy-start.8 = (f32[6,512]{1,0:T(8,128)S(1)}, f32[6,512]{1,0:T(8,128)}, u32[]{:S(2)}) copy-start(f32[6,512]{1,0:T(8,128)} %param.26) | copy-start | bytes 36868
  9.8 249.5 %copy-start.11 = (f32[6,512]{1,0:T(8,128)S(1)}, f32[6,512]{1,0:T(8,128)}, u32[]{:S(2)}) copy-start(f32[6,512]{1,0:T(8,128)} %param.27) | copy-start | bytes 36868
  553.8 2.7 copy-start.1

commit v6 on v2

--- a/solution.py
+++ b/solution.py
@@ -1,4 +1,5 @@
 import functools
+import math
 
 import jax
 import jax.numpy as jnp
@@ -38,71 +39,112 @@
     high = v.astype(jnp.bfloat16)
     return high, (v - high.astype(jnp.float32)).astype(jnp.bfloat16)
 
-def soap_pair(grad, left, right, moment_a, moment_b):
+def soap_blocks(grads, lefts, rights, moments):
     row = lax.broadcasted_iota(jnp.int32, (2 * BLOCK, 2 * BLOCK), 0) // BLOCK
     lane = lax.broadcasted_iota(jnp.int32, (2 * BLOCK, 2 * BLOCK), 1) // BLOCK
     own = row == lane
+
     def diagonal(v):
         return jnp.where(own, jnp.concatenate([v, v], axis=0), 0.0)
+
     def beside(v):
         return jnp.concatenate([v[0], v[1]], axis=1)
-    def dot(a, b, ca, cb):
-        return lax.dot_general(a, b, (((ca,), (cb,)), ((), ())), preferred_element_type=jnp.float32)
-    right_high, right_low = split(diagonal(beside(right)))
-    left_high, left_low = split(beside(left))
-    up_high, up_low = split(left.reshape(2 * BLOCK, BLOCK))
-    def turn(v, cb):
+
+    def stationary(v, axis):
         high, low = split(v)
-        return (dot(jnp.concatenate([high, low], axis=1), jnp.concatenate([right_high, right_high], axis=cb), 1, cb)
-                + dot(high, right_low, 1, cb))
-    high, low = split(diagonal(turn(grad, 0)))
-    rotated = dot(jnp.concatenate([up_high, up_high, up_low], axis=0), jnp.concatenate([high, low, high], axis=0), 0, 0)
-    first, second, direction = adam_part(moment_a, moment_b, rotated)
-    high, low = split(diagonal(turn(direction, 1)))
-    step = dot(jnp.concatenate([left_high, left_high, left_low], axis=1), jnp.concatenate([high, low, high], axis=0), 1, 0)
-    return first, second, step
-
-def soap_body(parts, weights, moment_a, moment_b, average, left, right, first, second, new_weights, new_average, copy):
+        return jnp.concatenate([high, high, low], axis=axis)
+
+    def moving(v, axis):
+        high, low = split(v)
+        return jnp.concatenate([high, low, high], axis=axis)
+
+    def dots(a, b, ca, cb):
+        dims = (((ca,), (cb,)), ((), ()))
+        return [lax.dot_general(x, y, dims, preferred_element_type=jnp.float32) for x, y in zip(a, b)]
+
+    right = [diagonal(beside(v)) for v in rights]
+    values = dots([moving(v, 1) for v in grads], [stationary(v, 0) for v in right], 1, 0)
+    values = dots([stationary(v.reshape(2 * BLOCK, BLOCK), 0) for v in lefts], [moving(diagonal(v), 0) for v in values], 0, 0)
+    states = [adam_part(a, b, v) for (a, b), v in zip(moments, values)]
+    values = dots([moving(v[2], 1) for v in states], [stationary(v, 1) for v in right], 1, 1)
+    values = dots([stationary(beside(v), 1) for v in lefts], [moving(diagonal(v), 0) for v in values], 1, 0)
+    return [(first, second, step) for (first, second, _), step in zip(states, values)]
+
+
+def soap_body(together, strips, full, parts_a, parts_b, stitched, d_a, d_b, weights, moment_a, moment_b, average, left, right,
+              first, second, new_weights, new_average, copy, stitched_out, d_feat_out):
     groups, pairs = left.shape[1], left.shape[2] // 2
-    def strip(g, _):
-        rows = pl.ds(pl.multiple_of(g * BLOCK, BLOCK), BLOCK)
-        for q in range(pairs):
-            cols = pl.ds(2 * BLOCK * q, 2 * BLOCK)
-            at = (0, rows, cols)
-            grad = parts[(0, 0) + at].astype(jnp.float32)
-            for k in range(1, parts.shape[0]):
-                grad = grad + parts[(k, 0) + at].astype(jnp.float32)
-            one, two, step = soap_pair(grad, left[0, g, 2 * q:2 * q + 2], right[0, g, 2 * q:2 * q + 2], moment_a[at], moment_b[at])
+    length = stitched.shape[1]
+    row = jnp.minimum(pl.program_id(1) * pl.num_programs(2) + pl.program_id(2), strips - 1) * length
+
+    first_tower = pl.program_id(0) == 0
+
+    def clear(i, _):
+        rows = pl.ds(pl.multiple_of(i * 16, 16), 16)
+        wanted = row + i * 16 < full[0]
+        stitched_out[0, rows] = jnp.where(wanted, stitched[0, rows], 0)
+        d_feat_out[0, rows] = jnp.where(wanted, jnp.where(first_tower, d_a[rows], d_b[rows]), 0)
+        return 0
+
+    lax.fori_loop(0, length // 16, clear, 0)
+
+    def blocks(g, _):
+        places = [(g * together + s, q) for s in range(together) for q in range(pairs)]
+        ats = [(0, pl.ds(pl.multiple_of(r * BLOCK, BLOCK), BLOCK), pl.ds(2 * BLOCK * q, 2 * BLOCK)) for r, q in places]
+        grads = []
+        for at in ats:
+            grads.append(sum(jnp.where(first_tower, parts_a[(k,) + at], parts_b[(k,) + at]).astype(jnp.float32)
+                             for k in range(parts_a.shape[0])))
+        done = soap_blocks(grads, [left[0, r, 2 * q : 2 * q + 2] for r, q in places],
+                           [right[0, r, 2 * q : 2 * q + 2] for r, q in places], [(moment_a[at], moment_b[at]) for at in ats])
+        olds = [(weights[at], average[at]) for at in ats]
+        for at, (one, two, step), (held, mean) in zip(ats, done, olds):
             first[at] = one
             second[at] = two
-            held = weights[at]
             fresh = held - rate_main * (step + decay_weight * held)
             new_weights[at] = fresh
-            new_average[at] = ema_decay * average[at] + (1.0 - ema_decay) * fresh
+            new_average[at] = ema_decay * mean + (1.0 - ema_decay) * fresh
             copy[at] = fresh.astype(jnp.bfloat16)
         return 0
-    lax.fori_loop(0, groups, strip, 0)
-
-def soap(parts, weights, moment_a, moment_b, average, left, right, group=3):
+
+    lax.fori_loop(0, groups // together, blocks, 0)
+
+
+def soap(parts, wanted, stitched, d_feat, weights, moment_a, moment_b, average, left, right, group=6):
     towers, rows, cols = weights.shape
-    half = parts.shape[3]
+    half = parts[0].shape[2]
     steps = half // (BLOCK * group)
     flat = lambda t, p, g: (t, p * steps + g, 0)
     basis = lambda t, p, g: (t, p * steps + g, 0, 0, 0)
     state = pl.BlockSpec((1, BLOCK * group, cols), flat)
     base = pl.BlockSpec((1, group, cols // BLOCK, BLOCK, BLOCK), basis)
     full = jax.ShapeDtypeStruct(weights.shape, jnp.float32)
+    strips = max(n for n in range(1, 2 * steps + 1) if stitched.shape[1] % (16 * n) == 0)
+
+    def strip(p, g):
+        return jnp.minimum(p * steps + g, strips - 1)
+
+    def through(shape):
+        return pl.BlockSpec((1, shape[1] // strips, shape[2]), lambda t, p, g: (t, strip(p, g), 0))
+
+    def of_tower(n, shape, index, last):
+        return pl.BlockSpec(shape, lambda t, p, g: tuple(jnp.where(t == n, a, b) for a, b in zip(index(p, g), last if n == 0 else index(0, 0))))
+
+    pieces = [of_tower(n, (v.shape[0], 1, BLOCK * group, cols), lambda p, g: (0, p, g, 0), (0, 1, steps - 1, 0)) for n, v in enumerate(parts)]
+    rows_of = [of_tower(n, (v.shape[0] // strips, v.shape[1]), lambda p, g: (strip(p, g), 0), (strips - 1, 0)) for n, v in enumerate(d_feat)]
+
     return pl.pallas_call(
-        soap_body,
+        functools.partial(soap_body, 2 - group % 2, strips),
         grid=(towers, 2, steps),
-        in_specs=[pl.BlockSpec((parts.shape[0], 1, 1, BLOCK * group, cols), lambda t, p, g: (0, p, t, g, 0)),
-                  state, state, state, state, base, base],
-        out_specs=[state] * 5,
-        out_shape=[full] * 4 + [jax.ShapeDtypeStruct(weights.shape, jnp.bfloat16)],
+        in_specs=[pl.BlockSpec(memory_space=pltpu.SMEM),
+                  *pieces, through(stitched.shape), *rows_of, state, state, state, state, base, base],
+        out_specs=[state] * 5 + [through(stitched.shape), through((towers,) + d_feat[0].shape)],
+        out_shape=[full] * 4 + [jax.ShapeDtypeStruct(weights.shape, jnp.bfloat16)]
+        + [jax.ShapeDtypeStruct(v, jnp.bfloat16) for v in (stitched.shape, (towers,) + d_feat[0].shape)],
         compiler_params=pltpu.CompilerParams(vmem_limit_bytes=48 * 2**20),
         cost_estimate=pl.CostEstimate(flops=8 * 2 * towers * rows * cols * 64, bytes_accessed=130 * 2**20, transcendentals=0),
         name="soap",
-    )(parts, weights, moment_a, moment_b, average, left, right)
+    )(wanted, *parts, stitched, *d_feat, weights, moment_a, moment_b, average, left, right)
 
 
 MESH = pl.DeviceIdType.MESH
@@ -124,42 +166,44 @@
     pl.semaphore_wait(barrier, expected)
 
 
-def gather_kernel(chips, chunks, f_ref, w_ref, fg_ref, wg_ref, f_send, f_recv, w_send, w_recv, own_sem):
+def gather_kernel(chips, ranges, f_ref, w_ref, fg_ref, wg_ref, f_send, f_recv, w_send, w_recv, own_sem):
     dp, chip, core = place()
     towers, rows, depth = f_ref.shape
     cols = w_ref.shape[2]
-    part = rows // chunks
     across, along = dp ^ 1, dp ^ 2
     at = lambda c, k: (c, 2 * chip + k)
 
     meet([(chip > 0, (dp, 2 * (chip - 1) + core)), (chip < chips - 1, (dp, 2 * (chip + 1) + core)),
           (chip >= 0, at(dp, 1 - core))] + [(chip >= 0, at(c, k)) for c in (across, along) for k in (0, 1)])
 
-    def feature(step, way, t, k):
-        shard = chip - step if way == 0 else chip + step
-        there = chip + 1 if way == 0 else chip - 1
+    def copies(step, way, t, k, shard, there):
         lanes = pl.ds(pl.multiple_of(shard * depth, 128), depth)
-        rws = pl.ds(k * part, part)
-        src = f_ref.at[t, rws] if step == 0 else fg_ref.at[t, rws, lanes]
-        n = ((way * (chips - 1) + step) * towers + t) * chunks + k
+        rws = pl.ds(*ranges[k])
+        src = fg_ref.at[t, rws, lanes]
+        if step == 0:
+            src = f_ref.at[t, rws]
+        n = ((way * (chips - 1) + step) * towers + t) * len(ranges) + k
         return pltpu.make_async_remote_copy(
             src_ref=src, dst_ref=fg_ref.at[t, rws, lanes], send_sem=f_send.at[n], recv_sem=f_recv.at[n],
             device_id=(dp, 2 * there + core), device_id_type=MESH)
 
+    def feature(step, way, t, k):
+        return copies(step, way, t, k, chip - step if way == 0 else chip + step, chip + 1 if way == 0 else chip - 1)
+
+    def incoming(step, way, t, k):
+        return copies(step, way, t, k, chip - 1 - step if way == 0 else chip + 1 + step, chip)
+
     def sends(step, way):
         return (chip < chips - 1) & (chip >= step) if way == 0 else (chip > 0) & (chip + step < chips)
 
     def receives(step, way):
         return chip > step if way == 0 else chip + step < chips - 1
 
-    def incoming(step, way, t, k):
-        shard = chip - 1 - step if way == 0 else chip + 1 + step
-        lanes = pl.ds(pl.multiple_of(shard * depth, 128), depth)
-        rws = pl.ds(k * part, part)
-        n = ((way * (chips - 1) + step) * towers + t) * chunks + k
-        return pltpu.make_async_remote_copy(
-            src_ref=f_ref.at[t, rws], dst_ref=fg_ref.at[t, rws, lanes], send_sem=f_send.at[n], recv_sem=f_recv.at[n],
-            device_id=(dp, 2 * chip + core), device_id_type=MESH)
+    def launch(t, k):
+        for way in (0, 1):
+            @pl.when(sends(0, way))
+            def _():
+                feature(0, way, t, k).start()
 
     def block(owner, slot, t):
         return wg_ref.at[t, pl.ds(pl.multiple_of(owner * depth, 128), depth), pl.ds(pl.multiple_of(slot * cols, 128), cols)]
@@ -185,25 +229,22 @@
             src_ref=block(owner, slot, t), dst_ref=block(owner, slot, t), send_sem=w_send.at[n], recv_sem=w_recv.at[n],
             device_id=at(dp, core), device_id_type=MESH).wait_recv()
 
-    own = [pltpu.make_async_copy(f_ref.at[t], fg_ref.at[t, :, pl.ds(pl.multiple_of(chip * depth, 128), depth)], own_sem.at[t])
-           for t in range(towers)]
+    mine = pl.ds(pl.multiple_of(chip * depth, 128), depth)
+    own = [pltpu.make_async_copy(f_ref.at[t], fg_ref.at[t, :, mine], own_sem.at[t]) for t in range(towers)]
     own += [pltpu.make_async_copy(w_ref.at[t, pl.ds(pl.multiple_of(core * depth, 128), depth)], block(dp, 0, t), own_sem.at[2 + t])
             for t in range(towers)]
 
-    pieces = [(t, k) for t in range(towers) for k in range(chunks)]
+    pieces = [(t, k) for k in range(len(ranges)) for t in range(towers)]
     for t, k in pieces:
-        for way in (0, 1):
-            @pl.when(sends(0, way))
-            def _():
-                feature(0, way, t, k).start()
+        launch(t, k)
+    for copy in own:
+        copy.start()
     for t in (0, 1):
         for k in (0, 1):
             weight(0, k, t).start()
             weight(1, k, 1 - t).start()
     for t in (0, 1):
         weight(2, 1 - core, t).start()
-    for copy in own:
-        copy.start()
 
     for step in range(chips - 1):
         for t, k in pieces:
@@ -215,7 +256,7 @@
                     @pl.when(sends(step + 1, way))
                     def _():
                         feature(step + 1, way, t, k).start()
-            if step == 0 and (t, k) == pieces[len(pieces) // 2 - 1]:
+            if step == 0 and (t, k) == pieces[-1]:
                 for slot in (0, 1):
                     arrived(0, slot, 0)
                     forward(0, slot).start()
@@ -247,17 +288,18 @@
         copy.wait()
 
 
-def gather(features, weights_low, chips, chunks, ident):
+def gather(features, weights_low, chips, ranges, ident):
     towers, rows, depth = features.shape
     cols = weights_low.shape[2]
-    count = 2 * (chips - 1) * towers * chunks
+    count = 2 * (chips - 1) * towers * len(ranges)
     dma = pltpu.SemaphoreType.DMA
+    anywhere = pl.BlockSpec(memory_space=pl.ANY)
     return pl.pallas_call(
-        functools.partial(gather_kernel, chips, chunks),
+        functools.partial(gather_kernel, chips, ranges),
         out_shape=[jax.ShapeDtypeStruct((towers, rows, chips * depth), jnp.bfloat16),
                    jax.ShapeDtypeStruct((towers, chips * depth, 2 * cols), jnp.bfloat16)],
-        in_specs=[pl.BlockSpec(memory_space=pl.ANY)] * 2,
-        out_specs=[pl.BlockSpec(memory_space=pl.ANY)] * 2,
+        in_specs=[anywhere] * 2,
+        out_specs=[anywhere] * 2,
         scratch_shapes=[dma((count,)), dma((count,)), dma((16,)), dma((16,)), dma((4,))],
         compiler_params=pltpu.CompilerParams(collective_id=ident, has_side_effects=True),
         cost_estimate=pl.CostEstimate(flops=0, bytes_accessed=800 * 2**20, transcendentals=0),
@@ -265,14 +307,13 @@
     )(features, weights_low)
 
 
-def reduce_kernel(chips, chunks, pd_ref, pg_ref, ps_ref, d_ref, gr_ref, sr_ref, held, term, total,
+def reduce_kernel(chips, ranges, pd_ref, pg_ref, ps_ref, d_ref, gr_ref, sr_ref, held, term, total,
                   d_send, d_recv, t_sem, o_sem, g_send, g_recv, s_send, s_recv, own_sem):
     dp, chip, core = place()
     towers, rows, depth = d_ref.shape
     cols = pg_ref.shape[2] // 2
-    part = rows // chunks
     across, along = dp ^ 1, dp ^ 2
-    others = (across, along, 3 - dp)
+    others = (across, along, dp ^ 3)
     at = lambda c, k: (c, 2 * chip + k)
 
     meet([(chip > 0, (dp, 2 * (chip - 1) + core)), (chip < chips - 1, (dp, 2 * (chip + 1) + core)),
@@ -306,23 +347,23 @@
         return (chip > 0) & (chip <= step + 1) if way == 0 else (chip < chips - 1) & (chips - 1 - chip <= step + 1)
 
     def own_term(goal, t, k):
-        return pd_ref.at[t, pl.ds(k * part, part), pl.ds(pl.multiple_of(goal * depth, 128), depth)]
+        return pd_ref.at[t, pl.ds(*ranges[k]), pl.ds(pl.multiple_of(goal * depth, 128), depth)]
 
     def partial(step, way, t, k, first):
-        n = ((way * (chips - 1) + step) * towers + t) * chunks + k
-        src = own_term(target(step, way), t, k) if first else held.at[way, step - 1, t, pl.ds(k * part, part)]
+        n = ((way * (chips - 1) + step) * towers + t) * len(ranges) + k
+        src = own_term(target(step, way), t, k) if first else held.at[way, step - 1, t, pl.ds(*ranges[k])]
         there = chip + 1 if way == 0 else chip - 1
         return pltpu.make_async_remote_copy(
-            src_ref=src, dst_ref=held.at[way, step, t, pl.ds(k * part, part)], send_sem=d_send.at[n], recv_sem=d_recv.at[n],
+            src_ref=src, dst_ref=held.at[way, step, t, pl.ds(*ranges[k])], send_sem=d_send.at[n], recv_sem=d_recv.at[n],
             device_id=(dp, 2 * there + core), device_id_type=MESH)
 
     def landed(step, way, t, k):
-        n = ((way * (chips - 1) + step) * towers + t) * chunks + k
-        ref = held.at[way, step, t, pl.ds(k * part, part)]
+        n = ((way * (chips - 1) + step) * towers + t) * len(ranges) + k
+        ref = held.at[way, step, t, pl.ds(*ranges[k])]
         pltpu.make_async_remote_copy(src_ref=ref, dst_ref=ref, send_sem=d_send.at[n], recv_sem=d_recv.at[n],
                                      device_id=(dp, 2 * chip + core), device_id_type=MESH).wait_recv()
 
-    pieces = [(t, k) for t in range(towers) for k in range(chunks)]
+    pieces = [(t, k) for t in range(towers) for k in range(len(ranges))]
     ends = (chip == 0, chip == chips - 1)
     for t, k in pieces:
         for way in (0, 1):
@@ -343,7 +384,7 @@
                 grad(kind, k, t).start()
         grad(3, 1 - core, t).start()
 
-    strip = 32
+    strip = 16
 
     for step in range(1, chips - 1):
         for t, k in pieces:
@@ -354,47 +395,50 @@
 
                 @pl.when(sends(step, way) & jnp.logical_not(ends[way]))
                 def _():
-                    load = pltpu.make_async_copy(own_term(target(step, way), t, k), term.at[way], t_sem.at[way])
+                    start, size = ranges[k]
+                    load = pltpu.make_async_copy(own_term(target(step, way), t, k), term.at[way, pl.ds(0, size)], t_sem.at[way])
                     load.start()
                     landed(step - 1, way, t, k)
                     load.wait()
 
                     def add(i, _):
                         rws = pl.ds(pl.multiple_of(i * strip, strip), strip)
-                        all_rows = pl.ds(pl.multiple_of(k * part + i * strip, strip), strip)
+                        all_rows = pl.ds(pl.multiple_of(start + i * strip, strip), strip)
                         held[way, step - 1, t, all_rows] = (
                             held[way, step - 1, t, all_rows].astype(jnp.float32) + term[way, rws].astype(jnp.float32)
                         ).astype(jnp.bfloat16)
                         return 0
-                    lax.fori_loop(0, part // strip, add, 0)
+                    lax.fori_loop(0, size // strip, add, 0)
                     partial(step, way, t, k, False).start()
 
+    stores = []
     for n, (t, k) in enumerate(pieces):
         s = n % 2
-        load = pltpu.make_async_copy(own_term(chip, t, k), term.at[s], t_sem.at[s])
+        start, size = ranges[k]
+        load = pltpu.make_async_copy(own_term(chip, t, k), term.at[s, pl.ds(0, size)], t_sem.at[s])
         load.start()
         for way in (0, 1):
             @pl.when(receives(chips - 2, way))
             def _():
                 landed(chips - 2, way, t, k)
         load.wait()
-        store = pltpu.make_async_copy(total.at[s], d_ref.at[t, pl.ds(k * part, part)], o_sem.at[s])
         if n >= 2:
-            store.wait()
+            stores[n - 2].wait()
 
         def finish(i, _):
             rws = pl.ds(pl.multiple_of(i * strip, strip), strip)
-            all_rows = pl.ds(pl.multiple_of(k * part + i * strip, strip), strip)
+            all_rows = pl.ds(pl.multiple_of(start + i * strip, strip), strip)
             value = term[s, rws].astype(jnp.float32)
             for way in (0, 1):
                 here = receives(chips - 2, way)
                 value = value + jnp.where(here, held[way, chips - 2, t, all_rows].astype(jnp.float32), 0.0)
             total[s, rws] = value.astype(jnp.bfloat16)
             return 0
-        lax.fori_loop(0, part // strip, finish, 0)
-        store.start()
-    for n in range(min(2, len(pieces))):
-        pltpu.make_async_copy(total.at[n], d_ref.at[0, pl.ds(0, part)], o_sem.at[n]).wait()
+        lax.fori_loop(0, size // strip, finish, 0)
+        stores.append(pltpu.make_async_copy(total.at[s, pl.ds(0, size)], d_ref.at[t, pl.ds(start, size)], o_sem.at[s]))
+        stores[n].start()
+    for store in stores[-2:]:
+        store.wait()
 
     for t in range(towers):
         for kind in range(3):
@@ -418,21 +462,23 @@
         copy.wait()
 
 
-def reduce(partial_d, partial_g, partial_s, chips, chunks, ident):
+def reduce(partial_d, partial_g, partial_s, chips, ranges, ident):
     towers, rows, wide = partial_d.shape
     depth, cols = wide // chips, partial_g.shape[2] // 2
-    count = 2 * (chips - 1) * towers * chunks
+    count = 2 * (chips - 1) * towers * len(ranges)
+    part = max(size for _, size in ranges)
     dma = pltpu.SemaphoreType.DMA
     bf16 = jnp.bfloat16
+    out_shape = [jax.ShapeDtypeStruct((towers, rows, depth), bf16),
+                 jax.ShapeDtypeStruct((4, 2, towers, depth, cols), bf16),
+                 jax.ShapeDtypeStruct((4,) + partial_s.shape, jnp.float32)]
     return pl.pallas_call(
-        functools.partial(reduce_kernel, chips, chunks),
-        out_shape=[jax.ShapeDtypeStruct((towers, rows, depth), bf16),
-                   jax.ShapeDtypeStruct((4, 2, towers, depth, cols), bf16),
-                   jax.ShapeDtypeStruct((4,) + partial_s.shape, jnp.float32)],
+        functools.partial(reduce_kernel, chips, ranges),
+        out_shape=out_shape,
         in_specs=[pl.BlockSpec(memory_space=pl.ANY)] * 3,
-        out_specs=[pl.BlockSpec(memory_space=pl.ANY)] * 3,
+        out_specs=[pl.BlockSpec(memory_space=pl.ANY)] * len(out_shape),
         scratch_shapes=[pltpu.VMEM((2, chips - 1, towers, rows, depth), bf16),
-                        pltpu.VMEM((2, rows // chunks, depth), bf16), pltpu.VMEM((2, rows // chunks, depth), bf16),
+                        pltpu.VMEM((2, part, depth), bf16), pltpu.VMEM((2, part, depth), bf16),
                         dma((count,)), dma((count,)), dma((2,)), dma((2,)), dma((16,)), dma((16,)), dma((3,)), dma((3,)), dma((towers + 1,))],
         compiler_params=pltpu.CompilerParams(collective_id=ident, has_side_effects=True, vmem_limit_bytes=56 * 2**20),
         cost_estimate=pl.CostEstimate(flops=0, bytes_accessed=800 * 2**20, transcendentals=0),
@@ -440,10 +486,1127 @@
     )(partial_d, partial_g, partial_s)
 
 
+def loop(count, body):
+    def step(i, _):
+        body(i)
+        return 0
+    lax.fori_loop(0, count, step, 0)
+
+
+def wait_for(ref, sem, other):
+    pltpu.make_async_remote_copy(src_ref=ref, dst_ref=ref, send_sem=other, recv_sem=sem, device_id=dict(dp=0, mp=0),
+                                 device_id_type=MESH).wait_recv()
+
+
+class Spot:
+    def __init__(self, chips):
+        self.dp, self.chip, self.core = place()
+        self.chips, self.steps = chips, chips - 1
+        self.others = (self.dp ^ 1, self.dp ^ 2, self.dp ^ 3)
+        self.ends = (self.chip == 0) | (self.chip == self.steps)
+
+    def at(self, dp, core):
+        return dp, 2 * self.chip + core
+
+    def on_line(self, chip):
+        return self.dp, 2 * chip + self.core
+
+    def passed(self, way):
+        return jnp.where(way == 0, self.chip, self.steps - self.chip)
+
+    def onward(self, way, n):
+        return jnp.where(way == 0, self.chip + n, self.chip - n)
+
+    def leaves(self, step, way):
+        return (self.passed(way) < self.steps) & (self.passed(way) >= step)
+
+    def comes(self, step, way):
+        return self.passed(way) > step
+
+    def greet(self):
+        meet([(self.chip > 0, self.on_line(self.chip - 1)), (self.chip < self.steps, self.on_line(self.chip + 1)),
+              (self.chip >= 0, self.at(self.dp, 1 - self.core))]
+             + [(self.chip >= 0, self.at(c, k)) for c in self.others for k in (0, 1)])
+
+
+class Features:
+    def __init__(self, spot, f_ref, taken, fg, size, send, recv):
+        self.spot, self.f_ref, self.taken, self.fg, self.size, self.send, self.recv = spot, f_ref, taken, fg, size, send, recv
+        self.depth = f_ref.shape[1]
+
+    def rows(self, q):
+        return pl.ds(pl.multiple_of(q * self.size, 16), self.size)
+
+    def lanes(self, shard):
+        return pl.ds(pl.multiple_of(shard * self.depth, 128), self.depth)
+
+    def copy(self, step, way, q, src=None):
+        ref = self.fg.at[self.rows(q), self.lanes(self.spot.onward(way, -step))]
+        return pltpu.make_async_remote_copy(
+            src_ref=ref if src is None else src, dst_ref=ref, send_sem=self.send.at[way, step, q], recv_sem=self.recv.at[way, step, q],
+            device_id=self.spot.on_line(self.spot.onward(way, 1)), device_id_type=MESH)
+
+    def launch(self, q, last):
+        def each(way):
+            @pl.when(self.spot.leaves(0, way))
+            def _():
+                self.copy(0, way, q, self.taken if last else self.f_ref.at[self.rows(q)]).start()
+        loop(2, each)
+
+    def arrive(self, step, q):
+        def each(way):
+            @pl.when(self.spot.comes(step, way))
+            def _():
+                ref = self.fg.at[self.rows(q), self.lanes(self.spot.onward(way, -1 - step))]
+                wait_for(ref, self.recv.at[way, step, q], self.send.at[way, step, q])
+        loop(2, each)
+
+    def serve(self, step, q):
+        self.arrive(step, q)
+
+        def each(way):
+            @pl.when(self.spot.leaves(step + 1, way))
+            def _():
+                self.copy(step + 1, way, q).start()
+        loop(2, each)
+
+    def settle(self, q):
+        for step in range(self.spot.steps):
+            def each(way):
+                @pl.when(self.spot.leaves(step, way))
+                def _():
+                    self.copy(step, way, q).wait_send()
+            loop(2, each)
+
+
+class Weights:
+    def __init__(self, spot, w_ref, wide, low, wg, wide_sem, own_sem, send, recv):
+        self.spot, self.w_ref, self.wide, self.low, self.wg = spot, w_ref, wide, low, wg
+        self.wide_sem, self.own_sem, self.send, self.recv = wide_sem, own_sem, send, recv
+        self.depth, self.cols = low.shape[1], low.shape[2]
+
+    def block(self, owner, slot):
+        return self.wg.at[pl.ds(pl.multiple_of(owner * self.depth, 128), self.depth), pl.ds(pl.multiple_of(slot * self.cols, 128), self.cols)]
+
+    def round(self):
+        part = self.wide.shape[1]
+        parts = self.depth // part
+
+        def load(n):
+            return pltpu.make_async_copy(self.w_ref.at[pl.ds(pl.multiple_of(n * part, 16), part)], self.wide.at[lax.rem(n, 2)],
+                                         self.wide_sem.at[lax.rem(n, 2)])
+
+        def one(n):
+            @pl.when(n + 1 < 2 * parts)
+            def _():
+                load(n + 1).start()
+            load(n).wait()
+
+            def strip(i):
+                rows = pl.ds(pl.multiple_of(i * 32, 32), 32)
+                to = pl.ds(pl.multiple_of(lax.rem(n, parts) * part + i * 32, 32), 32)
+                self.low[n // parts, to] = self.wide[lax.rem(n, 2), rows].astype(jnp.bfloat16)
+            loop(part // 32, strip)
+        load(jnp.int32(0)).start()
+        loop(2 * parts, one)
+
+    def send_own(self, kind, slot):
+        s = self.spot
+        k = s.core ^ slot
+        return pltpu.make_async_remote_copy(
+            src_ref=self.low.at[k], dst_ref=self.block(s.dp, slot), send_sem=self.send.at[kind, slot], recv_sem=self.recv.at[kind, slot],
+            device_id=s.at((s.others[0], s.others[1], s.dp)[kind], k), device_id_type=MESH)
+
+    def send_on(self, kind):
+        s = self.spot
+        ref = self.block(s.others[kind], kind)
+        return pltpu.make_async_remote_copy(
+            src_ref=ref, dst_ref=ref, send_sem=self.send.at[3, kind], recv_sem=self.recv.at[3, kind],
+            device_id=s.at(s.others[1 - kind], s.core), device_id_type=MESH)
+
+    def arrive(self, kind, slot):
+        owner = (self.spot.others[0], self.spot.others[1], self.spot.dp)[kind]
+        wait_for(self.block(owner, slot), self.recv.at[kind, slot], self.send.at[kind, slot])
+
+    def own(self):
+        return pltpu.make_async_copy(self.low.at[self.spot.core], self.block(self.spot.dp, 0), self.own_sem)
+
+    def start(self):
+        self.own().start()
+        for slot in (0, 1):
+            self.send_own(0, slot).start()
+            self.send_own(1, 1 - slot).start()
+        self.send_own(2, 1).start()
+
+    def relay(self):
+        for kind in (0, 1):
+            self.arrive(kind, kind)
+            self.send_on(kind).start()
+
+    def finish(self):
+        for kind in (0, 1):
+            self.arrive(kind, 1 - kind)
+            wait_for(self.block(self.spot.others[2], kind), self.recv.at[3, kind], self.send.at[3, kind])
+        self.arrive(2, 1)
+        self.own().wait()
+
+    def settle(self):
+        for kind in (0, 1):
+            for slot in (0, 1):
+                self.send_own(kind, slot).wait_send()
+            self.send_on(kind).wait_send()
+        self.send_own(2, 1).wait_send()
+
+
+class Products:
+    def __init__(self, spot, features, wg, f_tile, w_tile, acc, theirs, f_sem, w_sem, send, recv):
+        self.spot, self.features, self.wg, self.f_tile, self.w_tile, self.acc, self.theirs = spot, features, wg, f_tile, w_tile, acc, theirs
+        self.f_sem, self.w_sem, self.send, self.recv = f_sem, w_sem, send, recv
+        self.cols = theirs.shape[1]
+
+    def shard(self, j):
+        return jnp.where(self.spot.chip == self.spot.steps, self.spot.steps - j, j)
+
+    def load_w(self, j):
+        depth = self.features.depth
+        rows = pl.ds(pl.multiple_of(self.shard(j) * depth, 128), depth)
+        return pltpu.make_async_copy(self.wg.at[rows], self.w_tile.at[lax.rem(j, 2)], self.w_sem.at[lax.rem(j, 2)])
+
+    def load_f(self, j):
+        lanes = self.features.lanes(self.shard(j))
+        return pltpu.make_async_copy(self.features.fg.at[:, lanes], self.f_tile.at[lax.rem(j, 2)], self.f_sem.at[lax.rem(j, 2)])
+
+    def here(self, j):
+        return (j < self.spot.steps) | jnp.logical_not(self.spot.ends)
+
+    def add(self, slot, rows):
+        for col in range(0, 2 * self.cols, self.cols):
+            lanes = pl.ds(col, self.cols)
+            self.acc[rows, lanes] += jnp.dot(self.f_tile[slot, rows], self.w_tile[slot, :, lanes], preferred_element_type=jnp.float32)
+
+    def multiply(self):
+        def unit(j):
+            @pl.when(j < self.spot.steps)
+            def _():
+                self.load_w(j + 1).start()
+
+            @pl.when((j < self.spot.steps) & self.here(j + 1))
+            def _():
+                self.load_f(j + 1).start()
+            self.load_w(j).wait()
+
+            @pl.when(self.here(j))
+            def _():
+                self.load_f(j).wait()
+                loop(self.acc.shape[0] // self.features.size, lambda q: self.add(lax.rem(j, 2), self.features.rows(q)))
+        self.load_w(jnp.int32(0)).start()
+        self.load_f(jnp.int32(0)).start()
+        loop(self.spot.chips, unit)
+
+    def swap(self, q):
+        rows = self.features.rows(q)
+        return pltpu.make_async_remote_copy(
+            src_ref=self.acc.at[rows, pl.ds(self.cols, self.cols)], dst_ref=self.theirs.at[rows], send_sem=self.send.at[q],
+            recv_sem=self.recv.at[q], device_id=self.spot.at(self.spot.dp, 1 - self.spot.core), device_id_type=MESH)
+
+    def complete(self, q):
+        slot = self.spot.steps % 2
+        self.features.arrive(self.spot.steps - 1, q)
+
+        @pl.when(self.spot.ends)
+        def _():
+            rows = self.features.rows(q)
+            copy = pltpu.make_async_copy(self.features.fg.at[rows, self.features.lanes(self.shard(self.spot.steps))],
+                                         self.f_tile.at[slot, rows], self.f_sem.at[slot])
+            copy.start()
+            copy.wait()
+            self.add(slot, rows)
+        self.swap(q).start()
+
+
+class Backward:
+    def __init__(self, spot, size, dz_here, dz_ref, send, recv, out_sem):
+        self.spot, self.size, self.dz_here, self.dz_ref, self.send, self.recv, self.out_sem = spot, size, dz_here, dz_ref, send, recv, out_sem
+        self.cols = dz_here.shape[1]
+
+    def rows(self, q):
+        return pl.ds(pl.multiple_of(q * self.size, 16), self.size)
+
+    def swap(self, q):
+        return pltpu.make_async_remote_copy(
+            src_ref=self.dz_here.at[self.rows(q)], dst_ref=self.dz_ref.at[self.rows(q), pl.ds(self.cols, self.cols)],
+            send_sem=self.send.at[q], recv_sem=self.recv.at[q], device_id=self.spot.at(self.spot.dp, 1 - self.spot.core), device_id_type=MESH)
+
+    def keep(self, q):
+        return pltpu.make_async_copy(self.dz_here.at[self.rows(q)], self.dz_ref.at[self.rows(q), pl.ds(0, self.cols)], self.out_sem.at[q])
+
+    def start(self, q):
+        self.swap(q).start()
+        self.keep(q).start()
+
+    def settle(self, q):
+        self.swap(q).wait_recv()
+        self.swap(q).wait_send()
+        self.keep(q).wait()
+
+
+def gelu_and_slope(v):
+    factor, cubic = math.sqrt(2.0 / math.pi), 0.044715
+    square = v * v
+    th = jnp.tanh(factor * (v + cubic * (square * v)))
+    slope = 0.5 * (1.0 + th) + 0.5 * v * (1.0 - th * th) * (factor * (1.0 + 3.0 * cubic * square))
+    return 0.5 * v * (1.0 + th), slope
+
+
+def live_rows_of(tot, share, live):
+    keep = share[0][0]
+    cols = live.shape[1]
+
+    def strip(i):
+        row = lax.broadcasted_iota(jnp.int32, (16, cols), 0).astype(jnp.float32) + (i * 16).astype(jnp.float32)
+        here = jnp.where(row < tot[0, :1, :cols], 1.0, 0.0)
+        there = jnp.zeros_like(here)
+        for kind in range(4):
+            count = tot[kind, :1, :cols]
+            slot = row + float(share[kind][0] - keep)
+            valid = (slot < count) & (count > keep)
+            if kind == 3:
+                valid = valid & (slot >= share[2][0] + share[2][1])
+            there = there + jnp.where(valid, 1.0, 0.0)
+        live[pl.ds(pl.multiple_of(i * 16, 16), 16)] = jnp.where(row < keep, here, there)
+    loop(live.shape[0] // 16, strip)
+
+
+def clear(ref):
+    def strip(i):
+        ref[pl.ds(pl.multiple_of(i * 16, 16), 16)] = jnp.zeros((16, ref.shape[1]), ref.dtype)
+    loop(ref.shape[0] // 16, strip)
+
+
+def fold(term):
+    return term[:8] + term[8:]
+
+
+class Grads:
+    jobs, thirds = 8, 3
+
+    def __init__(self, spot, fg, dz_here, gr, pg, relay, f_part, g_part, r_part, f_sem, g_sem, r_sem, send, recv, relay_send, relay_recv, own_sem):
+        self.spot, self.fg, self.dz_here, self.gr, self.pg, self.relay_ref = spot, fg, dz_here, gr, pg, relay
+        self.f_part, self.g_part, self.r_part, self.f_sem, self.g_sem, self.r_sem = f_part, g_part, r_part, f_sem, g_sem, r_sem
+        self.send, self.recv, self.relay_send, self.relay_recv, self.own_sem = send, recv, relay_send, relay_recv, own_sem
+        self.depth, self.cols = pg.shape[1], pg.shape[2]
+        self.part = self.depth // self.thirds
+
+    def owner_of(self, m):
+        return jnp.where(m < 2, 3, jnp.where((m == 4) | (m == 5), 0, jnp.where((m == 2) | (m == 7), 1, 2)))
+
+    def third(self, n):
+        return pl.ds(pl.multiple_of(lax.rem(n, self.thirds) * self.part, 128), self.part)
+
+    def load(self, n):
+        first = (self.spot.dp ^ self.owner_of(n // self.thirds)) * self.depth + lax.rem(n, self.thirds) * self.part
+        return pltpu.make_async_copy(self.fg.at[:, pl.ds(pl.multiple_of(first, 128), self.part)], self.f_part.at[lax.rem(n, 2)],
+                                     self.f_sem.at[lax.rem(n, 2)])
+
+    def store(self, n):
+        return pltpu.make_async_copy(self.g_part.at[lax.rem(n, 2)], self.pg.at[n // self.thirds, self.third(n)], self.g_sem.at[lax.rem(n, 2)])
+
+    def relay(self, m):
+        return pltpu.make_async_remote_copy(
+            src_ref=self.pg.at[m], dst_ref=self.relay_ref.at[m], send_sem=self.relay_send.at[m], recv_sem=self.relay_recv.at[m],
+            device_id=self.spot.at(self.spot.dp ^ (m + 1), self.spot.core), device_id_type=MESH)
+
+    def relayed(self, n):
+        return pltpu.make_async_copy(self.relay_ref.at[jnp.maximum(n // self.thirds - (self.jobs - 2), 0), self.third(n)],
+                                     self.r_part.at[lax.rem(n, 2)], self.r_sem.at[lax.rem(n, 2)])
+
+    def job(self, m):
+        joins = m >= self.jobs - 2
+        lanes = pl.ds(pl.multiple_of(lax.rem(m, 2) * self.cols, 128), self.cols)
+
+        @pl.when(joins)
+        def _():
+            k = jnp.maximum(m - (self.jobs - 2), 0)
+            wait_for(self.relay_ref.at[k], self.relay_recv.at[k], self.relay_send.at[k])
+            self.relayed(m * self.thirds).start()
+
+        def part(c):
+            n = m * self.thirds + c
+
+            @pl.when(joins & (c + 1 < self.thirds))
+            def _():
+                self.relayed(n + 1).start()
+
+            @pl.when(n + 1 < self.jobs * self.thirds)
+            def _():
+                self.load(n + 1).start()
+            self.load(n).wait()
+
+            @pl.when((n >= 2) & (n != (self.jobs - 2) * self.thirds) & (n != (self.jobs - 2) * self.thirds + 1))
+            def _():
+                self.store(n - 2).wait()
+
+            @pl.when(joins)
+            def _():
+                self.relayed(n).wait()
+            value = lax.dot_general(self.f_part[lax.rem(n, 2)], self.dz_here[:, lanes], (((0,), (0,)), ((), ())),
+                                    preferred_element_type=jnp.float32)
+
+            @pl.when(joins)
+            def _():
+                self.g_part[lax.rem(n, 2)] = (value + self.r_part[lax.rem(n, 2)].astype(jnp.float32)).astype(jnp.bfloat16)
+
+            @pl.when(jnp.logical_not(joins))
+            def _():
+                self.g_part[lax.rem(n, 2)] = value.astype(jnp.bfloat16)
+            self.store(n).start()
+        loop(self.thirds, part)
+
+    def copy(self, m):
+        away, k = self.owner_of(m), self.spot.core ^ lax.rem(m, 2)
+        return pltpu.make_async_remote_copy(
+            src_ref=self.pg.at[m], dst_ref=self.gr.at[away, self.spot.core], send_sem=self.send.at[m],
+            recv_sem=self.recv.at[away, self.spot.core], device_id=self.spot.at(self.spot.dp ^ away, k), device_id_type=MESH)
+
+    def own(self):
+        return pltpu.make_async_copy(self.pg.at[4], self.gr.at[0, self.spot.core], self.own_sem)
+
+    def start(self, m):
+        @pl.when(m < 2)
+        def _():
+            self.relay(jnp.minimum(m, 1)).start()
+
+        @pl.when((m >= 2) & (m != 4))
+        def _():
+            self.copy(m).start()
+
+        @pl.when(m == 4)
+        def _():
+            self.own().start()
+
+    def turn(self, m, late):
+        early = self.jobs - 2
+
+        def job_at(m):
+            return jnp.where(m < early, m, m - late + early)
+
+        @pl.when((m == early) | (m == late + 2))
+        def _():
+            for c in (1, 2):
+                self.store(job_at(m - 1) * self.thirds + c).wait()
+
+        @pl.when((m < early) | (m == late) | (m == late + 1))
+        def _():
+            self.job(job_at(m))
+
+        @pl.when(((m > 0) & (m <= early)) | (m == late + 1) | (m == late + 2))
+        def _():
+            self.start(job_at(m - 1))
+
+    def settle(self):
+        for away in range(3):
+            for k in (0, 1):
+                @pl.when((away != 0) | (self.spot.core != k))
+                def _():
+                    wait_for(self.gr.at[away, k], self.recv.at[away, k], self.send.at[2])
+        self.own().wait()
+        for m in range(self.jobs):
+            if m < 2:
+                self.relay(m).wait_send()
+            elif m != 4:
+                self.copy(jnp.int32(m)).wait_send()
+
+
+class Sums:
+    window, lag = 3, 2
+
+    def __init__(self, spot, parts, share, d_ref, dz_here, w_here, held, total, send, recv, out_sem, back_send, back_recv):
+        self.spot, self.parts, self.share, self.d_ref, self.dz_here, self.w_here, self.held, self.total = spot, parts, share, d_ref, dz_here, w_here, held, total
+        self.send, self.recv, self.out_sem, self.back_send, self.back_recv = send, recv, out_sem, back_send, back_recv
+        self.size, self.depth = total.shape[1], total.shape[2]
+        self.turns = spot.steps * parts
+        self.skip = self.size - share[0][1]
+
+    def rows(self, piece):
+        return pl.ds(pl.multiple_of(lax.rem(piece + self.parts - 1, self.parts) * self.size, 16), self.size)
+
+    def third(self, n):
+        return pl.ds(pl.multiple_of(n * (self.depth // 3), 128), self.depth // 3)
+
+    def sends(self, step, way):
+        return (self.spot.passed(way) < self.spot.steps) & (self.spot.passed(way) <= step)
+
+    def passing(self, m, way, turn):
+        rows = self.rows(lax.rem(m, self.parts))
+        return pltpu.make_async_remote_copy(
+            src_ref=self.held.at[way, turn // self.parts, rows], dst_ref=self.held.at[way, m // self.parts, rows],
+            send_sem=self.send.at[way, m], recv_sem=self.recv.at[way, m], device_id=self.spot.on_line(self.spot.onward(way, 1)),
+            device_id_type=MESH)
+
+    def landed(self, m, way):
+        wait_for(self.held.at[way, m // self.parts, self.rows(lax.rem(m, self.parts))], self.recv.at[way, m], self.send.at[way, m])
+
+    def product(self, goal, rows, col):
+        return lax.dot_general(self.dz_here[rows], self.w_here[goal, self.third(col)], (((1,), (1,)), ((), ())),
+                               preferred_element_type=jnp.float32)
+
+    def store(self, piece):
+        s = lax.rem(piece, 2)
+        return pltpu.make_async_copy(self.total.at[s], self.d_ref.at[self.rows(piece)], self.out_sem.at[s])
+
+    def hand(self, kind):
+        to, taken = share_rows(self.share, kind)
+        return pltpu.make_async_remote_copy(
+            src_ref=self.total.at[0, pl.ds(self.skip + taken.start, taken.size)], dst_ref=self.d_ref.at[to], send_sem=self.back_send.at[kind],
+            recv_sem=self.back_recv.at[kind], device_id=self.spot.at(self.spot.others[kind], self.spot.core), device_id_type=MESH)
+
+    def send_sum(self, m, way):
+        step, rows = m // self.parts, self.rows(lax.rem(m, self.parts))
+        first = self.spot.passed(way) == 0
+        held = self.held
+
+        @pl.when(first & (m >= self.window))
+        def _():
+            self.passing(jnp.maximum(m - self.window, 0), way, 0).wait_send()
+
+        @pl.when(jnp.logical_not(first))
+        def _():
+            self.landed(m - self.parts, way)
+
+        def column(col):
+            lanes = self.third(col)
+            value = self.product(self.spot.onward(way, self.spot.steps - step), rows, col)
+
+            @pl.when(first)
+            def _():
+                held[way, step, rows, lanes] = value.astype(jnp.bfloat16)
+
+            @pl.when(jnp.logical_not(first))
+            def _():
+                held[way, step - 1, rows, lanes] = (value + held[way, step - 1, rows, lanes].astype(jnp.float32)).astype(jnp.bfloat16)
+        loop(3, column)
+        self.passing(m, way, jnp.where(first, m, m - self.parts)).start()
+
+    def finish(self, piece):
+        rows, s = self.rows(piece), lax.rem(piece, 2)
+        held, total, last = self.held, self.total, self.spot.steps - 1
+
+        @pl.when(piece >= 2)
+        def _():
+            self.store(piece - 2).wait()
+
+        @pl.when(piece == 2)
+        def _():
+            for kind in range(3):
+                self.hand(kind).wait_send()
+
+        def each(way):
+            @pl.when(self.spot.passed(way) > 0)
+            def _():
+                self.landed(self.turns - self.parts + piece, way)
+        loop(2, each)
+
+        def column(col):
+            value = self.product(self.spot.chip, rows, col)
+            lanes = self.third(col)
+
+            @pl.when(self.spot.ends)
+            def _():
+                way = jnp.where(self.spot.chip == 0, 1, 0)
+                total[s, :, lanes] = (value + held[way, last, rows, lanes].astype(jnp.float32)).astype(jnp.bfloat16)
+
+            @pl.when(jnp.logical_not(self.spot.ends))
+            def _():
+                total[s, :, lanes] = (value + held[0, last, rows, lanes].astype(jnp.float32)
+                                      + held[1, last, rows, lanes].astype(jnp.float32)).astype(jnp.bfloat16)
+        loop(3, column)
+        self.store(piece).start()
+
+        @pl.when(piece == 0)
+        def _():
+            for kind in (2, 0, 1):
+                self.hand(kind).start()
+
+    def turn(self, m):
+        def each(way):
+            @pl.when((m < self.turns) & self.sends(m // self.parts, way))
+            def _():
+                self.send_sum(m, way)
+        loop(2, each)
+
+    def turn_end(self, m):
+        first = self.turns - self.parts + self.lag
+
+        @pl.when((m >= first) & (m < first + self.parts))
+        def _():
+            self.finish(m - first)
+
+    def settle(self):
+        def drain(m):
+            def each(way):
+                first = self.spot.passed(way) == 0
+
+                @pl.when(self.sends(m // self.parts, way) & (jnp.logical_not(first) | (m >= self.turns - self.window)))
+                def _():
+                    self.passing(m, way, 0).wait_send()
+            loop(2, each)
+        loop(self.turns, drain)
+        for piece in (self.parts - 2, self.parts - 1):
+            self.store(piece).wait()
+        for kind in range(3):
+            self.hand(kind).wait_recv()
+
+
+def share_rows(share, kind):
+    skip = share[2][0] + share[2][1] - share[3][0] if kind == 2 else 0
+    first, length = share[1 + kind]
+    return pl.ds(first + skip, length - skip), pl.ds(skip, length - skip)
+
+
+class Stitched:
+    def __init__(self, spot, share, y_ref, st_ref, y_send, y_recv, core_send, core_recv, give_send, give_recv, given_send, given_recv, own_sem):
+        self.spot, self.share, self.y_ref, self.st_ref = spot, share, y_ref, st_ref
+        self.y_send, self.y_recv, self.core_send, self.core_recv = y_send, y_recv, core_send, core_recv
+        self.give_send, self.give_recv, self.given_send, self.given_recv, self.own_sem = give_send, give_recv, given_send, given_recv, own_sem
+        self.towers, self.cols = y_ref.shape[0], y_ref.shape[2]
+        self.bands = (share[0], (0, share[0][0]))
+        self.events = 2 * self.towers * spot.steps
+
+    def lanes(self, shard, k):
+        return pl.ds(pl.multiple_of((2 * shard + k) * self.cols, 128), self.cols)
+
+    def place(self, shard, k, t, b):
+        return self.st_ref.at[t, pl.ds(*self.bands[b]), self.lanes(shard, k)]
+
+    def source(self, t, b):
+        return self.y_ref.at[t, pl.ds(*self.bands[b])]
+
+    def leave(self, step, way, t, b, own=False):
+        s = self.spot
+        dst = self.place(s.onward(way, -step), s.core, t, b)
+        return pltpu.make_async_remote_copy(
+            src_ref=self.source(t, b) if own else dst, dst_ref=dst, send_sem=self.y_send.at[way, step, b, t],
+            recv_sem=self.y_recv.at[way, step, b, t], device_id=s.on_line(s.onward(way, 1)), device_id_type=MESH)
+
+    def to_core(self, shard, t, b, own=False):
+        s = self.spot
+        dst = self.place(shard, s.core, t, b)
+        return pltpu.make_async_remote_copy(
+            src_ref=self.source(t, b) if own else dst, dst_ref=dst, send_sem=self.core_send.at[shard, b, t],
+            recv_sem=self.core_recv.at[shard, b, t], device_id=s.at(s.dp, 1 - s.core), device_id_type=MESH)
+
+    def give(self, kind, shard, t, own=False):
+        s = self.spot
+        to, taken = share_rows(self.share, kind)
+        src = pl.ds(self.share[0][0] + taken.start, taken.size)
+        return pltpu.make_async_remote_copy(
+            src_ref=self.y_ref.at[t, src] if own else self.st_ref.at[t, src, self.lanes(shard, s.core)],
+            dst_ref=self.st_ref.at[t, to, self.lanes(shard, s.core)], send_sem=self.give_send.at[kind, shard, t],
+            recv_sem=self.give_recv.at[kind, shard, t], device_id=s.at(s.others[kind], s.core), device_id_type=MESH)
+
+    def given_place(self, kind, shard, t, k):
+        return self.st_ref.at[t, share_rows(self.share, kind)[0], self.lanes(shard, k)]
+
+    def given(self, kind, shard, t):
+        s = self.spot
+        ref = self.given_place(kind, shard, t, s.core)
+        return pltpu.make_async_remote_copy(
+            src_ref=ref, dst_ref=ref, send_sem=self.given_send.at[kind, shard, t], recv_sem=self.given_recv.at[kind, shard, t],
+            device_id=s.at(s.dp, 1 - s.core), device_id_type=MESH)
+
+    def own(self, t, b):
+        return pltpu.make_async_copy(self.source(t, b), self.place(self.spot.chip, self.spot.core, t, b), self.own_sem.at[b, t])
+
+    def start(self):
+        for b in (0, 1):
+            def tower(t):
+                def each(way):
+                    @pl.when(self.spot.leaves(0, way))
+                    def _():
+                        self.leave(0, way, t, b, True).start()
+                loop(2, each)
+                self.to_core(self.spot.chip, t, b, True).start()
+                if b == 0:
+                    for kind in (2, 0, 1):
+                        self.give(kind, self.spot.chip, t, True).start()
+                self.own(t, b).start()
+            loop(self.towers, tower)
+
+    def event(self, n):
+        step, t = n // (2 * self.towers), lax.rem(n, self.towers)
+        for b in (0, 1):
+            def each(way):
+                @pl.when(self.spot.comes(step, way))
+                def _():
+                    shard = self.spot.onward(way, -1 - step)
+                    wait_for(self.place(shard, self.spot.core, t, b), self.y_recv.at[way, step, b, t], self.y_send.at[way, step, b, t])
+
+                    @pl.when((step + 1 < self.spot.steps) & self.spot.leaves(step + 1, way))
+                    def _():
+                        self.leave(jnp.minimum(step + 1, self.spot.steps - 1), way, t, b).start()
+                    self.to_core(shard, t, b).start()
+                    if b == 0:
+                        for kind in (2, 0, 1):
+                            self.give(kind, shard, t).start()
+
+            @pl.when(lax.rem(n, 2 * self.towers) // self.towers == b)
+            def _():
+                loop(2, each)
+
+    def receive(self):
+        def one(n):
+            shard, t = n // self.towers, lax.rem(n, self.towers)
+            for kind in range(3):
+                wait_for(self.given_place(kind, shard, t, self.spot.core), self.give_recv.at[kind, shard, t], self.give_send.at[kind, shard, t])
+                self.given(kind, shard, t).start()
+        loop(self.spot.chips * self.towers, one)
+
+    def settle(self):
+        def one(n):
+            shard, t = n // self.towers, lax.rem(n, self.towers)
+            for b in (0, 1):
+                wait_for(self.place(shard, 1 - self.spot.core, t, b), self.core_recv.at[shard, b, t], self.core_send.at[shard, b, t])
+                self.to_core(shard, t, b).wait_send()
+
+                @pl.when(shard < self.spot.steps)
+                def _():
+                    def each(way):
+                        @pl.when(self.spot.leaves(shard, way))
+                        def _():
+                            self.leave(jnp.minimum(shard, self.spot.steps - 1), way, t, b).wait_send()
+                    loop(2, each)
+            for kind in range(3):
+                self.give(kind, shard, t).wait_send()
+                self.given(kind, shard, t).wait_send()
+                wait_for(self.given_place(kind, shard, t, 1 - self.spot.core), self.given_recv.at[kind, shard, t], self.given_send.at[kind, shard, t])
+        loop(self.spot.chips * self.towers, one)
+        for t in range(self.towers):
+            for b in (0, 1):
+                self.own(t, b).wait()
+
+
+def first_kernel(chips, parts, share, f_ref, w_ref, o_ref, n_ref, sp_ref, fg_ref, wg_ref, next_ref, og_ref, dz_ref, act_ref, sg_ref, tot_ref,
+                 offer_f, taken, offer_o, og, wide, low, f_tile, w_tile, acc, theirs, live, act, dz_here, sums_here, tot,
+                 f_send, f_recv, w_send, w_recv, wide_sem, p_sem, a_send, a_recv, z_send, z_recv, out_sem, x_send, x_recv, l_sem):
+    spot = Spot(chips)
+    keep, rows = share[0][0], sum(share[0])
+    size = rows // parts
+    fixed = rows - size
+    spare = keep - fixed
+    cols = o_ref.shape[2]
+    spot.greet()
+
+    def offer(kind, what):
+        src = (f_ref.at[0], f_ref.at[1], o_ref, n_ref)[what]
+        dst = (offer_f.at[0, 1 + kind], offer_f.at[1, 1 + kind], offer_o.at[1 + kind], tot.at[1 + kind])[what]
+        if what < 3:
+            src = src.at[pl.ds(*share[1 + kind])] if what < 2 else src.at[:, pl.ds(*share[1 + kind])]
+        return pltpu.make_async_remote_copy(
+            src_ref=src, dst_ref=dst, send_sem=x_send.at[what, kind], recv_sem=x_recv.at[what, kind],
+            device_id=spot.at(spot.others[kind], spot.core), device_id_type=MESH)
+
+    def choose(width, read, write):
+        weigh = [jnp.broadcast_to(jnp.where(tot[kind, :1, :width] > keep, 1.0, 0.0), (16, width)) for kind in range(4)]
+
+        def strip(i):
+            at = pl.ds(pl.multiple_of(i * 16, 16), 16)
+            value = read(0, at).astype(jnp.float32) * weigh[0]
+            for kind in range(1, 4):
+                value = value + read(kind, at).astype(jnp.float32) * weigh[kind]
+            write(i * 16, value.astype(jnp.bfloat16))
+        loop(share[0][1] // 16, strip)
+
+    features = Features(spot, f_ref.at[0], taken.at[0], fg_ref, size, f_send, f_recv)
+    weights = Weights(spot, w_ref.at[0], wide, low, wg_ref, wide_sem, p_sem.at[4], w_send, w_recv)
+    products = Products(spot, features, wg_ref, f_tile, w_tile, acc, theirs, p_sem.at[pl.ds(0, 2)], p_sem.at[pl.ds(2, 2)], a_send, a_recv)
+    backward = Backward(spot, size, dz_here, dz_ref, z_send, z_recv, out_sem)
+
+    for what in (3, 0):
+        for kind in (2, 0, 1):
+            offer(kind, what).start()
+    loop(parts - 1, lambda q: features.launch(q, False))
+    local = [(n_ref, tot.at[0])]
+    for t in (0, 1):
+        local += [(f_ref.at[t, pl.ds(*share[0])], offer_f.at[t, 0]), (f_ref.at[t, pl.ds(fixed, spare)], taken.at[t, pl.ds(0, spare)])]
+    local += [(o_ref.at[:, pl.ds(*share[0])], offer_o.at[0]), (o_ref.at[:, pl.ds(0, keep)], og.at[:, pl.ds(0, keep)]),
+              (f_ref.at[0, pl.ds(0, fixed)], fg_ref.at[pl.ds(0, fixed), features.lanes(spot.chip)])]
+    local = [pltpu.make_async_copy(src, dst, l_sem.at[n]) for n, (src, dst) in enumerate(local)]
+    for copy in local:
+        copy.start()
+    weights.round()
+    weights.start()
+    for copy in local[:3]:
+        copy.wait()
+    for what in (3, 0):
+        for kind in range(3):
+            offer(kind, what).wait_recv()
+
+    def take(t):
+        def write(row, value):
+            taken[t, pl.ds(pl.multiple_of(spare + row, 16), 16)] = value
+        choose(offer_f.shape[3], lambda kind, at: offer_f[t, kind, at], write)
+    take(0)
+    features.launch(parts - 1, True)
+    more = [pltpu.make_async_copy(tot, tot_ref, l_sem.at[8]),
+            pltpu.make_async_copy(taken.at[0], fg_ref.at[pl.ds(fixed, size), features.lanes(spot.chip)], l_sem.at[9])]
+    for copy in more:
+        copy.start()
+    live_rows_of(tot, share, live)
+    clear(acc)
+
+    loop(parts, lambda q: features.serve(0, q))
+    weights.relay()
+    for what in (2, 1):
+        for kind in (2, 0, 1):
+            offer(kind, what).start()
+    loop(parts, lambda q: features.serve(1, q))
+    weights.finish()
+    for copy in local[3:] + more:
+        copy.wait()
+    products.multiply()
+    for kind in range(3):
+        offer(kind, 2).wait_recv()
+    for t in range(2):
+        def write(row, value):
+            og[t, pl.ds(pl.multiple_of(keep + row, 16), 16)] = value
+        choose(cols, lambda kind, at: offer_o[kind, t, at], write)
+    keeps = [pltpu.make_async_copy(og, og_ref, l_sem.at[0])]
+    keeps[0].start()
+
+    sums_here[...] = jnp.zeros_like(sums_here)
+
+    def strip(at):
+        activated, slope = gelu_and_slope(acc[at, :cols] + theirs[at] + sp_ref[0:1])
+        mask = live[at]
+        dy = [og[t, at].astype(jnp.float32) * mask for t in range(2)]
+        dz = slope * (sp_ref[2:3] * dy[0] + sp_ref[4:5] * dy[1])
+        act[at] = activated
+        dz_here[at] = dz.astype(jnp.bfloat16)
+        for n, term in enumerate((dz, activated * dy[0], activated * dy[1])):
+            sums_here[n] += fold(term)
+
+    def stage(k):
+        @pl.when(k < parts)
+        def _():
+            products.complete(k)
+
+        @pl.when(k > 0)
+        def _():
+            products.swap(k - 1).wait_recv()
+            loop(size // 16, lambda i: strip(pl.ds(pl.multiple_of((k - 1) * size + i * 16, 16), 16)))
+            backward.start(k - 1)
+    loop(parts + 1, stage)
+    for kind in range(3):
+        offer(kind, 1).wait_recv()
+    take(1)
+    keeps += [pltpu.make_async_copy(act, act_ref, l_sem.at[1]), pltpu.make_async_copy(taken.at[1], next_ref, l_sem.at[2])]
+    for copy in keeps[1:]:
+        copy.start()
+    sg_ref[...] = jnp.zeros_like(sg_ref)
+    for n in range(3):
+        sg_ref[2 * n : 2 * n + 1] = jnp.sum(sums_here[n], axis=0, keepdims=True)
+
+    def settle(q):
+        backward.settle(q)
+        products.swap(q).wait_send()
+        features.settle(q)
+    loop(parts, settle)
+    weights.settle()
+    for copy in keeps:
+        copy.wait()
+    for what in range(4):
+        for kind in range(3):
+            offer(kind, what).wait_send()
+
+
+def second_kernel(chips, parts, share, f_ref, w_ref, next_ref, og_ref, tot, act_ref, sp_ref, fg_first, wg_first, dz_first,
+                  fg_ref, wg_ref, dz_ref, y_ref, sg_ref, d_ref, gr_ref, pg_ref, relay_ref,
+                  og, wide, low, f_tile, w_tile, acc, theirs, live, act, dz_here, y_here, sums_here,
+                  held, w_here, dz_wide, total, f_part, g_part, r_part,
+                  f_send, f_recv, w_send, w_recv, wide_sem, p_sem, a_send, a_recv, z_send, z_recv, out_sem, l_sem,
+                  d_send, d_recv, o_sem, b_send, b_recv, g_load, g_send, g_recv, rs_send, rs_recv, own_sem):
+    spot = Spot(chips)
+    rows = sum(share[0])
+    size = rows // parts
+    fixed = rows - size
+    cols = og_ref.shape[2]
+    spot.greet()
+    features = Features(spot, f_ref.at[1], next_ref, fg_ref, size, f_send, f_recv)
+    weights = Weights(spot, w_ref.at[1], wide, low, wg_ref, wide_sem, p_sem.at[4], w_send, w_recv)
+    products = Products(spot, features, wg_ref, f_tile, w_tile, acc, theirs, p_sem.at[pl.ds(0, 2)], p_sem.at[pl.ds(2, 2)], a_send, a_recv)
+    backward = Backward(spot, size, dz_here, dz_ref, z_send, z_recv, out_sem)
+    gradients = Sums(spot, parts, share, d_ref, dz_wide, w_here, held, total, d_send, d_recv, o_sem, b_send, b_recv)
+    grads = Grads(spot, fg_first, dz_wide, gr_ref, pg_ref, relay_ref, f_part, g_part, r_part, g_load.at[0], g_load.at[1], g_load.at[2],
+                  g_send, g_recv, rs_send, rs_recv, own_sem)
+
+    loop(parts - 1, lambda q: features.launch(q, False))
+    features.launch(parts - 1, True)
+    loads = first_loads(chips, wg_first, dz_first, w_here, dz_wide, l_sem)
+    grads.load(jnp.int32(0)).start()
+    weights.round()
+    weights.start()
+    local = [(og_ref, og), (act_ref, act), (f_ref.at[1, pl.ds(0, fixed)], fg_ref.at[pl.ds(0, fixed), features.lanes(spot.chip)]),
+             (next_ref, fg_ref.at[pl.ds(fixed, size), features.lanes(spot.chip)])]
+    local = [pltpu.make_async_copy(src, dst, l_sem.at[chips + 1 + n]) for n, (src, dst) in enumerate(local)]
+    for copy in local:
+        copy.start()
+    for copy in loads:
+        copy.wait()
+
+    def turn(m):
+        gradients.turn(m)
+        grads.turn(m, 9)
+
+        @pl.when(m == 4)
+        def _():
+            weights.relay()
+
+        @pl.when((m >= 2) & (m < 2 + parts))
+        def _():
+            features.serve(0, m - 2)
+
+        @pl.when((m >= 7) & (m < 7 + parts))
+        def _():
+            features.serve(1, m - 7)
+
+        @pl.when(m == 0)
+        def _():
+            live_rows_of(tot, share, live)
+            clear(acc)
+
+        @pl.when(m == 11)
+        def _():
+            weights.finish()
+            for copy in local:
+                copy.wait()
+            products.multiply()
+        gradients.turn_end(m)
+    loop(gradients.turns + gradients.lag, turn)
+
+    sums_here[...] = jnp.zeros_like(sums_here)
+
+    def strip(at):
+        activated, slope = gelu_and_slope(acc[at, :cols] + theirs[at] + sp_ref[1:2])
+        mask = live[at]
+        other = act[at]
+        dy = [og[t, at].astype(jnp.float32) * mask for t in range(2)]
+        dz = slope * (sp_ref[3:4] * dy[0] + sp_ref[5:6] * dy[1])
+        for t in range(2):
+            y_here[t, at] = ((sp_ref[2 + 2 * t : 3 + 2 * t] * other + sp_ref[3 + 2 * t : 4 + 2 * t] * activated) * mask).astype(jnp.bfloat16)
+        dz_here[at] = dz.astype(jnp.bfloat16)
+        for n, term in enumerate((dz, activated * dy[0], activated * dy[1])):
+            sums_here[n] += fold(term)
+
+    def stage(k):
+        @pl.when(k < parts)
+        def _():
+            products.complete(k)
+
+        @pl.when(k > 0)
+        def _():
+            products.swap(k - 1).wait_recv()
+            loop(size // 16, lambda i: strip(pl.ds(pl.multiple_of((k - 1) * size + i * 16, 16), 16)))
+            backward.start(k - 1)
+    loop(parts + 1, stage)
+    keep_y = pltpu.make_async_copy(y_here, y_ref, l_sem.at[0])
+    keep_y.start()
+    sg_ref[...] = jnp.zeros_like(sg_ref)
+    for n in range(3):
+        sg_ref[2 * n + 1 : 2 * n + 2] = jnp.sum(sums_here[n], axis=0, keepdims=True)
+
+    def settle(q):
+        backward.settle(q)
+        products.swap(q).wait_send()
+        features.settle(q)
+    loop(parts, settle)
+    weights.settle()
+    gradients.settle()
+    grads.settle()
+    keep_y.wait()
+
+
+def first_loads(chips, wg, dz, w_here, dz_wide, sem):
+    depth = w_here.shape[1]
+    loads = [pltpu.make_async_copy(dz, dz_wide, sem.at[chips])]
+    loads += [pltpu.make_async_copy(wg.at[pl.ds(n * depth, depth)], w_here.at[n], sem.at[n]) for n in range(chips)]
+    for copy in loads:
+        copy.start()
+    return loads
+
+
+def third_kernel(chips, parts, share, y_ref, fg_ref, wg_ref, dz_ref, ps_ref, st_ref, d_ref, gr_ref, sr_ref, pg_ref, relay_ref,
+                 held, w_here, dz_wide, total, f_part, g_part, r_part, l_sem,
+                 d_send, d_recv, o_sem, b_send, b_recv, g_load, g_send, g_recv, rs_send, rs_recv, own_sem, s_send, s_recv,
+                 y_send, y_recv, core_send, core_recv, give_send, give_recv, given_send, given_recv, y_own):
+    spot = Spot(chips)
+    spot.greet()
+    gradients = Sums(spot, parts, share, d_ref, dz_wide, w_here, held, total, d_send, d_recv, o_sem, b_send, b_recv)
+    grads = Grads(spot, fg_ref, dz_wide, gr_ref, pg_ref, relay_ref, f_part, g_part, r_part, g_load.at[0], g_load.at[1], g_load.at[2],
+                  g_send, g_recv, rs_send, rs_recv, own_sem)
+    stitched = Stitched(spot, share, y_ref, st_ref, y_send, y_recv, core_send, core_recv, give_send, give_recv, given_send, given_recv, y_own)
+
+    def small(kind):
+        return pltpu.make_async_remote_copy(
+            src_ref=ps_ref, dst_ref=sr_ref.at[spot.dp], send_sem=s_send.at[kind], recv_sem=s_recv.at[kind],
+            device_id=spot.at(spot.others[kind], spot.core), device_id_type=MESH)
+
+    loads = first_loads(chips, wg_ref, dz_ref, w_here, dz_wide, l_sem)
+    grads.load(jnp.int32(0)).start()
+    stitched.start()
+    own = pltpu.make_async_copy(ps_ref, sr_ref.at[spot.dp], l_sem.at[chips + 1])
+    own.start()
+    for kind in range(3):
+        small(kind).start()
+    for copy in loads:
+        copy.wait()
+
+    def turn(m):
+        gradients.turn(m)
+        grads.turn(m, 8)
+
+        @pl.when((m >= 1) & (m <= stitched.events))
+        def _():
+            stitched.event(m - 1)
+        gradients.turn_end(m)
+    loop(gradients.turns + gradients.lag, turn)
+    stitched.receive()
+    gradients.settle()
+    stitched.settle()
+    grads.settle()
+    for kind in range(3):
+        small(kind).wait()
+    own.wait()
+
+
+def call(kernel, name, ident, out, scratch, operands, small_in=(), small_out=(), flops=0):
+    anywhere, here = pl.BlockSpec(memory_space=pl.ANY), pl.BlockSpec(memory_space=pltpu.VMEM)
+    return pl.pallas_call(
+        kernel,
+        out_shape=out,
+        in_specs=[here if n in small_in else anywhere for n in range(len(operands))],
+        out_specs=[here if n in small_out else anywhere for n in range(len(out))],
+        scratch_shapes=scratch,
+        compiler_params=pltpu.CompilerParams(collective_id=ident, has_side_effects=True, vmem_limit_bytes=58 * 2**20),
+        cost_estimate=pl.CostEstimate(flops=flops, bytes_accessed=500 * 2**20, transcendentals=0),
+        name=name,
+    )(*operands)
+
+
+def shared_pass(features, weights, out_grad, count, small_params, chips, parts, share):
+    towers, slots, depth = features.shape
+    cols = weights.shape[2]
+    keep, size = share[0]
+    rows = keep + size
+    steps = chips - 1
+    piece = rows // parts
+    dma, vmem = pltpu.SemaphoreType.DMA, pltpu.VMEM
+    bf16, f32 = jnp.bfloat16, jnp.float32
+    S = jax.ShapeDtypeStruct
+    told = jnp.broadcast_to(count.astype(f32), (8, depth))
+    flops = 2 * rows * 2 * cols * depth * chips
+    line = [dma((2, steps, parts))] * 2 + [dma((4, 2))] * 2 + [dma((2,)), dma((5,))] + [dma((parts,))] * 5
+    tiles = [vmem((2, depth // 4, cols), f32), vmem((2, depth, cols), bf16), vmem((2, rows, depth), bf16), vmem((2, depth, 2 * cols), bf16),
+             vmem((rows, 2 * cols), f32), vmem((rows, cols), f32), vmem((rows, cols), f32), vmem((rows, cols), f32), vmem((rows, cols), bf16)]
+    folded = vmem((3, 8, cols), f32)
+    wide = [S((rows, chips * depth), bf16), S((chips * depth, 2 * cols), bf16)]
+    *first, start, grad_here, dz, act, small_first, told = call(
+        functools.partial(first_kernel, chips, parts, share), "first", 3,
+        wide + [S((piece, depth), bf16), S((towers, rows, cols), bf16), S((rows, 2 * cols), bf16), S((rows, cols), f32), S((8, cols), f32),
+                S((4, 8, depth), f32)],
+        [vmem((towers, 4, size, depth), bf16), vmem((towers, piece, depth), bf16), vmem((4, towers, size, cols), bf16), vmem((towers, rows, cols), bf16)]
+        + tiles + [folded, vmem((4, 8, depth), f32)] + line + [dma((4, 3)), dma((4, 3)), dma((10,))],
+        (features, weights, out_grad, told, small_params), (4,), (6,), flops)
+    *second, dz_second, result, small_second, d_first, gr_first, _, _ = call(
+        functools.partial(second_kernel, chips, parts, share), "second", 5,
+        wide + [S((rows, 2 * cols), bf16), S((towers, rows, cols), bf16), S((8, cols), f32)] + sums_out(slots, depth, cols),
+        [vmem((towers, rows, cols), bf16)] + tiles + [vmem((towers, rows, cols), bf16), folded] + sums_scratch(chips, rows, parts, depth, cols)
+        + line + [dma((chips + 5,))] + sums_dma(steps, parts),
+        (features, weights, start, grad_here, told, act, small_params, *first, dz), (4, 6), (4,), 3 * flops)
+    return told, (result, *second, dz_second, small_first + small_second), d_first, gr_first
+
+
+def sums_out(slots, depth, cols):
+    S, bf16 = jax.ShapeDtypeStruct, jnp.bfloat16
+    return [S((slots, depth), bf16), S((3, 2, depth, cols), bf16), S((8, depth, cols), bf16), S((2, depth, cols), bf16)]
+
+
+def sums_scratch(chips, rows, parts, depth, cols):
+    vmem, bf16 = pltpu.VMEM, jnp.bfloat16
+    return [vmem((2, chips - 1, rows, depth), bf16), vmem((chips, depth, 2 * cols), bf16), vmem((rows, 2 * cols), bf16),
+            vmem((2, rows // parts, depth), bf16), vmem((2, rows, depth // 3), bf16)] + [vmem((2, depth // 3, cols), bf16)] * 2
+
+
+def sums_dma(steps, parts):
+    dma = pltpu.SemaphoreType.DMA
+    return [dma((2, steps * parts))] * 2 + [dma((2,)), dma((3,)), dma((3,)), dma((3, 2)), dma((8,)), dma((3, 2)), dma((2,)), dma((2,)), dma(())]
+
+
+def shared_sums(result, wide_f, wide_w, wide_dz, partial_s, slots, chips, parts, share):
+    towers, rows, cols = result.shape
+    depth, steps = wide_w.shape[0] // chips, chips - 1
+    dma = pltpu.SemaphoreType.DMA
+    S = jax.ShapeDtypeStruct
+    stitched, d_feat, parts_of, smalls, _, _ = call(
+        functools.partial(third_kernel, chips, parts, share), "third", 4,
+        [S((towers, slots, 2 * chips * cols), jnp.bfloat16)] + sums_out(slots, depth, cols)[:2] + [S((4,) + partial_s.shape, jnp.float32)]
+        + sums_out(slots, depth, cols)[2:],
+        sums_scratch(chips, rows, parts, depth, cols) + [dma((chips + 2,))] + sums_dma(steps, parts) + [dma((3,))] * 2
+        + [dma((2, steps, 2, towers))] * 2 + [dma((chips, 2, towers))] * 2 + [dma((3, chips, towers))] * 4 + [dma((2, towers))],
+        (result, wide_f, wide_w, wide_dz, partial_s), flops=4 * rows * 2 * cols * depth * chips)
+    return stitched, d_feat, parts_of, smalls
+
+
 def small_step(small_params, small_moment_one, small_moment_two, small_average, small_grad):
     first, second, direction = adam_part(small_moment_one, small_moment_two, small_grad)
     fresh = small_params - rate_small * direction
     return first, second, fresh, ema_decay * small_average + (1.0 - ema_decay) * fresh
+
+
+def update(d_feat, stitched, full, parts, small_parts, states, small_states):
+    small_grad = jnp.sum(small_parts, 0)[: small_states[0].shape[0]]
+    *fresh, stitched, d_feat = soap(parts, full, stitched, d_feat, *states)
+    return (stitched, d_feat) + tuple(fresh) + small_step(*small_states, small_grad)
+
+
+def own_rows(features, out_grad, totals, passed, first, states, small_states):
+    _, rows, _ = features.shape
+    weights, small_params = states[0], small_states[0]
+    cols = weights.shape[2]
+    cores = lax.axis_size("mp")
+    swap = [(i, i ^ 1) for i in range(cores)]
+    ranges = ((0, rows // 2), (rows // 2, rows // 2))
+    live_rows = (jnp.arange(rows, dtype=jnp.float32) < totals[0]).astype(jnp.float32)
+    wide_f, wide_w = gather(features, weights.astype(jnp.bfloat16), cores // 2, ranges, 1)
+    partial = jnp.einsum("tri,tio->tro", wide_f, wide_w, preferred_element_type=jnp.float32)
+    product = partial[:, :, :cols] + lax.ppermute(partial[:, :, cols:], "mp", swap)
+    result, back = jax.vjp(lambda a, b: stitch_local(a, b, live_rows), product, small_params)
+    stitched = lax.all_gather(result.astype(jnp.bfloat16), "mp", axis=2, tiled=True)
+    dz, small_part = back(out_grad.astype(jnp.float32))
+    dz_low = dz.astype(jnp.bfloat16)
+    wide_dz = jnp.concatenate([dz_low, lax.ppermute(dz_low, "mp", swap)], axis=2)
+    partial_d = jnp.einsum("tro,tio->tri", wide_dz, wide_w, preferred_element_type=jnp.float32)
+    partial_g = jnp.einsum("tri,tro->tio", wide_f, wide_dz, preferred_element_type=jnp.float32)
+    small_part = jnp.pad(small_part, ((0, 2), (0, 0)))
+    d_feat, parts, small_parts = reduce(
+        partial_d.astype(jnp.bfloat16), partial_g.astype(jnp.bfloat16), small_part, cores // 2, ranges, 2
+    )
+    full = jnp.full((1,), rows, jnp.int32)
+    return update((d_feat[0], d_feat[1]), stitched, full, (parts[:, :, 0], parts[:, :, 1]), small_parts, states, small_states)
+
+
+def shares(rows):
+    keep = rows * 15 // 32 // 16 * 16
+    size = -(-(rows - keep) // 64) * 16
+    return keep, ((keep, size), (keep + size, size), (keep + 2 * size, size), (rows - size, size))
+
+
+def shared_rows(features, out_grad, totals, passed, first, states, small_states):
+    rows = features.shape[1]
+    keep, share = shares(rows)
+    d_first, gr_first = first
+    full = jnp.where(totals[:1] > keep, rows, keep)
+    stitched, d_second, gr_second, small_parts = shared_sums(*passed, rows, lax.axis_size("mp") // 2, 4, share)
+    return update((d_first, d_second), stitched, full, (gr_first, gr_second), small_parts, states, small_states)
 
 
 def line_body(
@@ -461,32 +1624,23 @@
     small_moment_two,
     small_average,
 ):
-    cores = lax.axis_size("mp")
-    chips = cores // 2
-    cols = weights.shape[2]
-    swap = [(i, i ^ 1) for i in range(cores)]
-    slot_count = features.shape[1]
-    total = jnp.sum(counts)
-    live_rows = (jnp.arange(slot_count, dtype=jnp.int32) < total).astype(jnp.float32)
-    wide_f, wide_w = gather(features, weights.astype(jnp.bfloat16), chips, 2, 1)
-    partial = jnp.einsum("tri,tio->tro", wide_f, wide_w, preferred_element_type=jnp.float32)
-    product = partial[:, :, :cols] + lax.ppermute(partial[:, :, cols:], "mp", swap)
-    result, back = jax.vjp(lambda a, b: stitch_local(a, b, live_rows), product, small_params)
-    stitched = lax.all_gather(result.astype(jnp.bfloat16), "mp", axis=2, tiled=True)
-    dz, small_part = back(out_grad.astype(jnp.float32))
-    dz_low = dz.astype(jnp.bfloat16)
-    wide_dz = jnp.concatenate([dz_low, lax.ppermute(dz_low, "mp", swap)], axis=2)
-    partial_d = jnp.einsum("tro,tio->tri", wide_dz, wide_w, preferred_element_type=jnp.float32)
-    partial_g = jnp.einsum("tri,tro->tio", wide_f, wide_dz, preferred_element_type=jnp.float32)
-    small_part = jnp.pad(small_part, ((0, 2), (0, 0)))
-    d_feat, parts, small_parts = reduce(
-        partial_d.astype(jnp.bfloat16), partial_g.astype(jnp.bfloat16), small_part, chips, 2, 2
+    keep, share = shares(features.shape[1])
+    told, passed, *first = shared_pass(
+        features, weights, out_grad, jnp.sum(counts), small_params, lax.axis_size("mp") // 2, 4, share
     )
-    states = soap(parts, weights, moment_one, moment_two, average, basis_left, basis_right)
-    small_states = small_step(
-        small_params, small_moment_one, small_moment_two, small_average, jnp.sum(small_parts, 0)[:6]
+    totals = told[:, 0, 0]
+    return lax.cond(
+        jnp.sum(totals > keep) == 1,
+        shared_rows,
+        own_rows,
+        features,
+        out_grad,
+        totals,
+        passed,
+        first,
+        (weights, moment_one, moment_two, average, basis_left, basis_right),
+        (small_params, small_moment_one, small_moment_two, small_average),
     )
-    return (stitched, d_feat) + tuple(states) + small_states
 
 
 def plain_body(

time: 1200 us -> 608 us (0.51); the launches traced: 1200 us -> 596 us
  Pallas kernels: 1030 us -> 573 us
  matrix products: 99.4 us -> 0 us
  local copies, waits for them, and re-layouts: 27.6 us -> 3.32 us
  other arithmetic: 26.2 us -> 4.03 us
    pallas_call x3 -> x4, Pallas kernels: 1030 us -> 573 us  [the longest x3 502 us: call(): pl.pallas_call(kernel, out_shape=out, in_specs=[here if n in small_in els...]
    dot_general x3 -> x0, matrix products: 99.4 us -> none  [the longest x1 34.2 us: line_body(): jnp.einsum('tri,tio->tro', wide_f, wide_w, preferred_element_type=jnp.flo...]
    unnamed x26 -> x10, local copies, waits for them, and re-layouts: 21.4 us -> 0.03 us
  transfers between devices with their start and end apart: 3 -> 0, of which waited for: 2 -> 0; matrix products, arithmetic and copies ran while one was open for 6% -> 0% of each run, Pallas kernels for 54% -> 0%
where the time goes in v6:
time: 608 us; the launch traced here: 596 us
  Pallas kernels  573 us (94%)
  between operations  15.4 us (3%)
    pallas_call x3, Pallas kernels, call(): pl.pallas_call(kernel, out_shape=out, in_specs=[here if n in small_in els...  502 us
    pallas_call x1, Pallas kernels, soap(): pl.pallas_call(functools.partial(soap_body, 2 - group % 2, strips), grid=...  70.6 us

profile of v6, /device:TPU:17, one launch (start us, length us, event | category | flops | bytes accessed | tf_op | source)
XLA Modules:
  0.0 595.8 jit_solution(7852351614166193326)
XLA Ops:
  7.2 1.3 reduce_sum.78
  9.1 0.6 broadcast_in_dim.4.n_ref
  9.7 0.0 copy-start.5
  9.7 135.4 %first.1 = (bf16[768,4608]{1,0:T(8,128)(2,1)}, bf16[4608,1024]{1,0:T(8,128)(2,1)}, bf16[192,1152]{1,0:T(8,128)(2,1)}, bf16[2,768,512]{2,1,0:T(8,128)(2,1)}, bf16...) custom-call(bf16[2,1280,1152]{2,1,0:T(8,128)(2,1)} %f_ref.3, ...), custom_call_target="tpu_custom_call" | custom-call | flops 7247757312 | bytes 524288000 | tf_op jit(solution)/shard_map/first/pallas_call | solution.py:1483
  145.1 0.8 slice_reduce_fusion
  146.0 0.6 fusion.13
  147.3 0.0 copy-done.5
  147.3 0.0 copy-start.3
  147.3 0.0 copy-start.6
  147.3 0.0 copy-start.9
  147.3 0.0 copy-start.12
  147.3 194.2 %second.1 = (bf16[768,4608]{1,0:T(8,128)(2,1)}, bf16[4608,1024]{1,0:T(8,128)(2,1)}, bf16[768,1024]{1,0:T(8,128)(2,1)}, bf16[2,768,512]{2,1,0:T(8,128)(2,1)}, f32...) custom-call(bf16[2,1280,1152]{2,1,0:T(8,128)(2,1)} %f_ref.3, ...), custom_call_target="tpu_custom_call" | custom-call | flops 21743271936 | bytes 524288000 | tf_op jit(solution)/shard_map/second/pallas_call | solution.py:1483
  341.6 0.0 copy-done.3
  341.6 0.0 copy-done.6
  341.6 0.0 copy-done.9
  341.6 0.0 copy-done.12
  341.6 247.4 %conditional.1 = (bf16[2,1280,4096]{2,1,0:T(8,128)(2,1)}, bf16[2,1280,1152]{2,1,0:T(8,128)(2,1)}, f32[2,2304,512]{2,1,0:T(8,128)}, f32[2,2304,512]{2,1,0:T(8,128...) conditional(s32[]{:T(128)} %convert_element_type.38, ...), branch_computations={%region_2.9_spmd, %region_9.11_spmd} | conditional | flops 74991869952 | bytes 2269207552 | solution.py:1632
  341.9 0.6 add.71.ps_ref
  342.5 172.6 %third.1 = (bf16[2,1280,4096]{2,1,0:T(8,128)(2,1)}, bf16[1280,1152]{1,0:T(8,128)(2,1)}, bf16[3,2,1152,512]{3,2,1,0:T(8,128)(2,1)}, f32[4,8,512]{2,1,0:T(8,128)},...) custom-call(bf16[2,768,512]{2,1,0:T(8,128)(2,1)} %get-tuple-element.92.y_ref, ...), custom_call_target="tpu_custom_call" | custom-call | flops 14495514624 | bytes 524288000 | tf_op jit(solution)/shard_map/cond/branch_1_fun/third/pallas_call | solution.py:1483
  515.1 0.9 reduce_sum.72
  516.0 0.6 add_multiply_fusion.1
  516.6 0.0 copy-done.2
  516.6 1.8 copy-done.1
  518.4 70.6 %soap.3 = (f32[2,2304,512]{2,1,0:T(8,128)}, f32[2,2304,512]{2,1,0:T(8,128)}, f32[2,2304,512]{2,1,0:T(8,128)}, f32[2,2304,512]{2,1,0:T(8,128)}, bf16[2,2304,512]{...) custom-call(s32[1]{0:T(128)S(6)} %select_n.3.full, ...), custom_call_target="tpu_custom_call" | custom-call | flops 2415919104 | bytes 136314880 | tf_op jit(solution)/shard_map/cond/branch_1_fun/soap/pallas_call | solution.py:136
  (2 shorter events, 0.0 us)
Async XLA Ops:
  9.7 137.5 %copy-start.5 = (f32[6,512]{1,0:T(8,128)S(1)}, f32[6,512]{1,0:T(8,128)}, u32[]{:S(2)}) copy-start(f32[6,512]{1,0:T(8,128)} %sp_ref.3) | copy-start | bytes 36868
  147.3 194.3 %copy-start.3 = (bf16[2,1280,512]{2,1,0:T(8,128)(2,1)S(1)}, bf16[2,1280,512]{2,1,0:T(8,128)(2,1)}, u32[]{:S(2)}) copy-start(bf16[2,1280,512]{2,1,0:T(8,128)(2,1)} %o_ref.1) | copy-start | bytes 7864324
  147.3 194.3 %copy-start.6 = (f32[6,512]{1,0:T(8,128)S(1)}, f32[6,512]{1,0:T(8,128)}, u32[]{:S(2)}) copy-start(f32[6,512]{1,0:T(8,128)} %param.25) | copy-start | bytes 36868
  147.3 194.3 %copy-start.9 = (f32[6,512]{1,0:T(8,128)S(1)}, f32[6,512]{1,0:T(8,128)}, u32[]{:S(2)}) copy-start(f32[6,512]{1,0:T(8,128)} %param.26) | copy-start | bytes 36868
  147.3 194.3 %copy-start.12 = (f32[6,512]{1,0:T(8,128)S(1)}, f32[6,512]{1,0:T(8,128)}, u32[]{:S(2)}) copy-start(f32[6,512]{1,0:T(8,128)} %param.27) | copy-start | bytes 36868
  342.5 174.1 %copy-start.2 = (bf16[1280,1152]{1,0:T(8,128)(2,1)S(1)}, bf16[1280,1152]{1,0:T(8,128)(2,1)}, u32[]{:S(2)}) copy-start(bf16[1280,1152]{1,0:T(8,128)(2,1)} %get-tuple-element.100.d_a) | copy-start | bytes 8847364 | tf_op jit(solution)/shard_map/cond
  516.6 1.8 copy-start.1

commit v7 on v6

--- a/solution.py
+++ b/solution.py
@@ -45,13 +45,9 @@
     own = row == lane
 
     def diagonal(v):
-        return jnp.where(own, jnp.concatenate([v, v], axis=0), 0.0)
-
-    def beside(v):
-        return jnp.concatenate([v[0], v[1]], axis=1)
-
-    def stationary(v, axis):
-        high, low = split(v)
+        return jnp.where(own, jnp.concatenate([v, v], axis=0), jnp.zeros((), v.dtype))
+
+    def stationary(high, low, axis):
         return jnp.concatenate([high, high, low], axis=axis)
 
     def moving(v, axis):
@@ -62,18 +58,19 @@
         dims = (((ca,), (cb,)), ((), ()))
         return [lax.dot_general(x, y, dims, preferred_element_type=jnp.float32) for x, y in zip(a, b)]
 
-    right = [diagonal(beside(v)) for v in rights]
-    values = dots([moving(v, 1) for v in grads], [stationary(v, 0) for v in right], 1, 0)
-    values = dots([stationary(v.reshape(2 * BLOCK, BLOCK), 0) for v in lefts], [moving(diagonal(v), 0) for v in values], 0, 0)
+    right = [(diagonal(high), diagonal(low)) for high, low in rights]
+    values = dots([moving(v, 1) for v in grads], [stationary(*v, 0) for v in right], 1, 0)
+    values = dots([stationary(*v, 0) for v in lefts], [moving(v, 0) for v in values], 0, 0)
+    values = [jnp.where(lane[:BLOCK] == 0, v[:BLOCK], v[BLOCK:]) for v in values]
     states = [adam_part(a, b, v) for (a, b), v in zip(moments, values)]
-    values = dots([moving(v[2], 1) for v in states], [stationary(v, 1) for v in right], 1, 1)
-    values = dots([stationary(beside(v), 1) for v in lefts], [moving(diagonal(v), 0) for v in values], 1, 0)
+    values = dots([moving(v[2], 1) for v in states], [stationary(*v, 1) for v in right], 1, 1)
+    values = dots([stationary(*v, 1) for v in lefts], [moving(diagonal(v), 0) for v in values], 1, 0)
     return [(first, second, step) for (first, second, _), step in zip(states, values)]
 
 
 def soap_body(together, strips, full, parts_a, parts_b, stitched, d_a, d_b, weights, moment_a, moment_b, average, left, right,
               first, second, new_weights, new_average, copy, stitched_out, d_feat_out):
-    groups, pairs = left.shape[1], left.shape[2] // 2
+    groups, pairs = left.shape[2], left.shape[4] // BLOCK
     length = stitched.shape[1]
     row = jnp.minimum(pl.program_id(1) * pl.num_programs(2) + pl.program_id(2), strips - 1) * length
 
@@ -95,8 +92,11 @@
         for at in ats:
             grads.append(sum(jnp.where(first_tower, parts_a[(k,) + at], parts_b[(k,) + at]).astype(jnp.float32)
                              for k in range(parts_a.shape[0])))
-        done = soap_blocks(grads, [left[0, r, 2 * q : 2 * q + 2] for r, q in places],
-                           [right[0, r, 2 * q : 2 * q + 2] for r, q in places], [(moment_a[at], moment_b[at]) for at in ats])
+        def basis(ref, r, q):
+            return tuple(ref[0, 0, r, k, BLOCK * q : BLOCK * (q + 1)] for k in (0, 1))
+
+        done = soap_blocks(grads, [basis(left, *place) for place in places], [basis(right, *place) for place in places],
+                           [(moment_a[at], moment_b[at]) for at in ats])
         olds = [(weights[at], average[at]) for at in ats]
         for at, (one, two, step), (held, mean) in zip(ats, done, olds):
             first[at] = one
@@ -110,14 +110,13 @@
     lax.fori_loop(0, groups // together, blocks, 0)
 
 
-def soap(parts, wanted, stitched, d_feat, weights, moment_a, moment_b, average, left, right, group=6):
+def soap(parts, wanted, stitched, d_feat, weights, moment_a, moment_b, average, bases, group=6):
     towers, rows, cols = weights.shape
     half = parts[0].shape[2]
     steps = half // (BLOCK * group)
     flat = lambda t, p, g: (t, p * steps + g, 0)
-    basis = lambda t, p, g: (t, p * steps + g, 0, 0, 0)
     state = pl.BlockSpec((1, BLOCK * group, cols), flat)
-    base = pl.BlockSpec((1, group, cols // BLOCK, BLOCK, BLOCK), basis)
+    base = [pl.BlockSpec((1, 1, group) + bases.shape[3:], lambda t, p, g, n=n: (n, t, p * steps + g, 0, 0, 0)) for n in (0, 1)]
     full = jax.ShapeDtypeStruct(weights.shape, jnp.float32)
     strips = max(n for n in range(1, 2 * steps + 1) if stitched.shape[1] % (16 * n) == 0)
 
@@ -137,14 +136,14 @@
         functools.partial(soap_body, 2 - group % 2, strips),
         grid=(towers, 2, steps),
         in_specs=[pl.BlockSpec(memory_space=pltpu.SMEM),
-                  *pieces, through(stitched.shape), *rows_of, state, state, state, state, base, base],
+                  *pieces, through(stitched.shape), *rows_of, state, state, state, state, *base],
         out_specs=[state] * 5 + [through(stitched.shape), through((towers,) + d_feat[0].shape)],
         out_shape=[full] * 4 + [jax.ShapeDtypeStruct(weights.shape, jnp.bfloat16)]
         + [jax.ShapeDtypeStruct(v, jnp.bfloat16) for v in (stitched.shape, (towers,) + d_feat[0].shape)],
-        compiler_params=pltpu.CompilerParams(vmem_limit_bytes=48 * 2**20),
+        compiler_params=pltpu.CompilerParams(vmem_limit_bytes=60 * 2**20),
         cost_estimate=pl.CostEstimate(flops=8 * 2 * towers * rows * cols * 64, bytes_accessed=130 * 2**20, transcendentals=0),
         name="soap",
-    )(wanted, *parts, stitched, *d_feat, weights, moment_a, moment_b, average, left, right)
+    )(wanted, *parts, stitched, *d_feat, weights, moment_a, moment_b, average, bases, bases)
 
 
 MESH = pl.DeviceIdType.MESH
@@ -580,21 +579,19 @@
 
 
 class Weights:
-    def __init__(self, spot, w_ref, wide, low, wg, wide_sem, own_sem, send, recv):
-        self.spot, self.w_ref, self.wide, self.low, self.wg = spot, w_ref, wide, low, wg
-        self.wide_sem, self.own_sem, self.send, self.recv = wide_sem, own_sem, send, recv
+    def __init__(self, spot, low, wg, own_sem, send, recv):
+        self.spot, self.low, self.wg, self.own_sem, self.send, self.recv = spot, low, wg, own_sem, send, recv
         self.depth, self.cols = low.shape[1], low.shape[2]
 
     def block(self, owner, slot):
         return self.wg.at[pl.ds(pl.multiple_of(owner * self.depth, 128), self.depth), pl.ds(pl.multiple_of(slot * self.cols, 128), self.cols)]
 
-    def round(self):
-        part = self.wide.shape[1]
+    def round(self, w_ref, wide, sem):
+        part = wide.shape[1]
         parts = self.depth // part
 
         def load(n):
-            return pltpu.make_async_copy(self.w_ref.at[pl.ds(pl.multiple_of(n * part, 16), part)], self.wide.at[lax.rem(n, 2)],
-                                         self.wide_sem.at[lax.rem(n, 2)])
+            return pltpu.make_async_copy(w_ref.at[pl.ds(pl.multiple_of(n * part, 16), part)], wide.at[lax.rem(n, 2)], sem.at[lax.rem(n, 2)])
 
         def one(n):
             @pl.when(n + 1 < 2 * parts)
@@ -605,7 +602,7 @@
             def strip(i):
                 rows = pl.ds(pl.multiple_of(i * 32, 32), 32)
                 to = pl.ds(pl.multiple_of(lax.rem(n, parts) * part + i * 32, 32), 32)
-                self.low[n // parts, to] = self.wide[lax.rem(n, 2), rows].astype(jnp.bfloat16)
+                self.low[n // parts, to] = wide[lax.rem(n, 2), rows].astype(jnp.bfloat16)
             loop(part // 32, strip)
         load(jnp.int32(0)).start()
         loop(2 * parts, one)
@@ -884,22 +881,23 @@
         def _():
             self.own().start()
 
-    def turn(self, m, late):
+    def turn(self, m, begin, late):
         early = self.jobs - 2
+        pause = begin + early
 
         def job_at(m):
-            return jnp.where(m < early, m, m - late + early)
-
-        @pl.when((m == early) | (m == late + 2))
+            return jnp.where(m < pause, m - begin, m - late + early)
+
+        @pl.when((m == pause) | (m == late + 2))
         def _():
             for c in (1, 2):
                 self.store(job_at(m - 1) * self.thirds + c).wait()
 
-        @pl.when((m < early) | (m == late) | (m == late + 1))
+        @pl.when(((m >= begin) & (m < pause)) | (m == late) | (m == late + 1))
         def _():
             self.job(job_at(m))
 
-        @pl.when(((m > 0) & (m <= early)) | (m == late + 1) | (m == late + 2))
+        @pl.when(((m > begin) & (m <= pause)) | (m == late + 1) | (m == late + 2))
         def _():
             self.start(job_at(m - 1))
 
@@ -918,7 +916,7 @@
 
 
 class Sums:
-    window, lag = 3, 2
+    window, lag = 5, 1
 
     def __init__(self, spot, parts, share, d_ref, dz_here, w_here, held, total, send, recv, out_sem, back_send, back_recv):
         self.spot, self.parts, self.share, self.d_ref, self.dz_here, self.w_here, self.held, self.total = spot, parts, share, d_ref, dz_here, w_here, held, total
@@ -1061,6 +1059,58 @@
     skip = share[2][0] + share[2][1] - share[3][0] if kind == 2 else 0
     first, length = share[1 + kind]
     return pl.ds(first + skip, length - skip), pl.ds(skip, length - skip)
+
+
+class Bases:
+    def __init__(self, left, right, out, held, parts, load_sem, store_sem):
+        self.sources, self.out, self.held, self.parts, self.load_sem, self.store_sem = (left, right), out, held, parts, load_sem, store_sem
+        self.groups, self.pairs = left.shape[1], left.shape[2] // 2
+        self.units = left.shape[0] * self.groups
+
+    def at(self, u):
+        return u // self.groups, lax.rem(u, self.groups), lax.rem(u, 2)
+
+    def load(self, u, start):
+        t, r, slot = self.at(u)
+        for n, source in enumerate(self.sources):
+            copy = pltpu.make_async_copy(source.at[t, r], self.held.at[slot, n], self.load_sem.at[slot, n])
+            (copy.start if start else copy.wait)()
+
+    def store(self, u, start):
+        t, r, slot = self.at(u)
+        for n in (0, 1):
+            copy = pltpu.make_async_copy(self.parts.at[slot, n], self.out.at[n, t, r], self.store_sem.at[slot, n])
+            (copy.start if start else copy.wait)()
+
+    def unit(self, u):
+        @pl.when(u + 1 < self.units)
+        def _():
+            self.load(u + 1, True)
+        self.load(u, False)
+
+        @pl.when(u >= 2)
+        def _():
+            self.store(u - 2, False)
+        slot = lax.rem(u, 2)
+        for n in (0, 1):
+            for q in range(self.pairs):
+                both = jnp.concatenate([self.held[slot, n, 2 * q], self.held[slot, n, 2 * q + 1]], axis=1)
+                high, low = split(both)
+                rows = pl.ds(q * BLOCK, BLOCK)
+                self.parts[slot, n, 0, rows] = high
+                self.parts[slot, n, 1, rows] = low
+        self.store(u, True)
+
+    def some(self, first, count):
+        def one(i):
+            @pl.when(first + i < self.units)
+            def _():
+                self.unit(first + i)
+        loop(count, one)
+
+    def settle(self):
+        for u in (self.units - 2, self.units - 1):
+            self.store(jnp.int32(u), False)
 
 
 class Stitched:
@@ -1185,9 +1235,10 @@
                 self.own(t, b).wait()
 
 
-def first_kernel(chips, parts, share, f_ref, w_ref, o_ref, n_ref, sp_ref, fg_ref, wg_ref, next_ref, og_ref, dz_ref, act_ref, sg_ref, tot_ref,
-                 offer_f, taken, offer_o, og, wide, low, f_tile, w_tile, acc, theirs, live, act, dz_here, sums_here, tot,
-                 f_send, f_recv, w_send, w_recv, wide_sem, p_sem, a_send, a_recv, z_send, z_recv, out_sem, x_send, x_recv, l_sem):
+def first_kernel(chips, parts, share, f_ref, w_ref, o_ref, n_ref, sp_ref, left_ref, right_ref,
+                 fg_ref, wg_ref, low_ref, next_ref, og_ref, dz_ref, act_ref, sg_ref, tot_ref, bases_ref,
+                 offer_f, taken, offer_o, og, wide, low, low_next, f_tile, w_tile, acc, theirs, live, act, dz_here, sums_here, tot, base_in, base_out,
+                 f_send, f_recv, w_send, w_recv, wide_sem, p_sem, a_send, a_recv, z_send, z_recv, out_sem, x_send, x_recv, l_sem, base_load, base_store):
     spot = Spot(chips)
     keep, rows = share[0][0], sum(share[0])
     size = rows // parts
@@ -1217,7 +1268,7 @@
         loop(share[0][1] // 16, strip)
 
     features = Features(spot, f_ref.at[0], taken.at[0], fg_ref, size, f_send, f_recv)
-    weights = Weights(spot, w_ref.at[0], wide, low, wg_ref, wide_sem, p_sem.at[4], w_send, w_recv)
+    weights = Weights(spot, low, wg_ref, p_sem.at[4], w_send, w_recv)
     products = Products(spot, features, wg_ref, f_tile, w_tile, acc, theirs, p_sem.at[pl.ds(0, 2)], p_sem.at[pl.ds(2, 2)], a_send, a_recv)
     backward = Backward(spot, size, dz_here, dz_ref, z_send, z_recv, out_sem)
 
@@ -1227,15 +1278,18 @@
     loop(parts - 1, lambda q: features.launch(q, False))
     local = [(n_ref, tot.at[0])]
     for t in (0, 1):
-        local += [(f_ref.at[t, pl.ds(*share[0])], offer_f.at[t, 0]), (f_ref.at[t, pl.ds(fixed, spare)], taken.at[t, pl.ds(0, spare)])]
+        local += [(f_ref.at[t, pl.ds(*share[0])], offer_f.at[t, 0])]
+        if spare:
+            local += [(f_ref.at[t, pl.ds(fixed, spare)], taken.at[t, pl.ds(0, spare)])]
+    need = len(local) // 2 + 1
     local += [(o_ref.at[:, pl.ds(*share[0])], offer_o.at[0]), (o_ref.at[:, pl.ds(0, keep)], og.at[:, pl.ds(0, keep)]),
               (f_ref.at[0, pl.ds(0, fixed)], fg_ref.at[pl.ds(0, fixed), features.lanes(spot.chip)])]
     local = [pltpu.make_async_copy(src, dst, l_sem.at[n]) for n, (src, dst) in enumerate(local)]
     for copy in local:
         copy.start()
-    weights.round()
+    weights.round(w_ref.at[0], wide, wide_sem)
     weights.start()
-    for copy in local[:3]:
+    for copy in local[:need]:
         copy.wait()
     for what in (3, 0):
         for kind in range(3):
@@ -1253,15 +1307,25 @@
         copy.start()
     live_rows_of(tot, share, live)
     clear(acc)
-
-    loop(parts, lambda q: features.serve(0, q))
+    Weights(spot, low_next, wg_ref, p_sem.at[4], w_send, w_recv).round(w_ref.at[1], wide, wide_sem)
+    more.append(pltpu.make_async_copy(low_next, low_ref, l_sem.at[10]))
+    more[2].start()
+
+    bases = Bases(left_ref, right_ref, bases_ref, base_in, base_out, base_load, base_store)
+    share_of = -(-bases.units // (2 * parts))
+
+    def serve(step, q):
+        features.serve(step, q)
+        bases.some((step * parts + q) * share_of, share_of)
+    bases.load(jnp.int32(0), True)
+    loop(parts, lambda q: serve(0, q))
     weights.relay()
     for what in (2, 1):
         for kind in (2, 0, 1):
             offer(kind, what).start()
-    loop(parts, lambda q: features.serve(1, q))
+    loop(parts, lambda q: serve(1, q))
     weights.finish()
-    for copy in local[3:] + more:
+    for copy in local[need:] + more:
         copy.wait()
     products.multiply()
     for kind in range(3):
@@ -1312,6 +1376,7 @@
         features.settle(q)
     loop(parts, settle)
     weights.settle()
+    bases.settle()
     for copy in keeps:
         copy.wait()
     for what in range(4):
@@ -1319,11 +1384,11 @@
             offer(kind, what).wait_send()
 
 
-def second_kernel(chips, parts, share, f_ref, w_ref, next_ref, og_ref, tot, act_ref, sp_ref, fg_first, wg_first, dz_first,
+def second_kernel(chips, parts, share, f_ref, low_ref, next_ref, og_ref, tot, act_ref, sp_ref, fg_first, wg_first, dz_first,
                   fg_ref, wg_ref, dz_ref, y_ref, sg_ref, d_ref, gr_ref, pg_ref, relay_ref,
-                  og, wide, low, f_tile, w_tile, acc, theirs, live, act, dz_here, y_here, sums_here,
+                  og, f_tile, w_tile, acc, theirs, live, act, dz_here, y_here, sums_here,
                   held, w_here, dz_wide, total, f_part, g_part, r_part,
-                  f_send, f_recv, w_send, w_recv, wide_sem, p_sem, a_send, a_recv, z_send, z_recv, out_sem, l_sem,
+                  f_send, f_recv, w_send, w_recv, p_sem, a_send, a_recv, z_send, z_recv, out_sem, l_sem,
                   d_send, d_recv, o_sem, b_send, b_recv, g_load, g_send, g_recv, rs_send, rs_recv, own_sem):
     spot = Spot(chips)
     rows = sum(share[0])
@@ -1332,7 +1397,7 @@
     cols = og_ref.shape[2]
     spot.greet()
     features = Features(spot, f_ref.at[1], next_ref, fg_ref, size, f_send, f_recv)
-    weights = Weights(spot, w_ref.at[1], wide, low, wg_ref, wide_sem, p_sem.at[4], w_send, w_recv)
+    weights = Weights(spot, low_ref, wg_ref, p_sem.at[4], w_send, w_recv)
     products = Products(spot, features, wg_ref, f_tile, w_tile, acc, theirs, p_sem.at[pl.ds(0, 2)], p_sem.at[pl.ds(2, 2)], a_send, a_recv)
     backward = Backward(spot, size, dz_here, dz_ref, z_send, z_recv, out_sem)
     gradients = Sums(spot, parts, share, d_ref, dz_wide, w_here, held, total, d_send, d_recv, o_sem, b_send, b_recv)
@@ -1341,10 +1406,9 @@
 
     loop(parts - 1, lambda q: features.launch(q, False))
     features.launch(parts - 1, True)
+    weights.start()
     loads = first_loads(chips, wg_first, dz_first, w_here, dz_wide, l_sem)
     grads.load(jnp.int32(0)).start()
-    weights.round()
-    weights.start()
     local = [(og_ref, og), (act_ref, act), (f_ref.at[1, pl.ds(0, fixed)], fg_ref.at[pl.ds(0, fixed), features.lanes(spot.chip)]),
              (next_ref, fg_ref.at[pl.ds(fixed, size), features.lanes(spot.chip)])]
     local = [pltpu.make_async_copy(src, dst, l_sem.at[chips + 1 + n]) for n, (src, dst) in enumerate(local)]
@@ -1355,7 +1419,7 @@
 
     def turn(m):
         gradients.turn(m)
-        grads.turn(m, 9)
+        grads.turn(m, 2, 10)
 
         @pl.when(m == 4)
         def _():
@@ -1365,16 +1429,16 @@
         def _():
             features.serve(0, m - 2)
 
-        @pl.when((m >= 7) & (m < 7 + parts))
-        def _():
-            features.serve(1, m - 7)
+        @pl.when((m >= 4 + parts) & (m < 4 + 2 * parts))
+        def _():
+            features.serve(1, m - 4 - parts)
 
         @pl.when(m == 0)
         def _():
             live_rows_of(tot, share, live)
             clear(acc)
 
-        @pl.when(m == 11)
+        @pl.when(m == 4 + 2 * parts)
         def _():
             weights.finish()
             for copy in local:
@@ -1462,7 +1526,7 @@
 
     def turn(m):
         gradients.turn(m)
-        grads.turn(m, 8)
+        grads.turn(m, 0, 8)
 
         @pl.when((m >= 1) & (m <= stitched.events))
         def _():
@@ -1492,7 +1556,13 @@
     )(*operands)
 
 
-def shared_pass(features, weights, out_grad, count, small_params, chips, parts, share):
+def parts_of(share):
+    rows = sum(share[0])
+    return max(n for n in range(1, rows // 16) if rows % (16 * n) == 0 and rows // n >= share[0][1])
+
+
+def shared_pass(features, weights, out_grad, count, small_params, left, right, chips, share):
+    parts = parts_of(share)
     towers, slots, depth = features.shape
     cols = weights.shape[2]
     keep, size = share[0]
@@ -1504,25 +1574,27 @@
     S = jax.ShapeDtypeStruct
     told = jnp.broadcast_to(count.astype(f32), (8, depth))
     flops = 2 * rows * 2 * cols * depth * chips
-    line = [dma((2, steps, parts))] * 2 + [dma((4, 2))] * 2 + [dma((2,)), dma((5,))] + [dma((parts,))] * 5
-    tiles = [vmem((2, depth // 4, cols), f32), vmem((2, depth, cols), bf16), vmem((2, rows, depth), bf16), vmem((2, depth, 2 * cols), bf16),
+    gathers = [dma((2, steps, parts))] * 2 + [dma((4, 2))] * 2
+    line = [dma((5,))] + [dma((parts,))] * 5
+    tiles = [vmem((2, rows, depth), bf16), vmem((2, depth, 2 * cols), bf16),
              vmem((rows, 2 * cols), f32), vmem((rows, cols), f32), vmem((rows, cols), f32), vmem((rows, cols), f32), vmem((rows, cols), bf16)]
     folded = vmem((3, 8, cols), f32)
     wide = [S((rows, chips * depth), bf16), S((chips * depth, 2 * cols), bf16)]
-    *first, start, grad_here, dz, act, small_first, told = call(
+    *first, low, start, grad_here, dz, act, small_first, told, bases = call(
         functools.partial(first_kernel, chips, parts, share), "first", 3,
-        wide + [S((piece, depth), bf16), S((towers, rows, cols), bf16), S((rows, 2 * cols), bf16), S((rows, cols), f32), S((8, cols), f32),
-                S((4, 8, depth), f32)],
-        [vmem((towers, 4, size, depth), bf16), vmem((towers, piece, depth), bf16), vmem((4, towers, size, cols), bf16), vmem((towers, rows, cols), bf16)]
-        + tiles + [folded, vmem((4, 8, depth), f32)] + line + [dma((4, 3)), dma((4, 3)), dma((10,))],
-        (features, weights, out_grad, told, small_params), (4,), (6,), flops)
+        wide + [S((2, depth, cols), bf16), S((piece, depth), bf16), S((towers, rows, cols), bf16), S((rows, 2 * cols), bf16), S((rows, cols), f32), S((8, cols), f32),
+                S((4, 8, depth), f32), S((2,) + left.shape[:2] + (2, left.shape[2] // 2 * BLOCK, 2 * BLOCK), bf16)],
+        [vmem((towers, 4, size, depth), bf16), vmem((towers, piece, depth), bf16), vmem((4, towers, size, cols), bf16), vmem((towers, rows, cols), bf16), vmem((2, depth // 4, cols), f32)]
+        + [vmem((2, depth, cols), bf16)] * 2 + tiles + [folded, vmem((4, 8, depth), f32), vmem((2, 2) + left.shape[2:], f32), vmem((2, 2, 2, left.shape[2] // 2 * BLOCK, 2 * BLOCK), bf16)] + gathers + [dma((2,))] + line
+        + [dma((4, 3)), dma((4, 3)), dma((11,)), dma((2, 2)), dma((2, 2))],
+        (features, weights, out_grad, told, small_params, left, right), (4,), (7,), flops)
     *second, dz_second, result, small_second, d_first, gr_first, _, _ = call(
         functools.partial(second_kernel, chips, parts, share), "second", 5,
         wide + [S((rows, 2 * cols), bf16), S((towers, rows, cols), bf16), S((8, cols), f32)] + sums_out(slots, depth, cols),
         [vmem((towers, rows, cols), bf16)] + tiles + [vmem((towers, rows, cols), bf16), folded] + sums_scratch(chips, rows, parts, depth, cols)
-        + line + [dma((chips + 5,))] + sums_dma(steps, parts),
-        (features, weights, start, grad_here, told, act, small_params, *first, dz), (4, 6), (4,), 3 * flops)
-    return told, (result, *second, dz_second, small_first + small_second), d_first, gr_first
+        + gathers + line + [dma((chips + 5,))] + sums_dma(steps, parts),
+        (features, low, start, grad_here, told, act, small_params, *first, dz), (4, 6), (4,), 3 * flops)
+    return told, bases, (result, *second, dz_second, small_first + small_second), d_first, gr_first
 
 
 def sums_out(slots, depth, cols):
@@ -1541,19 +1613,20 @@
     return [dma((2, steps * parts))] * 2 + [dma((2,)), dma((3,)), dma((3,)), dma((3, 2)), dma((8,)), dma((3, 2)), dma((2,)), dma((2,)), dma(())]
 
 
-def shared_sums(result, wide_f, wide_w, wide_dz, partial_s, slots, chips, parts, share):
+def shared_sums(result, wide_f, wide_w, wide_dz, partial_s, slots, chips, share):
+    parts = parts_of(share)
     towers, rows, cols = result.shape
     depth, steps = wide_w.shape[0] // chips, chips - 1
     dma = pltpu.SemaphoreType.DMA
     S = jax.ShapeDtypeStruct
-    stitched, d_feat, parts_of, smalls, _, _ = call(
+    stitched, d_feat, grad_parts, smalls, _, _ = call(
         functools.partial(third_kernel, chips, parts, share), "third", 4,
         [S((towers, slots, 2 * chips * cols), jnp.bfloat16)] + sums_out(slots, depth, cols)[:2] + [S((4,) + partial_s.shape, jnp.float32)]
         + sums_out(slots, depth, cols)[2:],
         sums_scratch(chips, rows, parts, depth, cols) + [dma((chips + 2,))] + sums_dma(steps, parts) + [dma((3,))] * 2
         + [dma((2, steps, 2, towers))] * 2 + [dma((chips, 2, towers))] * 2 + [dma((3, chips, towers))] * 4 + [dma((2, towers))],
         (result, wide_f, wide_w, wide_dz, partial_s), flops=4 * rows * 2 * cols * depth * chips)
-    return stitched, d_feat, parts_of, smalls
+    return stitched, d_feat, grad_parts, smalls
 
 
 def small_step(small_params, small_moment_one, small_moment_two, small_average, small_grad):
@@ -1605,7 +1678,7 @@
     keep, share = shares(rows)
     d_first, gr_first = first
     full = jnp.where(totals[:1] > keep, rows, keep)
-    stitched, d_second, gr_second, small_parts = shared_sums(*passed, rows, lax.axis_size("mp") // 2, 4, share)
+    stitched, d_second, gr_second, small_parts = shared_sums(*passed, rows, lax.axis_size("mp") // 2, share)
     return update((d_first, d_second), stitched, full, (gr_first, gr_second), small_parts, states, small_states)
 
 
@@ -1625,8 +1698,8 @@
     small_average,
 ):
     keep, share = shares(features.shape[1])
-    told, passed, *first = shared_pass(
-        features, weights, out_grad, jnp.sum(counts), small_params, lax.axis_size("mp") // 2, 4, share
+    told, bases, passed, *first = shared_pass(
+        features, weights, out_grad, jnp.sum(counts), small_params, basis_left, basis_right, lax.axis_size("mp") // 2, share
     )
     totals = told[:, 0, 0]
     return lax.cond(
@@ -1638,7 +1711,7 @@
         totals,
         passed,
         first,
-        (weights, moment_one, moment_two, average, basis_left, basis_right),
+        (weights, moment_one, moment_two, average, bases),
         (small_params, small_moment_one, small_moment_two, small_average),
     )
 

time: 608 us -> 578 us (0.951); the launches traced: 596 us -> 573 us
  Pallas kernels: 573 us -> 552 us
    pallas_call x3, Pallas kernels: 502 us -> 486 us  [call(): pl.pallas_call(kernel, out_shape=out, in_specs=[here if n in small_in els...]
where the time goes in v7:
time: 578 us; the launch traced here: 573 us
  Pallas kernels  552 us (96%)
  between operations  15.4 us (3%)
    pallas_call x3, Pallas kernels, call(): pl.pallas_call(kernel, out_shape=out, in_specs=[here if n in small_in els...  486 us
    pallas_call x1, Pallas kernels, soap(): pl.pallas_call(functools.partial(soap_body, 2 - group % 2, strips), grid=...  66.2 us

profile of v7, /device:TPU:17, one launch (start us, length us, event | category | flops | bytes accessed | tf_op | source)
XLA Modules:
  0.0 573.3 jit_solution(578639776912009506)
XLA Ops:
  7.2 1.3 reduce_sum.78
  9.1 0.6 broadcast_in_dim.4.n_ref
  9.7 0.0 copy-start.3
  9.7 135.5 %first.1 = (bf16[768,4608]{1,0:T(8,128)(2,1)}, bf16[4608,1024]{1,0:T(8,128)(2,1)}, bf16[2,1152,512]{2,1,0:T(8,128)(2,1)}, bf16[192,1152]{1,0:T(8,128)(2,1)}, bf1...) custom-call(bf16[2,1280,1152]{2,1,0:T(8,128)(2,1)} %f_ref.3, ...), custom_call_target="tpu_custom_call" | custom-call | flops 7247757312 | bytes 524288000 | tf_op jit(solution)/shard_map/first/pallas_call | solution.py:1547
  145.3 0.8 slice_reduce_fusion
  146.1 0.6 fusion.13
  147.4 0.0 copy-done.3
  147.4 0.0 copy-start
  147.4 0.0 copy-start.4
  147.4 0.0 copy-start.7
  147.5 0.0 copy-start.10
  147.5 181.0 %second.1 = (bf16[768,4608]{1,0:T(8,128)(2,1)}, bf16[4608,1024]{1,0:T(8,128)(2,1)}, bf16[768,1024]{1,0:T(8,128)(2,1)}, bf16[2,768,512]{2,1,0:T(8,128)(2,1)}, f32...) custom-call(bf16[2,1280,1152]{2,1,0:T(8,128)(2,1)} %f_ref.3, ...), custom_call_target="tpu_custom_call" | custom-call | flops 21743271936 | bytes 524288000 | tf_op jit(solution)/shard_map/second/pallas_call | solution.py:1547
  328.4 0.0 copy-done
  328.4 0.0 copy-done.4
  328.5 0.0 copy-done.7
  328.5 0.0 copy-done.10
  328.5 237.9 %conditional.1 = (bf16[2,1280,4096]{2,1,0:T(8,128)(2,1)}, bf16[2,1280,1152]{2,1,0:T(8,128)(2,1)}, f32[2,2304,512]{2,1,0:T(8,128)}, f32[2,2304,512]{2,1,0:T(8,128...) conditional(s32[]{:T(128)} %convert_element_type.38, ...), branch_computations={%region_2.9_spmd, %region_9.11_spmd} | conditional | flops 74991869952 | bytes 2257411072 | solution.py:1705
  328.8 0.6 add.71.ps_ref
  329.4 0.0 copy-start.1
  329.4 169.3 %third.1 = (bf16[2,1280,4096]{2,1,0:T(8,128)(2,1)}, bf16[1280,1152]{1,0:T(8,128)(2,1)}, bf16[3,2,1152,512]{3,2,1,0:T(8,128)(2,1)}, f32[4,8,512]{2,1,0:T(8,128)},...) custom-call(bf16[2,768,512]{2,1,0:T(8,128)(2,1)} %get-tuple-element.87.y_ref, ...), custom_call_target="tpu_custom_call" | custom-call | flops 14495514624 | bytes 524288000 | tf_op jit(solution)/shard_map/cond/branch_1_fun/third/pallas_call | solution.py:1547
  498.7 0.9 reduce_sum.72
  499.5 0.6 add_multiply_fusion.1
  500.2 0.0 copy-done.1
  500.2 66.2 %soap.3 = (f32[2,2304,512]{2,1,0:T(8,128)}, f32[2,2304,512]{2,1,0:T(8,128)}, f32[2,2304,512]{2,1,0:T(8,128)}, f32[2,2304,512]{2,1,0:T(8,128)}, bf16[2,2304,512]{...) custom-call(s32[1]{0:T(128)S(6)} %select_n.3.full, ...), custom_call_target="tpu_custom_call" | custom-call | flops 2415919104 | bytes 136314880 | tf_op jit(solution)/shard_map/cond/branch_1_fun/soap/pallas_call | solution.py:135
Async XLA Ops:
  9.7 137.7 %copy-start.3 = (f32[6,512]{1,0:T(8,128)S(1)}, f32[6,512]{1,0:T(8,128)}, u32[]{:S(2)}) copy-start(f32[6,512]{1,0:T(8,128)} %sp_ref.3) | copy-start | bytes 36868
  147.4 181.0 %copy-start = (bf16[2,1280,512]{2,1,0:T(8,128)(2,1)S(1)}, bf16[2,1280,512]{2,1,0:T(8,128)(2,1)}, u32[]{:S(2)}) copy-start(bf16[2,1280,512]{2,1,0:T(8,128)(2,1)} %o_ref.1) | copy-start | bytes 7864324
  147.4 181.0 %copy-start.4 = (f32[6,512]{1,0:T(8,128)S(1)}, f32[6,512]{1,0:T(8,128)}, u32[]{:S(2)}) copy-start(f32[6,512]{1,0:T(8,128)} %param.25) | copy-start | bytes 36868
  147.4 181.0 %copy-start.7 = (f32[6,512]{1,0:T(8,128)S(1)}, f32[6,512]{1,0:T(8,128)}, u32[]{:S(2)}) copy-start(f32[6,512]{1,0:T(8,128)} %param.26) | copy-start | bytes 36868
  147.5 181.0 %copy-start.10 = (f32[6,512]{1,0:T(8,128)S(1)}, f32[6,512]{1,0:T(8,128)}, u32[]{:S(2)}) copy-start(f32[6,512]{1,0:T(8,128)} %param.27) | copy-start | bytes 36868
  329.4 170.8 %copy-start.1 = (bf16[1280,1152]{1,0:T(8,128)(2,1)S(1)}, bf16[1280,1152]{1,0:T(8,128)(2,1)}, u32[]{:S(2)}) copy-start(bf16[1280,1152]{1,0:T(8,128)(2,1)} %get-tuple-element.95.d_a) | copy-start | bytes 8847364 | tf_op jit(solution)/shard_map/cond

commit v8 on v7

--- a/solution.py
+++ b/solution.py
@@ -133,7 +133,7 @@
     rows_of = [of_tower(n, (v.shape[0] // strips, v.shape[1]), lambda p, g: (strip(p, g), 0), (strips - 1, 0)) for n, v in enumerate(d_feat)]
 
     return pl.pallas_call(
-        functools.partial(soap_body, 2 - group % 2, strips),
+        functools.partial(soap_body, group, strips),
         grid=(towers, 2, steps),
         in_specs=[pl.BlockSpec(memory_space=pltpu.SMEM),
                   *pieces, through(stitched.shape), *rows_of, state, state, state, state, *base],
@@ -600,10 +600,10 @@
             load(n).wait()
 
             def strip(i):
-                rows = pl.ds(pl.multiple_of(i * 32, 32), 32)
-                to = pl.ds(pl.multiple_of(lax.rem(n, parts) * part + i * 32, 32), 32)
+                rows = pl.ds(pl.multiple_of(i * 16, 16), 16)
+                to = pl.ds(pl.multiple_of(lax.rem(n, parts) * part + i * 16, 16), 16)
                 self.low[n // parts, to] = wide[lax.rem(n, 2), rows].astype(jnp.bfloat16)
-            loop(part // 32, strip)
+            loop(part // 16, strip)
         load(jnp.int32(0)).start()
         loop(2 * parts, one)
 
@@ -1235,20 +1235,25 @@
                 self.own(t, b).wait()
 
 
-def first_kernel(chips, parts, share, f_ref, w_ref, o_ref, n_ref, sp_ref, left_ref, right_ref,
-                 fg_ref, wg_ref, low_ref, next_ref, og_ref, dz_ref, act_ref, sg_ref, tot_ref, bases_ref,
-                 offer_f, taken, offer_o, og, wide, low, low_next, f_tile, w_tile, acc, theirs, live, act, dz_here, sums_here, tot, base_in, base_out,
-                 f_send, f_recv, w_send, w_recv, wide_sem, p_sem, a_send, a_recv, z_send, z_recv, out_sem, x_send, x_recv, l_sem, base_load, base_store):
+def front_kernel(chips, parts, share, f_ref, w_ref, o_ref, n_ref, sp_ref, left_ref, right_ref,
+                 fg_first, wg_first, dz_first, fg_ref, wg_ref, dz_ref, y_ref, sg_ref, tot_ref, bases_ref, d_ref, gr_ref, pg_ref, relay_ref,
+                 offer_f, taken, offer_o, wide, low, base_in, base_out, tot,
+                 og, f_tile, w_tile, acc, theirs, live, act, dz_here, y_here, sums_here,
+                 held, w_here, dz_wide, total, f_part, g_part, r_part,
+                 f_send, f_recv, w_send, w_recv, a_send, a_recv, z_send, z_recv, out_sem,
+                 wide_sem, p_sem, x_send, x_recv, l_sem, base_load, base_store,
+                 d_send, d_recv, o_sem, b_send, b_recv, g_load, g_send, g_recv, rs_send, rs_recv, own_sem):
     spot = Spot(chips)
     keep, rows = share[0][0], sum(share[0])
     size = rows // parts
     fixed = rows - size
     spare = keep - fixed
     cols = o_ref.shape[2]
+    tot[0] = jnp.zeros_like(tot[0]) + jnp.sum(n_ref[...].astype(jnp.float32), axis=1, keepdims=True)
     spot.greet()
 
     def offer(kind, what):
-        src = (f_ref.at[0], f_ref.at[1], o_ref, n_ref)[what]
+        src = (f_ref.at[0], f_ref.at[1], o_ref, tot.at[0])[what]
         dst = (offer_f.at[0, 1 + kind], offer_f.at[1, 1 + kind], offer_o.at[1 + kind], tot.at[1 + kind])[what]
         if what < 3:
             src = src.at[pl.ds(*share[1 + kind])] if what < 2 else src.at[:, pl.ds(*share[1 + kind])]
@@ -1267,51 +1272,56 @@
             write(i * 16, value.astype(jnp.bfloat16))
         loop(share[0][1] // 16, strip)
 
-    features = Features(spot, f_ref.at[0], taken.at[0], fg_ref, size, f_send, f_recv)
-    weights = Weights(spot, low, wg_ref, p_sem.at[4], w_send, w_recv)
-    products = Products(spot, features, wg_ref, f_tile, w_tile, acc, theirs, p_sem.at[pl.ds(0, 2)], p_sem.at[pl.ds(2, 2)], a_send, a_recv)
-    backward = Backward(spot, size, dz_here, dz_ref, z_send, z_recv, out_sem)
+    def take(t):
+        def write(row, value):
+            taken[t, pl.ds(pl.multiple_of(spare + row, 16), 16)] = value
+        choose(offer_f.shape[3], lambda kind, at: offer_f[t, kind, at], write)
+
+    towers = []
+    for t, (fg, wg, dz) in enumerate(((fg_first, wg_first, dz_first), (fg_ref, wg_ref, dz_ref))):
+        features = Features(spot, f_ref.at[t], taken.at[t], fg, size, f_send.at[t], f_recv.at[t])
+        weights = Weights(spot, low.at[t], wg, p_sem.at[t, 4], w_send.at[t], w_recv.at[t])
+        products = Products(spot, features, wg, f_tile, w_tile, acc, theirs.at[t], p_sem.at[t, pl.ds(0, 2)], p_sem.at[t, pl.ds(2, 2)],
+                            a_send.at[t], a_recv.at[t])
+        backward = Backward(spot, size, dz_here, dz, z_send.at[t], z_recv.at[t], out_sem.at[t])
+        towers.append((features, weights, products, backward))
+    features, weights, products, backward = towers[0]
+    gradients = Sums(spot, parts, share, d_ref, dz_wide, w_here, held, total, d_send, d_recv, o_sem, b_send, b_recv)
+    grads = Grads(spot, fg_first, dz_wide, gr_ref, pg_ref, relay_ref, f_part, g_part, r_part, g_load.at[0], g_load.at[1], g_load.at[2],
+                  g_send, g_recv, rs_send, rs_recv, own_sem)
+    bases = Bases(left_ref, right_ref, bases_ref, base_in, base_out, base_load, base_store)
+
+    def copy(n, src, dst):
+        made = pltpu.make_async_copy(src, dst, l_sem.at[n])
+        made.start()
+        return made
 
     for what in (3, 0):
         for kind in (2, 0, 1):
             offer(kind, what).start()
     loop(parts - 1, lambda q: features.launch(q, False))
-    local = [(n_ref, tot.at[0])]
-    for t in (0, 1):
-        local += [(f_ref.at[t, pl.ds(*share[0])], offer_f.at[t, 0])]
-        if spare:
-            local += [(f_ref.at[t, pl.ds(fixed, spare)], taken.at[t, pl.ds(0, spare)])]
-    need = len(local) // 2 + 1
-    local += [(o_ref.at[:, pl.ds(*share[0])], offer_o.at[0]), (o_ref.at[:, pl.ds(0, keep)], og.at[:, pl.ds(0, keep)]),
-              (f_ref.at[0, pl.ds(0, fixed)], fg_ref.at[pl.ds(0, fixed), features.lanes(spot.chip)])]
-    local = [pltpu.make_async_copy(src, dst, l_sem.at[n]) for n, (src, dst) in enumerate(local)]
-    for copy in local:
-        copy.start()
+    needed = [copy(0, f_ref.at[0, pl.ds(*share[0])], offer_f.at[0, 0])]
+    later = [copy(1, f_ref.at[1, pl.ds(*share[0])], offer_f.at[1, 0])]
+    if spare:
+        needed.append(copy(2, f_ref.at[0, pl.ds(fixed, spare)], taken.at[0, pl.ds(0, spare)]))
+        later.append(copy(3, f_ref.at[1, pl.ds(fixed, spare)], taken.at[1, pl.ds(0, spare)]))
+    later += [copy(4, o_ref.at[:, pl.ds(*share[0])], offer_o.at[0]), copy(5, o_ref.at[:, pl.ds(0, keep)], og.at[:, pl.ds(0, keep)]),
+              copy(6, f_ref.at[0, pl.ds(0, fixed)], fg_first.at[pl.ds(0, fixed), features.lanes(spot.chip)]),
+              copy(7, f_ref.at[1, pl.ds(0, fixed)], fg_ref.at[pl.ds(0, fixed), features.lanes(spot.chip)])]
     weights.round(w_ref.at[0], wide, wide_sem)
     weights.start()
-    for copy in local[:need]:
-        copy.wait()
+    for made in needed:
+        made.wait()
     for what in (3, 0):
         for kind in range(3):
             offer(kind, what).wait_recv()
-
-    def take(t):
-        def write(row, value):
-            taken[t, pl.ds(pl.multiple_of(spare + row, 16), 16)] = value
-        choose(offer_f.shape[3], lambda kind, at: offer_f[t, kind, at], write)
     take(0)
     features.launch(parts - 1, True)
-    more = [pltpu.make_async_copy(tot, tot_ref, l_sem.at[8]),
-            pltpu.make_async_copy(taken.at[0], fg_ref.at[pl.ds(fixed, size), features.lanes(spot.chip)], l_sem.at[9])]
-    for copy in more:
-        copy.start()
+    later += [copy(8, tot, tot_ref), copy(9, taken.at[0], fg_first.at[pl.ds(fixed, size), features.lanes(spot.chip)])]
     live_rows_of(tot, share, live)
     clear(acc)
-    Weights(spot, low_next, wg_ref, p_sem.at[4], w_send, w_recv).round(w_ref.at[1], wide, wide_sem)
-    more.append(pltpu.make_async_copy(low_next, low_ref, l_sem.at[10]))
-    more[2].start()
-
-    bases = Bases(left_ref, right_ref, bases_ref, base_in, base_out, base_load, base_store)
+    sums_here[...] = jnp.zeros_like(sums_here)
+    towers[1][1].round(w_ref.at[1], wide, wide_sem)
     share_of = -(-bases.units // (2 * parts))
 
     def serve(step, q):
@@ -1325,8 +1335,9 @@
             offer(kind, what).start()
     loop(parts, lambda q: serve(1, q))
     weights.finish()
-    for copy in local[need:] + more:
-        copy.wait()
+    towers[1][1].start()
+    for made in later:
+        made.wait()
     products.multiply()
     for kind in range(3):
         offer(kind, 2).wait_recv()
@@ -1334,22 +1345,25 @@
         def write(row, value):
             og[t, pl.ds(pl.multiple_of(keep + row, 16), 16)] = value
         choose(cols, lambda kind, at: offer_o[kind, t, at], write)
-    keeps = [pltpu.make_async_copy(og, og_ref, l_sem.at[0])]
-    keeps[0].start()
-
-    sums_here[...] = jnp.zeros_like(sums_here)
-
-    def strip(at):
-        activated, slope = gelu_and_slope(acc[at, :cols] + theirs[at] + sp_ref[0:1])
+
+    def strip(t, at):
+        activated, slope = gelu_and_slope(acc[at, :cols] + theirs[t, at] + sp_ref[t : t + 1])
         mask = live[at]
-        dy = [og[t, at].astype(jnp.float32) * mask for t in range(2)]
-        dz = slope * (sp_ref[2:3] * dy[0] + sp_ref[4:5] * dy[1])
-        act[at] = activated
+        dy = [og[n, at].astype(jnp.float32) * mask for n in range(2)]
+        dz = slope * (sp_ref[2 + t : 3 + t] * dy[0] + sp_ref[4 + t : 5 + t] * dy[1])
+        if t == 0:
+            act[at] = activated
+        else:
+            other = act[at]
+            for n in range(2):
+                y_here[n, at] = ((sp_ref[2 + 2 * n : 3 + 2 * n] * other + sp_ref[3 + 2 * n : 4 + 2 * n] * activated) * mask).astype(jnp.bfloat16)
         dz_here[at] = dz.astype(jnp.bfloat16)
         for n, term in enumerate((dz, activated * dy[0], activated * dy[1])):
-            sums_here[n] += fold(term)
-
-    def stage(k):
+            sums_here[2 * n + t] += fold(term)
+
+    def stage(t, k):
+        _, _, products, backward = towers[t]
+
         @pl.when(k < parts)
         def _():
             products.complete(k)
@@ -1357,136 +1371,66 @@
         @pl.when(k > 0)
         def _():
             products.swap(k - 1).wait_recv()
-            loop(size // 16, lambda i: strip(pl.ds(pl.multiple_of((k - 1) * size + i * 16, 16), 16)))
+            loop(size // 16, lambda i: strip(t, pl.ds(pl.multiple_of((k - 1) * size + i * 16, 16), 16)))
             backward.start(k - 1)
-    loop(parts + 1, stage)
+    loop(parts + 1, lambda k: stage(0, k))
+
+    def settle(t, q):
+        towers[t][0].settle(q)
+        towers[t][2].swap(q).wait_send()
+        towers[t][3].settle(q)
     for kind in range(3):
         offer(kind, 1).wait_recv()
     take(1)
-    keeps += [pltpu.make_async_copy(act, act_ref, l_sem.at[1]), pltpu.make_async_copy(taken.at[1], next_ref, l_sem.at[2])]
-    for copy in keeps[1:]:
-        copy.start()
+    loop(parts, lambda q: settle(0, q))
+    loads = first_loads(chips, wg_first, dz_first, w_here, dz_wide, l_sem.at[pl.ds(11, chips + 1)])
+    features, weights, products, backward = towers[1]
+    loop(parts - 1, lambda q: features.launch(q, False))
+    features.launch(parts - 1, True)
+    last = copy(0, taken.at[1], fg_ref.at[pl.ds(fixed, size), features.lanes(spot.chip)])
+    grads.load(jnp.int32(0)).start()
+    clear(acc)
+    for made in loads:
+        made.wait()
+
+    def turn(m):
+        gradients.turn(m)
+        grads.turn(m, 2, 10)
+
+        @pl.when(m == 2)
+        def _():
+            weights.relay()
+
+        @pl.when((m >= 2) & (m < 2 + parts))
+        def _():
+            features.serve(0, m - 2)
+
+        @pl.when((m >= 4 + parts) & (m < 4 + 2 * parts))
+        def _():
+            features.serve(1, m - 4 - parts)
+
+        @pl.when(m == 4 + 2 * parts)
+        def _():
+            weights.finish()
+            last.wait()
+            products.multiply()
+        gradients.turn_end(m)
+    loop(gradients.turns + gradients.lag, turn)
+    loop(parts + 1, lambda k: stage(1, k))
+    last = copy(0, y_here, y_ref)
     sg_ref[...] = jnp.zeros_like(sg_ref)
-    for n in range(3):
-        sg_ref[2 * n : 2 * n + 1] = jnp.sum(sums_here[n], axis=0, keepdims=True)
-
-    def settle(q):
-        backward.settle(q)
-        products.swap(q).wait_send()
-        features.settle(q)
-    loop(parts, settle)
-    weights.settle()
+    for n in range(6):
+        sg_ref[n : n + 1] = jnp.sum(sums_here[n], axis=0, keepdims=True)
+    loop(parts, lambda q: settle(1, q))
+    for t in range(2):
+        towers[t][1].settle()
+    gradients.settle()
+    grads.settle()
     bases.settle()
-    for copy in keeps:
-        copy.wait()
+    last.wait()
     for what in range(4):
         for kind in range(3):
             offer(kind, what).wait_send()
-
-
-def second_kernel(chips, parts, share, f_ref, low_ref, next_ref, og_ref, tot, act_ref, sp_ref, fg_first, wg_first, dz_first,
-                  fg_ref, wg_ref, dz_ref, y_ref, sg_ref, d_ref, gr_ref, pg_ref, relay_ref,
-                  og, f_tile, w_tile, acc, theirs, live, act, dz_here, y_here, sums_here,
-                  held, w_here, dz_wide, total, f_part, g_part, r_part,
-                  f_send, f_recv, w_send, w_recv, p_sem, a_send, a_recv, z_send, z_recv, out_sem, l_sem,
-                  d_send, d_recv, o_sem, b_send, b_recv, g_load, g_send, g_recv, rs_send, rs_recv, own_sem):
-    spot = Spot(chips)
-    rows = sum(share[0])
-    size = rows // parts
-    fixed = rows - size
-    cols = og_ref.shape[2]
-    spot.greet()
-    features = Features(spot, f_ref.at[1], next_ref, fg_ref, size, f_send, f_recv)
-    weights = Weights(spot, low_ref, wg_ref, p_sem.at[4], w_send, w_recv)
-    products = Products(spot, features, wg_ref, f_tile, w_tile, acc, theirs, p_sem.at[pl.ds(0, 2)], p_sem.at[pl.ds(2, 2)], a_send, a_recv)
-    backward = Backward(spot, size, dz_here, dz_ref, z_send, z_recv, out_sem)
-    gradients = Sums(spot, parts, share, d_ref, dz_wide, w_here, held, total, d_send, d_recv, o_sem, b_send, b_recv)
-    grads = Grads(spot, fg_first, dz_wide, gr_ref, pg_ref, relay_ref, f_part, g_part, r_part, g_load.at[0], g_load.at[1], g_load.at[2],
-                  g_send, g_recv, rs_send, rs_recv, own_sem)
-
-    loop(parts - 1, lambda q: features.launch(q, False))
-    features.launch(parts - 1, True)
-    weights.start()
-    loads = first_loads(chips, wg_first, dz_first, w_here, dz_wide, l_sem)
-    grads.load(jnp.int32(0)).start()
-    local = [(og_ref, og), (act_ref, act), (f_ref.at[1, pl.ds(0, fixed)], fg_ref.at[pl.ds(0, fixed), features.lanes(spot.chip)]),
-             (next_ref, fg_ref.at[pl.ds(fixed, size), features.lanes(spot.chip)])]
-    local = [pltpu.make_async_copy(src, dst, l_sem.at[chips + 1 + n]) for n, (src, dst) in enumerate(local)]
-    for copy in local:
-        copy.start()
-    for copy in loads:
-        copy.wait()
-
-    def turn(m):
-        gradients.turn(m)
-        grads.turn(m, 2, 10)
-
-        @pl.when(m == 4)
-        def _():
-            weights.relay()
-
-        @pl.when((m >= 2) & (m < 2 + parts))
-        def _():
-            features.serve(0, m - 2)
-
-        @pl.when((m >= 4 + parts) & (m < 4 + 2 * parts))
-        def _():
-            features.serve(1, m - 4 - parts)
-
-        @pl.when(m == 0)
-        def _():
-            live_rows_of(tot, share, live)
-            clear(acc)
-
-        @pl.when(m == 4 + 2 * parts)
-        def _():
-            weights.finish()
-            for copy in local:
-                copy.wait()
-            products.multiply()
-        gradients.turn_end(m)
-    loop(gradients.turns + gradients.lag, turn)
-
-    sums_here[...] = jnp.zeros_like(sums_here)
-
-    def strip(at):
-        activated, slope = gelu_and_slope(acc[at, :cols] + theirs[at] + sp_ref[1:2])
-        mask = live[at]
-        other = act[at]
-        dy = [og[t, at].astype(jnp.float32) * mask for t in range(2)]
-        dz = slope * (sp_ref[3:4] * dy[0] + sp_ref[5:6] * dy[1])
-        for t in range(2):
-            y_here[t, at] = ((sp_ref[2 + 2 * t : 3 + 2 * t] * other + sp_ref[3 + 2 * t : 4 + 2 * t] * activated) * mask).astype(jnp.bfloat16)
-        dz_here[at] = dz.astype(jnp.bfloat16)
-        for n, term in enumerate((dz, activated * dy[0], activated * dy[1])):
-            sums_here[n] += fold(term)
-
-    def stage(k):
-        @pl.when(k < parts)
-        def _():
-            products.complete(k)
-
-        @pl.when(k > 0)
-        def _():
-            products.swap(k - 1).wait_recv()
-            loop(size // 16, lambda i: strip(pl.ds(pl.multiple_of((k - 1) * size + i * 16, 16), 16)))
-            backward.start(k - 1)
-    loop(parts + 1, stage)
-    keep_y = pltpu.make_async_copy(y_here, y_ref, l_sem.at[0])
-    keep_y.start()
-    sg_ref[...] = jnp.zeros_like(sg_ref)
-    for n in range(3):
-        sg_ref[2 * n + 1 : 2 * n + 2] = jnp.sum(sums_here[n], axis=0, keepdims=True)
-
-    def settle(q):
-        backward.settle(q)
-        products.swap(q).wait_send()
-        features.settle(q)
-    loop(parts, settle)
-    weights.settle()
-    gradients.settle()
-    grads.settle()
-    keep_y.wait()
 
 
 def first_loads(chips, wg, dz, w_here, dz_wide, sem):
@@ -1550,7 +1494,7 @@
         in_specs=[here if n in small_in else anywhere for n in range(len(operands))],
         out_specs=[here if n in small_out else anywhere for n in range(len(out))],
         scratch_shapes=scratch,
-        compiler_params=pltpu.CompilerParams(collective_id=ident, has_side_effects=True, vmem_limit_bytes=58 * 2**20),
+        compiler_params=pltpu.CompilerParams(collective_id=ident, has_side_effects=True, vmem_limit_bytes=62 * 2**20),
         cost_estimate=pl.CostEstimate(flops=flops, bytes_accessed=500 * 2**20, transcendentals=0),
         name=name,
     )(*operands)
@@ -1561,7 +1505,7 @@
     return max(n for n in range(1, rows // 16) if rows % (16 * n) == 0 and rows // n >= share[0][1])
 
 
-def shared_pass(features, weights, out_grad, count, small_params, left, right, chips, share):
+def shared_pass(features, weights, out_grad, counts, small_params, left, right, chips, share):
     parts = parts_of(share)
     towers, slots, depth = features.shape
     cols = weights.shape[2]
@@ -1572,29 +1516,22 @@
     dma, vmem = pltpu.SemaphoreType.DMA, pltpu.VMEM
     bf16, f32 = jnp.bfloat16, jnp.float32
     S = jax.ShapeDtypeStruct
-    told = jnp.broadcast_to(count.astype(f32), (8, depth))
-    flops = 2 * rows * 2 * cols * depth * chips
-    gathers = [dma((2, steps, parts))] * 2 + [dma((4, 2))] * 2
-    line = [dma((5,))] + [dma((parts,))] * 5
-    tiles = [vmem((2, rows, depth), bf16), vmem((2, depth, 2 * cols), bf16),
-             vmem((rows, 2 * cols), f32), vmem((rows, cols), f32), vmem((rows, cols), f32), vmem((rows, cols), f32), vmem((rows, cols), bf16)]
-    folded = vmem((3, 8, cols), f32)
-    wide = [S((rows, chips * depth), bf16), S((chips * depth, 2 * cols), bf16)]
-    *first, low, start, grad_here, dz, act, small_first, told, bases = call(
-        functools.partial(first_kernel, chips, parts, share), "first", 3,
-        wide + [S((2, depth, cols), bf16), S((piece, depth), bf16), S((towers, rows, cols), bf16), S((rows, 2 * cols), bf16), S((rows, cols), f32), S((8, cols), f32),
-                S((4, 8, depth), f32), S((2,) + left.shape[:2] + (2, left.shape[2] // 2 * BLOCK, 2 * BLOCK), bf16)],
-        [vmem((towers, 4, size, depth), bf16), vmem((towers, piece, depth), bf16), vmem((4, towers, size, cols), bf16), vmem((towers, rows, cols), bf16), vmem((2, depth // 4, cols), f32)]
-        + [vmem((2, depth, cols), bf16)] * 2 + tiles + [folded, vmem((4, 8, depth), f32), vmem((2, 2) + left.shape[2:], f32), vmem((2, 2, 2, left.shape[2] // 2 * BLOCK, 2 * BLOCK), bf16)] + gathers + [dma((2,))] + line
-        + [dma((4, 3)), dma((4, 3)), dma((11,)), dma((2, 2)), dma((2, 2))],
-        (features, weights, out_grad, told, small_params, left, right), (4,), (7,), flops)
-    *second, dz_second, result, small_second, d_first, gr_first, _, _ = call(
-        functools.partial(second_kernel, chips, parts, share), "second", 5,
-        wide + [S((rows, 2 * cols), bf16), S((towers, rows, cols), bf16), S((8, cols), f32)] + sums_out(slots, depth, cols),
-        [vmem((towers, rows, cols), bf16)] + tiles + [vmem((towers, rows, cols), bf16), folded] + sums_scratch(chips, rows, parts, depth, cols)
-        + gathers + line + [dma((chips + 5,))] + sums_dma(steps, parts),
-        (features, low, start, grad_here, told, act, small_params, *first, dz), (4, 6), (4,), 3 * flops)
-    return told, bases, (result, *second, dz_second, small_first + small_second), d_first, gr_first
+    beside = (left.shape[2] // 2 * BLOCK, 2 * BLOCK)
+    wide = [S((rows, chips * depth), bf16), S((chips * depth, 2 * cols), bf16), S((rows, 2 * cols), bf16)]
+    _, _, _, *second, result, small, told, bases, d_first, gr_first, _, _ = call(
+        functools.partial(front_kernel, chips, parts, share), "front", 3,
+        wide + wide + [S((towers, rows, cols), bf16), S((8, cols), f32), S((4, 8, depth), f32), S((2,) + left.shape[:2] + (2,) + beside, bf16)]
+        + sums_out(slots, depth, cols),
+        [vmem((towers, 4, size, depth), bf16), vmem((towers, piece, depth), bf16), vmem((4, towers, size, cols), bf16),
+         vmem((2, depth // 8, cols), f32), vmem((towers, 2, depth, cols), bf16), vmem((2, 2) + left.shape[2:], f32), vmem((2, 2, 2) + beside, bf16),
+         vmem((4, 8, depth), f32), vmem((towers, rows, cols), bf16), vmem((2, rows, depth), bf16), vmem((2, depth, 2 * cols), bf16),
+         vmem((rows, 2 * cols), f32), vmem((towers, rows, cols), f32), vmem((rows, cols), f32), vmem((rows, cols), f32), vmem((rows, cols), bf16),
+         vmem((towers, rows, cols), bf16), vmem((6, 8, cols), f32)] + sums_scratch(chips, rows, parts, depth, cols)
+        + [dma((towers, 2, steps, parts))] * 2 + [dma((towers, 4, 2))] * 2 + [dma((towers, parts))] * 5
+        + [dma((2,)), dma((towers, 5)), dma((4, 3)), dma((4, 3)), dma((12 + chips,)), dma((2, 2)), dma((2, 2))] + sums_dma(steps, parts),
+        (features, weights, out_grad, counts.reshape(1, -1), small_params, left, right), (3, 4), (7,), 5 * 2 * rows * 2 * cols * depth * chips)
+    wide_f, wide_w, wide_dz = second
+    return told, bases, (result, wide_f, wide_w, wide_dz, small), d_first, gr_first
 
 
 def sums_out(slots, depth, cols):
@@ -1699,7 +1636,7 @@
 ):
     keep, share = shares(features.shape[1])
     told, bases, passed, *first = shared_pass(
-        features, weights, out_grad, jnp.sum(counts), small_params, basis_left, basis_right, lax.axis_size("mp") // 2, share
+        features, weights, out_grad, counts, small_params, basis_left, basis_right, lax.axis_size("mp") // 2, share
     )
     totals = told[:, 0, 0]
     return lax.cond(

time: 578 us -> 568 us (0.983)
  Pallas kernels: 552 us -> 544 us
    pallas_call x3 -> x2, Pallas kernels: 486 us -> 481 us  [call(): pl.pallas_call(kernel, out_shape=out, in_specs=[here if n in small_in els...]
where the time goes in v8:
time: 568 us; the launch traced here: 562 us
  Pallas kernels  544 us (96%)
  between operations  14.8 us (3%)
    pallas_call x2, Pallas kernels, call(): pl.pallas_call(kernel, out_shape=out, in_specs=[here if n in small_in els...  481 us
    pallas_call x1, Pallas kernels, soap(): pl.pallas_call(functools.partial(soap_body, group, strips), grid=(towers,...  63 us

profile of v8, /device:TPU:17, one launch (start us, length us, event | category | flops | bytes accessed | tf_op | source)
XLA Modules:
  0.0 562.5 jit_solution(16851289248286006165)
XLA Ops:
  7.2 0.0 copy-start.2
  7.2 0.0 copy-start.3
  7.2 0.0 copy-start.6
  7.2 0.0 copy-start.9
  7.2 309.0 %front.1 = (bf16[768,4608]{1,0:T(8,128)(2,1)}, bf16[4608,1024]{1,0:T(8,128)(2,1)}, bf16[768,1024]{1,0:T(8,128)(2,1)}, bf16[768,4608]{1,0:T(8,128)(2,1)}, bf16[46...) custom-call(bf16[2,1280,1152]{2,1,0:T(8,128)(2,1)} %f_ref.1, ...), custom_call_target="tpu_custom_call" | custom-call | flops 36238786560 | bytes 524288000 | tf_op jit(solution)/shard_map/front/pallas_call | solution.py:1491
  316.2 0.8 slice_reduce_fusion
  317.0 0.6 fusion.13
  318.3 0.0 copy-done.2
  318.3 0.0 copy-done.3
  318.3 0.0 copy-done.6
  318.3 0.0 copy-done.9
  318.3 237.3 %conditional.1 = (bf16[2,1280,4096]{2,1,0:T(8,128)(2,1)}, bf16[2,1280,1152]{2,1,0:T(8,128)(2,1)}, f32[2,2304,512]{2,1,0:T(8,128)}, f32[2,2304,512]{2,1,0:T(8,128...) conditional(s32[]{:T(128)} %convert_element_type.34, ...), branch_computations={%region_1.8_spmd, %region_8.10_spmd} | conditional | flops 74991869952 | bytes 2267896832 | solution.py:1642
  318.6 172.5 %third.1 = (bf16[2,1280,4096]{2,1,0:T(8,128)(2,1)}, bf16[1280,1152]{1,0:T(8,128)(2,1)}, bf16[3,2,1152,512]{3,2,1,0:T(8,128)(2,1)}, f32[4,8,512]{2,1,0:T(8,128)},...) custom-call(bf16[2,768,512]{2,1,0:T(8,128)(2,1)} %get-tuple-element.84.y_ref, ...), custom_call_target="tpu_custom_call" | custom-call | flops 14495514624 | bytes 524288000 | tf_op jit(solution)/shard_map/cond/branch_1_fun/third/pallas_call | solution.py:1491
  491.1 0.9 reduce_sum.65
  492.0 0.6 add_multiply_fusion.1
  492.6 63.0 %soap.3 = (f32[2,2304,512]{2,1,0:T(8,128)}, f32[2,2304,512]{2,1,0:T(8,128)}, f32[2,2304,512]{2,1,0:T(8,128)}, f32[2,2304,512]{2,1,0:T(8,128)}, bf16[2,2304,512]{...) custom-call(s32[1]{0:T(128)S(6)} %select_n.3.full, ...), custom_call_target="tpu_custom_call" | custom-call | flops 2415919104 | bytes 136314880 | tf_op jit(solution)/shard_map/cond/branch_1_fun/soap/pallas_call | solution.py:135
Async XLA Ops:
  7.2 311.1 %copy-start.2 = (f32[6,512]{1,0:T(8,128)S(1)}, f32[6,512]{1,0:T(8,128)}, u32[]{:S(2)}) copy-start(f32[6,512]{1,0:T(8,128)} %sp_ref.1) | copy-start | bytes 36868
  7.2 311.1 %copy-start.3 = (f32[6,512]{1,0:T(8,128)S(1)}, f32[6,512]{1,0:T(8,128)}, u32[]{:S(2)}) copy-start(f32[6,512]{1,0:T(8,128)} %param.25) | copy-start | bytes 36868
  7.2 311.1 %copy-start.6 = (f32[6,512]{1,0:T(8,128)S(1)}, f32[6,512]{1,0:T(8,128)}, u32[]{:S(2)}) copy-start(f32[6,512]{1,0:T(8,128)} %param.26) | copy-start | bytes 36868
  7.2 311.1 %copy-start.9 = (f32[6,512]{1,0:T(8,128)S(1)}, f32[6,512]{1,0:T(8,128)}, u32[]{:S(2)}) copy-start(f32[6,512]{1,0:T(8,128)} %param.27) | copy-start | bytes 36868

commit v9 on v8

--- a/solution.py
+++ b/solution.py
@@ -1051,6 +1051,8 @@
         loop(self.turns, drain)
         for piece in (self.parts - 2, self.parts - 1):
             self.store(piece).wait()
+
+    def returned(self):
         for kind in range(3):
             self.hand(kind).wait_recv()
 
@@ -1236,13 +1238,15 @@
 
 
 def front_kernel(chips, parts, share, f_ref, w_ref, o_ref, n_ref, sp_ref, left_ref, right_ref,
-                 fg_first, wg_first, dz_first, fg_ref, wg_ref, dz_ref, y_ref, sg_ref, tot_ref, bases_ref, d_ref, gr_ref, pg_ref, relay_ref,
+                 fg_first, wg_first, dz_first, fg_ref, wg_ref, dz_ref, tot_ref, bases_ref, st_ref, sr_ref,
+                 d_first, gr_first, pg_first, relay_first, d_ref, gr_ref, pg_ref, relay_ref,
                  offer_f, taken, offer_o, wide, low, base_in, base_out, tot,
-                 og, f_tile, w_tile, acc, theirs, live, act, dz_here, y_here, sums_here,
+                 og, f_tile, w_tile, acc, theirs, live, act, dz_here, y_here, sums_here, sg,
                  held, w_here, dz_wide, total, f_part, g_part, r_part,
                  f_send, f_recv, w_send, w_recv, a_send, a_recv, z_send, z_recv, out_sem,
                  wide_sem, p_sem, x_send, x_recv, l_sem, base_load, base_store,
-                 d_send, d_recv, o_sem, b_send, b_recv, g_load, g_send, g_recv, rs_send, rs_recv, own_sem):
+                 d_send, d_recv, o_sem, b_send, b_recv, g_load, g_send, g_recv, rs_send, rs_recv, own_sem, s_send, s_recv, ready,
+                 y_send, y_recv, core_send, core_recv, give_send, give_recv, given_send, given_recv, y_own):
     spot = Spot(chips)
     keep, rows = share[0][0], sum(share[0])
     size = rows // parts
@@ -1286,9 +1290,13 @@
         backward = Backward(spot, size, dz_here, dz, z_send.at[t], z_recv.at[t], out_sem.at[t])
         towers.append((features, weights, products, backward))
     features, weights, products, backward = towers[0]
-    gradients = Sums(spot, parts, share, d_ref, dz_wide, w_here, held, total, d_send, d_recv, o_sem, b_send, b_recv)
-    grads = Grads(spot, fg_first, dz_wide, gr_ref, pg_ref, relay_ref, f_part, g_part, r_part, g_load.at[0], g_load.at[1], g_load.at[2],
-                  g_send, g_recv, rs_send, rs_recv, own_sem)
+    sums = []
+    for t, (fg, d, gr, pg, relay) in enumerate(((fg_first, d_first, gr_first, pg_first, relay_first), (fg_ref, d_ref, gr_ref, pg_ref, relay_ref))):
+        sums.append((Sums(spot, parts, share, d, dz_wide, w_here, held, total, d_send.at[t], d_recv.at[t], o_sem, b_send.at[t], b_recv.at[t]),
+                     Grads(spot, fg, dz_wide, gr, pg, relay, f_part, g_part, r_part, g_load.at[0], g_load.at[1], g_load.at[2],
+                           g_send.at[t], g_recv.at[t], rs_send.at[t], rs_recv.at[t], own_sem.at[t])))
+    gradients, grads = sums[0]
+    stitched = Stitched(spot, share, y_here, st_ref, y_send, y_recv, core_send, core_recv, give_send, give_recv, given_send, given_recv, y_own)
     bases = Bases(left_ref, right_ref, bases_ref, base_in, base_out, base_load, base_store)
 
     def copy(n, src, dst):
@@ -1383,7 +1391,8 @@
         offer(kind, 1).wait_recv()
     take(1)
     loop(parts, lambda q: settle(0, q))
-    loads = first_loads(chips, wg_first, dz_first, w_here, dz_wide, l_sem.at[pl.ds(11, chips + 1)])
+    loads = weight_loads(chips, wg_first, w_here, l_sem.at[pl.ds(11, chips)])
+    loads.append(copy(11 + chips, dz_first, dz_wide))
     features, weights, products, backward = towers[1]
     loop(parts - 1, lambda q: features.launch(q, False))
     features.launch(parts - 1, True)
@@ -1405,94 +1414,89 @@
         def _():
             features.serve(0, m - 2)
 
-        @pl.when((m >= 4 + parts) & (m < 4 + 2 * parts))
-        def _():
-            features.serve(1, m - 4 - parts)
-
-        @pl.when(m == 4 + 2 * parts)
+        @pl.when((m >= 3 + parts) & (m < 3 + 2 * parts))
+        def _():
+            features.serve(1, m - 3 - parts)
+
+        @pl.when(m == 3 + 2 * parts)
         def _():
             weights.finish()
             last.wait()
             products.multiply()
         gradients.turn_end(m)
     loop(gradients.turns + gradients.lag, turn)
+
+    gradients.settle()
+
+    def neighbours(method):
+        for side, here, chip in ((0, spot.chip > 0, spot.chip - 1), (1, spot.chip < spot.steps, spot.chip + 1)):
+            @pl.when(here)
+            def _():
+                method(side, chip)
+    neighbours(lambda side, chip: pl.semaphore_signal(ready.at[1 - side], inc=1, device_id=spot.on_line(chip), device_id_type=MESH))
+    loads = weight_loads(chips, wg_ref, w_here, l_sem.at[pl.ds(11, chips)])
     loop(parts + 1, lambda k: stage(1, k))
-    last = copy(0, y_here, y_ref)
-    sg_ref[...] = jnp.zeros_like(sg_ref)
+    stitched.start()
+    sg[...] = jnp.zeros_like(sg)
     for n in range(6):
-        sg_ref[n : n + 1] = jnp.sum(sums_here[n], axis=0, keepdims=True)
+        sg[n : n + 1] = jnp.sum(sums_here[n], axis=0, keepdims=True)
+    own = copy(1, sg, sr_ref.at[spot.dp])
+
+    def small(kind):
+        return pltpu.make_async_remote_copy(
+            src_ref=sg, dst_ref=sr_ref.at[spot.dp], send_sem=s_send.at[kind], recv_sem=s_recv.at[kind],
+            device_id=spot.at(spot.others[kind], spot.core), device_id_type=MESH)
+    for kind in range(3):
+        small(kind).start()
     loop(parts, lambda q: settle(1, q))
+    wide_dz = copy(11 + chips, dz_ref, dz_wide)
+    gradients, grads = sums[1]
+    grads.load(jnp.int32(0)).start()
+    for made in loads:
+        made.wait()
+    wide_dz.wait()
+    neighbours(lambda side, chip: pl.semaphore_wait(ready.at[side], 1))
+
+    def second_turn(m):
+        gradients.turn(m)
+        grads.turn(m, 0, 7)
+
+        @pl.when((m >= 1) & (m <= stitched.events))
+        def _():
+            stitched.event(m - 1)
+        gradients.turn_end(m)
+    loop(gradients.turns + gradients.lag, second_turn)
+    stitched.receive()
+    gradients.settle()
+    stitched.settle()
     for t in range(2):
+        sums[t][0].returned()
+        sums[t][1].settle()
         towers[t][1].settle()
-    gradients.settle()
-    grads.settle()
     bases.settle()
-    last.wait()
+    own.wait()
+    for kind in range(3):
+        small(kind).wait()
     for what in range(4):
         for kind in range(3):
             offer(kind, what).wait_send()
 
 
-def first_loads(chips, wg, dz, w_here, dz_wide, sem):
+def weight_loads(chips, wg, w_here, sem):
     depth = w_here.shape[1]
-    loads = [pltpu.make_async_copy(dz, dz_wide, sem.at[chips])]
-    loads += [pltpu.make_async_copy(wg.at[pl.ds(n * depth, depth)], w_here.at[n], sem.at[n]) for n in range(chips)]
+    loads = [pltpu.make_async_copy(wg.at[pl.ds(n * depth, depth)], w_here.at[n], sem.at[n]) for n in range(chips)]
     for copy in loads:
         copy.start()
     return loads
 
 
-def third_kernel(chips, parts, share, y_ref, fg_ref, wg_ref, dz_ref, ps_ref, st_ref, d_ref, gr_ref, sr_ref, pg_ref, relay_ref,
-                 held, w_here, dz_wide, total, f_part, g_part, r_part, l_sem,
-                 d_send, d_recv, o_sem, b_send, b_recv, g_load, g_send, g_recv, rs_send, rs_recv, own_sem, s_send, s_recv,
-                 y_send, y_recv, core_send, core_recv, give_send, give_recv, given_send, given_recv, y_own):
-    spot = Spot(chips)
-    spot.greet()
-    gradients = Sums(spot, parts, share, d_ref, dz_wide, w_here, held, total, d_send, d_recv, o_sem, b_send, b_recv)
-    grads = Grads(spot, fg_ref, dz_wide, gr_ref, pg_ref, relay_ref, f_part, g_part, r_part, g_load.at[0], g_load.at[1], g_load.at[2],
-                  g_send, g_recv, rs_send, rs_recv, own_sem)
-    stitched = Stitched(spot, share, y_ref, st_ref, y_send, y_recv, core_send, core_recv, give_send, give_recv, given_send, given_recv, y_own)
-
-    def small(kind):
-        return pltpu.make_async_remote_copy(
-            src_ref=ps_ref, dst_ref=sr_ref.at[spot.dp], send_sem=s_send.at[kind], recv_sem=s_recv.at[kind],
-            device_id=spot.at(spot.others[kind], spot.core), device_id_type=MESH)
-
-    loads = first_loads(chips, wg_ref, dz_ref, w_here, dz_wide, l_sem)
-    grads.load(jnp.int32(0)).start()
-    stitched.start()
-    own = pltpu.make_async_copy(ps_ref, sr_ref.at[spot.dp], l_sem.at[chips + 1])
-    own.start()
-    for kind in range(3):
-        small(kind).start()
-    for copy in loads:
-        copy.wait()
-
-    def turn(m):
-        gradients.turn(m)
-        grads.turn(m, 0, 8)
-
-        @pl.when((m >= 1) & (m <= stitched.events))
-        def _():
-            stitched.event(m - 1)
-        gradients.turn_end(m)
-    loop(gradients.turns + gradients.lag, turn)
-    stitched.receive()
-    gradients.settle()
-    stitched.settle()
-    grads.settle()
-    for kind in range(3):
-        small(kind).wait()
-    own.wait()
-
-
-def call(kernel, name, ident, out, scratch, operands, small_in=(), small_out=(), flops=0):
+def call(kernel, name, ident, out, scratch, operands, small_in=(), flops=0):
     anywhere, here = pl.BlockSpec(memory_space=pl.ANY), pl.BlockSpec(memory_space=pltpu.VMEM)
     return pl.pallas_call(
         kernel,
         out_shape=out,
         in_specs=[here if n in small_in else anywhere for n in range(len(operands))],
-        out_specs=[here if n in small_out else anywhere for n in range(len(out))],
+        out_specs=[anywhere] * len(out),
         scratch_shapes=scratch,
         compiler_params=pltpu.CompilerParams(collective_id=ident, has_side_effects=True, vmem_limit_bytes=62 * 2**20),
         cost_estimate=pl.CostEstimate(flops=flops, bytes_accessed=500 * 2**20, transcendentals=0),
@@ -1518,52 +1522,26 @@
     S = jax.ShapeDtypeStruct
     beside = (left.shape[2] // 2 * BLOCK, 2 * BLOCK)
     wide = [S((rows, chips * depth), bf16), S((chips * depth, 2 * cols), bf16), S((rows, 2 * cols), bf16)]
-    _, _, _, *second, result, small, told, bases, d_first, gr_first, _, _ = call(
-        functools.partial(front_kernel, chips, parts, share), "front", 3,
-        wide + wide + [S((towers, rows, cols), bf16), S((8, cols), f32), S((4, 8, depth), f32), S((2,) + left.shape[:2] + (2,) + beside, bf16)]
-        + sums_out(slots, depth, cols),
+    sums = [S((slots, depth), bf16), S((3, 2, depth, cols), bf16), S((8, depth, cols), bf16), S((2, depth, cols), bf16)]
+    out = call(
+        functools.partial(front_kernel, chips, parts, share), "passes", 3,
+        wide + wide + [S((4, 8, depth), f32), S((2,) + left.shape[:2] + (2,) + beside, bf16),
+                       S((towers, slots, 2 * chips * cols), bf16), S((4, 8, cols), f32)] + sums + sums,
         [vmem((towers, 4, size, depth), bf16), vmem((towers, piece, depth), bf16), vmem((4, towers, size, cols), bf16),
          vmem((2, depth // 8, cols), f32), vmem((towers, 2, depth, cols), bf16), vmem((2, 2) + left.shape[2:], f32), vmem((2, 2, 2) + beside, bf16),
          vmem((4, 8, depth), f32), vmem((towers, rows, cols), bf16), vmem((2, rows, depth), bf16), vmem((2, depth, 2 * cols), bf16),
          vmem((rows, 2 * cols), f32), vmem((towers, rows, cols), f32), vmem((rows, cols), f32), vmem((rows, cols), f32), vmem((rows, cols), bf16),
-         vmem((towers, rows, cols), bf16), vmem((6, 8, cols), f32)] + sums_scratch(chips, rows, parts, depth, cols)
+         vmem((towers, rows, cols), bf16), vmem((6, 8, cols), f32), vmem((8, cols), f32),
+         vmem((2, steps, rows, depth), bf16), vmem((chips, depth, 2 * cols), bf16), vmem((rows, 2 * cols), bf16),
+         vmem((2, piece, depth), bf16), vmem((2, rows, depth // 3), bf16)] + [vmem((2, depth // 3, cols), bf16)] * 2
         + [dma((towers, 2, steps, parts))] * 2 + [dma((towers, 4, 2))] * 2 + [dma((towers, parts))] * 5
-        + [dma((2,)), dma((towers, 5)), dma((4, 3)), dma((4, 3)), dma((12 + chips,)), dma((2, 2)), dma((2, 2))] + sums_dma(steps, parts),
-        (features, weights, out_grad, counts.reshape(1, -1), small_params, left, right), (3, 4), (7,), 5 * 2 * rows * 2 * cols * depth * chips)
-    wide_f, wide_w, wide_dz = second
-    return told, bases, (result, wide_f, wide_w, wide_dz, small), d_first, gr_first
-
-
-def sums_out(slots, depth, cols):
-    S, bf16 = jax.ShapeDtypeStruct, jnp.bfloat16
-    return [S((slots, depth), bf16), S((3, 2, depth, cols), bf16), S((8, depth, cols), bf16), S((2, depth, cols), bf16)]
-
-
-def sums_scratch(chips, rows, parts, depth, cols):
-    vmem, bf16 = pltpu.VMEM, jnp.bfloat16
-    return [vmem((2, chips - 1, rows, depth), bf16), vmem((chips, depth, 2 * cols), bf16), vmem((rows, 2 * cols), bf16),
-            vmem((2, rows // parts, depth), bf16), vmem((2, rows, depth // 3), bf16)] + [vmem((2, depth // 3, cols), bf16)] * 2
-
-
-def sums_dma(steps, parts):
-    dma = pltpu.SemaphoreType.DMA
-    return [dma((2, steps * parts))] * 2 + [dma((2,)), dma((3,)), dma((3,)), dma((3, 2)), dma((8,)), dma((3, 2)), dma((2,)), dma((2,)), dma(())]
-
-
-def shared_sums(result, wide_f, wide_w, wide_dz, partial_s, slots, chips, share):
-    parts = parts_of(share)
-    towers, rows, cols = result.shape
-    depth, steps = wide_w.shape[0] // chips, chips - 1
-    dma = pltpu.SemaphoreType.DMA
-    S = jax.ShapeDtypeStruct
-    stitched, d_feat, grad_parts, smalls, _, _ = call(
-        functools.partial(third_kernel, chips, parts, share), "third", 4,
-        [S((towers, slots, 2 * chips * cols), jnp.bfloat16)] + sums_out(slots, depth, cols)[:2] + [S((4,) + partial_s.shape, jnp.float32)]
-        + sums_out(slots, depth, cols)[2:],
-        sums_scratch(chips, rows, parts, depth, cols) + [dma((chips + 2,))] + sums_dma(steps, parts) + [dma((3,))] * 2
+        + [dma((2,)), dma((towers, 5)), dma((4, 3)), dma((4, 3)), dma((12 + chips,)), dma((2, 2)), dma((2, 2))]
+        + [dma((towers, 2, steps * parts))] * 2 + [dma((2,)), dma((towers, 3)), dma((towers, 3)), dma((3, 2)), dma((towers, 8)), dma((towers, 3, 2)),
+                                                   dma((towers, 2)), dma((towers, 2)), dma((towers,)), dma((3,)), dma((3,)), pltpu.SemaphoreType.REGULAR((2,))]
         + [dma((2, steps, 2, towers))] * 2 + [dma((chips, 2, towers))] * 2 + [dma((3, chips, towers))] * 4 + [dma((2, towers))],
-        (result, wide_f, wide_w, wide_dz, partial_s), flops=4 * rows * 2 * cols * depth * chips)
-    return stitched, d_feat, grad_parts, smalls
+        (features, weights, out_grad, counts.reshape(1, -1), small_params, left, right), (3, 4), 6 * 2 * rows * 2 * cols * depth * chips)
+    told, bases, stitched, smalls, d_first, gr_first, _, _, d_second, gr_second, _, _ = out[6:]
+    return told, bases, ((d_first, d_second), stitched, (gr_first, gr_second), smalls)
 
 
 def small_step(small_params, small_moment_one, small_moment_two, small_average, small_grad):
@@ -1578,7 +1556,7 @@
     return (stitched, d_feat) + tuple(fresh) + small_step(*small_states, small_grad)
 
 
-def own_rows(features, out_grad, totals, passed, first, states, small_states):
+def own_rows(features, out_grad, totals, passed, states, small_states):
     _, rows, _ = features.shape
     weights, small_params = states[0], small_states[0]
     cols = weights.shape[2]
@@ -1610,13 +1588,12 @@
     return keep, ((keep, size), (keep + size, size), (keep + 2 * size, size), (rows - size, size))
 
 
-def shared_rows(features, out_grad, totals, passed, first, states, small_states):
+def shared_rows(features, out_grad, totals, passed, states, small_states):
     rows = features.shape[1]
-    keep, share = shares(rows)
-    d_first, gr_first = first
+    keep, _ = shares(rows)
+    d_feat, stitched, parts, small_parts = passed
     full = jnp.where(totals[:1] > keep, rows, keep)
-    stitched, d_second, gr_second, small_parts = shared_sums(*passed, rows, lax.axis_size("mp") // 2, share)
-    return update((d_first, d_second), stitched, full, (gr_first, gr_second), small_parts, states, small_states)
+    return update(d_feat, stitched, full, parts, small_parts, states, small_states)
 
 
 def line_body(
@@ -1635,7 +1612,7 @@
     small_average,
 ):
     keep, share = shares(features.shape[1])
-    told, bases, passed, *first = shared_pass(
+    told, bases, passed = shared_pass(
         features, weights, out_grad, counts, small_params, basis_left, basis_right, lax.axis_size("mp") // 2, share
     )
     totals = told[:, 0, 0]
@@ -1647,7 +1624,6 @@
         out_grad,
         totals,
         passed,
-        first,
         (weights, moment_one, moment_two, average, bases),
         (small_params, small_moment_one, small_moment_two, small_average),
     )

time: 568 us -> 570 us (level)
    pallas_call x2 -> x1, Pallas kernels: 481 us -> 485 us  [call(): pl.pallas_call(kernel, out_shape=out, in_specs=[here if n in small_in els...]
where the time goes in v9:
time: 570 us; the launch traced here: 565 us
  Pallas kernels  548 us (96%)
  between operations  14.8 us (3%)
    pallas_call x1, Pallas kernels, call(): pl.pallas_call(kernel, out_shape=out, in_specs=[here if n in small_in els...  485 us
    pallas_call x1, Pallas kernels, soap(): pl.pallas_call(functools.partial(soap_body, group, strips), grid=(towers,...  63 us

profile of v9, /device:TPU:17, one launch (start us, length us, event | category | flops | bytes accessed | tf_op | source)
XLA Modules:
  0.0 565.1 jit_solution(7516192071107187451)
XLA Ops:
  7.2 0.0 copy-start.2
  7.2 0.0 copy-start.3
  7.2 0.0 copy-start.6
  7.2 0.0 copy-start.9
  7.2 484.9 %passes.1 = (bf16[768,4608]{1,0:T(8,128)(2,1)}, bf16[4608,1024]{1,0:T(8,128)(2,1)}, bf16[768,1024]{1,0:T(8,128)(2,1)}, bf16[768,4608]{1,0:T(8,128)(2,1)}, bf16[4...) custom-call(bf16[2,1280,1152]{2,1,0:T(8,128)(2,1)} %f_ref.1, ...), custom_call_target="tpu_custom_call" | custom-call | flops 43486543872 | bytes 524288000 | tf_op jit(solution)/shard_map/passes/pallas_call | solution.py:1495
  492.1 0.8 slice_reduce_fusion
  492.9 0.6 fusion.13
  494.2 0.0 copy-done.2
  494.2 0.0 copy-done.3
  494.3 0.0 copy-done.6
  494.3 0.0 copy-done.9
  494.3 64.0 %conditional.1 = (bf16[2,1280,4096]{2,1,0:T(8,128)(2,1)}, bf16[2,1280,1152]{2,1,0:T(8,128)(2,1)}, f32[2,2304,512]{2,1,0:T(8,128)}, f32[2,2304,512]{2,1,0:T(8,128...) conditional(s32[]{:T(128)} %convert_element_type.34, ...), branch_computations={%region_1.8_spmd, %region_8.10_spmd} | conditional | flops 74991869952 | bytes 2267896832 | solution.py:1619
  494.6 0.6 add_multiply_fusion.1
  495.2 63.0 %soap.3 = (f32[2,2304,512]{2,1,0:T(8,128)}, f32[2,2304,512]{2,1,0:T(8,128)}, f32[2,2304,512]{2,1,0:T(8,128)}, f32[2,2304,512]{2,1,0:T(8,128)}, bf16[2,2304,512]{...) custom-call(s32[1]{0:T(128)S(6)} %select_n.3.full, ...), custom_call_target="tpu_custom_call" | custom-call | flops 2415919104 | bytes 136314880 | tf_op jit(solution)/shard_map/cond/branch_1_fun/soap/pallas_call | solution.py:135
  (1 shorter events, 0.0 us)
Async XLA Ops:
  7.2 487.1 %copy-start.2 = (f32[6,512]{1,0:T(8,128)S(1)}, f32[6,512]{1,0:T(8,128)}, u32[]{:S(2)}) copy-start(f32[6,512]{1,0:T(8,128)} %sp_ref.1) | copy-start | bytes 36868
  7.2 487.1 %copy-start.3 = (f32[6,512]{1,0:T(8,128)S(1)}, f32[6,512]{1,0:T(8,128)}, u32[]{:S(2)}) copy-start(f32[6,512]{1,0:T(8,128)} %param.25) | copy-start | bytes 36868
  7.2 487.1 %copy-start.6 = (f32[6,512]{1,0:T(8,128)S(1)}, f32[6,512]{1,0:T(8,128)}, u32[]{:S(2)}) copy-start(f32[6,512]{1,0:T(8,128)} %param.26) | copy-start | bytes 36868
  7.2 487.1 %copy-start.9 = (f32[6,512]{1,0:T(8,128)S(1)}, f32[6,512]{1,0:T(8,128)}, u32[]{:S(2)}) copy-start(f32[6,512]{1,0:T(8,128)} %param.27) | copy-start | bytes 36868

commit v10 on v9

--- a/solution.py
+++ b/solution.py
@@ -1414,11 +1414,11 @@
         def _():
             features.serve(0, m - 2)
 
-        @pl.when((m >= 3 + parts) & (m < 3 + 2 * parts))
-        def _():
-            features.serve(1, m - 3 - parts)
-
-        @pl.when(m == 3 + 2 * parts)
+        @pl.when((m >= 4 + parts) & (m < 4 + 2 * parts))
+        def _():
+            features.serve(1, m - 4 - parts)
+
+        @pl.when(m == 4 + 2 * parts)
         def _():
             weights.finish()
             last.wait()

time: 570 us -> 560 us (0.982)
  Pallas kernels: 548 us -> 537 us
    pallas_call x1, Pallas kernels: 485 us -> 474 us  [call(): pl.pallas_call(kernel, out_shape=out, in_specs=[here if n in small_in els...]
where the time goes in v10:
time: 560 us; the launch traced here: 554 us
  Pallas kernels  537 us (96%)
  between operations  14.8 us (3%)
    pallas_call x1, Pallas kernels, call(): pl.pallas_call(kernel, out_shape=out, in_specs=[here if n in small_in els...  474 us
    pallas_call x1, Pallas kernels, soap(): pl.pallas_call(functools.partial(soap_body, group, strips), grid=(towers,...  63 us

profile of v10, /device:TPU:17, one launch (start us, length us, event | category | flops | bytes accessed | tf_op | source)
XLA Modules:
  0.0 554.2 jit_solution(17647098577444965199)
XLA Ops:
  7.2 0.0 copy-start.2
  7.2 0.0 copy-start.3
  7.2 0.0 copy-start.6
  7.2 0.0 copy-start.9
  7.2 474.0 %passes.1 = (bf16[768,4608]{1,0:T(8,128)(2,1)}, bf16[4608,1024]{1,0:T(8,128)(2,1)}, bf16[768,1024]{1,0:T(8,128)(2,1)}, bf16[768,4608]{1,0:T(8,128)(2,1)}, bf16[4...) custom-call(bf16[2,1280,1152]{2,1,0:T(8,128)(2,1)} %f_ref.1, ...), custom_call_target="tpu_custom_call" | custom-call | flops 43486543872 | bytes 524288000 | tf_op jit(solution)/shard_map/passes/pallas_call | solution.py:1495
  481.2 0.8 slice_reduce_fusion
  482.0 0.6 fusion.13
  483.3 0.0 copy-done.2
  483.3 0.0 copy-done.3
  483.4 0.0 copy-done.6
  483.4 0.0 copy-done.9
  483.4 64.0 %conditional.1 = (bf16[2,1280,4096]{2,1,0:T(8,128)(2,1)}, bf16[2,1280,1152]{2,1,0:T(8,128)(2,1)}, f32[2,2304,512]{2,1,0:T(8,128)}, f32[2,2304,512]{2,1,0:T(8,128...) conditional(s32[]{:T(128)} %convert_element_type.34, ...), branch_computations={%region_1.8_spmd, %region_8.10_spmd} | conditional | flops 74991869952 | bytes 2267896832 | solution.py:1619
  483.7 0.6 add_multiply_fusion.1
  484.3 63.0 %soap.3 = (f32[2,2304,512]{2,1,0:T(8,128)}, f32[2,2304,512]{2,1,0:T(8,128)}, f32[2,2304,512]{2,1,0:T(8,128)}, f32[2,2304,512]{2,1,0:T(8,128)}, bf16[2,2304,512]{...) custom-call(s32[1]{0:T(128)S(6)} %select_n.3.full, ...), custom_call_target="tpu_custom_call" | custom-call | flops 2415919104 | bytes 136314880 | tf_op jit(solution)/shard_map/cond/branch_1_fun/soap/pallas_call | solution.py:135
  (1 shorter events, 0.0 us)
Async XLA Ops:
  7.2 476.2 %copy-start.2 = (f32[6,512]{1,0:T(8,128)S(1)}, f32[6,512]{1,0:T(8,128)}, u32[]{:S(2)}) copy-start(f32[6,512]{1,0:T(8,128)} %sp_ref.1) | copy-start | bytes 36868
  7.2 476.2 %copy-start.3 = (f32[6,512]{1,0:T(8,128)S(1)}, f32[6,512]{1,0:T(8,128)}, u32[]{:S(2)}) copy-start(f32[6,512]{1,0:T(8,128)} %param.25) | copy-start | bytes 36868
  7.2 476.2 %copy-start.6 = (f32[6,512]{1,0:T(8,128)S(1)}, f32[6,512]{1,0:T(8,128)}, u32[]{:S(2)}) copy-start(f32[6,512]{1,0:T(8,128)} %param.26) | copy-start | bytes 36868
  7.2 476.2 %copy-start.9 = (f32[6,512]{1,0:T(8,128)S(1)}, f32[6,512]{1,0:T(8,128)}, u32[]{:S(2)}) copy-start(f32[6,512]{1,0:T(8,128)} %param.27) | copy-start | bytes 36868

commit v11 on v9

--- a/solution.py
+++ b/solution.py
@@ -1418,7 +1418,7 @@
         def _():
             features.serve(1, m - 3 - parts)
 
-        @pl.when(m == 3 + 2 * parts)
+        @pl.when(m == 4 + 2 * parts)
         def _():
             weights.finish()
             last.wait()

time: 570 us -> 558 us (0.979)
  Pallas kernels: 548 us -> 536 us
    pallas_call x1, Pallas kernels: 485 us -> 473 us  [call(): pl.pallas_call(kernel, out_shape=out, in_specs=[here if n in small_in els...]
where the time goes in v11:
time: 558 us; the launch traced here: 553 us
  Pallas kernels  536 us (96%)
  between operations  14.8 us (3%)
    pallas_call x1, Pallas kernels, call(): pl.pallas_call(kernel, out_shape=out, in_specs=[here if n in small_in els...  473 us
    pallas_call x1, Pallas kernels, soap(): pl.pallas_call(functools.partial(soap_body, group, strips), grid=(towers,...  63 us

profile of v11, /device:TPU:17, one launch (start us, length us, event | category | flops | bytes accessed | tf_op | source)
XLA Modules:
  0.0 553.0 jit_solution(15002316218774858685)
XLA Ops:
  7.2 0.0 copy-start.2
  7.2 0.0 copy-start.3
  7.2 0.0 copy-start.6
  7.2 0.0 copy-start.9
  7.2 472.8 %passes.1 = (bf16[768,4608]{1,0:T(8,128)(2,1)}, bf16[4608,1024]{1,0:T(8,128)(2,1)}, bf16[768,1024]{1,0:T(8,128)(2,1)}, bf16[768,4608]{1,0:T(8,128)(2,1)}, bf16[4...) custom-call(bf16[2,1280,1152]{2,1,0:T(8,128)(2,1)} %f_ref.1, ...), custom_call_target="tpu_custom_call" | custom-call | flops 43486543872 | bytes 524288000 | tf_op jit(solution)/shard_map/passes/pallas_call | solution.py:1495
  480.1 0.8 slice_reduce_fusion
  480.9 0.6 fusion.13
  482.2 0.0 copy-done.2
  482.2 0.0 copy-done.3
  482.2 0.0 copy-done.6
  482.2 0.0 copy-done.9
  482.2 64.0 %conditional.1 = (bf16[2,1280,4096]{2,1,0:T(8,128)(2,1)}, bf16[2,1280,1152]{2,1,0:T(8,128)(2,1)}, f32[2,2304,512]{2,1,0:T(8,128)}, f32[2,2304,512]{2,1,0:T(8,128...) conditional(s32[]{:T(128)} %convert_element_type.34, ...), branch_computations={%region_1.8_spmd, %region_8.10_spmd} | conditional | flops 74991869952 | bytes 2267896832 | solution.py:1619
  482.5 0.6 add_multiply_fusion.1
  483.2 63.0 %soap.3 = (f32[2,2304,512]{2,1,0:T(8,128)}, f32[2,2304,512]{2,1,0:T(8,128)}, f32[2,2304,512]{2,1,0:T(8,128)}, f32[2,2304,512]{2,1,0:T(8,128)}, bf16[2,2304,512]{...) custom-call(s32[1]{0:T(128)S(6)} %select_n.3.full, ...), custom_call_target="tpu_custom_call" | custom-call | flops 2415919104 | bytes 136314880 | tf_op jit(solution)/shard_map/cond/branch_1_fun/soap/pallas_call | solution.py:135
  (1 shorter events, 0.0 us)
Async XLA Ops:
  7.2 475.0 %copy-start.2 = (f32[6,512]{1,0:T(8,128)S(1)}, f32[6,512]{1,0:T(8,128)}, u32[]{:S(2)}) copy-start(f32[6,512]{1,0:T(8,128)} %sp_ref.1) | copy-start | bytes 36868
  7.2 475.0 %copy-start.3 = (f32[6,512]{1,0:T(8,128)S(1)}, f32[6,512]{1,0:T(8,128)}, u32[]{:S(2)}) copy-start(f32[6,512]{1,0:T(8,128)} %param.25) | copy-start | bytes 36868
  7.2 475.0 %copy-start.6 = (f32[6,512]{1,0:T(8,128)S(1)}, f32[6,512]{1,0:T(8,128)}, u32[]{:S(2)}) copy-start(f32[6,512]{1,0:T(8,128)} %param.26) | copy-start | bytes 36868
  7.2 475.0 %copy-start.9 = (f32[6,512]{1,0:T(8,128)S(1)}, f32[6,512]{1,0:T(8,128)}, u32[]{:S(2)}) copy-start(f32[6,512]{1,0:T(8,128)} %param.27) | copy-start | bytes 36868
